TPU v7x, 32 devices: a whole 2x2x4 slice. The times are simulated.
32 devices in a mesh: grp: 2 (over y), ma: 4 (over z), af: 2 (over x), pa: 2 (over core).
Axes of the slice: x: 2, y: 2, z: 4, core: 2. Of those that a mesh axis runs over, the one named last changes fastest.
Arguments:
- panels: bfloat16 [64, 512, 2048], P('grp', ('af', 'ma'), 'pa'), parts along dimension 0, may hold values from -6 to 6
- svd_basis: bfloat16 [512, 2048, 256], P(('af', 'ma'), 'pa'), may hold values from -0.125 to 0.125
- kl_basis: bfloat16 [32, 128, 512], P(('pa', 'ma'), None, 'af'), may hold values from -0.25 to 0.25
- slot_of_m: int32 [32], replicated, may hold values from 0 to 31, as said below
- svd_keep: int32 [32], replicated, may hold values from 32 to 256, as said below
- kl_keep: int32 [32], replicated, may hold values from 16 to 128, as said below
Outputs:
- klmodes: float32 [64, 128, 256], P(('grp', 'pa', 'ma'), 'af'), parts along dimension 0
There are 2 independent parts, one for each index of `grp`. A program takes and returns all parts, laid end to end along the dimension named above; an argument that names none is the same for every part. Nothing has to cross between parts.
Inputs may be any that keep to these rules, and one draw needn't show every extreme that they name: `slot_of_m`: each slot 0 to 31 belongs to exactly one m-mode. `svd_keep`: over the m-modes of slots 4 * i to 4 * i + 3 the counts sum to at most 576, exactly 576 for some i. `kl_keep`: m-mode 0 keeps all 128; counts tend to fall with m.
All inputs are finite; a program needn't handle non-finite values.
Results may differ from a plain program's by a relative error of at most 0.0029.
Values may be sent and summed in bfloat16 or wider, within the bound.
No kernel may reach another device: no remote copies, remote signals or barrier semaphores. Data moves between devices by JAX's collectives and lax.ppermute only.
A program may use at most 128 MiB of HBM per device.

v0:
```python
import jax
import jax.numpy as jnp
from jax import lax
from jax.sharding import PartitionSpec as P


def shards(panels, svd_basis, kl_basis, slot_of_m, svd_keep, kl_keep):
    slot_count = slot_of_m.shape[0]
    order_slots = jnp.argsort(slot_of_m)
    keep_slots = jnp.take(svd_keep, order_slots, axis=0)
    modes_slots = jnp.take(kl_keep, order_slots, axis=0)
    width_modes = svd_basis.shape[2]
    owner_rows = kl_basis.shape[0]
    slot_rows = slot_count // lax.axis_size("pa")
    slot_start = lax.axis_index("pa") * slot_rows
    owner_start = slot_start + lax.axis_index("ma") * owner_rows
    modes_owner = lax.dynamic_slice_in_dim(modes_slots, owner_start, owner_rows, 0)
    chosen = jnp.take(panels, order_slots, axis=0)
    summed_whole = lax.psum(
        jnp.einsum("mfb,fbr->mfr", chosen, svd_basis, preferred_element_type=jnp.float32), "pa"
    )
    summed = lax.dynamic_slice_in_dim(summed_whole, slot_start, slot_rows, 0)
    keep_here = lax.dynamic_slice_in_dim(keep_slots, slot_start, slot_rows, 0)
    columns = jnp.arange(width_modes, dtype=jnp.int32)
    retained = jnp.where(columns[None, None, :] < keep_here[:, None, None], summed, 0.0).astype(
        jnp.bfloat16
    )
    relaid = lax.all_to_all(retained, "ma", split_axis=0, concat_axis=1, tiled=True)
    partial_sums = jnp.einsum("mkf,mfr->mkr", kl_basis, relaid, preferred_element_type=jnp.float32)
    modes = jnp.arange(kl_basis.shape[1], dtype=jnp.int32)
    partial_sums = jnp.where(modes[None, :, None] < modes_owner[:, None, None], partial_sums, 0.0)
    summed_all = lax.psum(partial_sums, "af")
    share_rows = kl_basis.shape[1] // lax.axis_size("af")
    return lax.dynamic_slice_in_dim(summed_all, lax.axis_index("af") * share_rows, share_rows, 1)


def solution(mesh):
    in_specs = (
        P("grp", ("af", "ma"), "pa"),
        P(("af", "ma"), "pa", None),
        P(("pa", "ma"), None, "af"),
        P(),
        P(),
        P(),
    )
    out_specs = P(("grp", "pa", "ma"), "af", None)
    return jax.shard_map(shards, mesh=mesh, in_specs=in_specs, out_specs=out_specs, check_vma=False)
```

profile of v0, /device:TPU:0, one launch (start us, length us, event | category | flops | bytes accessed | tf_op | source)
XLA Modules:
  0.0 107.2 jit_solution(3938520246957020169)
XLA Ops:
  6.5 0.0 copy-start
  6.5 2.3 %sort.17 = (s32[32]{0:T(128)}, s32[32]{0:T(128)S(1)}) sort(s32[32]{0:T(128)} %param.11, s32[32]{0:T(128)S(1)} %iota.20), dimensions={0}, to_apply=%region_0.0 | sort | flops 160 | bytes 512 | tf_op jit(solution)/shard_map/jit(argsort)/sort | solution.py:9
  8.9 0.0 copy-start.1
  8.9 4.9 %gather_fusion = bf16[32,64,1024]{2,1,0:T(8,128)(2,1)} fusion(bf16[32,64,1024]{2,1,0:T(8,128)(2,1)} %param.8, s32[1024]{0:T(1024)S(1)} %pad_clamp_fusion), kind=kCustom, calls=%fused_computation.2 | custom fusion | bytes 8388736 | tf_op jit(solution)/shard_map/jit(_take)/gather | solution.py:18
  13.8 0.0 copy-done.1
  13.8 0.7 gather_fusion.1
  14.5 4.6 %broadcast_select_fusion = bf16[32,64,1024]{2,1,0:T(8,128)(2,1)} fusion(bf16[32,64,1024]{2,1,0:T(8,128)(2,1)} %gather_fusion, pred[32]{0:T(512)(128)(4,1)S(1)} %get-tuple-element.9), kind=kLoop, calls=%fused_computation.5 | loop fusion | flops 2097152 | bytes 8388640 | tf_op jit(solution)/shard_map/jit(_take)/select_n | solution.py:18
  19.1 0.0 copy-start.2
  19.1 17.7 %fusion.2 = f32[32,64,256]{2,0,1:T(8,128)S(1)} fusion(bf16[64,1024,256]{2,1,0:T(8,128)(2,1)} %param.9, bf16[32,64,1024]{2,1,0:T(8,128)(2,1)} %broadcast_select_fusion), kind=kOutput, calls=%fused_computation.6 | convolution fusion | flops 1073741824 | bytes 39845888 | tf_op jit(solution)/shard_map/mfb,fbr->mfr/dot_general | solution.py:20
  36.8 9.3 %all-reduce.4 = bf16[32,64,256]{2,0,1:T(8,128)(2,1)S(1)} all-reduce(f32[32,64,256]{2,0,1:T(8,128)S(1)} %fusion.2), channel_id=1, replica_groups=mesh['grp'=2,'ma'=4,'af'=2,'pa'=2] {'pa'}, use_global_device_ids=true, to_apply=%region_1.3 | all-reduce | flops 524288 | bytes 3145728 | tf_op jit(solution)/shard_map/psum | solution.py:19
  46.1 0.0 copy-done.2
  46.1 0.7 gather_fusion.2
  46.8 0.1 dynamic_slice.13
  46.9 0.1 iota_compare_fusion
  47.0 0.1 select_convert_fusion
  47.1 0.9 copy.19
  48.1 6.0 %all-to-all-start = ((bf16[16,64,256]{2,1,0:T(8,128)(2,1)}), bf16[16,64,256]{2,1,0:T(8,128)(2,1)S(1)}, u32[]{:S(2)}, u32[]{:S(2)}) async-start(bf16[16,64,256]{2,1,0:T(8,128)(2,1)} %copy.19), calls=%async_computation | async-start | bytes 1048576 | tf_op jit(solution)/shard_map/all_to_all | solution.py:28
  54.1 0.0 all-reduce.3.cloned.1.call-start
  54.1 0.1 dynamic_slice.12
  54.2 0.1 iota_compare_fusion.1
  54.2 14.9 %all-to-all-done = bf16[16,64,256]{2,1,0:T(8,128)(2,1)S(1)} async-done(((bf16[16,64,256]{2,1,0:T(8,128)(2,1)}), bf16[16,64,256]{2,1,0:T(8,128)(2,1)S(1)}, u32[]{:S(2)}, u32[]{:S(2)}) %all-to-all-start) | async-done | bytes 524320 | tf_op jit(solution)/shard_map/all_to_all | solution.py:28
  69.1 0.0 copy-done
  69.1 1.2 %fusion.5 = f32[4,128,256]{1,2,0:T(8,128)} fusion(bf16[4,256,256]{2,1,0:T(8,128)(2,1)S(1)} %bitcast.11, bf16[4,128,256]{2,1,0:T(8,128)(2,1)S(1)} %copy-done, pred[4,128]{1,0:T(4,128)(4,1)S(1)} %iota_compare_fusion.1), kind=kOutput, calls=%fused_computation.8 | convolution fusion | flops 67239936 | bytes 1311232 | tf_op jit(solution)/shard_map/mkf,mfr->mkr/dot_general | solution.py:29
  70.3 0.0 all-reduce.3.cloned.1.call-update
  70.3 27.9 %all-reduce.3.cloned.1.call-done = f32[4,128,256]{1,2,0:T(8,128)} async-done(((f32[4,128,256]{1,2,0:T(8,128)}), f32[4,128,256]{1,2,0:T(8,128)}) %all-reduce.3.cloned.1.call-update) | async-done | bytes 524304 | tf_op jit(solution)/shard_map/psum | solution.py:32
  98.2 1.2 %constant_dynamic-slice_fusion = f32[4,64,256]{1,2,0:T(8,128)S(1)} fusion(f32[4,128,256]{1,2,0:T(8,128)} %all-reduce.3.cloned.1.call-done, s32[]{:T(128)S(6)} %select_n.43), kind=kLoop, calls=%fused_computation.15 | loop fusion | bytes 524292 | tf_op jit(solution)/shard_map/dynamic_slice | solution.py:34
  99.4 0.9 copy.22
  (6 shorter events, 0.1 us)
Async XLA Ops:
  6.5 62.6 %copy-start = (bf16[4,128,256]{2,1,0:T(8,128)(2,1)S(1)}, bf16[4,128,256]{2,1,0:T(8,128)(2,1)}, u32[]{:S(2)}) copy-start(bf16[4,128,256]{2,1,0:T(8,128)(2,1)} %param.10) | copy-start | bytes 786436
  8.9 4.9 %copy-start.1 = (s32[32]{0:T(128)S(1)}, s32[32]{0:T(128)}, u32[]{:S(2)}) copy-start(s32[32]{0:T(128)} %param.13) | copy-start | bytes 388
  19.1 27.0 %copy-start.2 = (s32[32]{0:T(128)S(1)}, s32[32]{0:T(128)}, u32[]{:S(2)}) copy-start(s32[32]{0:T(128)} %param.12) | copy-start | bytes 388
  48.1 21.0 %all-to-all-start = ((bf16[16,64,256]{2,1,0:T(8,128)(2,1)}), bf16[16,64,256]{2,1,0:T(8,128)(2,1)S(1)}, u32[]{:S(2)}, u32[]{:S(2)}) async-start(bf16[16,64,256]{2,1,0:T(8,128)(2,1)} %copy.19), calls=%async_computation | async-start | bytes 1048576 | tf_op jit(solution)/shard_map/all_to_all | solution.py:28
  54.1 44.1 %all-reduce.3.cloned.1.call-start = ((), (), s32[]{:S(2)}) async-start(), calls=%async_computation.1 | async-start | bytes 1048576 | tf_op jit(solution)/shard_map/psum | solution.py:32
Sparse Core Ops, SparseCore 0:
  70.4 27.6 all-reduce.2
where the time goes:
time: 107 us
  waiting for transfers between devices  42.7 us (40%)
  matrix products  18.9 us (18%)
  between operations  13.5 us (13%)
  local copies, waits for them, and re-layouts  9.61 us (9%)
  blocking collectives  9.28 us (9%)
  other arithmetic  7.19 us (7%)
  starting transfers between devices  6.02 us (6%)
    psum x1, waiting for transfers between devices, shards(): summed_all = lax.psum(partial_sums, 'af')  27.9 us
    dot_general x1, matrix products, shards(): jnp.einsum('mfb,fbr->mfr', chosen, svd_basis, preferred_element_type=jnp....  17.7 us
    all_to_all x1, waiting for transfers between devices, shards(): lax.all_to_all(retained, 'ma', split_axis=0, concat_axis=1, tiled=True)  14.9 us
    psum x1, blocking collectives, shards(): lax.psum(jnp.einsum('mfb,fbr->mfr', chosen, svd_basis, preferred_element_...  9.28 us
    all_to_all x1, starting transfers between devices, shards(): lax.all_to_all(retained, 'ma', split_axis=0, concat_axis=1, tiled=True)  6.02 us
    gather x1, local copies, waits for them, and re-layouts, shards(): chosen = jnp.take(panels, order_slots, axis=0)  4.93 us
    select_n x1, other arithmetic, shards(): chosen = jnp.take(panels, order_slots, axis=0)  4.59 us
    sort x1, other arithmetic, shards(): order_slots = jnp.argsort(slot_of_m)  2.3 us
  transfers between devices with their start and end apart: 2, of which 2 were waited for; matrix products, arithmetic and copies ran while one was open for 0% of the time, Pallas kernels for 0%

commit v1 on v0

v1 whole, which is shorter than its diff:
```python
import functools

import jax
import jax.numpy as jnp
from jax import lax
from jax.experimental import pallas as pl
from jax.experimental.pallas import tpu as pltpu
from jax.sharding import PartitionSpec as P

LANES = 128
GROUP = 16
OWNER_BUDGET = 576
MIB = 2**20


def shards_plain(panels, svd_basis, kl_basis, slot_of_m, svd_keep, kl_keep):
    slot_count = slot_of_m.shape[0]
    order_slots = jnp.argsort(slot_of_m)
    keep_slots = jnp.take(svd_keep, order_slots, axis=0)
    modes_slots = jnp.take(kl_keep, order_slots, axis=0)
    width_modes = svd_basis.shape[2]
    owner_rows = kl_basis.shape[0]
    slot_rows = slot_count // lax.axis_size("pa")
    slot_start = lax.axis_index("pa") * slot_rows
    owner_start = slot_start + lax.axis_index("ma") * owner_rows
    modes_owner = lax.dynamic_slice_in_dim(modes_slots, owner_start, owner_rows, 0)
    chosen = jnp.take(panels, order_slots, axis=0)
    summed = lax.psum_scatter(
        jnp.einsum("mfb,fbr->mfr", chosen, svd_basis, preferred_element_type=jnp.float32),
        "pa",
        scatter_dimension=0,
        tiled=True,
    )
    keep_here = lax.dynamic_slice_in_dim(keep_slots, slot_start, slot_rows, 0)
    columns = jnp.arange(width_modes, dtype=jnp.int32)
    retained = jnp.where(columns[None, None, :] < keep_here[:, None, None], summed, 0.0).astype(
        jnp.bfloat16
    )
    relaid = lax.all_to_all(retained, "ma", split_axis=0, concat_axis=1, tiled=True)
    partial_sums = jnp.einsum("mkf,mfr->mkr", kl_basis, relaid, preferred_element_type=jnp.float32)
    modes = jnp.arange(kl_basis.shape[1], dtype=jnp.int32)
    partial_sums = jnp.where(modes[None, :, None] < modes_owner[:, None, None], partial_sums, 0.0)
    return lax.psum_scatter(partial_sums, "af", scatter_dimension=1, tiled=True)


def cyclic(value, count):
    return lax.rem(value + count, count)


def packed_place(offset, width, span):
    last = (width - span) // LANES
    tile = jnp.minimum(lax.div(offset, LANES), last)
    return pl.multiple_of(tile * LANES, LANES), offset - tile * LANES


def project_kernel(
    start, owner_slots, slot_hbm, keep_hbm, panels, basis, mine, send,
    slot_s, keep_s, place_s, panels_v, basis_v, lhs_v, out_v, small_sem, panel_sem, basis_sem,
):
    slots = panels_v.shape[0]
    freqs = panels_v.shape[1]
    per_copy = freqs // basis_sem.shape[0]
    halves, owners = lax.axis_size("pa"), lax.axis_size("ma")
    my_half, my_owner = lax.axis_index("pa"), lax.axis_index("ma")
    half_slots = slots // halves
    width, modes = mine.shape[-1], basis.shape[-1]
    span = modes + LANES

    table_copies = [
        pltpu.make_async_copy(slot_hbm, slot_s, small_sem.at[0]),
        pltpu.make_async_copy(keep_hbm, keep_s, small_sem.at[1]),
    ]
    for copy in table_copies:
        copy.start()

    def basis_copy(i):
        return pltpu.make_async_copy(
            basis.at[pl.ds(start + i * per_copy, per_copy)],
            basis_v.at[pl.ds(i * per_copy, per_copy)],
            basis_sem.at[i],
        )

    for i in range(basis_sem.shape[0]):
        basis_copy(i).start()
    for copy in table_copies:
        copy.wait()

    @pl.loop(0, slots)
    def _(m):
        slot = slot_s[m]
        half = cyclic(lax.div(slot, half_slots) - my_half, halves)
        within = lax.rem(slot, half_slots)
        owner = cyclic(lax.div(within, owner_slots) - my_owner, owners)
        place = half * half_slots + owner * owner_slots + lax.rem(within, owner_slots)
        place_s[place] = keep_s[m]
        pltpu.make_async_copy(
            panels.at[m, pl.ds(start, freqs)], panels_v.at[place], panel_sem
        ).start()

    side = GROUP * GROUP
    row = lax.broadcasted_iota(jnp.int32, (side, side), 0)
    column = lax.broadcasted_iota(jnp.int32, (side, side), 1)
    swap = (column == (row % GROUP) * GROUP + row // GROUP).astype(jnp.float32).astype(jnp.bfloat16)
    lane = lax.broadcasted_iota(jnp.int32, (GROUP, modes), 1)
    blank = jnp.zeros((GROUP, LANES), jnp.float32)

    pltpu.make_async_copy(panels_v, panels_v, panel_sem).wait()

    for group in range(freqs // GROUP):
        here = slice(group * GROUP, (group + 1) * GROUP)
        for block in range(slots // GROUP):
            blocks = slice(block * GROUP, (block + 1) * GROUP)
            tile = panels_v[blocks, here, :].reshape(side, panels_v.shape[2])
            turned = jnp.dot(swap, tile, preferred_element_type=jnp.float32).astype(jnp.bfloat16)
            lhs_v[:, blocks, :] = turned.reshape(GROUP, GROUP, panels_v.shape[2])
        copies = GROUP // per_copy

        @pl.loop(0, copies)
        def _(i):
            basis_copy(group * copies + i).wait()
            for k in range(per_copy):
                f = i * per_copy + k
                out_v[f] = jnp.dot(
                    lhs_v[f], basis_v[group * GROUP + f], preferred_element_type=jnp.float32
                )

        for half in range(halves):
            to = (mine, send)[half]
            for owner in range(owners):
                to[owner, here, :] = jnp.zeros((GROUP, width), jnp.float32)
                offset = jnp.int32(0)
                for j in range(owner_slots):
                    place = half * half_slots + owner * owner_slots + j
                    keep = place_s[place]
                    kept = jnp.where(lane < keep, out_v[:, place, :], 0.0)
                    first, shift = packed_place(offset, width, span)
                    wide = jnp.concatenate([kept, blank], axis=1)
                    to[owner, here, pl.ds(first, span)] += pltpu.roll(wide, shift, 1)
                    offset = offset + keep


def owner_tables(slot_s, keep_s, table_s, slots):
    @pl.loop(0, slots)
    def _(m):
        table_s[slot_s[m]] = keep_s[m]


def kl_kernel(
    starts, counts, mine_too, slot_hbm, keep_hbm, rows_hbm, kl, *refs
):
    blocks = refs[: len(starts) * counts]
    rest = refs[len(starts) * counts :]
    send, mine, slot_s, keep_s, rows_s, keep_t, rows_t, packed_v, small_sem = rest
    owner_slots, rows, freqs = kl.shape
    slots = slot_s.shape[0]
    owners, shares = lax.axis_size("ma"), lax.axis_size("af")
    per_source = freqs // owners
    copies = [
        pltpu.make_async_copy(slot_hbm, slot_s, small_sem.at[0]),
        pltpu.make_async_copy(keep_hbm, keep_s, small_sem.at[1]),
        pltpu.make_async_copy(rows_hbm, rows_s, small_sem.at[2]),
    ]
    for copy in copies:
        copy.start()
    me = lax.axis_index("ma")
    for c, begin in enumerate(starts):
        for step in range(owners):
            block = blocks[c * owners + step]
            source = cyclic(me - step, owners)
            at = pl.multiple_of(source * per_source + begin, GROUP)
            packed_v[pl.ds(at, block.shape[0]), :] = block[...]
    for copy in copies:
        copy.wait()

    @pl.loop(0, slots)
    def _(m):
        keep_t[slot_s[m]] = keep_s[m]
        rows_t[slot_s[m]] = rows_s[m]

    width = send.shape[1]
    share_rows = rows // shares
    my_share = lax.axis_index("af")
    first = (lax.axis_index("pa") * owners + me) * owner_slots
    lane = lax.broadcasted_iota(jnp.int32, (share_rows, width), 1)
    line = lax.broadcasted_iota(jnp.int32, (share_rows, width), 0)
    for part, out in ((1, send), (0, mine)):
        share = cyclic(my_share + part, shares)
        at = pl.multiple_of(share * share_rows, GROUP)
        total = jnp.zeros((share_rows, width), jnp.float32)
        offset = jnp.int32(0)
        for j in range(owner_slots):
            keep = keep_t[first + j]
            product = jnp.dot(
                kl[j, pl.ds(at, share_rows), :], packed_v[...], preferred_element_type=jnp.float32
            )
            within = (lane >= offset) & (lane < offset + keep) & (line < rows_t[first + j] - at)
            total = jnp.where(within, product, total)
            offset = offset + keep
        out[...] = total.astype(out.dtype)


def final_kernel(slot_hbm, keep_hbm, mine, got, out, slot_s, keep_s, keep_t, sum_v, small_sem):
    owner_slots, rows, modes = out.shape
    slots = slot_s.shape[0]
    width = mine.shape[1]
    span = modes + LANES
    copies = [
        pltpu.make_async_copy(slot_hbm, slot_s, small_sem.at[0]),
        pltpu.make_async_copy(keep_hbm, keep_s, small_sem.at[1]),
    ]
    for copy in copies:
        copy.start()
    sum_v[...] = mine[...] + got[...].astype(jnp.float32)
    for copy in copies:
        copy.wait()

    @pl.loop(0, slots)
    def _(m):
        keep_t[slot_s[m]] = keep_s[m]

    first = (lax.axis_index("pa") * lax.axis_size("ma") + lax.axis_index("ma")) * owner_slots
    lane = lax.broadcasted_iota(jnp.int32, (rows, modes), 1)
    offset = jnp.int32(0)
    for j in range(owner_slots):
        keep = keep_t[first + j]
        at, shift = packed_place(offset, width, span)
        window = pltpu.roll(sum_v[:, pl.ds(at, span)], lax.rem(span - shift, span), 1)
        out[j] = jnp.where(lane < keep, window[:, :modes], 0.0)
        offset = offset + keep


ANY = pl.BlockSpec(memory_space=pl.ANY)
VMEM = pl.BlockSpec(memory_space=pltpu.VMEM)


def project(panels, svd_basis, slot_of_m, svd_keep, start, freqs, owner_slots, width):
    slots, _, depth = panels.shape
    modes = svd_basis.shape[2]
    owners = lax.axis_size("ma")
    shape = jax.ShapeDtypeStruct((owners, freqs, width), jnp.float32)
    return pl.pallas_call(
        functools.partial(project_kernel, start, owner_slots),
        out_shape=(shape, shape),
        in_specs=[ANY] * 4,
        out_specs=(VMEM, VMEM),
        scratch_shapes=[
            pltpu.SMEM((slots,), jnp.int32),
            pltpu.SMEM((slots,), jnp.int32),
            pltpu.SMEM((slots,), jnp.int32),
            pltpu.VMEM((slots, freqs, depth), jnp.bfloat16),
            pltpu.VMEM((freqs, depth, modes), jnp.bfloat16),
            pltpu.VMEM((GROUP, slots, depth), jnp.bfloat16),
            pltpu.VMEM((GROUP, slots, modes), jnp.float32),
            pltpu.SemaphoreType.DMA((2,)),
            pltpu.SemaphoreType.DMA,
            pltpu.SemaphoreType.DMA((freqs // 4,)),
        ],
        compiler_params=pltpu.CompilerParams(vmem_limit_bytes=40 * MIB),
        cost_estimate=pl.CostEstimate(
            flops=2 * slots * freqs * depth * modes,
            bytes_accessed=2 * freqs * depth * (modes + slots),
            transcendentals=0,
        ),
        name="project",
    )(slot_of_m, svd_keep, panels, svd_basis)


def kl_project(kl_basis, slot_of_m, svd_keep, kl_keep, blocks, starts, width):
    owners, shares = lax.axis_size("ma"), lax.axis_size("af")
    slots = slot_of_m.shape[0]
    rows, freqs = kl_basis.shape[1:]
    return pl.pallas_call(
        functools.partial(kl_kernel, starts, owners, True),
        out_shape=(
            jax.ShapeDtypeStruct((rows // shares, width), jnp.bfloat16),
            jax.ShapeDtypeStruct((rows // shares, width), jnp.float32),
        ),
        in_specs=[ANY] * 3 + [VMEM] * (1 + len(blocks)),
        out_specs=(VMEM, VMEM),
        scratch_shapes=[pltpu.SMEM((slots,), jnp.int32)] * 5
        + [pltpu.VMEM((freqs, width), jnp.bfloat16), pltpu.SemaphoreType.DMA((3,))],
        cost_estimate=pl.CostEstimate(
            flops=2 * kl_basis.size * width, bytes_accessed=2 * kl_basis.size, transcendentals=0
        ),
        name="kl_project",
    )(slot_of_m, svd_keep, kl_keep, kl_basis, *blocks)


def unpack(mine, got, slot_of_m, svd_keep, owner_slots, modes):
    slots = slot_of_m.shape[0]
    rows, width = mine.shape
    return pl.pallas_call(
        final_kernel,
        out_shape=jax.ShapeDtypeStruct((owner_slots, rows, modes), jnp.float32),
        in_specs=[ANY] * 2 + [VMEM] * 2,
        out_specs=VMEM,
        scratch_shapes=[pltpu.SMEM((slots,), jnp.int32)] * 3
        + [pltpu.VMEM((rows, width), jnp.float32), pltpu.SemaphoreType.DMA((2,))],
        cost_estimate=pl.CostEstimate(
            flops=rows * width, bytes_accessed=10 * rows * width, transcendentals=0
        ),
        name="unpack",
    )(slot_of_m, svd_keep, mine, got)


def ring(axis, step):
    size = lax.axis_size(axis)
    return [(i, (i + step) % size) for i in range(size)]


def shards(panels, svd_basis, kl_basis, slot_of_m, svd_keep, kl_keep):
    freqs = svd_basis.shape[0]
    owner_slots, modes = kl_basis.shape[0], svd_basis.shape[2]
    owners = lax.axis_size("ma")
    width = -(-min(OWNER_BUDGET, owner_slots * modes) // LANES) * LANES
    chunk = GROUP
    starts = tuple(range(0, freqs, chunk))
    blocks = []
    for start in starts:
        mine, send = project(
            panels, svd_basis, slot_of_m, svd_keep, start, chunk, owner_slots, width
        )
        got = lax.ppermute(send, "pa", ring("pa", 1))
        summed = [(mine[step] + got[step]).astype(jnp.bfloat16) for step in range(owners)]
        blocks += [summed[0]] + [
            lax.ppermute(summed[step], "ma", ring("ma", step)) for step in range(1, owners)
        ]
    send, mine = kl_project(kl_basis, slot_of_m, svd_keep, kl_keep, blocks, starts, width)
    got = lax.ppermute(send, "af", ring("af", 1))
    return unpack(mine, got, slot_of_m, svd_keep, owner_slots, modes)


def kernels_fit(mesh, args):
    panels, svd_basis, kl_basis = args[:3]
    slots = panels.shape[0] // mesh.shape["grp"]
    freqs = svd_basis.shape[0] // (mesh.shape["af"] * mesh.shape["ma"])
    owner_slots = kl_basis.shape[0] // (mesh.shape["pa"] * mesh.shape["ma"])
    share_rows = kl_basis.shape[1] // mesh.shape["af"]
    return (
        freqs % GROUP == 0
        and slots % (GROUP * mesh.shape["pa"]) == 0
        and owner_slots == 4
        and svd_basis.shape[2] == 2 * LANES
        and share_rows % GROUP == 0
        and mesh.shape["pa"] == 2
        and mesh.shape["af"] == 2
        and mesh.shape["ma"] <= 4
    )


def solution(mesh):
    in_specs = (
        P("grp", ("af", "ma"), "pa"),
        P(("af", "ma"), "pa", None),
        P(("pa", "ma"), None, "af"),
        P(),
        P(),
        P(),
    )
    out_specs = P(("grp", "pa", "ma"), "af", None)

    def run(*args):
        body = shards if kernels_fit(mesh, args) else shards_plain
        mapped = jax.shard_map(
            body, mesh=mesh, in_specs=in_specs, out_specs=out_specs, check_vma=False
        )
        return mapped(*args)

    return run
```

time: 107 us -> 65.1 us (0.61)
  waiting for transfers between devices: 42.7 us -> 8.69 us
  Pallas kernels: 0 us -> 27.2 us
  matrix products: 18.9 us -> 0 us
  starting transfers between devices: 6.02 us -> 21.6 us
  between operations: 13.5 us -> 0.17 us
  blocking collectives: 9.28 us -> 0 us
  local copies, waits for them, and re-layouts: 9.61 us -> 4.68 us
  other arithmetic: 7.19 us -> 2.48 us
    psum x1 -> x0, waiting for transfers between devices: 27.9 us -> none  [shards(): summed_all = lax.psum(partial_sums, 'af')]
    pallas_call x0 -> x6, Pallas kernels: none -> 27.2 us  [the longest x4 21.2 us: project(): pl.pallas_call(functools.partial(project_kernel, start, owner_slots), out...]
    ppermute x0 -> x17, starting transfers between devices: none -> 21.6 us  [the longest x12 18.8 us: shards(): lax.ppermute(summed[step], 'ma', ring('ma', step))]
    dot_general x2 -> x0, matrix products: 18.9 us -> none  [the longest x1 17.7 us: shards(): jnp.einsum('mfb,fbr->mfr', chosen, svd_basis, preferred_element_type=jnp....]
    all_to_all x1 -> x0, waiting for transfers between devices: 14.9 us -> none  [shards(): lax.all_to_all(retained, 'ma', split_axis=0, concat_axis=1, tiled=True)]
    psum x1 -> x0, blocking collectives: 9.28 us -> none  [shards(): lax.psum(jnp.einsum('mfb,fbr->mfr', chosen, svd_basis, preferred_element_...]
    ppermute x0 -> x17, waiting for transfers between devices: none -> 8.69 us  [the longest x12 5.52 us: shards(): lax.ppermute(summed[step], 'ma', ring('ma', step))]
    gather x3 -> x0, local copies, waits for them, and re-layouts: 6.33 us -> none  [the longest x1 4.93 us: shards(): chosen = jnp.take(panels, order_slots, axis=0)]
  transfers between devices with their start and end apart: 2 -> 17, of which waited for: 2 -> 4; matrix products, arithmetic and copies ran while one was open for 0% -> 4% of each run, Pallas kernels for 0% -> 25%
where the time goes in v1:
time: 65.1 us; the launch traced here: 64.9 us
  Pallas kernels  27.2 us (42%)
  starting transfers between devices  21.6 us (33%)
  waiting for transfers between devices  8.69 us (13%)
  local copies, waits for them, and re-layouts  4.68 us (7%)
  other arithmetic  2.48 us (4%)
    pallas_call x4, Pallas kernels, project(): pl.pallas_call(functools.partial(project_kernel, start, owner_slots), out...  21.2 us
    ppermute x12, starting transfers between devices, shards(): lax.ppermute(summed[step], 'ma', ring('ma', step))  18.8 us
    ppermute x12, waiting for transfers between devices, shards(): lax.ppermute(summed[step], 'ma', ring('ma', step))  5.52 us
    unnamed x32, local copies, waits for them, and re-layouts  4.68 us
    pallas_call x1, Pallas kernels, kl_project(): pl.pallas_call(functools.partial(kl_kernel, starts, owners, True), out_sh...  3.24 us
    ppermute x1, waiting for transfers between devices, shards(): got = lax.ppermute(send, 'af', ring('af', 1))  3.16 us
    pallas_call x1, Pallas kernels, unpack(): pl.pallas_call(final_kernel, out_shape=jax.ShapeDtypeStruct((owner_slots,...  2.73 us
    convert_element_type x4, other arithmetic, shards(): (mine[step] + got[step]).astype(jnp.bfloat16)  2.48 us
  transfers between devices with their start and end apart: 17, of which 4 were waited for; matrix products, arithmetic and copies ran while one was open for 4% of the time, Pallas kernels for 25%

profile of v1, /device:TPU:0, one launch (start us, length us, event | category | flops | bytes accessed | tf_op | source)
XLA Modules:
  0.0 64.9 jit_solution(13609159619011988303)
XLA Ops:
  0.0 2.2 %copy-done = bf16[32,64,1024]{2,1,0:T(8,128)(2,1)S(1)} copy-done((bf16[32,64,1024]{2,1,0:T(8,128)(2,1)S(1)}, bf16[32,64,1024]{2,1,0:T(8,128)(2,1)}, u32[]{:S(2)}) %copy-start) | copy-done | bytes 4194328
  2.2 0.7 %copy-done.1 = s32[32]{0:T(128)S(1)} copy-done((s32[32]{0:T(128)S(1)}, s32[32]{0:T(128)}, u32[]{:S(2)}) %copy-start.1) | copy-done | bytes 152
  2.8 0.7 %copy-done.2 = s32[32]{0:T(128)S(1)} copy-done((s32[32]{0:T(128)S(1)}, s32[32]{0:T(128)}, u32[]{:S(2)}) %copy-start.2) | copy-done | bytes 152
  3.5 5.3 %project.5 = (f32[4,16,640]{2,1,0:T(8,128)S(1)}, f32[4,16,640]{2,1,0:T(8,128)S(1)}) custom-call(s32[32]{0:T(128)S(1)} %copy-done.1, s32[32]{0:T(128)S(1)} %copy-done.2, bf16[32,64,1024]{2,1,0:T(8,128)(2,1)S(1)} %copy-done, bf16[64,1024,256]{2,1,0:T(8,128)(2,1)} %basis.7), custom_call_target="tpu_custom_call" | custom-call | flops 268435456 | bytes 9437184 | tf_op jit(solution)/shard_map/project/pallas_call | solution.py:241
  8.8 0.5 collective-permute-start.4
  9.3 5.3 %project.4 = (f32[4,16,640]{2,1,0:T(8,128)S(1)}, f32[4,16,640]{2,1,0:T(8,128)S(1)}) custom-call(s32[32]{0:T(128)S(1)} %copy-done.1, s32[32]{0:T(128)S(1)} %copy-done.2, bf16[32,64,1024]{2,1,0:T(8,128)(2,1)S(1)} %copy-done, bf16[64,1024,256]{2,1,0:T(8,128)(2,1)} %basis.7), custom_call_target="tpu_custom_call" | custom-call | flops 268435456 | bytes 9437184 | tf_op jit(solution)/shard_map/project/pallas_call | solution.py:241
  14.6 0.1 collective-permute-start
  14.8 5.3 %project.7 = (f32[4,16,640]{2,1,0:T(8,128)S(1)}, f32[4,16,640]{2,1,0:T(8,128)S(1)}) custom-call(s32[32]{0:T(128)S(1)} %copy-done.1, s32[32]{0:T(128)S(1)} %copy-done.2, bf16[32,64,1024]{2,1,0:T(8,128)(2,1)S(1)} %copy-done, bf16[64,1024,256]{2,1,0:T(8,128)(2,1)} %basis.7), custom_call_target="tpu_custom_call" | custom-call | flops 268435456 | bytes 9437184 | tf_op jit(solution)/shard_map/project/pallas_call | solution.py:241
  20.1 0.5 collective-permute-start.12
  20.6 5.3 %project.6 = (f32[4,16,640]{2,1,0:T(8,128)S(1)}, f32[4,16,640]{2,1,0:T(8,128)S(1)}) custom-call(s32[32]{0:T(128)S(1)} %copy-done.1, s32[32]{0:T(128)S(1)} %copy-done.2, bf16[32,64,1024]{2,1,0:T(8,128)(2,1)S(1)} %copy-done, bf16[64,1024,256]{2,1,0:T(8,128)(2,1)} %basis.7), custom_call_target="tpu_custom_call" | custom-call | flops 268435456 | bytes 9437184 | tf_op jit(solution)/shard_map/project/pallas_call | solution.py:241
  25.9 0.1 collective-permute-start.8
  26.1 0.0 collective-permute-done.4
  26.1 0.6 fusion.23
  26.7 5.0 %collective-permute-start.7 = (bf16[16,640]{1,0:T(8,128)(2,1)S(1)}, bf16[16,640]{1,0:T(8,128)(2,1)S(1)}, u32[]{:S(2)}, u32[]{:S(2)}) collective-permute-start(bf16[16,640]{1,0:T(8,128)(2,1)S(1)} %get-tuple-element.33), channel_id=1, source_target_pairs={{0,12},{4,0},{8,4},{12,8},{1,13},{5,1},{9,5},{13,9},{2,14},{6,2},{... | collective-permute-start | bytes 61448 | tf_op jit(solution)/shard_map/ppermute | solution.py:326
  31.7 0.0 collective-permute-start.6
  31.7 0.0 collective-permute-done
  31.7 1.0 %collective-permute-start.5 = (bf16[16,640]{1,0:T(8,128)(2,1)S(1)}, bf16[16,640]{1,0:T(8,128)(2,1)S(1)}, u32[]{:S(2)}, u32[]{:S(2)}) collective-permute-start(bf16[16,640]{1,0:T(8,128)(2,1)S(1)} %get-tuple-element.35), channel_id=1, source_target_pairs={{0,4},{4,8},{8,12},{12,0},{1,5},{5,9},{9,13},{13,1},{2,6},{6,10},{... | collective-permute-start | bytes 61448 | tf_op jit(solution)/shard_map/ppermute | solution.py:326
  32.7 0.6 fusion.19
  33.3 0.0 collective-permute-done.12
  33.3 2.8 %collective-permute-start.3 = (bf16[16,640]{1,0:T(8,128)(2,1)S(1)}, bf16[16,640]{1,0:T(8,128)(2,1)S(1)}, u32[]{:S(2)}, u32[]{:S(2)}) collective-permute-start(bf16[16,640]{1,0:T(8,128)(2,1)S(1)} %get-tuple-element.37), channel_id=1, source_target_pairs={{0,12},{4,0},{8,4},{12,8},{1,13},{5,1},{9,5},{13,9},{2,14},{6,2},{... | collective-permute-start | bytes 61448 | tf_op jit(solution)/shard_map/ppermute | solution.py:326
  36.2 0.6 fusion.31
  36.8 0.0 collective-permute-done.8
  36.8 1.1 %collective-permute-start.2 = (bf16[16,640]{1,0:T(8,128)(2,1)S(1)}, bf16[16,640]{1,0:T(8,128)(2,1)S(1)}, u32[]{:S(2)}, u32[]{:S(2)}) collective-permute-start(bf16[16,640]{1,0:T(8,128)(2,1)S(1)} %get-tuple-element.38), channel_id=1, source_target_pairs={{0,8},{4,12},{8,0},{12,4},{1,9},{5,13},{9,1},{13,5},{2,10},{6,14},... | collective-permute-start | bytes 61448 | tf_op jit(solution)/shard_map/ppermute | solution.py:326
  37.9 0.0 collective-permute-done.7.refs_7_
  37.9 0.0 collective-permute-start.1
  37.9 0.0 collective-permute-done.6.refs_6_
  37.9 3.8 %collective-permute-start.15 = (bf16[16,640]{1,0:T(8,128)(2,1)S(1)}, bf16[16,640]{1,0:T(8,128)(2,1)S(1)}, u32[]{:S(2)}, u32[]{:S(2)}) collective-permute-start(bf16[16,640]{1,0:T(8,128)(2,1)S(1)} %get-tuple-element.25), channel_id=1, source_target_pairs={{0,12},{4,0},{8,4},{12,8},{1,13},{5,1},{9,5},{13,9},{2,14},{6,2},{... | collective-permute-start | bytes 61448 | tf_op jit(solution)/shard_map/ppermute | solution.py:326
  41.8 0.6 fusion.27
  42.4 0.0 collective-permute-done.5.refs_5_
  42.4 0.0 collective-permute-start.14
  42.4 0.0 collective-permute-done.3.refs_3_
  42.4 0.6 collective-permute-start.13
  43.0 0.0 collective-permute-done.2.refs_2_
  43.0 3.3 %collective-permute-start.11 = (bf16[16,640]{1,0:T(8,128)(2,1)S(1)}, bf16[16,640]{1,0:T(8,128)(2,1)S(1)}, u32[]{:S(2)}, u32[]{:S(2)}) collective-permute-start(bf16[16,640]{1,0:T(8,128)(2,1)S(1)} %get-tuple-element.29), channel_id=1, source_target_pairs={{0,12},{4,0},{8,4},{12,8},{1,13},{5,1},{9,5},{13,9},{2,14},{6,2},{... | collective-permute-start | bytes 61448 | tf_op jit(solution)/shard_map/ppermute | solution.py:326
  46.3 0.0 collective-permute-done.1.refs_1_
  46.3 1.1 %collective-permute-start.10 = (bf16[16,640]{1,0:T(8,128)(2,1)S(1)}, bf16[16,640]{1,0:T(8,128)(2,1)S(1)}, u32[]{:S(2)}, u32[]{:S(2)}) collective-permute-start(bf16[16,640]{1,0:T(8,128)(2,1)S(1)} %get-tuple-element.30), channel_id=1, source_target_pairs={{0,8},{4,12},{8,0},{12,4},{1,9},{5,13},{9,1},{13,5},{2,10},{6,14},... | collective-permute-start | bytes 61448 | tf_op jit(solution)/shard_map/ppermute | solution.py:326
  47.4 0.0 collective-permute-done.15.refs_15_
  47.4 0.1 collective-permute-start.9
  47.4 0.6 collective-permute-done.13.refs_13_
  48.1 0.0 collective-permute-done.11.refs_11_
  48.1 2.9 %collective-permute-done.10.refs_10_ = bf16[16,640]{1,0:T(8,128)(2,1)S(1)} collective-permute-done((bf16[16,640]{1,0:T(8,128)(2,1)S(1)}, bf16[16,640]{1,0:T(8,128)(2,1)S(1)}, u32[]{:S(2)}, u32[]{:S(2)}) %collective-permute-start.10) | collective-permute-done | bytes 20512 | tf_op jit(solution)/shard_map/ppermute | solution.py:326
  51.0 2.0 %collective-permute-done.9.refs_9_ = bf16[16,640]{1,0:T(8,128)(2,1)S(1)} collective-permute-done((bf16[16,640]{1,0:T(8,128)(2,1)S(1)}, bf16[16,640]{1,0:T(8,128)(2,1)S(1)}, u32[]{:S(2)}, u32[]{:S(2)}) %collective-permute-start.9) | collective-permute-done | bytes 20512 | tf_op jit(solution)/shard_map/ppermute | solution.py:326
  53.0 0.5 copy-done.15
  53.6 3.2 %kl_project.1 = (bf16[64,640]{1,0:T(8,128)(2,1)}, f32[64,640]{1,0:T(8,128)}) custom-call(s32[32]{0:T(128)} %slot_hbm.11, s32[32]{0:T(128)} %keep_hbm.11, s32[32]{0:T(128)} %rows_hbm.1, bf16[4,128,256]{2,1,0:T(8,128)(2,1)} %kl.1, bf16[16,640]{1,0:T(8,128)(2,1)} %get-tuple-element.40.refs_0_, bf16[16,640]{1,0:T(8,128)(2,1)} %copy-done.9, ...), custom_call_target="tpu_custom_call" | custom-call | flops 167772160 | bytes 262144 | tf_op jit(solution)/shard_map/kl_project/pallas_call | solution.py:272
  56.8 1.6 %collective-permute-start.16 = (bf16[64,640]{1,0:T(8,128)(2,1)}, bf16[64,640]{1,0:T(8,128)(2,1)S(1)}, u32[]{:S(2)}, u32[]{:S(2)}) collective-permute-start(bf16[64,640]{1,0:T(8,128)(2,1)} %get-tuple-element.24), channel_id=1, source_target_pairs={{0,2},{2,0},{1,3},{3,1},{4,6},{6,4},{5,7},{7,5},{8,10},{10,8},{9,1... | collective-permute-start | bytes 245768 | tf_op jit(solution)/shard_map/ppermute | solution.py:329
  58.4 3.2 %collective-permute-done.16.got = bf16[64,640]{1,0:T(8,128)(2,1)S(1)} collective-permute-done((bf16[64,640]{1,0:T(8,128)(2,1)}, bf16[64,640]{1,0:T(8,128)(2,1)S(1)}, u32[]{:S(2)}, u32[]{:S(2)}) %collective-permute-start.16) | collective-permute-done | bytes 81952 | tf_op jit(solution)/shard_map/ppermute | solution.py:329
  61.5 0.6 copy-done.3
  62.2 2.7 %unpack.1 = f32[4,64,256]{2,1,0:T(8,128)} custom-call(s32[32]{0:T(128)} %slot_hbm.11, s32[32]{0:T(128)} %keep_hbm.11, f32[64,640]{1,0:T(8,128)} %get-tuple-element.23.mine, bf16[64,640]{1,0:T(8,128)(2,1)} %copy-done.3), custom_call_target="tpu_custom_call" | custom-call | flops 40960 | bytes 409600 | tf_op jit(solution)/shard_map/unpack/pallas_call | solution.py:292
  (28 shorter events, 0.1 us)
Async XLA Ops:
  0.0 2.2 %copy-start = (bf16[32,64,1024]{2,1,0:T(8,128)(2,1)S(1)}, bf16[32,64,1024]{2,1,0:T(8,128)(2,1)}, u32[]{:S(2)}) copy-start(bf16[32,64,1024]{2,1,0:T(8,128)(2,1)} %panels.7) | copy-start | bytes 12582916
  2.2 0.7 %copy-start.1 = (s32[32]{0:T(128)S(1)}, s32[32]{0:T(128)}, u32[]{:S(2)}) copy-start(s32[32]{0:T(128)} %slot_hbm.11) | copy-start | bytes 388
  2.8 0.7 %copy-start.2 = (s32[32]{0:T(128)S(1)}, s32[32]{0:T(128)}, u32[]{:S(2)}) copy-start(s32[32]{0:T(128)} %keep_hbm.11) | copy-start | bytes 388
  8.8 17.2 %collective-permute-start.4 = (f32[4,16,640]{2,1,0:T(8,128)S(1)}, f32[4,16,640]{2,1,0:T(8,128)S(1)}, u32[]{:S(2)}, u32[]{:S(2)}) collective-permute-start(f32[4,16,640]{2,1,0:T(8,128)S(1)} %get-tuple-element.18), channel_id=1, source_target_pairs={{0,1},{1,0},{2,3},{3,2},{4,5},{5,4},{6,7},{7,6},{8,9},{9,8},{10,11... | collective-permute-start | bytes 491528 | tf_op jit(solution)/shard_map/ppermute | solution.py:323
  14.6 17.1 %collective-permute-start = (f32[4,16,640]{2,1,0:T(8,128)S(1)}, f32[4,16,640]{2,1,0:T(8,128)S(1)}, u32[]{:S(2)}, u32[]{:S(2)}) collective-permute-start(f32[4,16,640]{2,1,0:T(8,128)S(1)} %get-tuple-element.16), channel_id=1, source_target_pairs={{0,1},{1,0},{2,3},{3,2},{4,5},{5,4},{6,7},{7,6},{8,9},{9,8},{10,11... | collective-permute-start | bytes 491528 | tf_op jit(solution)/shard_map/ppermute | solution.py:323
  20.1 13.3 %collective-permute-start.12 = (f32[4,16,640]{2,1,0:T(8,128)S(1)}, f32[4,16,640]{2,1,0:T(8,128)S(1)}, u32[]{:S(2)}, u32[]{:S(2)}) collective-permute-start(f32[4,16,640]{2,1,0:T(8,128)S(1)} %get-tuple-element.22), channel_id=1, source_target_pairs={{0,1},{1,0},{2,3},{3,2},{4,5},{5,4},{6,7},{7,6},{8,9},{9,8},{10,11... | collective-permute-start | bytes 491528 | tf_op jit(solution)/shard_map/ppermute | solution.py:323
  25.9 10.9 %collective-permute-start.8 = (f32[4,16,640]{2,1,0:T(8,128)S(1)}, f32[4,16,640]{2,1,0:T(8,128)S(1)}, u32[]{:S(2)}, u32[]{:S(2)}) collective-permute-start(f32[4,16,640]{2,1,0:T(8,128)S(1)} %get-tuple-element.20), channel_id=1, source_target_pairs={{0,1},{1,0},{2,3},{3,2},{4,5},{5,4},{6,7},{7,6},{8,9},{9,8},{10,11... | collective-permute-start | bytes 491528 | tf_op jit(solution)/shard_map/ppermute | solution.py:323
  26.7 11.2 %collective-permute-start.7 = (bf16[16,640]{1,0:T(8,128)(2,1)S(1)}, bf16[16,640]{1,0:T(8,128)(2,1)S(1)}, u32[]{:S(2)}, u32[]{:S(2)}) collective-permute-start(bf16[16,640]{1,0:T(8,128)(2,1)S(1)} %get-tuple-element.33), channel_id=1, source_target_pairs={{0,12},{4,0},{8,4},{12,8},{1,13},{5,1},{9,5},{13,9},{2,14},{6,2},{... | collective-permute-start | bytes 61448 | tf_op jit(solution)/shard_map/ppermute | solution.py:326
  31.7 6.2 %collective-permute-start.6 = (bf16[16,640]{1,0:T(8,128)(2,1)S(1)}, bf16[16,640]{1,0:T(8,128)(2,1)S(1)}, u32[]{:S(2)}, u32[]{:S(2)}) collective-permute-start(bf16[16,640]{1,0:T(8,128)(2,1)S(1)} %get-tuple-element.34), channel_id=1, source_target_pairs={{0,8},{4,12},{8,0},{12,4},{1,9},{5,13},{9,1},{13,5},{2,10},{6,14},... | collective-permute-start | bytes 61448 | tf_op jit(solution)/shard_map/ppermute | solution.py:326
  31.7 10.7 %collective-permute-start.5 = (bf16[16,640]{1,0:T(8,128)(2,1)S(1)}, bf16[16,640]{1,0:T(8,128)(2,1)S(1)}, u32[]{:S(2)}, u32[]{:S(2)}) collective-permute-start(bf16[16,640]{1,0:T(8,128)(2,1)S(1)} %get-tuple-element.35), channel_id=1, source_target_pairs={{0,4},{4,8},{8,12},{12,0},{1,5},{5,9},{9,13},{13,1},{2,6},{6,10},{... | collective-permute-start | bytes 61448 | tf_op jit(solution)/shard_map/ppermute | solution.py:326
  33.3 9.1 %collective-permute-start.3 = (bf16[16,640]{1,0:T(8,128)(2,1)S(1)}, bf16[16,640]{1,0:T(8,128)(2,1)S(1)}, u32[]{:S(2)}, u32[]{:S(2)}) collective-permute-start(bf16[16,640]{1,0:T(8,128)(2,1)S(1)} %get-tuple-element.37), channel_id=1, source_target_pairs={{0,12},{4,0},{8,4},{12,8},{1,13},{5,1},{9,5},{13,9},{2,14},{6,2},{... | collective-permute-start | bytes 61448 | tf_op jit(solution)/shard_map/ppermute | solution.py:326
  36.8 6.2 %collective-permute-start.2 = (bf16[16,640]{1,0:T(8,128)(2,1)S(1)}, bf16[16,640]{1,0:T(8,128)(2,1)S(1)}, u32[]{:S(2)}, u32[]{:S(2)}) collective-permute-start(bf16[16,640]{1,0:T(8,128)(2,1)S(1)} %get-tuple-element.38), channel_id=1, source_target_pairs={{0,8},{4,12},{8,0},{12,4},{1,9},{5,13},{9,1},{13,5},{2,10},{6,14},... | collective-permute-start | bytes 61448 | tf_op jit(solution)/shard_map/ppermute | solution.py:326
  37.9 15.0 %copy-start.4 = (bf16[16,640]{1,0:T(8,128)(2,1)}, bf16[16,640]{1,0:T(8,128)(2,1)S(1)}, u32[]{:S(2)}) copy-start(bf16[16,640]{1,0:T(8,128)(2,1)S(1)} %collective-permute-done.7.refs_7_) | copy-start | bytes 61444
  37.9 8.4 %collective-permute-start.1 = (bf16[16,640]{1,0:T(8,128)(2,1)S(1)}, bf16[16,640]{1,0:T(8,128)(2,1)S(1)}, u32[]{:S(2)}, u32[]{:S(2)}) collective-permute-start(bf16[16,640]{1,0:T(8,128)(2,1)S(1)} %get-tuple-element.39), channel_id=1, source_target_pairs={{0,4},{4,8},{8,12},{12,0},{1,5},{5,9},{9,13},{13,1},{2,6},{6,10},{... | collective-permute-start | bytes 61448 | tf_op jit(solution)/shard_map/ppermute | solution.py:326
  37.9 15.0 %copy-start.5 = (bf16[16,640]{1,0:T(8,128)(2,1)}, bf16[16,640]{1,0:T(8,128)(2,1)S(1)}, u32[]{:S(2)}) copy-start(bf16[16,640]{1,0:T(8,128)(2,1)S(1)} %collective-permute-done.6.refs_6_) | copy-start | bytes 61444
  37.9 9.4 %collective-permute-start.15 = (bf16[16,640]{1,0:T(8,128)(2,1)S(1)}, bf16[16,640]{1,0:T(8,128)(2,1)S(1)}, u32[]{:S(2)}, u32[]{:S(2)}) collective-permute-start(bf16[16,640]{1,0:T(8,128)(2,1)S(1)} %get-tuple-element.25), channel_id=1, source_target_pairs={{0,12},{4,0},{8,4},{12,8},{1,13},{5,1},{9,5},{13,9},{2,14},{6,2},{... | collective-permute-start | bytes 61448 | tf_op jit(solution)/shard_map/ppermute | solution.py:326
  42.4 10.6 %copy-start.6 = (bf16[16,640]{1,0:T(8,128)(2,1)}, bf16[16,640]{1,0:T(8,128)(2,1)S(1)}, u32[]{:S(2)}) copy-start(bf16[16,640]{1,0:T(8,128)(2,1)S(1)} %collective-permute-done.5.refs_5_) | copy-start | bytes 61444
  42.4 5.1 %collective-permute-start.14 = (bf16[16,640]{1,0:T(8,128)(2,1)S(1)}, bf16[16,640]{1,0:T(8,128)(2,1)S(1)}, u32[]{:S(2)}, u32[]{:S(2)}) collective-permute-start(bf16[16,640]{1,0:T(8,128)(2,1)S(1)} %get-tuple-element.26), channel_id=1, source_target_pairs={{0,8},{4,12},{8,0},{12,4},{1,9},{5,13},{9,1},{13,5},{2,10},{6,14},... | collective-permute-start | bytes 61448 | tf_op jit(solution)/shard_map/ppermute | solution.py:326
  42.4 10.6 %copy-start.7 = (bf16[16,640]{1,0:T(8,128)(2,1)}, bf16[16,640]{1,0:T(8,128)(2,1)S(1)}, u32[]{:S(2)}) copy-start(bf16[16,640]{1,0:T(8,128)(2,1)S(1)} %collective-permute-done.3.refs_3_) | copy-start | bytes 61444
  42.4 5.6 %collective-permute-start.13 = (bf16[16,640]{1,0:T(8,128)(2,1)S(1)}, bf16[16,640]{1,0:T(8,128)(2,1)S(1)}, u32[]{:S(2)}, u32[]{:S(2)}) collective-permute-start(bf16[16,640]{1,0:T(8,128)(2,1)S(1)} %get-tuple-element.27), channel_id=1, source_target_pairs={{0,4},{4,8},{8,12},{12,0},{1,5},{5,9},{9,13},{13,1},{2,6},{6,10},{... | collective-permute-start | bytes 61448 | tf_op jit(solution)/shard_map/ppermute | solution.py:326
  43.0 10.0 %copy-start.8 = (bf16[16,640]{1,0:T(8,128)(2,1)}, bf16[16,640]{1,0:T(8,128)(2,1)S(1)}, u32[]{:S(2)}) copy-start(bf16[16,640]{1,0:T(8,128)(2,1)S(1)} %collective-permute-done.2.refs_2_) | copy-start | bytes 61444
  43.0 5.1 %collective-permute-start.11 = (bf16[16,640]{1,0:T(8,128)(2,1)S(1)}, bf16[16,640]{1,0:T(8,128)(2,1)S(1)}, u32[]{:S(2)}, u32[]{:S(2)}) collective-permute-start(bf16[16,640]{1,0:T(8,128)(2,1)S(1)} %get-tuple-element.29), channel_id=1, source_target_pairs={{0,12},{4,0},{8,4},{12,8},{1,13},{5,1},{9,5},{13,9},{2,14},{6,2},{... | collective-permute-start | bytes 61448 | tf_op jit(solution)/shard_map/ppermute | solution.py:326
  46.3 6.7 %copy-start.9 = (bf16[16,640]{1,0:T(8,128)(2,1)}, bf16[16,640]{1,0:T(8,128)(2,1)S(1)}, u32[]{:S(2)}) copy-start(bf16[16,640]{1,0:T(8,128)(2,1)S(1)} %collective-permute-done.1.refs_1_) | copy-start | bytes 61444
  46.3 4.7 %collective-permute-start.10 = (bf16[16,640]{1,0:T(8,128)(2,1)S(1)}, bf16[16,640]{1,0:T(8,128)(2,1)S(1)}, u32[]{:S(2)}, u32[]{:S(2)}) collective-permute-start(bf16[16,640]{1,0:T(8,128)(2,1)S(1)} %get-tuple-element.30), channel_id=1, source_target_pairs={{0,8},{4,12},{8,0},{12,4},{1,9},{5,13},{9,1},{13,5},{2,10},{6,14},... | collective-permute-start | bytes 61448 | tf_op jit(solution)/shard_map/ppermute | solution.py:326
  47.4 5.6 %copy-start.10 = (bf16[16,640]{1,0:T(8,128)(2,1)}, bf16[16,640]{1,0:T(8,128)(2,1)S(1)}, u32[]{:S(2)}) copy-start(bf16[16,640]{1,0:T(8,128)(2,1)S(1)} %collective-permute-done.15.refs_15_) | copy-start | bytes 61444
  47.4 5.6 %collective-permute-start.9 = (bf16[16,640]{1,0:T(8,128)(2,1)S(1)}, bf16[16,640]{1,0:T(8,128)(2,1)S(1)}, u32[]{:S(2)}, u32[]{:S(2)}) collective-permute-start(bf16[16,640]{1,0:T(8,128)(2,1)S(1)} %get-tuple-element.31), channel_id=1, source_target_pairs={{0,4},{4,8},{8,12},{12,0},{1,5},{5,9},{9,13},{13,1},{2,6},{6,10},{... | collective-permute-start | bytes 61448 | tf_op jit(solution)/shard_map/ppermute | solution.py:326
  47.4 5.6 %copy-start.11 = (bf16[16,640]{1,0:T(8,128)(2,1)}, bf16[16,640]{1,0:T(8,128)(2,1)S(1)}, u32[]{:S(2)}) copy-start(bf16[16,640]{1,0:T(8,128)(2,1)S(1)} %collective-permute-done.14.refs_14_) | copy-start | bytes 61444
  48.0 5.0 %copy-start.12 = (bf16[16,640]{1,0:T(8,128)(2,1)}, bf16[16,640]{1,0:T(8,128)(2,1)S(1)}, u32[]{:S(2)}) copy-start(bf16[16,640]{1,0:T(8,128)(2,1)S(1)} %collective-permute-done.13.refs_13_) | copy-start | bytes 61444
  48.1 5.0 %copy-start.13 = (bf16[16,640]{1,0:T(8,128)(2,1)}, bf16[16,640]{1,0:T(8,128)(2,1)S(1)}, u32[]{:S(2)}) copy-start(bf16[16,640]{1,0:T(8,128)(2,1)S(1)} %collective-permute-done.11.refs_11_) | copy-start | bytes 61444
  51.0 2.0 %copy-start.14 = (bf16[16,640]{1,0:T(8,128)(2,1)}, bf16[16,640]{1,0:T(8,128)(2,1)S(1)}, u32[]{:S(2)}) copy-start(bf16[16,640]{1,0:T(8,128)(2,1)S(1)} %collective-permute-done.10.refs_10_) | copy-start | bytes 61444
  52.9 0.6 copy-start.15
  56.8 4.7 %collective-permute-start.16 = (bf16[64,640]{1,0:T(8,128)(2,1)}, bf16[64,640]{1,0:T(8,128)(2,1)S(1)}, u32[]{:S(2)}, u32[]{:S(2)}) collective-permute-start(bf16[64,640]{1,0:T(8,128)(2,1)} %get-tuple-element.24), channel_id=1, source_target_pairs={{0,2},{2,0},{1,3},{3,1},{4,6},{6,4},{5,7},{7,5},{8,10},{10,8},{9,1... | collective-permute-start | bytes 245768 | tf_op jit(solution)/shard_map/ppermute | solution.py:329
  61.5 0.6 copy-start.3

commit v2 on v0

v2 whole, which is shorter than its diff:
```python
import functools

import jax
import jax.numpy as jnp
from jax import lax
from jax.experimental import pallas as pl
from jax.experimental.pallas import tpu as pltpu
from jax.sharding import PartitionSpec as P

LANES = 128
GROUP = 16
OWNER_BUDGET = 576
MIB = 2**20


def shards_plain(panels, svd_basis, kl_basis, slot_of_m, svd_keep, kl_keep):
    slot_count = slot_of_m.shape[0]
    order_slots = jnp.argsort(slot_of_m)
    keep_slots = jnp.take(svd_keep, order_slots, axis=0)
    modes_slots = jnp.take(kl_keep, order_slots, axis=0)
    width_modes = svd_basis.shape[2]
    owner_rows = kl_basis.shape[0]
    slot_rows = slot_count // lax.axis_size("pa")
    slot_start = lax.axis_index("pa") * slot_rows
    owner_start = slot_start + lax.axis_index("ma") * owner_rows
    modes_owner = lax.dynamic_slice_in_dim(modes_slots, owner_start, owner_rows, 0)
    chosen = jnp.take(panels, order_slots, axis=0)
    summed = lax.psum_scatter(
        jnp.einsum("mfb,fbr->mfr", chosen, svd_basis, preferred_element_type=jnp.float32),
        "pa",
        scatter_dimension=0,
        tiled=True,
    )
    keep_here = lax.dynamic_slice_in_dim(keep_slots, slot_start, slot_rows, 0)
    columns = jnp.arange(width_modes, dtype=jnp.int32)
    retained = jnp.where(columns[None, None, :] < keep_here[:, None, None], summed, 0.0).astype(
        jnp.bfloat16
    )
    relaid = lax.all_to_all(retained, "ma", split_axis=0, concat_axis=1, tiled=True)
    partial_sums = jnp.einsum("mkf,mfr->mkr", kl_basis, relaid, preferred_element_type=jnp.float32)
    modes = jnp.arange(kl_basis.shape[1], dtype=jnp.int32)
    partial_sums = jnp.where(modes[None, :, None] < modes_owner[:, None, None], partial_sums, 0.0)
    return lax.psum_scatter(partial_sums, "af", scatter_dimension=1, tiled=True)


def cyclic(value, count):
    return lax.rem(value + count, count)


def shifted(tiles, shift, lane):
    low, high = (pltpu.roll(tile, shift, 1) for tile in tiles)
    left = lane < shift
    return jnp.where(left, 0.0, low), jnp.where(left, low, high), jnp.where(left, high, 0.0)


def project_kernel(
    owner_slots, slot_hbm, keep_hbm, rows_hbm, panels, basis,
    mine, send, slot_column, rows_column, scalars,
    slot_s, keep_s, rows_s, keep_place, rows_place,
    panels_v, basis_v, lhs_v, out_v, pack_v, small_sem, panel_sem, basis_sem,
):
    slots, freqs, depth = panels_v.shape
    groups = freqs // GROUP
    copies = basis_sem.shape[0] // groups
    per_copy = GROUP // copies
    halves, owners = lax.axis_size("pa"), lax.axis_size("ma")
    my_half, my_owner = lax.axis_index("pa"), lax.axis_index("ma")
    half_slots = slots // halves
    width, modes = mine.shape[-1], basis.shape[-1]

    table_copies = [
        pltpu.make_async_copy(slot_hbm, slot_s, small_sem.at[0]),
        pltpu.make_async_copy(keep_hbm, keep_s, small_sem.at[1]),
        pltpu.make_async_copy(rows_hbm, rows_s, small_sem.at[2]),
    ]
    for copy in table_copies:
        copy.start()

    def basis_copy(i):
        part = pl.ds(i * per_copy, per_copy)
        return pltpu.make_async_copy(basis.at[part], basis_v.at[part], basis_sem.at[i])

    ahead = 2
    for i in range(ahead):
        basis_copy(i).start()
    for copy in table_copies:
        copy.wait()

    for group in range(groups):
        part = pl.ds(group * GROUP, GROUP)

        @pl.loop(0, slots)
        def _(m):
            slot = slot_s[m]
            half = cyclic(lax.div(slot, half_slots) - my_half, halves)
            within = lax.rem(slot, half_slots)
            owner = cyclic(lax.div(within, owner_slots) - my_owner, owners)
            place = half * half_slots + owner * owner_slots + lax.rem(within, owner_slots)
            if group == 0:
                keep_place[place] = keep_s[m]
                rows_place[place] = rows_s[m]
            pltpu.make_async_copy(
                panels.at[m, part], panels_v.at[place, part], panel_sem.at[group]
            ).start()

        for i in range(ahead + group * copies, min(ahead + (group + 1) * copies, groups * copies)):
            basis_copy(i).start()

    column = lax.broadcasted_iota(jnp.int32, slot_column.shape, 1)
    slot_at = jnp.full(slot_column.shape, owner_slots, jnp.int32)
    rows_at = jnp.zeros(slot_column.shape, jnp.int32)
    offset = jnp.int32(0)
    for j in range(owner_slots):
        keep = keep_place[j]
        within = (column >= offset) & (column < offset + keep)
        slot_at = jnp.where(within, j, slot_at)
        rows_at = jnp.where(within, rows_place[j], rows_at)
        scalars[j : j + 1, :] = jnp.full((1, LANES), offset, jnp.int32)
        scalars[owner_slots + j : owner_slots + j + 1, :] = jnp.full((1, LANES), keep, jnp.int32)
        offset = offset + keep
    slot_column[...] = slot_at
    rows_column[...] = rows_at

    side = GROUP * GROUP
    row = lax.broadcasted_iota(jnp.int32, (side, side), 0)
    column = lax.broadcasted_iota(jnp.int32, (side, side), 1)
    swap = (column == (row % GROUP) * GROUP + row // GROUP).astype(jnp.float32).astype(jnp.bfloat16)
    lane = lax.broadcasted_iota(jnp.int32, (GROUP, LANES), 1)

    @pl.loop(0, groups)
    def _(group):
        here = pl.ds(pl.multiple_of(group * GROUP, GROUP), GROUP)
        pltpu.make_async_copy(
            panels_v.at[:, here], panels_v.at[:, here], panel_sem.at[group]
        ).wait()
        for block in range(slots // GROUP):
            blocks = slice(block * GROUP, (block + 1) * GROUP)
            tile = panels_v[blocks, here, :].reshape(side, depth)
            turned = jnp.dot(swap, tile, preferred_element_type=jnp.float32).astype(jnp.bfloat16)
            lhs_v[:, blocks, :] = turned.reshape(GROUP, GROUP, depth)

        @pl.loop(0, copies)
        def _(i):
            basis_copy(group * copies + i).wait()
            for k in range(per_copy):
                f = i * per_copy + k
                out_v[f] = jnp.dot(
                    lhs_v[f], basis_v[group * GROUP + f], preferred_element_type=jnp.float32
                )

        pack_v[...] = jnp.zeros(pack_v.shape, jnp.float32)
        for half in range(halves):
            to = (mine, send)[half]
            for owner in range(owners):
                offset = jnp.int32(0)
                at = half * owners + owner
                for j in range(owner_slots):
                    place = at * owner_slots + j
                    keep = keep_place[place]
                    tiles = [
                        jnp.where(
                            lane < keep - t * LANES,
                            out_v[:, place, t * LANES : (t + 1) * LANES],
                            0.0,
                        )
                        for t in range(modes // LANES)
                    ]
                    tile = lax.div(offset, LANES)
                    moved = shifted(tiles, offset - tile * LANES, lane)
                    for t, value in enumerate(moved):
                        lanes = pl.ds(pl.multiple_of((tile + t) * LANES, LANES), LANES)
                        pack_v[at, :, lanes] += value
                    offset = offset + keep
                to[owner, here, :] = pack_v[at, :, :width]


def kl_kernel(part, owners, slot_column, rows_column, kl, *refs):
    blocks, (out, packed_v) = refs[:owners], refs[owners:]
    owner_slots, rows, freqs = kl.shape
    shares = lax.axis_size("af")
    per_source = freqs // owners
    me = lax.axis_index("ma")
    for step in range(owners):
        source = cyclic(me - step, owners)
        at = pl.multiple_of(source * per_source, GROUP)
        packed_v[pl.ds(at, per_source), :] = blocks[step][...]
    share_rows, width = out.shape
    at = pl.multiple_of(cyclic(lax.axis_index("af") + part, shares) * share_rows, GROUP)
    lhs = kl[:, pl.ds(at, share_rows), :].reshape(owner_slots * share_rows, freqs)
    product = jnp.dot(lhs, packed_v[...], preferred_element_type=jnp.float32)
    line = lax.broadcasted_iota(jnp.int32, (share_rows, width), 0) + at
    slot_at = slot_column[0:1, :]
    total = jnp.zeros((share_rows, width), jnp.float32)
    for j in range(owner_slots):
        here = product[j * share_rows : (j + 1) * share_rows]
        total = jnp.where(slot_at == j, here, total)
    out[...] = jnp.where(line < rows_column[0:1, :], total, 0.0).astype(out.dtype)


def unpack_kernel(scalars, mine, got, out, sum_v):
    owner_slots, rows, modes = out.shape
    width = mine.shape[1]
    sum_v[:, :width] = mine[...] + got[...].astype(jnp.float32)
    lane = lax.broadcasted_iota(jnp.int32, (rows, LANES), 1)
    for j in range(owner_slots):
        offset = jnp.max(scalars[j : j + 1, :])
        keep = jnp.max(scalars[owner_slots + j : owner_slots + j + 1, :])
        tile = lax.div(offset, LANES)
        shift = offset - tile * LANES
        back = lax.rem(LANES - shift, LANES)
        turned = [
            pltpu.roll(
                sum_v[:, pl.ds(pl.multiple_of((tile + t) * LANES, LANES), LANES)], back, 1
            )
            for t in range(modes // LANES + 1)
        ]
        for t in range(modes // LANES):
            value = jnp.where(lane < LANES - shift, turned[t], turned[t + 1])
            value = jnp.where(lane < keep - t * LANES, value, 0.0)
            out[j, :, t * LANES : (t + 1) * LANES] = value


HBM = pl.BlockSpec(memory_space=pltpu.HBM)
VMEM = pl.BlockSpec(memory_space=pltpu.VMEM)


def in_hbm(operand):
    return pltpu.with_memory_space_constraint(operand, pltpu.HBM)


def project(panels, svd_basis, slot_of_m, svd_keep, kl_keep, owner_slots, width):
    slots, freqs, depth = panels.shape
    modes = svd_basis.shape[2]
    owners, halves = lax.axis_size("ma"), lax.axis_size("pa")
    packed = jax.ShapeDtypeStruct((owners, freqs, width), jnp.float32)
    column = jax.ShapeDtypeStruct((8, width), jnp.int32)
    table = pltpu.SMEM((slots,), jnp.int32)
    wide = width + modes + LANES
    return pl.pallas_call(
        functools.partial(project_kernel, owner_slots),
        out_shape=(packed, packed, column, column, jax.ShapeDtypeStruct((8, LANES), jnp.int32)),
        in_specs=[HBM] * 5,
        out_specs=(VMEM,) * 5,
        scratch_shapes=[table] * 5
        + [
            pltpu.VMEM((slots, freqs, depth), jnp.bfloat16),
            pltpu.VMEM((freqs, depth, modes), jnp.bfloat16),
            pltpu.VMEM((GROUP, slots, depth), jnp.bfloat16),
            pltpu.VMEM((GROUP, slots, modes), jnp.float32),
            pltpu.VMEM((halves * owners, GROUP, wide), jnp.float32),
            pltpu.SemaphoreType.DMA((3,)),
            pltpu.SemaphoreType.DMA((freqs // GROUP,)),
            pltpu.SemaphoreType.DMA((freqs // 4,)),
        ],
        compiler_params=pltpu.CompilerParams(vmem_limit_bytes=48 * MIB),
        cost_estimate=pl.CostEstimate(
            flops=2 * slots * freqs * depth * modes,
            bytes_accessed=2 * freqs * depth * (modes + slots),
            transcendentals=0,
        ),
        name="project",
    )(*map(in_hbm, (slot_of_m, svd_keep, kl_keep, panels, svd_basis)))


def kl_project(part, kind, slot_column, rows_column, kl_basis, blocks):
    owners, shares = lax.axis_size("ma"), lax.axis_size("af")
    rows, freqs = kl_basis.shape[1:]
    width = slot_column.shape[1]
    return pl.pallas_call(
        functools.partial(kl_kernel, part, owners),
        out_shape=jax.ShapeDtypeStruct((rows // shares, width), kind),
        in_specs=[VMEM] * (3 + owners),
        out_specs=VMEM,
        scratch_shapes=[pltpu.VMEM((freqs, width), jnp.bfloat16)],
        cost_estimate=pl.CostEstimate(
            flops=2 * kl_basis.size * width // shares,
            bytes_accessed=2 * kl_basis.size,
            transcendentals=0,
        ),
        name="kl_project",
    )(slot_column, rows_column, kl_basis, *blocks)


def unpack(scalars, mine, got, owner_slots, modes):
    rows, width = mine.shape
    return pl.pallas_call(
        unpack_kernel,
        out_shape=jax.ShapeDtypeStruct((owner_slots, rows, modes), jnp.float32),
        in_specs=[VMEM] * 3,
        out_specs=VMEM,
        scratch_shapes=[pltpu.VMEM((rows, width + modes + LANES), jnp.float32)],
        cost_estimate=pl.CostEstimate(
            flops=rows * width, bytes_accessed=10 * rows * width, transcendentals=0
        ),
        name="unpack",
    )(scalars, mine, got)


def ring(axis, step):
    size = lax.axis_size(axis)
    return [(i, (i + step) % size) for i in range(size)]


def shards(panels, svd_basis, kl_basis, slot_of_m, svd_keep, kl_keep):
    owner_slots, modes = kl_basis.shape[0], svd_basis.shape[2]
    owners = lax.axis_size("ma")
    width = -(-min(OWNER_BUDGET, owner_slots * modes) // LANES) * LANES
    mine, send, slot_column, rows_column, scalars = project(
        panels, svd_basis, slot_of_m, svd_keep, kl_keep, owner_slots, width
    )
    got = lax.ppermute(send, "pa", ring("pa", 1))
    summed = [(mine[step] + got[step]).astype(jnp.bfloat16) for step in range(owners)]
    blocks = [summed[0]] + [
        lax.ppermute(summed[step], "ma", ring("ma", step)) for step in range(1, owners)
    ]
    send = kl_project(1, jnp.bfloat16, slot_column, rows_column, kl_basis, blocks)
    got = lax.ppermute(send, "af", ring("af", 1))
    mine = kl_project(0, jnp.float32, slot_column, rows_column, kl_basis, blocks)
    return unpack(scalars, mine, got, owner_slots, modes)


def kernels_fit(mesh, args):
    panels, svd_basis, kl_basis = args[:3]
    slots = panels.shape[0] // mesh.shape["grp"]
    freqs = svd_basis.shape[0] // (mesh.shape["af"] * mesh.shape["ma"])
    owner_slots = kl_basis.shape[0] // (mesh.shape["pa"] * mesh.shape["ma"])
    share_rows = kl_basis.shape[1] // mesh.shape["af"]
    return (
        freqs % GROUP == 0
        and slots % (GROUP * mesh.shape["pa"]) == 0
        and owner_slots == 4
        and svd_basis.shape[2] == 2 * LANES
        and share_rows % GROUP == 0
        and mesh.shape["pa"] == 2
        and mesh.shape["af"] == 2
        and mesh.shape["ma"] <= 4
    )


def solution(mesh):
    in_specs = (
        P("grp", ("af", "ma"), "pa"),
        P(("af", "ma"), "pa", None),
        P(("pa", "ma"), None, "af"),
        P(),
        P(),
        P(),
    )
    out_specs = P(("grp", "pa", "ma"), "af", None)

    def run(*args):
        body = shards if kernels_fit(mesh, args) else shards_plain
        mapped = jax.shard_map(
            body, mesh=mesh, in_specs=in_specs, out_specs=out_specs, check_vma=False
        )
        return mapped(*args)

    return run
```

time: 107 us -> 41 us (0.38)
  waiting for transfers between devices: 42.7 us -> 9.77 us
  Pallas kernels: 0 us -> 21.1 us
  matrix products: 18.9 us -> 0 us
  between operations: 13.5 us -> 0.05 us
  blocking collectives: 9.28 us -> 0 us
  local copies, waits for them, and re-layouts: 9.61 us -> 1.3 us
  other arithmetic: 7.19 us -> 0.71 us
  starting transfers between devices: 6.02 us -> 7.98 us
    psum x1 -> x0, waiting for transfers between devices: 27.9 us -> none  [shards(): summed_all = lax.psum(partial_sums, 'af')]
    pallas_call x0 -> x4, Pallas kernels: none -> 21.1 us  [the longest x1 14.9 us: project(): pl.pallas_call(functools.partial(project_kernel, owner_slots), out_shape=...]
    dot_general x2 -> x0, matrix products: 18.9 us -> none  [the longest x1 17.7 us: shards(): jnp.einsum('mfb,fbr->mfr', chosen, svd_basis, preferred_element_type=jnp....]
    all_to_all x1 -> x0, waiting for transfers between devices: 14.9 us -> none  [shards(): lax.all_to_all(retained, 'ma', split_axis=0, concat_axis=1, tiled=True)]
    ppermute x0 -> x5, waiting for transfers between devices: none -> 9.77 us  [the longest x3 6.98 us: shards(): lax.ppermute(summed[step], 'ma', ring('ma', step))]
    psum x1 -> x0, blocking collectives: 9.28 us -> none  [shards(): lax.psum(jnp.einsum('mfb,fbr->mfr', chosen, svd_basis, preferred_element_...]
    ppermute x0 -> x5, starting transfers between devices: none -> 7.98 us  [the longest x3 5.98 us: shards(): lax.ppermute(summed[step], 'ma', ring('ma', step))]
    gather x3 -> x0, local copies, waits for them, and re-layouts: 6.33 us -> none  [the longest x1 4.93 us: shards(): chosen = jnp.take(panels, order_slots, axis=0)]
  transfers between devices with their start and end apart: 2 -> 5, of which waited for: 2 -> 4; matrix products, arithmetic and copies ran while one was open for 0% -> 0% of each run, Pallas kernels for 0% -> 5%
where the time goes in v2:
time: 41 us; the launch traced here: 40.9 us
  Pallas kernels  21.1 us (51%)
  waiting for transfers between devices  9.77 us (24%)
  starting transfers between devices  7.98 us (19%)
  local copies, waits for them, and re-layouts  1.3 us (3%)
  other arithmetic  0.71 us (2%)
    pallas_call x1, Pallas kernels, project(): pl.pallas_call(functools.partial(project_kernel, owner_slots), out_shape=...  14.9 us
    ppermute x3, waiting for transfers between devices, shards(): lax.ppermute(summed[step], 'ma', ring('ma', step))  6.98 us
    ppermute x3, starting transfers between devices, shards(): lax.ppermute(summed[step], 'ma', ring('ma', step))  5.98 us
    pallas_call x2, Pallas kernels, kl_project(): pl.pallas_call(functools.partial(kl_kernel, part, owners), out_shape=jax....  4.15 us
    pallas_call x1, Pallas kernels, unpack(): pl.pallas_call(unpack_kernel, out_shape=jax.ShapeDtypeStruct((owner_slots...  2.06 us
    ppermute x1, waiting for transfers between devices, shards(): got = lax.ppermute(send, 'pa', ring('pa', 1))  1.72 us
    ppermute x1, starting transfers between devices, shards(): got = lax.ppermute(send, 'af', ring('af', 1))  1.49 us
    unnamed x14, local copies, waits for them, and re-layouts  1.3 us
  transfers between devices with their start and end apart: 5, of which 4 were waited for; matrix products, arithmetic and copies ran while one was open for 0% of the time, Pallas kernels for 5%

profile of v2, /device:TPU:0, one launch (start us, length us, event | category | flops | bytes accessed | tf_op | source)
XLA Modules:
  0.0 40.9 jit_solution(16346762477892408907)
XLA Ops:
  0.0 14.9 %project.1 = (f32[4,64,640]{2,1,0:T(8,128)S(1)}, f32[4,64,640]{2,1,0:T(8,128)S(1)}, s32[8,640]{1,0:T(8,128)S(1)}, s32[8,640]{1,0:T(8,128)S(1)}, s32[8,128]{1,0:T(8,128)S(1)}) custom-call(s32[32]{0:T(128)} %slot_hbm.1, s32[32]{0:T(128)} %keep_hbm.1, s32[32]{0:T(128)} %rows_hbm.1, bf16[32,64,1024]{2,1,0:T(8,128)(2,1)} %panels.1, bf16[64,1024,256]{2,1,0:T(8,128)(2,1)} %basis.1), custom_call_target="tpu_custom_call" | custom-call | flops 1073741824 | bytes 37748736 | tf_op jit(solution)/shard_map/project/pallas_call | solution.py:239
  14.9 0.0 copy-start
  14.9 0.0 copy-start.1
  14.9 0.0 copy-start.2
  14.9 0.5 %collective-permute-start = (f32[4,64,640]{2,1,0:T(8,128)S(1)}, f32[4,64,640]{2,1,0:T(8,128)S(1)}, u32[]{:S(2)}, u32[]{:S(2)}) collective-permute-start(f32[4,64,640]{2,1,0:T(8,128)S(1)} %get-tuple-element.14), channel_id=1, source_target_pairs={{0,1},{1,0},{2,3},{3,2},{4,5},{5,4},{6,7},{7,6},{8,9},{9,8},{10,11... | collective-permute-start | bytes 1966088 | tf_op jit(solution)/shard_map/ppermute | solution.py:311
  15.4 1.7 %collective-permute-done = f32[4,64,640]{2,1,0:T(8,128)S(1)} collective-permute-done((f32[4,64,640]{2,1,0:T(8,128)S(1)}, f32[4,64,640]{2,1,0:T(8,128)S(1)}, u32[]{:S(2)}, u32[]{:S(2)}) %collective-permute-start) | collective-permute-done | bytes 655392 | tf_op jit(solution)/shard_map/ppermute | solution.py:311
  17.1 0.7 %fusion.7 = (bf16[64,640]{1,0:T(8,128)(2,1)S(1)}, bf16[64,640]{1,0:T(8,128)(2,1)S(1)}, bf16[64,640]{1,0:T(8,128)(2,1)S(1)}, bf16[64,640]{1,0:T(8,128)(2,1)}) fusion(f32[4,64,640]{2,1,0:T(8,128)S(1)} %collective-permute-done, f32[4,64,640]{2,1,0:T(8,128)S(1)} %get-tuple-element.13), kind=kLoop, calls=%fused_computation.11 | loop fusion | flops 327680 | bytes 1638400 | tf_op jit(solution)/shard_map/convert_element_type | solution.py:312
  17.8 0.0 copy-done
  17.8 0.0 copy-done.1
  17.8 5.0 %collective-permute-start.3 = (bf16[64,640]{1,0:T(8,128)(2,1)S(1)}, bf16[64,640]{1,0:T(8,128)(2,1)S(1)}, u32[]{:S(2)}, u32[]{:S(2)}) collective-permute-start(bf16[64,640]{1,0:T(8,128)(2,1)S(1)} %get-tuple-element.15), channel_id=1, source_target_pairs={{0,12},{4,0},{8,4},{12,8},{1,13},{5,1},{9,5},{13,9},{2,14},{6,2},{... | collective-permute-start | bytes 245768 | tf_op jit(solution)/shard_map/ppermute | solution.py:314
  22.8 0.0 copy-done.2
  22.8 0.0 collective-permute-start.2
  22.8 1.0 %collective-permute-start.1 = (bf16[64,640]{1,0:T(8,128)(2,1)S(1)}, bf16[64,640]{1,0:T(8,128)(2,1)S(1)}, u32[]{:S(2)}, u32[]{:S(2)}) collective-permute-start(bf16[64,640]{1,0:T(8,128)(2,1)S(1)} %get-tuple-element.17), channel_id=1, source_target_pairs={{0,4},{4,8},{8,12},{12,0},{1,5},{5,9},{9,13},{13,1},{2,6},{6,10},{... | collective-permute-start | bytes 245768 | tf_op jit(solution)/shard_map/ppermute | solution.py:314
  23.8 1.8 %collective-permute-done.3.refs_3_ = bf16[64,640]{1,0:T(8,128)(2,1)S(1)} collective-permute-done((bf16[64,640]{1,0:T(8,128)(2,1)S(1)}, bf16[64,640]{1,0:T(8,128)(2,1)S(1)}, u32[]{:S(2)}, u32[]{:S(2)}) %collective-permute-start.3) | collective-permute-done | bytes 81952 | tf_op jit(solution)/shard_map/ppermute | solution.py:314
  25.7 0.0 copy-start.3
  25.7 5.1 %collective-permute-done.2.refs_2_ = bf16[64,640]{1,0:T(8,128)(2,1)S(1)} collective-permute-done((bf16[64,640]{1,0:T(8,128)(2,1)S(1)}, bf16[64,640]{1,0:T(8,128)(2,1)S(1)}, u32[]{:S(2)}, u32[]{:S(2)}) %collective-permute-start.2) | collective-permute-done | bytes 81952 | tf_op jit(solution)/shard_map/ppermute | solution.py:314
  30.8 0.0 copy-start.4
  30.8 0.0 collective-permute-done.1.refs_1_
  30.8 0.0 copy-start.5
  30.8 0.0 copy-done.3
  30.8 0.6 %copy-done.4 = bf16[64,640]{1,0:T(8,128)(2,1)} copy-done((bf16[64,640]{1,0:T(8,128)(2,1)}, bf16[64,640]{1,0:T(8,128)(2,1)S(1)}, u32[]{:S(2)}) %copy-start.4) | copy-done | bytes 81944
  31.4 0.0 copy-done.5
  31.5 2.1 %kl_project.3 = bf16[64,640]{1,0:T(8,128)(2,1)} custom-call(s32[8,640]{1,0:T(8,128)} %copy-done, s32[8,640]{1,0:T(8,128)} %copy-done.1, bf16[4,128,256]{2,1,0:T(8,128)(2,1)} %kl.3, bf16[64,640]{1,0:T(8,128)(2,1)} %get-tuple-element.18.refs_0_, bf16[64,640]{1,0:T(8,128)(2,1)} %copy-done.5, bf16[64,640]{1,0:T(8,128)(2,1)} %copy-done.4, bf16[64,640]{1,0:T(8,128)(2,1)} %copy-done.3), custom_call_target="tpu_custom_call" | custom-call | flops 83886080 | bytes 262144 | tf_op jit(solution)/shard_map/kl_project/pallas_call | solution.py:269
  33.5 1.5 %collective-permute-start.4 = (bf16[64,640]{1,0:T(8,128)(2,1)}, bf16[64,640]{1,0:T(8,128)(2,1)S(1)}, u32[]{:S(2)}, u32[]{:S(2)}) collective-permute-start(bf16[64,640]{1,0:T(8,128)(2,1)} %kl_project.3), channel_id=1, source_target_pairs={{0,2},{2,0},{1,3},{3,1},{4,6},{6,4},{5,7},{7,5},{8,10},{10,8},{9,1... | collective-permute-start | bytes 245768 | tf_op jit(solution)/shard_map/ppermute | solution.py:317
  35.0 2.1 %kl_project.2.mine = f32[64,640]{1,0:T(8,128)} custom-call(s32[8,640]{1,0:T(8,128)} %copy-done, s32[8,640]{1,0:T(8,128)} %copy-done.1, bf16[4,128,256]{2,1,0:T(8,128)(2,1)} %kl.3, bf16[64,640]{1,0:T(8,128)(2,1)} %get-tuple-element.18.refs_0_, bf16[64,640]{1,0:T(8,128)(2,1)} %copy-done.5, bf16[64,640]{1,0:T(8,128)(2,1)} %copy-done.4, bf16[64,640]{1,0:T(8,128)(2,1)} %copy-done.3), custom_call_target="tpu_custom_call" | custom-call | flops 83886080 | bytes 262144 | tf_op jit(solution)/shard_map/kl_project/pallas_call | solution.py:269
  37.1 1.1 %collective-permute-done.4.got = bf16[64,640]{1,0:T(8,128)(2,1)S(1)} collective-permute-done((bf16[64,640]{1,0:T(8,128)(2,1)}, bf16[64,640]{1,0:T(8,128)(2,1)S(1)}, u32[]{:S(2)}, u32[]{:S(2)}) %collective-permute-start.4) | collective-permute-done | bytes 81952 | tf_op jit(solution)/shard_map/ppermute | solution.py:317
  38.2 0.0 copy-start.6
  38.2 0.6 %copy-done.6 = bf16[64,640]{1,0:T(8,128)(2,1)} copy-done((bf16[64,640]{1,0:T(8,128)(2,1)}, bf16[64,640]{1,0:T(8,128)(2,1)S(1)}, u32[]{:S(2)}) %copy-start.6) | copy-done | bytes 81944
  38.8 2.1 %unpack.1 = f32[4,64,256]{2,1,0:T(8,128)} custom-call(s32[8,128]{1,0:T(8,128)} %copy-done.2, f32[64,640]{1,0:T(8,128)} %kl_project.2.mine, bf16[64,640]{1,0:T(8,128)(2,1)} %copy-done.6), custom_call_target="tpu_custom_call" | custom-call | flops 40960 | bytes 409600 | tf_op jit(solution)/shard_map/unpack/pallas_call | solution.py:286
Async XLA Ops:
  14.9 3.0 %copy-start = (s32[8,640]{1,0:T(8,128)}, s32[8,640]{1,0:T(8,128)S(1)}, u32[]{:S(2)}) copy-start(s32[8,640]{1,0:T(8,128)S(1)} %get-tuple-element.11.slot_column) | copy-start | bytes 61444
  14.9 3.0 %copy-start.1 = (s32[8,640]{1,0:T(8,128)}, s32[8,640]{1,0:T(8,128)S(1)}, u32[]{:S(2)}) copy-start(s32[8,640]{1,0:T(8,128)S(1)} %get-tuple-element.12.rows_column) | copy-start | bytes 61444
  14.9 7.9 %copy-start.2 = (s32[8,128]{1,0:T(8,128)}, s32[8,128]{1,0:T(8,128)S(1)}, u32[]{:S(2)}) copy-start(s32[8,128]{1,0:T(8,128)S(1)} %get-tuple-element.10.scalars) | copy-start | bytes 12292
  14.9 2.2 %collective-permute-start = (f32[4,64,640]{2,1,0:T(8,128)S(1)}, f32[4,64,640]{2,1,0:T(8,128)S(1)}, u32[]{:S(2)}, u32[]{:S(2)}) collective-permute-start(f32[4,64,640]{2,1,0:T(8,128)S(1)} %get-tuple-element.14), channel_id=1, source_target_pairs={{0,1},{1,0},{2,3},{3,2},{4,5},{5,4},{6,7},{7,6},{8,9},{9,8},{10,11... | collective-permute-start | bytes 1966088 | tf_op jit(solution)/shard_map/ppermute | solution.py:311
  17.8 7.8 %collective-permute-start.3 = (bf16[64,640]{1,0:T(8,128)(2,1)S(1)}, bf16[64,640]{1,0:T(8,128)(2,1)S(1)}, u32[]{:S(2)}, u32[]{:S(2)}) collective-permute-start(bf16[64,640]{1,0:T(8,128)(2,1)S(1)} %get-tuple-element.15), channel_id=1, source_target_pairs={{0,12},{4,0},{8,4},{12,8},{1,13},{5,1},{9,5},{13,9},{2,14},{6,2},{... | collective-permute-start | bytes 245768 | tf_op jit(solution)/shard_map/ppermute | solution.py:314
  22.8 8.0 %collective-permute-start.2 = (bf16[64,640]{1,0:T(8,128)(2,1)S(1)}, bf16[64,640]{1,0:T(8,128)(2,1)S(1)}, u32[]{:S(2)}, u32[]{:S(2)}) collective-permute-start(bf16[64,640]{1,0:T(8,128)(2,1)S(1)} %get-tuple-element.16), channel_id=1, source_target_pairs={{0,8},{4,12},{8,0},{12,4},{1,9},{5,13},{9,1},{13,5},{2,10},{6,14},... | collective-permute-start | bytes 245768 | tf_op jit(solution)/shard_map/ppermute | solution.py:314
  22.8 8.0 %collective-permute-start.1 = (bf16[64,640]{1,0:T(8,128)(2,1)S(1)}, bf16[64,640]{1,0:T(8,128)(2,1)S(1)}, u32[]{:S(2)}, u32[]{:S(2)}) collective-permute-start(bf16[64,640]{1,0:T(8,128)(2,1)S(1)} %get-tuple-element.17), channel_id=1, source_target_pairs={{0,4},{4,8},{8,12},{12,0},{1,5},{5,9},{9,13},{13,1},{2,6},{6,10},{... | collective-permute-start | bytes 245768 | tf_op jit(solution)/shard_map/ppermute | solution.py:314
  25.7 5.2 %copy-start.3 = (bf16[64,640]{1,0:T(8,128)(2,1)}, bf16[64,640]{1,0:T(8,128)(2,1)S(1)}, u32[]{:S(2)}) copy-start(bf16[64,640]{1,0:T(8,128)(2,1)S(1)} %collective-permute-done.3.refs_3_) | copy-start | bytes 245764
  30.8 0.6 %copy-start.4 = (bf16[64,640]{1,0:T(8,128)(2,1)}, bf16[64,640]{1,0:T(8,128)(2,1)S(1)}, u32[]{:S(2)}) copy-start(bf16[64,640]{1,0:T(8,128)(2,1)S(1)} %collective-permute-done.2.refs_2_) | copy-start | bytes 245764
  30.8 0.7 %copy-start.5 = (bf16[64,640]{1,0:T(8,128)(2,1)}, bf16[64,640]{1,0:T(8,128)(2,1)S(1)}, u32[]{:S(2)}) copy-start(bf16[64,640]{1,0:T(8,128)(2,1)S(1)} %collective-permute-done.1.refs_1_) | copy-start | bytes 245764
  33.5 4.7 %collective-permute-start.4 = (bf16[64,640]{1,0:T(8,128)(2,1)}, bf16[64,640]{1,0:T(8,128)(2,1)S(1)}, u32[]{:S(2)}, u32[]{:S(2)}) collective-permute-start(bf16[64,640]{1,0:T(8,128)(2,1)} %kl_project.3), channel_id=1, source_target_pairs={{0,2},{2,0},{1,3},{3,1},{4,6},{6,4},{5,7},{7,5},{8,10},{10,8},{9,1... | collective-permute-start | bytes 245768 | tf_op jit(solution)/shard_map/ppermute | solution.py:317
  38.2 0.6 %copy-start.6 = (bf16[64,640]{1,0:T(8,128)(2,1)}, bf16[64,640]{1,0:T(8,128)(2,1)S(1)}, u32[]{:S(2)}) copy-start(bf16[64,640]{1,0:T(8,128)(2,1)S(1)} %collective-permute-done.4.got) | copy-start | bytes 245764

commit v3 on v2

--- a/solution.py
+++ b/solution.py
@@ -94,7 +94,7 @@
             slot = slot_s[m]
             half = cyclic(lax.div(slot, half_slots) - my_half, halves)
             within = lax.rem(slot, half_slots)
-            owner = cyclic(lax.div(within, owner_slots) - my_owner, owners)
+            owner = lax.div(within, owner_slots) ^ my_owner
             place = half * half_slots + owner * owner_slots + lax.rem(within, owner_slots)
             if group == 0:
                 keep_place[place] = keep_s[m]
@@ -181,7 +181,7 @@
     per_source = freqs // owners
     me = lax.axis_index("ma")
     for step in range(owners):
-        source = cyclic(me - step, owners)
+        source = me ^ step
         at = pl.multiple_of(source * per_source, GROUP)
         packed_v[pl.ds(at, per_source), :] = blocks[step][...]
     share_rows, width = out.shape
@@ -222,6 +222,7 @@
 
 HBM = pl.BlockSpec(memory_space=pltpu.HBM)
 VMEM = pl.BlockSpec(memory_space=pltpu.VMEM)
+SMALL = pltpu.CompilerParams(vmem_limit_bytes=8 * MIB)
 
 
 def in_hbm(operand):
@@ -272,6 +273,7 @@
         in_specs=[VMEM] * (3 + owners),
         out_specs=VMEM,
         scratch_shapes=[pltpu.VMEM((freqs, width), jnp.bfloat16)],
+        compiler_params=SMALL,
         cost_estimate=pl.CostEstimate(
             flops=2 * kl_basis.size * width // shares,
             bytes_accessed=2 * kl_basis.size,
@@ -289,6 +291,7 @@
         in_specs=[VMEM] * 3,
         out_specs=VMEM,
         scratch_shapes=[pltpu.VMEM((rows, width + modes + LANES), jnp.float32)],
+        compiler_params=SMALL,
         cost_estimate=pl.CostEstimate(
             flops=rows * width, bytes_accessed=10 * rows * width, transcendentals=0
         ),
@@ -296,9 +299,8 @@
     )(scalars, mine, got)
 
 
-def ring(axis, step):
-    size = lax.axis_size(axis)
-    return [(i, (i + step) % size) for i in range(size)]
+def pairs(axis, step):
+    return [(i, i ^ step) for i in range(lax.axis_size(axis))]
 
 
 def shards(panels, svd_basis, kl_basis, slot_of_m, svd_keep, kl_keep):
@@ -308,13 +310,13 @@
     mine, send, slot_column, rows_column, scalars = project(
         panels, svd_basis, slot_of_m, svd_keep, kl_keep, owner_slots, width
     )
-    got = lax.ppermute(send, "pa", ring("pa", 1))
+    got = lax.ppermute(send, "pa", pairs("pa", 1))
     summed = [(mine[step] + got[step]).astype(jnp.bfloat16) for step in range(owners)]
     blocks = [summed[0]] + [
-        lax.ppermute(summed[step], "ma", ring("ma", step)) for step in range(1, owners)
+        lax.ppermute(summed[step], "ma", pairs("ma", step)) for step in range(1, owners)
     ]
     send = kl_project(1, jnp.bfloat16, slot_column, rows_column, kl_basis, blocks)
-    got = lax.ppermute(send, "af", ring("af", 1))
+    got = lax.ppermute(send, "af", pairs("af", 1))
     mine = kl_project(0, jnp.float32, slot_column, rows_column, kl_basis, blocks)
     return unpack(scalars, mine, got, owner_slots, modes)
 
@@ -333,7 +335,7 @@
         and share_rows % GROUP == 0
         and mesh.shape["pa"] == 2
         and mesh.shape["af"] == 2
-        and mesh.shape["ma"] <= 4
+        and mesh.shape["ma"] in (2, 4)
     )
 
 

time: 41 us -> 35.1 us (0.86)
  Pallas kernels: 21.1 us -> 16.2 us
  local copies, waits for them, and re-layouts: 1.3 us -> 0.01 us
  waiting for transfers between devices: 9.77 us -> 10.9 us
  other arithmetic: 0.71 us -> 0.06 us
    pallas_call x2, Pallas kernels: 4.15 us -> 0.61 us  [kl_project(): pl.pallas_call(functools.partial(kl_kernel, part, owners), out_shape=jax....]
    unnamed x14 -> x2, local copies, waits for them, and re-layouts: 1.3 us -> 0.01 us
    ppermute x5, waiting for transfers between devices: 9.77 us -> 10.9 us  [the longest x3 6.49 us: shards(): lax.ppermute(summed[step], 'ma', pairs('ma', step))]
    pallas_call x1, Pallas kernels: 2.06 us -> 1.09 us  [unpack(): pl.pallas_call(unpack_kernel, out_shape=jax.ShapeDtypeStruct((owner_slots...]
    convert_element_type x1, other arithmetic: 0.71 us -> 0.06 us  [shards(): (mine[step] + got[step]).astype(jnp.bfloat16)]
  transfers between devices with their start and end apart: 5 -> 5, of which waited for: 4 -> 4; matrix products, arithmetic and copies ran while one was open for 0% -> 0% of each run, Pallas kernels for 5% -> 1%
where the time goes in v3:
time: 35.1 us; the launch traced here: 35 us
  Pallas kernels  16.2 us (46%)
  waiting for transfers between devices  10.9 us (31%)
  starting transfers between devices  7.78 us (22%)
    pallas_call x1, Pallas kernels, project(): pl.pallas_call(functools.partial(project_kernel, owner_slots), out_shape=...  14.5 us
    ppermute x3, waiting for transfers between devices, shards(): lax.ppermute(summed[step], 'ma', pairs('ma', step))  6.49 us
    ppermute x3, starting transfers between devices, shards(): lax.ppermute(summed[step], 'ma', pairs('ma', step))  5.7 us
    ppermute x1, waiting for transfers between devices, shards(): got = lax.ppermute(send, 'af', pairs('af', 1))  2.64 us
    ppermute x1, waiting for transfers between devices, shards(): got = lax.ppermute(send, 'pa', pairs('pa', 1))  1.72 us
    ppermute x1, starting transfers between devices, shards(): got = lax.ppermute(send, 'af', pairs('af', 1))  1.55 us
    pallas_call x1, Pallas kernels, unpack(): pl.pallas_call(unpack_kernel, out_shape=jax.ShapeDtypeStruct((owner_slots...  1.09 us
  transfers between devices with their start and end apart: 5, of which 4 were waited for; matrix products, arithmetic and copies ran while one was open for 0% of the time, Pallas kernels for 1%

profile of v3, /device:TPU:0, one launch (start us, length us, event | category | flops | bytes accessed | tf_op | source)
XLA Modules:
  0.0 35.0 jit_solution(10974510755857697763)
XLA Ops:
  0.0 0.0 copy-start
  0.0 14.5 %project.1 = (f32[4,64,640]{2,1,0:T(8,128)S(1)}, f32[4,64,640]{2,1,0:T(8,128)S(1)}, s32[8,640]{1,0:T(8,128)S(1)}, s32[8,640]{1,0:T(8,128)S(1)}, s32[8,128]{1,0:T(8,128)S(1)}) custom-call(s32[32]{0:T(128)} %slot_hbm.1, s32[32]{0:T(128)} %keep_hbm.1, s32[32]{0:T(128)} %rows_hbm.1, bf16[32,64,1024]{2,1,0:T(8,128)(2,1)} %panels.1, bf16[64,1024,256]{2,1,0:T(8,128)(2,1)} %basis.1), custom_call_target="tpu_custom_call" | custom-call | flops 1073741824 | bytes 37748736 | tf_op jit(solution)/shard_map/project/pallas_call | solution.py:240
  14.5 0.5 %collective-permute-start = (f32[4,64,640]{2,1,0:T(8,128)S(1)}, f32[4,64,640]{2,1,0:T(8,128)S(1)}, u32[]{:S(2)}, u32[]{:S(2)}) collective-permute-start(f32[4,64,640]{2,1,0:T(8,128)S(1)} %get-tuple-element.14), channel_id=1, source_target_pairs={{0,1},{1,0},{2,3},{3,2},{4,5},{5,4},{6,7},{7,6},{8,9},{9,8},{10,11... | collective-permute-start | bytes 1966088 | tf_op jit(solution)/shard_map/ppermute | solution.py:313
  15.1 1.7 %collective-permute-done = f32[4,64,640]{2,1,0:T(8,128)S(1)} collective-permute-done((f32[4,64,640]{2,1,0:T(8,128)S(1)}, f32[4,64,640]{2,1,0:T(8,128)S(1)}, u32[]{:S(2)}, u32[]{:S(2)}) %collective-permute-start) | collective-permute-done | bytes 655392 | tf_op jit(solution)/shard_map/ppermute | solution.py:313
  16.8 0.1 fusion.7
  16.9 5.1 %collective-permute-start.3 = (bf16[64,640]{1,0:T(8,128)(2,1)S(1)}, bf16[64,640]{1,0:T(8,128)(2,1)S(1)}, u32[]{:S(2)}, u32[]{:S(2)}) collective-permute-start(bf16[64,640]{1,0:T(8,128)(2,1)S(1)} %get-tuple-element.15), channel_id=1, source_target_pairs={{0,12},{4,8},{8,4},{12,0},{1,13},{5,9},{9,5},{13,1},{2,14},{6,10},... | collective-permute-start | bytes 245768 | tf_op jit(solution)/shard_map/ppermute | solution.py:316
  21.9 0.0 collective-permute-start.2
  21.9 0.6 %collective-permute-start.1 = (bf16[64,640]{1,0:T(8,128)(2,1)S(1)}, bf16[64,640]{1,0:T(8,128)(2,1)S(1)}, u32[]{:S(2)}, u32[]{:S(2)}) collective-permute-start(bf16[64,640]{1,0:T(8,128)(2,1)S(1)} %get-tuple-element.17), channel_id=1, source_target_pairs={{0,4},{4,0},{8,12},{12,8},{1,5},{5,1},{9,13},{13,9},{2,6},{6,2},{1... | collective-permute-start | bytes 245768 | tf_op jit(solution)/shard_map/ppermute | solution.py:316
  22.6 2.7 %collective-permute-done.3.refs_3_ = bf16[64,640]{1,0:T(8,128)(2,1)S(1)} collective-permute-done((bf16[64,640]{1,0:T(8,128)(2,1)S(1)}, bf16[64,640]{1,0:T(8,128)(2,1)S(1)}, u32[]{:S(2)}, u32[]{:S(2)}) %collective-permute-start.3) | collective-permute-done | bytes 81952 | tf_op jit(solution)/shard_map/ppermute | solution.py:316
  25.3 3.8 %collective-permute-done.2.refs_2_ = bf16[64,640]{1,0:T(8,128)(2,1)S(1)} collective-permute-done((bf16[64,640]{1,0:T(8,128)(2,1)S(1)}, bf16[64,640]{1,0:T(8,128)(2,1)S(1)}, u32[]{:S(2)}, u32[]{:S(2)}) %collective-permute-start.2) | collective-permute-done | bytes 81952 | tf_op jit(solution)/shard_map/ppermute | solution.py:316
  29.1 0.0 collective-permute-done.1.refs_1_
  29.1 0.0 copy-done
  29.1 0.3 kl_project.3
  29.4 1.6 %collective-permute-start.4 = (bf16[64,640]{1,0:T(8,128)(2,1)S(1)}, bf16[64,640]{1,0:T(8,128)(2,1)S(1)}, u32[]{:S(2)}, u32[]{:S(2)}) collective-permute-start(bf16[64,640]{1,0:T(8,128)(2,1)S(1)} %kl_project.3), channel_id=1, source_target_pairs={{0,2},{2,0},{1,3},{3,1},{4,6},{6,4},{5,7},{7,5},{8,10},{10,8},{9,1... | collective-permute-start | bytes 245768 | tf_op jit(solution)/shard_map/ppermute | solution.py:319
  30.9 0.3 kl_project.2.mine
  31.2 2.6 %collective-permute-done.4.got = bf16[64,640]{1,0:T(8,128)(2,1)S(1)} collective-permute-done((bf16[64,640]{1,0:T(8,128)(2,1)S(1)}, bf16[64,640]{1,0:T(8,128)(2,1)S(1)}, u32[]{:S(2)}, u32[]{:S(2)}) %collective-permute-start.4) | collective-permute-done | bytes 81952 | tf_op jit(solution)/shard_map/ppermute | solution.py:319
  33.9 1.1 %unpack.1 = f32[4,64,256]{2,1,0:T(8,128)} custom-call(s32[8,128]{1,0:T(8,128)S(1)} %get-tuple-element.10.scalars, f32[64,640]{1,0:T(8,128)S(1)} %kl_project.2.mine, bf16[64,640]{1,0:T(8,128)(2,1)S(1)} %collective-permute-done.4.got), custom_call_target="tpu_custom_call" | custom-call | flops 40960 | bytes 409600 | tf_op jit(solution)/shard_map/unpack/pallas_call | solution.py:288
Async XLA Ops:
  0.0 29.1 %copy-start = (bf16[4,128,256]{2,1,0:T(8,128)(2,1)S(1)}, bf16[4,128,256]{2,1,0:T(8,128)(2,1)}, u32[]{:S(2)}) copy-start(bf16[4,128,256]{2,1,0:T(8,128)(2,1)} %kl.3) | copy-start | bytes 786436
  14.5 2.3 %collective-permute-start = (f32[4,64,640]{2,1,0:T(8,128)S(1)}, f32[4,64,640]{2,1,0:T(8,128)S(1)}, u32[]{:S(2)}, u32[]{:S(2)}) collective-permute-start(f32[4,64,640]{2,1,0:T(8,128)S(1)} %get-tuple-element.14), channel_id=1, source_target_pairs={{0,1},{1,0},{2,3},{3,2},{4,5},{5,4},{6,7},{7,6},{8,9},{9,8},{10,11... | collective-permute-start | bytes 1966088 | tf_op jit(solution)/shard_map/ppermute | solution.py:313
  16.9 8.4 %collective-permute-start.3 = (bf16[64,640]{1,0:T(8,128)(2,1)S(1)}, bf16[64,640]{1,0:T(8,128)(2,1)S(1)}, u32[]{:S(2)}, u32[]{:S(2)}) collective-permute-start(bf16[64,640]{1,0:T(8,128)(2,1)S(1)} %get-tuple-element.15), channel_id=1, source_target_pairs={{0,12},{4,8},{8,4},{12,0},{1,13},{5,9},{9,5},{13,1},{2,14},{6,10},... | collective-permute-start | bytes 245768 | tf_op jit(solution)/shard_map/ppermute | solution.py:316
  21.9 7.1 %collective-permute-start.2 = (bf16[64,640]{1,0:T(8,128)(2,1)S(1)}, bf16[64,640]{1,0:T(8,128)(2,1)S(1)}, u32[]{:S(2)}, u32[]{:S(2)}) collective-permute-start(bf16[64,640]{1,0:T(8,128)(2,1)S(1)} %get-tuple-element.16), channel_id=1, source_target_pairs={{0,8},{4,12},{8,0},{12,4},{1,9},{5,13},{9,1},{13,5},{2,10},{6,14},... | collective-permute-start | bytes 245768 | tf_op jit(solution)/shard_map/ppermute | solution.py:316
  21.9 7.1 %collective-permute-start.1 = (bf16[64,640]{1,0:T(8,128)(2,1)S(1)}, bf16[64,640]{1,0:T(8,128)(2,1)S(1)}, u32[]{:S(2)}, u32[]{:S(2)}) collective-permute-start(bf16[64,640]{1,0:T(8,128)(2,1)S(1)} %get-tuple-element.17), channel_id=1, source_target_pairs={{0,4},{4,0},{8,12},{12,8},{1,5},{5,1},{9,13},{13,9},{2,6},{6,2},{1... | collective-permute-start | bytes 245768 | tf_op jit(solution)/shard_map/ppermute | solution.py:316
  29.4 4.5 %collective-permute-start.4 = (bf16[64,640]{1,0:T(8,128)(2,1)S(1)}, bf16[64,640]{1,0:T(8,128)(2,1)S(1)}, u32[]{:S(2)}, u32[]{:S(2)}) collective-permute-start(bf16[64,640]{1,0:T(8,128)(2,1)S(1)} %kl_project.3), channel_id=1, source_target_pairs={{0,2},{2,0},{1,3},{3,1},{4,6},{6,4},{5,7},{7,5},{8,10},{10,8},{9,1... | collective-permute-start | bytes 245768 | tf_op jit(solution)/shard_map/ppermute | solution.py:319

commit v4 on v3

v4 whole, which is shorter than its diff:
```python
import functools

import jax
import jax.numpy as jnp
from jax import lax
from jax.experimental import pallas as pl
from jax.experimental.pallas import tpu as pltpu
from jax.sharding import PartitionSpec as P

LANES = 128
GROUP = 16
PACKED = 8
PER_COPY = 2
LATER = 16
EARLY = 8
OWNER_BUDGET = 576
MIB = 2**20


def shards_plain(panels, svd_basis, kl_basis, slot_of_m, svd_keep, kl_keep):
    slot_count = slot_of_m.shape[0]
    order_slots = jnp.argsort(slot_of_m)
    keep_slots = jnp.take(svd_keep, order_slots, axis=0)
    modes_slots = jnp.take(kl_keep, order_slots, axis=0)
    width_modes = svd_basis.shape[2]
    owner_rows = kl_basis.shape[0]
    slot_rows = slot_count // lax.axis_size("pa")
    slot_start = lax.axis_index("pa") * slot_rows
    owner_start = slot_start + lax.axis_index("ma") * owner_rows
    modes_owner = lax.dynamic_slice_in_dim(modes_slots, owner_start, owner_rows, 0)
    chosen = jnp.take(panels, order_slots, axis=0)
    summed = lax.psum_scatter(
        jnp.einsum("mfb,fbr->mfr", chosen, svd_basis, preferred_element_type=jnp.float32),
        "pa",
        scatter_dimension=0,
        tiled=True,
    )
    keep_here = lax.dynamic_slice_in_dim(keep_slots, slot_start, slot_rows, 0)
    columns = jnp.arange(width_modes, dtype=jnp.int32)
    retained = jnp.where(columns[None, None, :] < keep_here[:, None, None], summed, 0.0).astype(
        jnp.bfloat16
    )
    relaid = lax.all_to_all(retained, "ma", split_axis=0, concat_axis=1, tiled=True)
    partial_sums = jnp.einsum("mkf,mfr->mkr", kl_basis, relaid, preferred_element_type=jnp.float32)
    modes = jnp.arange(kl_basis.shape[1], dtype=jnp.int32)
    partial_sums = jnp.where(modes[None, :, None] < modes_owner[:, None, None], partial_sums, 0.0)
    return lax.psum_scatter(partial_sums, "af", scatter_dimension=1, tiled=True)


def cyclic(value, count):
    return lax.rem(value + count, count)


def place_of(slot, owner_slots, half_slots):
    half = cyclic(lax.div(slot, half_slots) - lax.axis_index("pa"), lax.axis_size("pa"))
    within = lax.rem(slot, half_slots)
    owner = lax.div(within, owner_slots) ^ lax.axis_index("ma")
    return half * half_slots + owner * owner_slots + lax.rem(within, owner_slots)


def offsets_of(keep_place, tile_place, shift_place, owner_slots):
    @pl.loop(0, keep_place.shape[0] // owner_slots)
    def _(at):
        offset = jnp.int32(0)
        for j in range(owner_slots):
            place = at * owner_slots + j
            tile = lax.div(offset, LANES)
            tile_place[place] = tile
            shift_place[place] = offset - tile * LANES
            offset = offset + keep_place[place]


def multiply_and_pack(lhs, basis_of, wait, first, out_v, pack_v, mine, send, line, tables):
    tile_place, shift_place, owner_slots = tables
    width, modes = mine.shape[-1], out_v.shape[-1]
    for k in range(PACKED):
        if k % PER_COPY == 0:
            wait(k // PER_COPY)
        out_v[k] = jnp.dot(lhs[first + k], basis_of(k), preferred_element_type=jnp.float32)
    lane = lax.broadcasted_iota(jnp.int32, (PACKED, LANES), 1)
    owners = mine.shape[0]
    rows = pl.ds(pl.multiple_of(line, PACKED), PACKED)
    for at in range(2 * owners):
        for j in range(owner_slots):
            place = at * owner_slots + j
            tile, shift = tile_place[place], shift_place[place]
            left = lane < shift
            before = None
            for t in range(modes // LANES + 1):
                lanes = pl.ds(pl.multiple_of((tile + t) * LANES, LANES), LANES)
                turned = before
                if t < modes // LANES:
                    turned = pltpu.roll(out_v[:, place, t * LANES : (t + 1) * LANES], shift, 1)
                if t == 0:
                    value = jnp.where(left, pack_v[at, :, lanes], turned)
                elif t < modes // LANES:
                    value = jnp.where(left, before, turned)
                else:
                    value = before
                pack_v[at, :, lanes] = value
                before = turned
        to = (mine, send)[at // owners]
        to[at % owners, rows, :] = pack_v[at, :, :width]


def first_kernel(
    owner_slots, slot_hbm, keep_hbm, rows_hbm, panels, basis,
    mine, send, slot_column, rows_column, scalars, lhs_later, basis_later,
    slot_s, keep_s, rows_s, keep_place, rows_place, tile_place, shift_place,
    panels_v, basis_v, lhs_v, out_v, pack_v, small_sem, panel_sem, basis_sem, later_sem,
):
    slots, all_freqs, depth = panels_v.shape
    freqs, later = basis_v.shape[0], basis_later.shape[0]
    groups = freqs // GROUP
    half_slots = slots // lax.axis_size("pa")

    table_copies = [
        pltpu.make_async_copy(slot_hbm, slot_s, small_sem.at[0]),
        pltpu.make_async_copy(keep_hbm, keep_s, small_sem.at[1]),
        pltpu.make_async_copy(rows_hbm, rows_s, small_sem.at[2]),
    ]
    for copy in table_copies:
        copy.start()

    def basis_copy(i):
        part = pl.ds(i * PER_COPY, PER_COPY)
        return pltpu.make_async_copy(basis.at[part], basis_v.at[part], basis_sem.at[i])

    later_copy = pltpu.make_async_copy(basis.at[pl.ds(freqs, later)], basis_later, later_sem)
    ahead = 4
    for i in range(ahead):
        basis_copy(i).start()
    for copy in table_copies:
        copy.wait()

    per_group = GROUP // PER_COPY
    for group in range(groups):
        part = pl.ds(group * GROUP, GROUP if group < groups - 1 else all_freqs - group * GROUP)

        @pl.loop(0, slots)
        def _(m):
            place = place_of(slot_s[m], owner_slots, half_slots)
            if group == 0:
                keep_place[place] = keep_s[m]
                rows_place[place] = rows_s[m]
            pltpu.make_async_copy(
                panels.at[m, part], panels_v.at[place, part], panel_sem.at[group]
            ).start()

        for i in range(ahead + group * per_group, min(ahead + (group + 1) * per_group, groups * per_group)):
            basis_copy(i).start()
    later_copy.start()

    offsets_of(keep_place, tile_place, shift_place, owner_slots)
    column = lax.broadcasted_iota(jnp.int32, slot_column.shape, 1)
    slot_at = jnp.full(slot_column.shape, owner_slots, jnp.int32)
    rows_at = jnp.zeros(slot_column.shape, jnp.int32)
    for j in range(owner_slots):
        keep = keep_place[j]
        offset = tile_place[j] * LANES + shift_place[j]
        within = (column >= offset) & (column < offset + keep)
        slot_at = jnp.where(within, j, slot_at)
        rows_at = jnp.where(within, rows_place[j], rows_at)
        scalars[j : j + 1, :] = jnp.full((1, LANES), offset, jnp.int32)
        scalars[owner_slots + j : owner_slots + j + 1, :] = jnp.full((1, LANES), keep, jnp.int32)
    slot_column[...] = slot_at
    rows_column[...] = rows_at

    side = GROUP * GROUP
    row = lax.broadcasted_iota(jnp.int32, (side, side), 0)
    column = lax.broadcasted_iota(jnp.int32, (side, side), 1)
    swap = (column == (row % GROUP) * GROUP + row // GROUP).astype(jnp.float32).astype(jnp.bfloat16)

    def turn(here, to):
        for block in range(slots // GROUP):
            blocks = slice(block * GROUP, (block + 1) * GROUP)
            tile = panels_v[blocks, here, :].reshape(side, depth)
            turned = jnp.dot(swap, tile, preferred_element_type=jnp.float32).astype(jnp.bfloat16)
            to[:, blocks, :] = turned.reshape(GROUP, GROUP, depth)

    def panels_wait(here, group):
        pltpu.make_async_copy(
            panels_v.at[:, here], panels_v.at[:, here], panel_sem.at[group]
        ).wait()

    @pl.loop(0, groups)
    def _(group):
        here = pl.ds(pl.multiple_of(group * GROUP, GROUP), GROUP)

        @pl.when(group < groups - 1)
        def _():
            panels_wait(here, group)

        @pl.when(group == groups - 1)
        def _():
            rest = pl.ds((groups - 1) * GROUP, all_freqs - (groups - 1) * GROUP)
            panels_wait(rest, groups - 1)
            turn(pl.ds(freqs, GROUP), lhs_later)

        turn(here, lhs_v)

        @pl.loop(0, GROUP // PACKED)
        def _(part):
            line = group * GROUP + part * PACKED
            multiply_and_pack(
                lhs_v,
                lambda k: basis_v[line + k],
                lambda c: basis_copy(line // PER_COPY + c).wait(),
                part * PACKED,
                out_v, pack_v, mine, send, line,
                (tile_place, shift_place, owner_slots),
            )

    later_copy.wait()


def second_kernel(
    start, owner_slots, slot_hbm, keep_hbm, basis, lhs, basis_early,
    mine, send,
    slot_s, keep_s, keep_place, tile_place, shift_place,
    basis_v, out_v, pack_v, small_sem, basis_sem,
):
    slots = lhs.shape[1]
    early, rest = basis_early.shape[0], basis_v.shape[0]
    half_slots = slots // lax.axis_size("pa")

    def basis_copy(i):
        part = pl.ds(start + early + i * PER_COPY, PER_COPY)
        return pltpu.make_async_copy(
            basis.at[part], basis_v.at[pl.ds(i * PER_COPY, PER_COPY)], basis_sem.at[i]
        )

    for i in range(rest // PER_COPY):
        basis_copy(i).start()
    table_copies = [
        pltpu.make_async_copy(slot_hbm, slot_s, small_sem.at[0]),
        pltpu.make_async_copy(keep_hbm, keep_s, small_sem.at[1]),
    ]
    for copy in table_copies:
        copy.start()
    for copy in table_copies:
        copy.wait()

    @pl.loop(0, slots)
    def _(m):
        keep_place[place_of(slot_s[m], owner_slots, half_slots)] = keep_s[m]

    offsets_of(keep_place, tile_place, shift_place, owner_slots)
    tables = (tile_place, shift_place, owner_slots)
    for line in range(0, early, PACKED):
        multiply_and_pack(
            lhs, lambda k: basis_early[line + k], lambda c: None, line,
            out_v, pack_v, mine, send, line, tables,
        )
    for line in range(0, rest, PACKED):
        multiply_and_pack(
            lhs,
            lambda k: basis_v[line + k],
            lambda c: basis_copy(line // PER_COPY + c).wait(),
            early + line,
            out_v, pack_v, mine, send, early + line, tables,
        )


def kl_kernel(part, owners, starts, slot_column, rows_column, kl, *refs):
    count = owners * len(starts)
    blocks, (out, packed_v) = refs[:count], refs[count:]
    owner_slots, rows, freqs = kl.shape
    shares = lax.axis_size("af")
    per_source = freqs // owners
    me = lax.axis_index("ma")
    for i, block in enumerate(blocks):
        source = me ^ (i % owners)
        at = pl.multiple_of(source * per_source + starts[i // owners], GROUP)
        packed_v[pl.ds(at, block.shape[0]), :] = block[...]
    share_rows, width = out.shape
    at = pl.multiple_of(cyclic(lax.axis_index("af") + part, shares) * share_rows, GROUP)
    lhs = kl[:, pl.ds(at, share_rows), :].reshape(owner_slots * share_rows, freqs)
    product = jnp.dot(lhs, packed_v[...], preferred_element_type=jnp.float32)
    line = lax.broadcasted_iota(jnp.int32, (share_rows, width), 0) + at
    slot_at = slot_column[0:1, :]
    total = jnp.zeros((share_rows, width), jnp.float32)
    for j in range(owner_slots):
        here = product[j * share_rows : (j + 1) * share_rows]
        total = jnp.where(slot_at == j, here, total)
    out[...] = jnp.where(line < rows_column[0:1, :], total, 0.0).astype(out.dtype)


def unpack_kernel(scalars, mine, got, out, sum_v):
    owner_slots, rows, modes = out.shape
    width = mine.shape[1]
    sum_v[:, :width] = mine[...] + got[...].astype(jnp.float32)
    lane = lax.broadcasted_iota(jnp.int32, (rows, LANES), 1)
    for j in range(owner_slots):
        offset = jnp.max(scalars[j : j + 1, :])
        keep = jnp.max(scalars[owner_slots + j : owner_slots + j + 1, :])
        tile = lax.div(offset, LANES)
        shift = offset - tile * LANES
        back = lax.rem(LANES - shift, LANES)
        turned = [
            pltpu.roll(
                sum_v[:, pl.ds(pl.multiple_of((tile + t) * LANES, LANES), LANES)], back, 1
            )
            for t in range(modes // LANES + 1)
        ]
        for t in range(modes // LANES):
            value = jnp.where(lane < LANES - shift, turned[t], turned[t + 1])
            value = jnp.where(lane < keep - t * LANES, value, 0.0)
            out[j, :, t * LANES : (t + 1) * LANES] = value


HBM = pl.BlockSpec(memory_space=pltpu.HBM)
VMEM = pl.BlockSpec(memory_space=pltpu.VMEM)
SMALL = pltpu.CompilerParams(vmem_limit_bytes=8 * MIB)


def in_hbm(operand):
    return pltpu.with_memory_space_constraint(operand, pltpu.HBM)


def project_cost(slots, freqs, depth, modes):
    return pl.CostEstimate(
        flops=2 * slots * freqs * depth * modes,
        bytes_accessed=2 * freqs * depth * (modes + slots),
        transcendentals=0,
    )


def project(panels, svd_basis, slot_of_m, svd_keep, kl_keep, owner_slots, width):
    slots, all_freqs, depth = panels.shape
    modes = svd_basis.shape[2]
    freqs = all_freqs - LATER
    owners, halves = lax.axis_size("ma"), lax.axis_size("pa")
    table = pltpu.SMEM((slots,), jnp.int32)
    wide = width + modes + LANES

    def packed(count):
        return jax.ShapeDtypeStruct((owners, count, width), jnp.float32)

    column = jax.ShapeDtypeStruct((8, width), jnp.int32)
    work = [
        pltpu.VMEM((PACKED, slots, modes), jnp.float32),
        pltpu.VMEM((halves * owners, PACKED, wide), jnp.float32),
    ]
    mine, send, slot_column, rows_column, scalars, lhs, early = pl.pallas_call(
        functools.partial(first_kernel, owner_slots),
        out_shape=(
            packed(freqs),
            packed(freqs),
            column,
            column,
            jax.ShapeDtypeStruct((8, LANES), jnp.int32),
            jax.ShapeDtypeStruct((LATER, slots, depth), jnp.bfloat16),
            jax.ShapeDtypeStruct((EARLY, depth, modes), jnp.bfloat16),
        ),
        in_specs=[HBM] * 5,
        out_specs=(VMEM,) * 7,
        scratch_shapes=[table] * 7
        + [
            pltpu.VMEM((slots, all_freqs, depth), jnp.bfloat16),
            pltpu.VMEM((freqs, depth, modes), jnp.bfloat16),
            pltpu.VMEM((GROUP, slots, depth), jnp.bfloat16),
        ]
        + work
        + [
            pltpu.SemaphoreType.DMA((3,)),
            pltpu.SemaphoreType.DMA((freqs // GROUP,)),
            pltpu.SemaphoreType.DMA((freqs // PER_COPY,)),
            pltpu.SemaphoreType.DMA,
        ],
        compiler_params=pltpu.CompilerParams(vmem_limit_bytes=44 * MIB),
        cost_estimate=project_cost(slots, freqs, depth, modes),
        name="project_first",
    )(*map(in_hbm, (slot_of_m, svd_keep, kl_keep, panels, svd_basis)))
    rest = LATER - EARLY
    second = pl.pallas_call(
        functools.partial(second_kernel, freqs, owner_slots),
        out_shape=(packed(LATER), packed(LATER)),
        in_specs=[HBM] * 3 + [VMEM] * 2,
        out_specs=(VMEM,) * 2,
        scratch_shapes=[table] * 5
        + [pltpu.VMEM((rest, depth, modes), jnp.bfloat16)]
        + work
        + [
            pltpu.SemaphoreType.DMA((2,)),
            pltpu.SemaphoreType.DMA((rest // PER_COPY,)),
        ],
        compiler_params=pltpu.CompilerParams(vmem_limit_bytes=16 * MIB),
        cost_estimate=project_cost(slots, LATER, depth, modes),
        name="project_second",
    )(*map(in_hbm, (slot_of_m, svd_keep, svd_basis)), lhs, early)
    return ((mine, send), tuple(second)), slot_column, rows_column, scalars


def kl_project(part, kind, slot_column, rows_column, kl_basis, blocks, starts):
    owners, shares = lax.axis_size("ma"), lax.axis_size("af")
    rows, freqs = kl_basis.shape[1:]
    width = slot_column.shape[1]
    return pl.pallas_call(
        functools.partial(kl_kernel, part, owners, starts),
        out_shape=jax.ShapeDtypeStruct((rows // shares, width), kind),
        in_specs=[VMEM] * (3 + len(blocks)),
        out_specs=VMEM,
        scratch_shapes=[pltpu.VMEM((freqs, width), jnp.bfloat16)],
        compiler_params=SMALL,
        cost_estimate=pl.CostEstimate(
            flops=2 * kl_basis.size * width // shares,
            bytes_accessed=2 * kl_basis.size,
            transcendentals=0,
        ),
        name="kl_project",
    )(slot_column, rows_column, kl_basis, *blocks)


def unpack(scalars, mine, got, owner_slots, modes):
    rows, width = mine.shape
    return pl.pallas_call(
        unpack_kernel,
        out_shape=jax.ShapeDtypeStruct((owner_slots, rows, modes), jnp.float32),
        in_specs=[VMEM] * 3,
        out_specs=VMEM,
        scratch_shapes=[pltpu.VMEM((rows, width + modes + LANES), jnp.float32)],
        compiler_params=SMALL,
        cost_estimate=pl.CostEstimate(
            flops=rows * width, bytes_accessed=10 * rows * width, transcendentals=0
        ),
        name="unpack",
    )(scalars, mine, got)


def pairs(axis, step):
    return [(i, i ^ step) for i in range(lax.axis_size(axis))]


def shards(panels, svd_basis, kl_basis, slot_of_m, svd_keep, kl_keep):
    owner_slots, modes = kl_basis.shape[0], svd_basis.shape[2]
    owners = lax.axis_size("ma")
    width = -(-min(OWNER_BUDGET, owner_slots * modes) // LANES) * LANES
    chunks, slot_column, rows_column, scalars = project(
        panels, svd_basis, slot_of_m, svd_keep, kl_keep, owner_slots, width
    )
    blocks, starts, start = [], [], 0
    for mine, send in chunks:
        got = lax.ppermute(send, "pa", pairs("pa", 1))
        summed = [(mine[step] + got[step]).astype(jnp.bfloat16) for step in range(owners)]
        blocks += [summed[0]] + [
            lax.ppermute(summed[step], "ma", pairs("ma", step)) for step in range(1, owners)
        ]
        starts.append(start)
        start += mine.shape[1]
    tables = (slot_column, rows_column, kl_basis, blocks, tuple(starts))
    send = kl_project(1, jnp.bfloat16, *tables)
    got = lax.ppermute(send, "af", pairs("af", 1))
    mine = kl_project(0, jnp.float32, *tables)
    return unpack(scalars, mine, got, owner_slots, modes)


def kernels_fit(mesh, args):
    panels, svd_basis, kl_basis = args[:3]
    slots = panels.shape[0] // mesh.shape["grp"]
    freqs = svd_basis.shape[0] // (mesh.shape["af"] * mesh.shape["ma"])
    owner_slots = kl_basis.shape[0] // (mesh.shape["pa"] * mesh.shape["ma"])
    share_rows = kl_basis.shape[1] // mesh.shape["af"]
    return (
        freqs % GROUP == 0
        and freqs > LATER
        and slots % (GROUP * mesh.shape["pa"]) == 0
        and owner_slots == 4
        and svd_basis.shape[2] == 2 * LANES
        and share_rows % GROUP == 0
        and mesh.shape["pa"] == 2
        and mesh.shape["af"] == 2
        and mesh.shape["ma"] in (2, 4)
    )


def solution(mesh):
    in_specs = (
        P("grp", ("af", "ma"), "pa"),
        P(("af", "ma"), "pa", None),
        P(("pa", "ma"), None, "af"),
        P(),
        P(),
        P(),
    )
    out_specs = P(("grp", "pa", "ma"), "af", None)

    def run(*args):
        body = shards if kernels_fit(mesh, args) else shards_plain
        mapped = jax.shard_map(
            body, mesh=mesh, in_specs=in_specs, out_specs=out_specs, check_vma=False
        )
        return mapped(*args)

    return run
```

time: 35.1 us -> 40.8 us (1.16)
  starting transfers between devices: 7.78 us -> 11.9 us
  Pallas kernels: 16.2 us -> 20.1 us
  waiting for transfers between devices: 10.9 us -> 8.62 us
    ppermute x3 -> x6, starting transfers between devices: 5.7 us -> 9.7 us  [shards(): lax.ppermute(summed[step], 'ma', pairs('ma', step))]
    pallas_call x3 -> x4, Pallas kernels: 15.1 us -> 19 us  [the longest x1 14.1 us: project(): pl.pallas_call(functools.partial(first_kernel, owner_slots), out_shape=(p...]
    ppermute x1 -> x2, waiting for transfers between devices: 1.72 us -> 0.01 us  [shards(): got = lax.ppermute(send, 'pa', pairs('pa', 1))]
    ppermute x3 -> x6, waiting for transfers between devices: 6.49 us -> 5.98 us  [shards(): lax.ppermute(summed[step], 'ma', pairs('ma', step))]
  transfers between devices with their start and end apart: 5 -> 9, of which waited for: 4 -> 4; matrix products, arithmetic and copies ran while one was open for 0% -> 0% of each run, Pallas kernels for 1% -> 11%
where the time goes in v4:
time: 40.8 us; the launch traced here: 40.7 us
  Pallas kernels  20.1 us (49%)
  starting transfers between devices  11.9 us (29%)
  waiting for transfers between devices  8.62 us (21%)
    pallas_call x1, Pallas kernels, project(): pl.pallas_call(functools.partial(first_kernel, owner_slots), out_shape=(p...  14.1 us
    ppermute x6, starting transfers between devices, shards(): lax.ppermute(summed[step], 'ma', pairs('ma', step))  9.7 us
    ppermute x6, waiting for transfers between devices, shards(): lax.ppermute(summed[step], 'ma', pairs('ma', step))  5.98 us
    pallas_call x1, Pallas kernels, project(): pl.pallas_call(functools.partial(second_kernel, freqs, owner_slots), out_...  4.27 us
    ppermute x1, waiting for transfers between devices, shards(): got = lax.ppermute(send, 'af', pairs('af', 1))  2.64 us
    ppermute x1, starting transfers between devices, shards(): got = lax.ppermute(send, 'af', pairs('af', 1))  1.55 us
    pallas_call x1, Pallas kernels, unpack(): pl.pallas_call(unpack_kernel, out_shape=jax.ShapeDtypeStruct((owner_slots...  1.09 us
  transfers between devices with their start and end apart: 9, of which 4 were waited for; matrix products, arithmetic and copies ran while one was open for 0% of the time, Pallas kernels for 11%

profile of v4, /device:TPU:0, one launch (start us, length us, event | category | flops | bytes accessed | tf_op | source)
XLA Modules:
  0.0 40.7 jit_solution(1594850336402691429)
XLA Ops:
  0.0 14.1 %project_first.1 = (f32[4,48,640]{2,1,0:T(8,128)S(1)}, f32[4,48,640]{2,1,0:T(8,128)S(1)}, s32[8,640]{1,0:T(8,128)S(1)}, s32[8,640]{1,0:T(8,128)S(1)}, s32[8,128]...) custom-call(s32[32]{0:T(128)} %slot_hbm.3, s32[32]{0:T(128)} %keep_hbm.3, ...), custom_call_target="tpu_custom_call" | custom-call | flops 805306368 | bytes 28311552 | tf_op jit(solution)/shard_map/project_first/pallas_call | solution.py:345
  14.1 0.5 %collective-permute-start = (f32[4,48,640]{2,1,0:T(8,128)S(1)}, f32[4,48,640]{2,1,0:T(8,128)S(1)}, u32[]{:S(2)}, u32[]{:S(2)}) collective-permute-start(f32[4,48,640]{2,1,0:T(8,128)S(1)} %get-tuple-element.18), channel_id=1, source_target_pairs={{0,1},{1,0},{2,3},{3,2},{4,5},{5,4},{6,7},{7,6},{8,9},{9,8},{10,11... | collective-permute-start | bytes 1474568 | tf_op jit(solution)/shard_map/ppermute | solution.py:444
  14.6 0.0 copy-start
  14.6 4.3 %project_second.1 = (f32[4,16,640]{2,1,0:T(8,128)S(1)}, f32[4,16,640]{2,1,0:T(8,128)S(1)}) custom-call(s32[32]{0:T(128)} %slot_hbm.3, s32[32]{0:T(128)} %keep_hbm.3, bf16[64,1024,256]{2,1,0:T(8,128)(2,1)} %basis.3, bf16[16,32,1024]{2,1,0:T(8,128)(2,1)S(1)} %get-tuple-element.19.lhs, bf16[8,1024,256]{2,1,0:T(8,128)(2,1)S(1)} %get-tuple-element.20.basis_early), custom_call_target="tpu_custom_call" | custom-call | flops 268435456 | bytes 9437184 | tf_op jit(solution)/shard_map/project_second/pallas_call | solution.py:376
  18.9 0.1 collective-permute-start.4
  19.0 0.0 collective-permute-done
  19.1 5.1 %collective-permute-start.3 = (bf16[48,640]{1,0:T(8,128)(2,1)S(1)}, bf16[48,640]{1,0:T(8,128)(2,1)S(1)}, u32[]{:S(2)}, u32[]{:S(2)}) collective-permute-start(bf16[48,640]{1,0:T(8,128)(2,1)S(1)} %get-tuple-element.23), channel_id=1, source_target_pairs={{0,12},{4,8},{8,4},{12,0},{1,13},{5,9},{9,5},{13,1},{2,14},{6,10},... | collective-permute-start | bytes 184328 | tf_op jit(solution)/shard_map/ppermute | solution.py:447
  24.2 0.0 collective-permute-start.2
  24.2 0.6 %collective-permute-start.1 = (bf16[48,640]{1,0:T(8,128)(2,1)S(1)}, bf16[48,640]{1,0:T(8,128)(2,1)S(1)}, u32[]{:S(2)}, u32[]{:S(2)}) collective-permute-start(bf16[48,640]{1,0:T(8,128)(2,1)S(1)} %get-tuple-element.25), channel_id=1, source_target_pairs={{0,4},{4,0},{8,12},{12,8},{1,5},{5,1},{9,13},{13,9},{2,6},{6,2},{1... | collective-permute-start | bytes 184328 | tf_op jit(solution)/shard_map/ppermute | solution.py:447
  24.8 0.0 collective-permute-done.4
  24.8 3.8 %collective-permute-start.7 = (bf16[16,640]{1,0:T(8,128)(2,1)S(1)}, bf16[16,640]{1,0:T(8,128)(2,1)S(1)}, u32[]{:S(2)}, u32[]{:S(2)}) collective-permute-start(bf16[16,640]{1,0:T(8,128)(2,1)S(1)} %get-tuple-element.27), channel_id=1, source_target_pairs={{0,12},{4,8},{8,4},{12,0},{1,13},{5,9},{9,5},{13,1},{2,14},{6,10},... | collective-permute-start | bytes 61448 | tf_op jit(solution)/shard_map/ppermute | solution.py:447
  28.7 0.0 collective-permute-start.6
  28.7 2.3 %collective-permute-done.7.refs_7_ = bf16[16,640]{1,0:T(8,128)(2,1)S(1)} collective-permute-done((bf16[16,640]{1,0:T(8,128)(2,1)S(1)}, bf16[16,640]{1,0:T(8,128)(2,1)S(1)}, u32[]{:S(2)}, u32[]{:S(2)}) %collective-permute-start.7) | collective-permute-done | bytes 20512 | tf_op jit(solution)/shard_map/ppermute | solution.py:447
  31.0 0.1 collective-permute-start.5
  31.1 2.2 %collective-permute-done.6.refs_6_ = bf16[16,640]{1,0:T(8,128)(2,1)S(1)} collective-permute-done((bf16[16,640]{1,0:T(8,128)(2,1)S(1)}, bf16[16,640]{1,0:T(8,128)(2,1)S(1)}, u32[]{:S(2)}, u32[]{:S(2)}) %collective-permute-start.6) | collective-permute-done | bytes 20512 | tf_op jit(solution)/shard_map/ppermute | solution.py:447
  33.3 1.4 %collective-permute-done.5.refs_5_ = bf16[16,640]{1,0:T(8,128)(2,1)S(1)} collective-permute-done((bf16[16,640]{1,0:T(8,128)(2,1)S(1)}, bf16[16,640]{1,0:T(8,128)(2,1)S(1)}, u32[]{:S(2)}, u32[]{:S(2)}) %collective-permute-start.5) | collective-permute-done | bytes 20512 | tf_op jit(solution)/shard_map/ppermute | solution.py:447
  34.8 0.0 collective-permute-done.3.refs_3_
  34.8 0.0 collective-permute-done.2.refs_2_
  34.8 0.0 collective-permute-done.1.refs_1_
  34.8 0.0 copy-done
  34.8 0.3 kl_project.3
  35.1 1.6 %collective-permute-start.8 = (bf16[64,640]{1,0:T(8,128)(2,1)S(1)}, bf16[64,640]{1,0:T(8,128)(2,1)S(1)}, u32[]{:S(2)}, u32[]{:S(2)}) collective-permute-start(bf16[64,640]{1,0:T(8,128)(2,1)S(1)} %kl_project.3), channel_id=1, source_target_pairs={{0,2},{2,0},{1,3},{3,1},{4,6},{6,4},{5,7},{7,5},{8,10},{10,8},{9,1... | collective-permute-start | bytes 245768 | tf_op jit(solution)/shard_map/ppermute | solution.py:453
  36.7 0.3 kl_project.2.mine
  37.0 2.6 %collective-permute-done.8.got = bf16[64,640]{1,0:T(8,128)(2,1)S(1)} collective-permute-done((bf16[64,640]{1,0:T(8,128)(2,1)S(1)}, bf16[64,640]{1,0:T(8,128)(2,1)S(1)}, u32[]{:S(2)}, u32[]{:S(2)}) %collective-permute-start.8) | collective-permute-done | bytes 81952 | tf_op jit(solution)/shard_map/ppermute | solution.py:453
  39.6 1.1 %unpack.1 = f32[4,64,256]{2,1,0:T(8,128)} custom-call(s32[8,128]{1,0:T(8,128)S(1)} %get-tuple-element.14.scalars, f32[64,640]{1,0:T(8,128)S(1)} %kl_project.2.mine, bf16[64,640]{1,0:T(8,128)(2,1)S(1)} %collective-permute-done.8.got), custom_call_target="tpu_custom_call" | custom-call | flops 40960 | bytes 409600 | tf_op jit(solution)/shard_map/unpack/pallas_call | solution.py:417
  (2 shorter events, 0.1 us)
Async XLA Ops:
  14.1 4.9 %collective-permute-start = (f32[4,48,640]{2,1,0:T(8,128)S(1)}, f32[4,48,640]{2,1,0:T(8,128)S(1)}, u32[]{:S(2)}, u32[]{:S(2)}) collective-permute-start(f32[4,48,640]{2,1,0:T(8,128)S(1)} %get-tuple-element.18), channel_id=1, source_target_pairs={{0,1},{1,0},{2,3},{3,2},{4,5},{5,4},{6,7},{7,6},{8,9},{9,8},{10,11... | collective-permute-start | bytes 1474568 | tf_op jit(solution)/shard_map/ppermute | solution.py:444
  14.6 20.2 %copy-start = (bf16[4,128,256]{2,1,0:T(8,128)(2,1)S(1)}, bf16[4,128,256]{2,1,0:T(8,128)(2,1)}, u32[]{:S(2)}) copy-start(bf16[4,128,256]{2,1,0:T(8,128)(2,1)} %kl.3) | copy-start | bytes 786436
  18.9 5.9 %collective-permute-start.4 = (f32[4,16,640]{2,1,0:T(8,128)S(1)}, f32[4,16,640]{2,1,0:T(8,128)S(1)}, u32[]{:S(2)}, u32[]{:S(2)}) collective-permute-start(f32[4,16,640]{2,1,0:T(8,128)S(1)} %get-tuple-element.22), channel_id=1, source_target_pairs={{0,1},{1,0},{2,3},{3,2},{4,5},{5,4},{6,7},{7,6},{8,9},{9,8},{10,11... | collective-permute-start | bytes 491528 | tf_op jit(solution)/shard_map/ppermute | solution.py:444
  19.1 15.7 %collective-permute-start.3 = (bf16[48,640]{1,0:T(8,128)(2,1)S(1)}, bf16[48,640]{1,0:T(8,128)(2,1)S(1)}, u32[]{:S(2)}, u32[]{:S(2)}) collective-permute-start(bf16[48,640]{1,0:T(8,128)(2,1)S(1)} %get-tuple-element.23), channel_id=1, source_target_pairs={{0,12},{4,8},{8,4},{12,0},{1,13},{5,9},{9,5},{13,1},{2,14},{6,10},... | collective-permute-start | bytes 184328 | tf_op jit(solution)/shard_map/ppermute | solution.py:447
  24.2 10.6 %collective-permute-start.2 = (bf16[48,640]{1,0:T(8,128)(2,1)S(1)}, bf16[48,640]{1,0:T(8,128)(2,1)S(1)}, u32[]{:S(2)}, u32[]{:S(2)}) collective-permute-start(bf16[48,640]{1,0:T(8,128)(2,1)S(1)} %get-tuple-element.24), channel_id=1, source_target_pairs={{0,8},{4,12},{8,0},{12,4},{1,9},{5,13},{9,1},{13,5},{2,10},{6,14},... | collective-permute-start | bytes 184328 | tf_op jit(solution)/shard_map/ppermute | solution.py:447
  24.2 10.6 %collective-permute-start.1 = (bf16[48,640]{1,0:T(8,128)(2,1)S(1)}, bf16[48,640]{1,0:T(8,128)(2,1)S(1)}, u32[]{:S(2)}, u32[]{:S(2)}) collective-permute-start(bf16[48,640]{1,0:T(8,128)(2,1)S(1)} %get-tuple-element.25), channel_id=1, source_target_pairs={{0,4},{4,0},{8,12},{12,8},{1,5},{5,1},{9,13},{13,9},{2,6},{6,2},{1... | collective-permute-start | bytes 184328 | tf_op jit(solution)/shard_map/ppermute | solution.py:447
  24.8 6.1 %collective-permute-start.7 = (bf16[16,640]{1,0:T(8,128)(2,1)S(1)}, bf16[16,640]{1,0:T(8,128)(2,1)S(1)}, u32[]{:S(2)}, u32[]{:S(2)}) collective-permute-start(bf16[16,640]{1,0:T(8,128)(2,1)S(1)} %get-tuple-element.27), channel_id=1, source_target_pairs={{0,12},{4,8},{8,4},{12,0},{1,13},{5,9},{9,5},{13,1},{2,14},{6,10},... | collective-permute-start | bytes 61448 | tf_op jit(solution)/shard_map/ppermute | solution.py:447
  28.7 4.7 %collective-permute-start.6 = (bf16[16,640]{1,0:T(8,128)(2,1)S(1)}, bf16[16,640]{1,0:T(8,128)(2,1)S(1)}, u32[]{:S(2)}, u32[]{:S(2)}) collective-permute-start(bf16[16,640]{1,0:T(8,128)(2,1)S(1)} %get-tuple-element.28), channel_id=1, source_target_pairs={{0,8},{4,12},{8,0},{12,4},{1,9},{5,13},{9,1},{13,5},{2,10},{6,14},... | collective-permute-start | bytes 61448 | tf_op jit(solution)/shard_map/ppermute | solution.py:447
  31.0 3.8 %collective-permute-start.5 = (bf16[16,640]{1,0:T(8,128)(2,1)S(1)}, bf16[16,640]{1,0:T(8,128)(2,1)S(1)}, u32[]{:S(2)}, u32[]{:S(2)}) collective-permute-start(bf16[16,640]{1,0:T(8,128)(2,1)S(1)} %get-tuple-element.29), channel_id=1, source_target_pairs={{0,4},{4,0},{8,12},{12,8},{1,5},{5,1},{9,13},{13,9},{2,6},{6,2},{1... | collective-permute-start | bytes 61448 | tf_op jit(solution)/shard_map/ppermute | solution.py:447
  35.1 4.5 %collective-permute-start.8 = (bf16[64,640]{1,0:T(8,128)(2,1)S(1)}, bf16[64,640]{1,0:T(8,128)(2,1)S(1)}, u32[]{:S(2)}, u32[]{:S(2)}) collective-permute-start(bf16[64,640]{1,0:T(8,128)(2,1)S(1)} %kl_project.3), channel_id=1, source_target_pairs={{0,2},{2,0},{1,3},{3,1},{4,6},{6,4},{5,7},{7,5},{8,10},{10,8},{9,1... | collective-permute-start | bytes 245768 | tf_op jit(solution)/shard_map/ppermute | solution.py:453

commit v5 on v3

--- a/solution.py
+++ b/solution.py
@@ -9,6 +9,8 @@
 
 LANES = 128
 GROUP = 16
+PACKED = 8
+PER_COPY = 2
 OWNER_BUDGET = 576
 MIB = 2**20
 
@@ -47,26 +49,79 @@
     return lax.rem(value + count, count)
 
 
-def shifted(tiles, shift, lane):
-    low, high = (pltpu.roll(tile, shift, 1) for tile in tiles)
-    left = lane < shift
-    return jnp.where(left, 0.0, low), jnp.where(left, low, high), jnp.where(left, high, 0.0)
+def place_of(slot, owner_slots, half_slots):
+    half = cyclic(lax.div(slot, half_slots) - lax.axis_index("pa"), lax.axis_size("pa"))
+    within = lax.rem(slot, half_slots)
+    owner = lax.div(within, owner_slots) ^ lax.axis_index("ma")
+    return half * half_slots + owner * owner_slots + lax.rem(within, owner_slots)
+
+
+def offsets_of(keep_place, tile_place, shift_place, owner_slots):
+    @pl.loop(0, keep_place.shape[0] // owner_slots)
+    def _(at):
+        offset = jnp.int32(0)
+        for j in range(owner_slots):
+            place = at * owner_slots + j
+            tile = lax.div(offset, LANES)
+            tile_place[place] = tile
+            shift_place[place] = offset - tile * LANES
+            offset = offset + keep_place[place]
+
+
+def multiply_and_pack(lhs, basis_of, wait, first, out_v, mine, send, line, tables):
+    tile_place, shift_place, owner_slots = tables
+    slots = lhs.shape[1]
+    tiles = out_v.shape[0] // (PACKED * slots)
+    last = mine.shape[-1] // LANES - 1
+    for k in range(PACKED):
+        if k % PER_COPY == 0:
+            wait(k // PER_COPY)
+        product = jnp.dot(lhs[first + k], basis_of(k), preferred_element_type=jnp.float32)
+        for t in range(tiles):
+            at = (t * PACKED + k) * slots
+            out_v[at : at + slots, :] = product[:, t * LANES : (t + 1) * LANES]
+    lane = lax.broadcasted_iota(jnp.int32, (PACKED, LANES), 1)
+    owners = mine.shape[0]
+    rows = pl.ds(pl.multiple_of(line, PACKED), PACKED)
+    for at in range(2 * owners):
+        to, owner = (mine, send)[at // owners], at % owners
+        values, tile_before = None, None
+        for j in range(owner_slots):
+            place = at * owner_slots + j
+            tile, shift = tile_place[place], shift_place[place]
+            left = lane < shift
+            turned = [
+                pltpu.roll(
+                    out_v[pl.ds(t * PACKED * slots + place, PACKED, stride=slots), :], shift, 1
+                )
+                for t in range(tiles)
+            ]
+            shared = turned[0]
+            if j > 0:
+                step = tile - tile_before
+                shared = values[0]
+                for t in range(1, tiles + 1):
+                    shared = jnp.where(step == t, values[t], shared)
+            values = (
+                [jnp.where(left, shared, turned[0])]
+                + [jnp.where(left, turned[t - 1], turned[t]) for t in range(1, tiles)]
+                + [turned[tiles - 1]]
+            )
+            tile_before = tile
+            for t in reversed(range(tiles + 1)):
+                at_lane = pl.multiple_of(jnp.minimum(tile + t, last) * LANES, LANES)
+                to[owner, rows, pl.ds(at_lane, LANES)] = values[t]
 
 
 def project_kernel(
     owner_slots, slot_hbm, keep_hbm, rows_hbm, panels, basis,
     mine, send, slot_column, rows_column, scalars,
-    slot_s, keep_s, rows_s, keep_place, rows_place,
-    panels_v, basis_v, lhs_v, out_v, pack_v, small_sem, panel_sem, basis_sem,
+    slot_s, keep_s, rows_s, keep_place, rows_place, tile_place, shift_place,
+    panels_v, basis_v, lhs_v, out_v, small_sem, panel_sem, basis_sem,
 ):
     slots, freqs, depth = panels_v.shape
     groups = freqs // GROUP
-    copies = basis_sem.shape[0] // groups
-    per_copy = GROUP // copies
-    halves, owners = lax.axis_size("pa"), lax.axis_size("ma")
-    my_half, my_owner = lax.axis_index("pa"), lax.axis_index("ma")
-    half_slots = slots // halves
-    width, modes = mine.shape[-1], basis.shape[-1]
+    half_slots = slots // lax.axis_size("pa")
 
     table_copies = [
         pltpu.make_async_copy(slot_hbm, slot_s, small_sem.at[0]),
@@ -77,25 +132,22 @@
         copy.start()
 
     def basis_copy(i):
-        part = pl.ds(i * per_copy, per_copy)
+        part = pl.ds(i * PER_COPY, PER_COPY)
         return pltpu.make_async_copy(basis.at[part], basis_v.at[part], basis_sem.at[i])
 
-    ahead = 2
+    ahead = 4
     for i in range(ahead):
         basis_copy(i).start()
     for copy in table_copies:
         copy.wait()
 
+    per_group = GROUP // PER_COPY
     for group in range(groups):
         part = pl.ds(group * GROUP, GROUP)
 
         @pl.loop(0, slots)
         def _(m):
-            slot = slot_s[m]
-            half = cyclic(lax.div(slot, half_slots) - my_half, halves)
-            within = lax.rem(slot, half_slots)
-            owner = lax.div(within, owner_slots) ^ my_owner
-            place = half * half_slots + owner * owner_slots + lax.rem(within, owner_slots)
+            place = place_of(slot_s[m], owner_slots, half_slots)
             if group == 0:
                 keep_place[place] = keep_s[m]
                 rows_place[place] = rows_s[m]
@@ -103,21 +155,21 @@
                 panels.at[m, part], panels_v.at[place, part], panel_sem.at[group]
             ).start()
 
-        for i in range(ahead + group * copies, min(ahead + (group + 1) * copies, groups * copies)):
+        for i in range(ahead + group * per_group, min(ahead + (group + 1) * per_group, groups * per_group)):
             basis_copy(i).start()
 
+    offsets_of(keep_place, tile_place, shift_place, owner_slots)
     column = lax.broadcasted_iota(jnp.int32, slot_column.shape, 1)
     slot_at = jnp.full(slot_column.shape, owner_slots, jnp.int32)
     rows_at = jnp.zeros(slot_column.shape, jnp.int32)
-    offset = jnp.int32(0)
     for j in range(owner_slots):
         keep = keep_place[j]
+        offset = tile_place[j] * LANES + shift_place[j]
         within = (column >= offset) & (column < offset + keep)
         slot_at = jnp.where(within, j, slot_at)
         rows_at = jnp.where(within, rows_place[j], rows_at)
         scalars[j : j + 1, :] = jnp.full((1, LANES), offset, jnp.int32)
         scalars[owner_slots + j : owner_slots + j + 1, :] = jnp.full((1, LANES), keep, jnp.int32)
-        offset = offset + keep
     slot_column[...] = slot_at
     rows_column[...] = rows_at
 
@@ -125,7 +177,6 @@
     row = lax.broadcasted_iota(jnp.int32, (side, side), 0)
     column = lax.broadcasted_iota(jnp.int32, (side, side), 1)
     swap = (column == (row % GROUP) * GROUP + row // GROUP).astype(jnp.float32).astype(jnp.bfloat16)
-    lane = lax.broadcasted_iota(jnp.int32, (GROUP, LANES), 1)
 
     @pl.loop(0, groups)
     def _(group):
@@ -139,39 +190,17 @@
             turned = jnp.dot(swap, tile, preferred_element_type=jnp.float32).astype(jnp.bfloat16)
             lhs_v[:, blocks, :] = turned.reshape(GROUP, GROUP, depth)
 
-        @pl.loop(0, copies)
-        def _(i):
-            basis_copy(group * copies + i).wait()
-            for k in range(per_copy):
-                f = i * per_copy + k
-                out_v[f] = jnp.dot(
-                    lhs_v[f], basis_v[group * GROUP + f], preferred_element_type=jnp.float32
-                )
-
-        pack_v[...] = jnp.zeros(pack_v.shape, jnp.float32)
-        for half in range(halves):
-            to = (mine, send)[half]
-            for owner in range(owners):
-                offset = jnp.int32(0)
-                at = half * owners + owner
-                for j in range(owner_slots):
-                    place = at * owner_slots + j
-                    keep = keep_place[place]
-                    tiles = [
-                        jnp.where(
-                            lane < keep - t * LANES,
-                            out_v[:, place, t * LANES : (t + 1) * LANES],
-                            0.0,
-                        )
-                        for t in range(modes // LANES)
-                    ]
-                    tile = lax.div(offset, LANES)
-                    moved = shifted(tiles, offset - tile * LANES, lane)
-                    for t, value in enumerate(moved):
-                        lanes = pl.ds(pl.multiple_of((tile + t) * LANES, LANES), LANES)
-                        pack_v[at, :, lanes] += value
-                    offset = offset + keep
-                to[owner, here, :] = pack_v[at, :, :width]
+        @pl.loop(0, GROUP // PACKED)
+        def _(part):
+            line = group * GROUP + part * PACKED
+            multiply_and_pack(
+                lhs_v,
+                lambda k: basis_v[line + k],
+                lambda c: basis_copy(line // PER_COPY + c).wait(),
+                part * PACKED,
+                out_v, mine, send, line,
+                (tile_place, shift_place, owner_slots),
+            )
 
 
 def kl_kernel(part, owners, slot_column, rows_column, kl, *refs):
@@ -232,26 +261,22 @@
 def project(panels, svd_basis, slot_of_m, svd_keep, kl_keep, owner_slots, width):
     slots, freqs, depth = panels.shape
     modes = svd_basis.shape[2]
-    owners, halves = lax.axis_size("ma"), lax.axis_size("pa")
-    packed = jax.ShapeDtypeStruct((owners, freqs, width), jnp.float32)
+    packed = jax.ShapeDtypeStruct((lax.axis_size("ma"), freqs, width), jnp.float32)
     column = jax.ShapeDtypeStruct((8, width), jnp.int32)
-    table = pltpu.SMEM((slots,), jnp.int32)
-    wide = width + modes + LANES
     return pl.pallas_call(
         functools.partial(project_kernel, owner_slots),
         out_shape=(packed, packed, column, column, jax.ShapeDtypeStruct((8, LANES), jnp.int32)),
         in_specs=[HBM] * 5,
         out_specs=(VMEM,) * 5,
-        scratch_shapes=[table] * 5
+        scratch_shapes=[pltpu.SMEM((slots,), jnp.int32)] * 7
         + [
             pltpu.VMEM((slots, freqs, depth), jnp.bfloat16),
             pltpu.VMEM((freqs, depth, modes), jnp.bfloat16),
             pltpu.VMEM((GROUP, slots, depth), jnp.bfloat16),
-            pltpu.VMEM((GROUP, slots, modes), jnp.float32),
-            pltpu.VMEM((halves * owners, GROUP, wide), jnp.float32),
+            pltpu.VMEM((modes // LANES * PACKED * slots, LANES), jnp.float32),
             pltpu.SemaphoreType.DMA((3,)),
             pltpu.SemaphoreType.DMA((freqs // GROUP,)),
-            pltpu.SemaphoreType.DMA((freqs // 4,)),
+            pltpu.SemaphoreType.DMA((freqs // PER_COPY,)),
         ],
         compiler_params=pltpu.CompilerParams(vmem_limit_bytes=48 * MIB),
         cost_estimate=pl.CostEstimate(
@@ -315,9 +340,10 @@
     blocks = [summed[0]] + [
         lax.ppermute(summed[step], "ma", pairs("ma", step)) for step in range(1, owners)
     ]
-    send = kl_project(1, jnp.bfloat16, slot_column, rows_column, kl_basis, blocks)
+    tables = (slot_column, rows_column, kl_basis, blocks)
+    send = kl_project(1, jnp.bfloat16, *tables)
     got = lax.ppermute(send, "af", pairs("af", 1))
-    mine = kl_project(0, jnp.float32, slot_column, rows_column, kl_basis, blocks)
+    mine = kl_project(0, jnp.float32, *tables)
     return unpack(scalars, mine, got, owner_slots, modes)
 
 

time: 35.1 us -> 39 us (1.11)
  Pallas kernels: 16.2 us -> 20.2 us
    pallas_call x1, Pallas kernels: 14.5 us -> 18.5 us  [project(): pl.pallas_call(functools.partial(project_kernel, owner_slots), out_shape=...]
where the time goes in v5:
time: 39 us; the launch traced here: 38.9 us
  Pallas kernels  20.2 us (52%)
  waiting for transfers between devices  10.8 us (28%)
  starting transfers between devices  7.75 us (20%)
    pallas_call x1, Pallas kernels, project(): pl.pallas_call(functools.partial(project_kernel, owner_slots), out_shape=...  18.5 us
    ppermute x3, waiting for transfers between devices, shards(): lax.ppermute(summed[step], 'ma', pairs('ma', step))  6.52 us
    ppermute x3, starting transfers between devices, shards(): lax.ppermute(summed[step], 'ma', pairs('ma', step))  5.65 us
    ppermute x1, waiting for transfers between devices, shards(): got = lax.ppermute(send, 'af', pairs('af', 1))  2.6 us
    ppermute x1, waiting for transfers between devices, shards(): got = lax.ppermute(send, 'pa', pairs('pa', 1))  1.72 us
    ppermute x1, starting transfers between devices, shards(): got = lax.ppermute(send, 'af', pairs('af', 1))  1.59 us
    pallas_call x1, Pallas kernels, unpack(): pl.pallas_call(unpack_kernel, out_shape=jax.ShapeDtypeStruct((owner_slots...  1.09 us
  transfers between devices with their start and end apart: 5, of which 4 were waited for; matrix products, arithmetic and copies ran while one was open for 0% of the time, Pallas kernels for 1%

profile of v5, /device:TPU:0, one launch (start us, length us, event | category | flops | bytes accessed | tf_op | source)
XLA Modules:
  0.0 38.9 jit_solution(8533058325081812157)
XLA Ops:
  0.0 0.0 copy-start
  0.0 18.5 %project.1 = (f32[4,64,640]{2,1,0:T(8,128)S(1)}, f32[4,64,640]{2,1,0:T(8,128)S(1)}, s32[8,640]{1,0:T(8,128)S(1)}, s32[8,640]{1,0:T(8,128)S(1)}, s32[8,128]{1,0:T(8,128)S(1)}) custom-call(s32[32]{0:T(128)} %slot_hbm.1, s32[32]{0:T(128)} %keep_hbm.1, s32[32]{0:T(128)} %rows_hbm.1, bf16[32,64,1024]{2,1,0:T(8,128)(2,1)} %panels.1, bf16[64,1024,256]{2,1,0:T(8,128)(2,1)} %basis.1), custom_call_target="tpu_custom_call" | custom-call | flops 1073741824 | bytes 37748736 | tf_op jit(solution)/shard_map/project/pallas_call | solution.py:266
  18.5 0.5 %collective-permute-start = (f32[4,64,640]{2,1,0:T(8,128)S(1)}, f32[4,64,640]{2,1,0:T(8,128)S(1)}, u32[]{:S(2)}, u32[]{:S(2)}) collective-permute-start(f32[4,64,640]{2,1,0:T(8,128)S(1)} %get-tuple-element.14), channel_id=1, source_target_pairs={{0,1},{1,0},{2,3},{3,2},{4,5},{5,4},{6,7},{7,6},{8,9},{9,8},{10,11... | collective-permute-start | bytes 1966088 | tf_op jit(solution)/shard_map/ppermute | solution.py:338
  19.0 1.7 %collective-permute-done = f32[4,64,640]{2,1,0:T(8,128)S(1)} collective-permute-done((f32[4,64,640]{2,1,0:T(8,128)S(1)}, f32[4,64,640]{2,1,0:T(8,128)S(1)}, u32[]{:S(2)}, u32[]{:S(2)}) %collective-permute-start) | collective-permute-done | bytes 655392 | tf_op jit(solution)/shard_map/ppermute | solution.py:338
  20.7 0.1 fusion.7
  20.8 5.0 %collective-permute-start.3 = (bf16[64,640]{1,0:T(8,128)(2,1)S(1)}, bf16[64,640]{1,0:T(8,128)(2,1)S(1)}, u32[]{:S(2)}, u32[]{:S(2)}) collective-permute-start(bf16[64,640]{1,0:T(8,128)(2,1)S(1)} %get-tuple-element.15), channel_id=1, source_target_pairs={{0,12},{4,8},{8,4},{12,0},{1,13},{5,9},{9,5},{13,1},{2,14},{6,10},... | collective-permute-start | bytes 245768 | tf_op jit(solution)/shard_map/ppermute | solution.py:341
  25.8 0.0 collective-permute-start.2
  25.8 0.6 %collective-permute-start.1 = (bf16[64,640]{1,0:T(8,128)(2,1)S(1)}, bf16[64,640]{1,0:T(8,128)(2,1)S(1)}, u32[]{:S(2)}, u32[]{:S(2)}) collective-permute-start(bf16[64,640]{1,0:T(8,128)(2,1)S(1)} %get-tuple-element.17), channel_id=1, source_target_pairs={{0,4},{4,0},{8,12},{12,8},{1,5},{5,1},{9,13},{13,9},{2,6},{6,2},{1... | collective-permute-start | bytes 245768 | tf_op jit(solution)/shard_map/ppermute | solution.py:341
  26.4 2.7 %collective-permute-done.3.refs_3_ = bf16[64,640]{1,0:T(8,128)(2,1)S(1)} collective-permute-done((bf16[64,640]{1,0:T(8,128)(2,1)S(1)}, bf16[64,640]{1,0:T(8,128)(2,1)S(1)}, u32[]{:S(2)}, u32[]{:S(2)}) %collective-permute-start.3) | collective-permute-done | bytes 81952 | tf_op jit(solution)/shard_map/ppermute | solution.py:341
  29.1 3.8 %collective-permute-done.2.refs_2_ = bf16[64,640]{1,0:T(8,128)(2,1)S(1)} collective-permute-done((bf16[64,640]{1,0:T(8,128)(2,1)S(1)}, bf16[64,640]{1,0:T(8,128)(2,1)S(1)}, u32[]{:S(2)}, u32[]{:S(2)}) %collective-permute-start.2) | collective-permute-done | bytes 81952 | tf_op jit(solution)/shard_map/ppermute | solution.py:341
  33.0 0.0 collective-permute-done.1.refs_1_
  33.0 0.0 copy-done
  33.0 0.3 kl_project.3
  33.3 1.6 %collective-permute-start.4 = (bf16[64,640]{1,0:T(8,128)(2,1)S(1)}, bf16[64,640]{1,0:T(8,128)(2,1)S(1)}, u32[]{:S(2)}, u32[]{:S(2)}) collective-permute-start(bf16[64,640]{1,0:T(8,128)(2,1)S(1)} %kl_project.3), channel_id=1, source_target_pairs={{0,2},{2,0},{1,3},{3,1},{4,6},{6,4},{5,7},{7,5},{8,10},{10,8},{9,1... | collective-permute-start | bytes 245768 | tf_op jit(solution)/shard_map/ppermute | solution.py:345
  34.9 0.3 kl_project.2.mine
  35.2 2.6 %collective-permute-done.4.got = bf16[64,640]{1,0:T(8,128)(2,1)S(1)} collective-permute-done((bf16[64,640]{1,0:T(8,128)(2,1)S(1)}, bf16[64,640]{1,0:T(8,128)(2,1)S(1)}, u32[]{:S(2)}, u32[]{:S(2)}) %collective-permute-start.4) | collective-permute-done | bytes 81952 | tf_op jit(solution)/shard_map/ppermute | solution.py:345
  37.8 1.1 %unpack.1 = f32[4,64,256]{2,1,0:T(8,128)} custom-call(s32[8,128]{1,0:T(8,128)S(1)} %get-tuple-element.10.scalars, f32[64,640]{1,0:T(8,128)S(1)} %kl_project.2.mine, bf16[64,640]{1,0:T(8,128)(2,1)S(1)} %collective-permute-done.4.got), custom_call_target="tpu_custom_call" | custom-call | flops 40960 | bytes 409600 | tf_op jit(solution)/shard_map/unpack/pallas_call | solution.py:313
Async XLA Ops:
  0.0 33.0 %copy-start = (bf16[4,128,256]{2,1,0:T(8,128)(2,1)S(1)}, bf16[4,128,256]{2,1,0:T(8,128)(2,1)}, u32[]{:S(2)}) copy-start(bf16[4,128,256]{2,1,0:T(8,128)(2,1)} %kl.3) | copy-start | bytes 786436
  18.5 2.2 %collective-permute-start = (f32[4,64,640]{2,1,0:T(8,128)S(1)}, f32[4,64,640]{2,1,0:T(8,128)S(1)}, u32[]{:S(2)}, u32[]{:S(2)}) collective-permute-start(f32[4,64,640]{2,1,0:T(8,128)S(1)} %get-tuple-element.14), channel_id=1, source_target_pairs={{0,1},{1,0},{2,3},{3,2},{4,5},{5,4},{6,7},{7,6},{8,9},{9,8},{10,11... | collective-permute-start | bytes 1966088 | tf_op jit(solution)/shard_map/ppermute | solution.py:338
  20.8 8.4 %collective-permute-start.3 = (bf16[64,640]{1,0:T(8,128)(2,1)S(1)}, bf16[64,640]{1,0:T(8,128)(2,1)S(1)}, u32[]{:S(2)}, u32[]{:S(2)}) collective-permute-start(bf16[64,640]{1,0:T(8,128)(2,1)S(1)} %get-tuple-element.15), channel_id=1, source_target_pairs={{0,12},{4,8},{8,4},{12,0},{1,13},{5,9},{9,5},{13,1},{2,14},{6,10},... | collective-permute-start | bytes 245768 | tf_op jit(solution)/shard_map/ppermute | solution.py:341
  25.8 7.2 %collective-permute-start.2 = (bf16[64,640]{1,0:T(8,128)(2,1)S(1)}, bf16[64,640]{1,0:T(8,128)(2,1)S(1)}, u32[]{:S(2)}, u32[]{:S(2)}) collective-permute-start(bf16[64,640]{1,0:T(8,128)(2,1)S(1)} %get-tuple-element.16), channel_id=1, source_target_pairs={{0,8},{4,12},{8,0},{12,4},{1,9},{5,13},{9,1},{13,5},{2,10},{6,14},... | collective-permute-start | bytes 245768 | tf_op jit(solution)/shard_map/ppermute | solution.py:341
  25.8 7.2 %collective-permute-start.1 = (bf16[64,640]{1,0:T(8,128)(2,1)S(1)}, bf16[64,640]{1,0:T(8,128)(2,1)S(1)}, u32[]{:S(2)}, u32[]{:S(2)}) collective-permute-start(bf16[64,640]{1,0:T(8,128)(2,1)S(1)} %get-tuple-element.17), channel_id=1, source_target_pairs={{0,4},{4,0},{8,12},{12,8},{1,5},{5,1},{9,13},{13,9},{2,6},{6,2},{1... | collective-permute-start | bytes 245768 | tf_op jit(solution)/shard_map/ppermute | solution.py:341
  33.3 4.5 %collective-permute-start.4 = (bf16[64,640]{1,0:T(8,128)(2,1)S(1)}, bf16[64,640]{1,0:T(8,128)(2,1)S(1)}, u32[]{:S(2)}, u32[]{:S(2)}) collective-permute-start(bf16[64,640]{1,0:T(8,128)(2,1)S(1)} %kl_project.3), channel_id=1, source_target_pairs={{0,2},{2,0},{1,3},{3,1},{4,6},{6,4},{5,7},{7,5},{8,10},{10,8},{9,1... | collective-permute-start | bytes 245768 | tf_op jit(solution)/shard_map/ppermute | solution.py:345

commit v6 on v5

--- a/solution.py
+++ b/solution.py
@@ -9,8 +9,9 @@
 
 LANES = 128
 GROUP = 16
-PACKED = 8
-PER_COPY = 2
+PACKED = 16
+BATCH = 2
+PER_COPY = 4
 OWNER_BUDGET = 576
 MIB = 2**20
 
@@ -68,49 +69,44 @@
             offset = offset + keep_place[place]
 
 
-def multiply_and_pack(lhs, basis_of, wait, first, out_v, mine, send, line, tables):
+def pack(out_v, mine, send, line, tables):
     tile_place, shift_place, owner_slots = tables
-    slots = lhs.shape[1]
+    owners, _, width = mine.shape
+    slots = 2 * owners * owner_slots
     tiles = out_v.shape[0] // (PACKED * slots)
-    last = mine.shape[-1] // LANES - 1
-    for k in range(PACKED):
-        if k % PER_COPY == 0:
-            wait(k // PER_COPY)
-        product = jnp.dot(lhs[first + k], basis_of(k), preferred_element_type=jnp.float32)
-        for t in range(tiles):
-            at = (t * PACKED + k) * slots
-            out_v[at : at + slots, :] = product[:, t * LANES : (t + 1) * LANES]
+    last = width // LANES - 1
     lane = lax.broadcasted_iota(jnp.int32, (PACKED, LANES), 1)
-    owners = mine.shape[0]
     rows = pl.ds(pl.multiple_of(line, PACKED), PACKED)
-    for at in range(2 * owners):
-        to, owner = (mine, send)[at // owners], at % owners
-        values, tile_before = None, None
-        for j in range(owner_slots):
-            place = at * owner_slots + j
-            tile, shift = tile_place[place], shift_place[place]
-            left = lane < shift
-            turned = [
-                pltpu.roll(
-                    out_v[pl.ds(t * PACKED * slots + place, PACKED, stride=slots), :], shift, 1
+    for begin in range(0, 2 * owners, BATCH):
+        turned = {
+            place: pltpu.roll(
+                out_v[pl.ds(place, tiles * PACKED, stride=slots), :], shift_place[place], 1
+            )
+            for place in range(begin * owner_slots, (begin + BATCH) * owner_slots)
+        }
+        for at in range(begin, begin + BATCH):
+            to, owner = (mine, send)[at // owners], at % owners
+            values, tile_before = None, None
+            for j in range(owner_slots):
+                place = at * owner_slots + j
+                tile = tile_place[place]
+                left = lane < shift_place[place]
+                moved = [turned[place][t * PACKED : (t + 1) * PACKED] for t in range(tiles)]
+                shared = moved[0]
+                if j > 0:
+                    step = tile - tile_before
+                    shared = values[0]
+                    for t in range(1, tiles + 1):
+                        shared = jnp.where(step == t, values[t], shared)
+                values = (
+                    [jnp.where(left, shared, moved[0])]
+                    + [jnp.where(left, moved[t - 1], moved[t]) for t in range(1, tiles)]
+                    + [moved[tiles - 1]]
                 )
-                for t in range(tiles)
-            ]
-            shared = turned[0]
-            if j > 0:
-                step = tile - tile_before
-                shared = values[0]
-                for t in range(1, tiles + 1):
-                    shared = jnp.where(step == t, values[t], shared)
-            values = (
-                [jnp.where(left, shared, turned[0])]
-                + [jnp.where(left, turned[t - 1], turned[t]) for t in range(1, tiles)]
-                + [turned[tiles - 1]]
-            )
-            tile_before = tile
-            for t in reversed(range(tiles + 1)):
-                at_lane = pl.multiple_of(jnp.minimum(tile + t, last) * LANES, LANES)
-                to[owner, rows, pl.ds(at_lane, LANES)] = values[t]
+                tile_before = tile
+                for t in reversed(range(tiles + 1)):
+                    at_lane = pl.multiple_of(jnp.minimum(tile + t, last) * LANES, LANES)
+                    to[owner, rows, pl.ds(at_lane, LANES)] = values[t]
 
 
 def project_kernel(
@@ -135,7 +131,7 @@
         part = pl.ds(i * PER_COPY, PER_COPY)
         return pltpu.make_async_copy(basis.at[part], basis_v.at[part], basis_sem.at[i])
 
-    ahead = 4
+    ahead = 2
     for i in range(ahead):
         basis_copy(i).start()
     for copy in table_copies:
@@ -190,17 +186,19 @@
             turned = jnp.dot(swap, tile, preferred_element_type=jnp.float32).astype(jnp.bfloat16)
             lhs_v[:, blocks, :] = turned.reshape(GROUP, GROUP, depth)
 
-        @pl.loop(0, GROUP // PACKED)
-        def _(part):
-            line = group * GROUP + part * PACKED
-            multiply_and_pack(
-                lhs_v,
-                lambda k: basis_v[line + k],
-                lambda c: basis_copy(line // PER_COPY + c).wait(),
-                part * PACKED,
-                out_v, mine, send, line,
-                (tile_place, shift_place, owner_slots),
-            )
+        @pl.loop(0, per_group)
+        def _(i):
+            basis_copy(group * per_group + i).wait()
+            for k in range(PER_COPY):
+                f = i * PER_COPY + k
+                product = jnp.dot(
+                    lhs_v[f], basis_v[group * GROUP + f], preferred_element_type=jnp.float32
+                )
+                for t in range(product.shape[1] // LANES):
+                    at = pl.multiple_of((t * PACKED + f) * slots, slots)
+                    out_v[pl.ds(at, slots), :] = product[:, t * LANES : (t + 1) * LANES]
+
+        pack(out_v, mine, send, group * GROUP, (tile_place, shift_place, owner_slots))
 
 
 def kl_kernel(part, owners, slot_column, rows_column, kl, *refs):

time: 39 us -> 35.8 us (0.918)
  Pallas kernels: 20.2 us -> 17 us
    pallas_call x1, Pallas kernels: 18.5 us -> 15.3 us  [project(): pl.pallas_call(functools.partial(project_kernel, owner_slots), out_shape=...]
where the time goes in v6:
time: 35.8 us; the launch traced here: 35.7 us
  Pallas kernels  17 us (47%)
  waiting for transfers between devices  10.9 us (30%)
  starting transfers between devices  7.75 us (22%)
    pallas_call x1, Pallas kernels, project(): pl.pallas_call(functools.partial(project_kernel, owner_slots), out_shape=...  15.3 us
    ppermute x3, waiting for transfers between devices, shards(): lax.ppermute(summed[step], 'ma', pairs('ma', step))  6.52 us
    ppermute x3, starting transfers between devices, shards(): lax.ppermute(summed[step], 'ma', pairs('ma', step))  5.67 us
    ppermute x1, waiting for transfers between devices, shards(): got = lax.ppermute(send, 'af', pairs('af', 1))  2.64 us
    ppermute x1, waiting for transfers between devices, shards(): got = lax.ppermute(send, 'pa', pairs('pa', 1))  1.72 us
    ppermute x1, starting transfers between devices, shards(): got = lax.ppermute(send, 'af', pairs('af', 1))  1.55 us
    pallas_call x1, Pallas kernels, unpack(): pl.pallas_call(unpack_kernel, out_shape=jax.ShapeDtypeStruct((owner_slots...  1.09 us
  transfers between devices with their start and end apart: 5, of which 4 were waited for; matrix products, arithmetic and copies ran while one was open for 0% of the time, Pallas kernels for 1%

profile of v6, /device:TPU:0, one launch (start us, length us, event | category | flops | bytes accessed | tf_op | source)
XLA Modules:
  0.0 35.7 jit_solution(10397539769892116059)
XLA Ops:
  0.0 0.0 copy-start
  0.0 15.3 %project.1 = (f32[4,64,640]{2,1,0:T(8,128)S(1)}, f32[4,64,640]{2,1,0:T(8,128)S(1)}, s32[8,640]{1,0:T(8,128)S(1)}, s32[8,640]{1,0:T(8,128)S(1)}, s32[8,128]{1,0:T(8,128)S(1)}) custom-call(s32[32]{0:T(128)} %slot_hbm.1, s32[32]{0:T(128)} %keep_hbm.1, s32[32]{0:T(128)} %rows_hbm.1, bf16[32,64,1024]{2,1,0:T(8,128)(2,1)} %panels.1, bf16[64,1024,256]{2,1,0:T(8,128)(2,1)} %basis.1), custom_call_target="tpu_custom_call" | custom-call | flops 1073741824 | bytes 37748736 | tf_op jit(solution)/shard_map/project/pallas_call | solution.py:264
  15.3 0.5 %collective-permute-start = (f32[4,64,640]{2,1,0:T(8,128)S(1)}, f32[4,64,640]{2,1,0:T(8,128)S(1)}, u32[]{:S(2)}, u32[]{:S(2)}) collective-permute-start(f32[4,64,640]{2,1,0:T(8,128)S(1)} %get-tuple-element.14), channel_id=1, source_target_pairs={{0,1},{1,0},{2,3},{3,2},{4,5},{5,4},{6,7},{7,6},{8,9},{9,8},{10,11... | collective-permute-start | bytes 1966088 | tf_op jit(solution)/shard_map/ppermute | solution.py:336
  15.8 1.7 %collective-permute-done = f32[4,64,640]{2,1,0:T(8,128)S(1)} collective-permute-done((f32[4,64,640]{2,1,0:T(8,128)S(1)}, f32[4,64,640]{2,1,0:T(8,128)S(1)}, u32[]{:S(2)}, u32[]{:S(2)}) %collective-permute-start) | collective-permute-done | bytes 655392 | tf_op jit(solution)/shard_map/ppermute | solution.py:336
  17.5 0.1 fusion.7
  17.6 5.0 %collective-permute-start.3 = (bf16[64,640]{1,0:T(8,128)(2,1)S(1)}, bf16[64,640]{1,0:T(8,128)(2,1)S(1)}, u32[]{:S(2)}, u32[]{:S(2)}) collective-permute-start(bf16[64,640]{1,0:T(8,128)(2,1)S(1)} %get-tuple-element.15), channel_id=1, source_target_pairs={{0,12},{4,8},{8,4},{12,0},{1,13},{5,9},{9,5},{13,1},{2,14},{6,10},... | collective-permute-start | bytes 245768 | tf_op jit(solution)/shard_map/ppermute | solution.py:339
  22.6 0.0 collective-permute-start.2
  22.6 0.6 %collective-permute-start.1 = (bf16[64,640]{1,0:T(8,128)(2,1)S(1)}, bf16[64,640]{1,0:T(8,128)(2,1)S(1)}, u32[]{:S(2)}, u32[]{:S(2)}) collective-permute-start(bf16[64,640]{1,0:T(8,128)(2,1)S(1)} %get-tuple-element.17), channel_id=1, source_target_pairs={{0,4},{4,0},{8,12},{12,8},{1,5},{5,1},{9,13},{13,9},{2,6},{6,2},{1... | collective-permute-start | bytes 245768 | tf_op jit(solution)/shard_map/ppermute | solution.py:339
  23.3 2.7 %collective-permute-done.3.refs_3_ = bf16[64,640]{1,0:T(8,128)(2,1)S(1)} collective-permute-done((bf16[64,640]{1,0:T(8,128)(2,1)S(1)}, bf16[64,640]{1,0:T(8,128)(2,1)S(1)}, u32[]{:S(2)}, u32[]{:S(2)}) %collective-permute-start.3) | collective-permute-done | bytes 81952 | tf_op jit(solution)/shard_map/ppermute | solution.py:339
  25.9 3.9 %collective-permute-done.2.refs_2_ = bf16[64,640]{1,0:T(8,128)(2,1)S(1)} collective-permute-done((bf16[64,640]{1,0:T(8,128)(2,1)S(1)}, bf16[64,640]{1,0:T(8,128)(2,1)S(1)}, u32[]{:S(2)}, u32[]{:S(2)}) %collective-permute-start.2) | collective-permute-done | bytes 81952 | tf_op jit(solution)/shard_map/ppermute | solution.py:339
  29.8 0.0 collective-permute-done.1.refs_1_
  29.8 0.0 copy-done
  29.8 0.3 kl_project.3
  30.1 1.6 %collective-permute-start.4 = (bf16[64,640]{1,0:T(8,128)(2,1)S(1)}, bf16[64,640]{1,0:T(8,128)(2,1)S(1)}, u32[]{:S(2)}, u32[]{:S(2)}) collective-permute-start(bf16[64,640]{1,0:T(8,128)(2,1)S(1)} %kl_project.3), channel_id=1, source_target_pairs={{0,2},{2,0},{1,3},{3,1},{4,6},{6,4},{5,7},{7,5},{8,10},{10,8},{9,1... | collective-permute-start | bytes 245768 | tf_op jit(solution)/shard_map/ppermute | solution.py:343
  31.6 0.3 kl_project.2.mine
  32.0 2.6 %collective-permute-done.4.got = bf16[64,640]{1,0:T(8,128)(2,1)S(1)} collective-permute-done((bf16[64,640]{1,0:T(8,128)(2,1)S(1)}, bf16[64,640]{1,0:T(8,128)(2,1)S(1)}, u32[]{:S(2)}, u32[]{:S(2)}) %collective-permute-start.4) | collective-permute-done | bytes 81952 | tf_op jit(solution)/shard_map/ppermute | solution.py:343
  34.6 1.1 %unpack.1 = f32[4,64,256]{2,1,0:T(8,128)} custom-call(s32[8,128]{1,0:T(8,128)S(1)} %get-tuple-element.10.scalars, f32[64,640]{1,0:T(8,128)S(1)} %kl_project.2.mine, bf16[64,640]{1,0:T(8,128)(2,1)S(1)} %collective-permute-done.4.got), custom_call_target="tpu_custom_call" | custom-call | flops 40960 | bytes 409600 | tf_op jit(solution)/shard_map/unpack/pallas_call | solution.py:311
Async XLA Ops:
  0.0 29.8 %copy-start = (bf16[4,128,256]{2,1,0:T(8,128)(2,1)S(1)}, bf16[4,128,256]{2,1,0:T(8,128)(2,1)}, u32[]{:S(2)}) copy-start(bf16[4,128,256]{2,1,0:T(8,128)(2,1)} %kl.3) | copy-start | bytes 786436
  15.3 2.3 %collective-permute-start = (f32[4,64,640]{2,1,0:T(8,128)S(1)}, f32[4,64,640]{2,1,0:T(8,128)S(1)}, u32[]{:S(2)}, u32[]{:S(2)}) collective-permute-start(f32[4,64,640]{2,1,0:T(8,128)S(1)} %get-tuple-element.14), channel_id=1, source_target_pairs={{0,1},{1,0},{2,3},{3,2},{4,5},{5,4},{6,7},{7,6},{8,9},{9,8},{10,11... | collective-permute-start | bytes 1966088 | tf_op jit(solution)/shard_map/ppermute | solution.py:336
  17.6 8.3 %collective-permute-start.3 = (bf16[64,640]{1,0:T(8,128)(2,1)S(1)}, bf16[64,640]{1,0:T(8,128)(2,1)S(1)}, u32[]{:S(2)}, u32[]{:S(2)}) collective-permute-start(bf16[64,640]{1,0:T(8,128)(2,1)S(1)} %get-tuple-element.15), channel_id=1, source_target_pairs={{0,12},{4,8},{8,4},{12,0},{1,13},{5,9},{9,5},{13,1},{2,14},{6,10},... | collective-permute-start | bytes 245768 | tf_op jit(solution)/shard_map/ppermute | solution.py:339
  22.6 7.2 %collective-permute-start.2 = (bf16[64,640]{1,0:T(8,128)(2,1)S(1)}, bf16[64,640]{1,0:T(8,128)(2,1)S(1)}, u32[]{:S(2)}, u32[]{:S(2)}) collective-permute-start(bf16[64,640]{1,0:T(8,128)(2,1)S(1)} %get-tuple-element.16), channel_id=1, source_target_pairs={{0,8},{4,12},{8,0},{12,4},{1,9},{5,13},{9,1},{13,5},{2,10},{6,14},... | collective-permute-start | bytes 245768 | tf_op jit(solution)/shard_map/ppermute | solution.py:339
  22.6 7.2 %collective-permute-start.1 = (bf16[64,640]{1,0:T(8,128)(2,1)S(1)}, bf16[64,640]{1,0:T(8,128)(2,1)S(1)}, u32[]{:S(2)}, u32[]{:S(2)}) collective-permute-start(bf16[64,640]{1,0:T(8,128)(2,1)S(1)} %get-tuple-element.17), channel_id=1, source_target_pairs={{0,4},{4,0},{8,12},{12,8},{1,5},{5,1},{9,13},{13,9},{2,6},{6,2},{1... | collective-permute-start | bytes 245768 | tf_op jit(solution)/shard_map/ppermute | solution.py:339
  30.1 4.5 %collective-permute-start.4 = (bf16[64,640]{1,0:T(8,128)(2,1)S(1)}, bf16[64,640]{1,0:T(8,128)(2,1)S(1)}, u32[]{:S(2)}, u32[]{:S(2)}) collective-permute-start(bf16[64,640]{1,0:T(8,128)(2,1)S(1)} %kl_project.3), channel_id=1, source_target_pairs={{0,2},{2,0},{1,3},{3,1},{4,6},{6,4},{5,7},{7,5},{8,10},{10,8},{9,1... | collective-permute-start | bytes 245768 | tf_op jit(solution)/shard_map/ppermute | solution.py:343

commit v7 on v5

--- a/solution.py
+++ b/solution.py
@@ -9,8 +9,7 @@
 
 LANES = 128
 GROUP = 16
-PACKED = 8
-PER_COPY = 2
+PER_COPY = 4
 OWNER_BUDGET = 576
 MIB = 2**20
 
@@ -68,56 +67,48 @@
             offset = offset + keep_place[place]
 
 
-def multiply_and_pack(lhs, basis_of, wait, first, out_v, mine, send, line, tables):
+def pack(out_v, mine, send, line, tables, owners_at):
     tile_place, shift_place, owner_slots = tables
-    slots = lhs.shape[1]
-    tiles = out_v.shape[0] // (PACKED * slots)
-    last = mine.shape[-1] // LANES - 1
-    for k in range(PACKED):
-        if k % PER_COPY == 0:
-            wait(k // PER_COPY)
-        product = jnp.dot(lhs[first + k], basis_of(k), preferred_element_type=jnp.float32)
-        for t in range(tiles):
-            at = (t * PACKED + k) * slots
-            out_v[at : at + slots, :] = product[:, t * LANES : (t + 1) * LANES]
-    lane = lax.broadcasted_iota(jnp.int32, (PACKED, LANES), 1)
-    owners = mine.shape[0]
-    rows = pl.ds(pl.multiple_of(line, PACKED), PACKED)
-    for at in range(2 * owners):
+    owners, width_tiles = mine.shape[:2]
+    slots = 2 * owners * owner_slots
+    tiles = out_v.shape[0] // (GROUP * slots)
+    lane = lax.broadcasted_iota(jnp.int32, (GROUP, LANES), 1)
+    rows = pl.ds(pl.multiple_of(line, GROUP), GROUP)
+    turned = {
+        place: pltpu.roll(
+            out_v[pl.ds(place, tiles * GROUP, stride=slots), :], shift_place[place], 1
+        )
+        for place in range(owners_at[0] * owner_slots, (owners_at[-1] + 1) * owner_slots)
+    }
+    for at in owners_at:
         to, owner = (mine, send)[at // owners], at % owners
         values, tile_before = None, None
         for j in range(owner_slots):
             place = at * owner_slots + j
-            tile, shift = tile_place[place], shift_place[place]
-            left = lane < shift
-            turned = [
-                pltpu.roll(
-                    out_v[pl.ds(t * PACKED * slots + place, PACKED, stride=slots), :], shift, 1
-                )
-                for t in range(tiles)
-            ]
-            shared = turned[0]
+            tile = tile_place[place]
+            left = lane < shift_place[place]
+            moved = [turned[place][t * GROUP : (t + 1) * GROUP] for t in range(tiles)]
+            shared = moved[0]
             if j > 0:
                 step = tile - tile_before
                 shared = values[0]
                 for t in range(1, tiles + 1):
                     shared = jnp.where(step == t, values[t], shared)
             values = (
-                [jnp.where(left, shared, turned[0])]
-                + [jnp.where(left, turned[t - 1], turned[t]) for t in range(1, tiles)]
-                + [turned[tiles - 1]]
+                [jnp.where(left, shared, moved[0])]
+                + [jnp.where(left, moved[t - 1], moved[t]) for t in range(1, tiles)]
+                + [moved[tiles - 1]]
             )
             tile_before = tile
             for t in reversed(range(tiles + 1)):
-                at_lane = pl.multiple_of(jnp.minimum(tile + t, last) * LANES, LANES)
-                to[owner, rows, pl.ds(at_lane, LANES)] = values[t]
+                to[owner, jnp.minimum(tile + t, width_tiles - 1), rows, :] = values[t]
 
 
 def project_kernel(
     owner_slots, slot_hbm, keep_hbm, rows_hbm, panels, basis,
     mine, send, slot_column, rows_column, scalars,
     slot_s, keep_s, rows_s, keep_place, rows_place, tile_place, shift_place,
-    panels_v, basis_v, lhs_v, out_v, small_sem, panel_sem, basis_sem,
+    panels_v, basis_v, lhs_v, out_even, out_odd, small_sem, panel_sem, basis_sem,
 ):
     slots, freqs, depth = panels_v.shape
     groups = freqs // GROUP
@@ -135,7 +126,7 @@
         part = pl.ds(i * PER_COPY, PER_COPY)
         return pltpu.make_async_copy(basis.at[part], basis_v.at[part], basis_sem.at[i])
 
-    ahead = 4
+    ahead = 2
     for i in range(ahead):
         basis_copy(i).start()
     for copy in table_copies:
@@ -178,8 +169,11 @@
     column = lax.broadcasted_iota(jnp.int32, (side, side), 1)
     swap = (column == (row % GROUP) * GROUP + row // GROUP).astype(jnp.float32).astype(jnp.bfloat16)
 
-    @pl.loop(0, groups)
-    def _(group):
+    tables = (tile_place, shift_place, owner_slots)
+    all_owners = range(mine.shape[0] * lax.axis_size("pa"))
+    share = len(all_owners) // per_group
+
+    def group_step(group, out_v, out_before):
         here = pl.ds(pl.multiple_of(group * GROUP, GROUP), GROUP)
         pltpu.make_async_copy(
             panels_v.at[:, here], panels_v.at[:, here], panel_sem.at[group]
@@ -189,18 +183,26 @@
             tile = panels_v[blocks, here, :].reshape(side, depth)
             turned = jnp.dot(swap, tile, preferred_element_type=jnp.float32).astype(jnp.bfloat16)
             lhs_v[:, blocks, :] = turned.reshape(GROUP, GROUP, depth)
-
-        @pl.loop(0, GROUP // PACKED)
-        def _(part):
-            line = group * GROUP + part * PACKED
-            multiply_and_pack(
-                lhs_v,
-                lambda k: basis_v[line + k],
-                lambda c: basis_copy(line // PER_COPY + c).wait(),
-                part * PACKED,
-                out_v, mine, send, line,
-                (tile_place, shift_place, owner_slots),
-            )
+        for i in range(per_group):
+            basis_copy(group * per_group + i).wait()
+            for f in range(i * PER_COPY, (i + 1) * PER_COPY):
+                product = jnp.dot(
+                    lhs_v[f], basis_v[group * GROUP + f], preferred_element_type=jnp.float32
+                )
+                for t in range(product.shape[1] // LANES):
+                    at = (t * GROUP + f) * slots
+                    out_v[at : at + slots, :] = product[:, t * LANES : (t + 1) * LANES]
+            line = jnp.maximum(group - 1, 0) * GROUP
+            pack(out_before, mine, send, line, tables, all_owners[i * share : (i + 1) * share])
+
+    @pl.loop(0, groups // 2)
+    def _(pair):
+        group_step(2 * pair, out_even, out_odd)
+        group_step(2 * pair + 1, out_odd, out_even)
+
+    for i in range(per_group):
+        part = all_owners[i * share : (i + 1) * share]
+        pack(out_odd, mine, send, (groups - 1) * GROUP, tables, part)
 
 
 def kl_kernel(part, owners, slot_column, rows_column, kl, *refs):
@@ -212,7 +214,8 @@
     for step in range(owners):
         source = me ^ step
         at = pl.multiple_of(source * per_source, GROUP)
-        packed_v[pl.ds(at, per_source), :] = blocks[step][...]
+        for t in range(blocks[step].shape[0]):
+            packed_v[pl.ds(at, per_source), t * LANES : (t + 1) * LANES] = blocks[step][t]
     share_rows, width = out.shape
     at = pl.multiple_of(cyclic(lax.axis_index("af") + part, shares) * share_rows, GROUP)
     lhs = kl[:, pl.ds(at, share_rows), :].reshape(owner_slots * share_rows, freqs)
@@ -261,7 +264,9 @@
 def project(panels, svd_basis, slot_of_m, svd_keep, kl_keep, owner_slots, width):
     slots, freqs, depth = panels.shape
     modes = svd_basis.shape[2]
-    packed = jax.ShapeDtypeStruct((lax.axis_size("ma"), freqs, width), jnp.float32)
+    packed = jax.ShapeDtypeStruct(
+        (lax.axis_size("ma"), width // LANES, freqs, LANES), jnp.float32
+    )
     column = jax.ShapeDtypeStruct((8, width), jnp.int32)
     return pl.pallas_call(
         functools.partial(project_kernel, owner_slots),
@@ -273,7 +278,8 @@
             pltpu.VMEM((slots, freqs, depth), jnp.bfloat16),
             pltpu.VMEM((freqs, depth, modes), jnp.bfloat16),
             pltpu.VMEM((GROUP, slots, depth), jnp.bfloat16),
-            pltpu.VMEM((modes // LANES * PACKED * slots, LANES), jnp.float32),
+            pltpu.VMEM((modes // LANES * GROUP * slots, LANES), jnp.float32),
+            pltpu.VMEM((modes // LANES * GROUP * slots, LANES), jnp.float32),
             pltpu.SemaphoreType.DMA((3,)),
             pltpu.SemaphoreType.DMA((freqs // GROUP,)),
             pltpu.SemaphoreType.DMA((freqs // PER_COPY,)),
@@ -354,7 +360,7 @@
     owner_slots = kl_basis.shape[0] // (mesh.shape["pa"] * mesh.shape["ma"])
     share_rows = kl_basis.shape[1] // mesh.shape["af"]
     return (
-        freqs % GROUP == 0
+        freqs % (2 * GROUP) == 0
         and slots % (GROUP * mesh.shape["pa"]) == 0
         and owner_slots == 4
         and svd_basis.shape[2] == 2 * LANES

time: 39 us -> 34.7 us (0.89)
  Pallas kernels: 20.2 us -> 15.8 us
    pallas_call x1, Pallas kernels: 18.5 us -> 14.1 us  [project(): pl.pallas_call(functools.partial(project_kernel, owner_slots), out_shape=...]
where the time goes in v7:
time: 34.7 us; the launch traced here: 34.6 us
  Pallas kernels  15.8 us (46%)
  waiting for transfers between devices  10.8 us (31%)
  starting transfers between devices  7.75 us (22%)
    pallas_call x1, Pallas kernels, project(): pl.pallas_call(functools.partial(project_kernel, owner_slots), out_shape=...  14.1 us
    ppermute x3, waiting for transfers between devices, shards(): lax.ppermute(summed[step], 'ma', pairs('ma', step))  6.52 us
    ppermute x3, starting transfers between devices, shards(): lax.ppermute(summed[step], 'ma', pairs('ma', step))  5.67 us
    ppermute x1, waiting for transfers between devices, shards(): got = lax.ppermute(send, 'af', pairs('af', 1))  2.6 us
    ppermute x1, waiting for transfers between devices, shards(): got = lax.ppermute(send, 'pa', pairs('pa', 1))  1.72 us
    ppermute x1, starting transfers between devices, shards(): got = lax.ppermute(send, 'af', pairs('af', 1))  1.56 us
    pallas_call x1, Pallas kernels, unpack(): pl.pallas_call(unpack_kernel, out_shape=jax.ShapeDtypeStruct((owner_slots...  1.09 us
  transfers between devices with their start and end apart: 5, of which 4 were waited for; matrix products, arithmetic and copies ran while one was open for 0% of the time, Pallas kernels for 1%

profile of v7, /device:TPU:0, one launch (start us, length us, event | category | flops | bytes accessed | tf_op | source)
XLA Modules:
  0.0 34.6 jit_solution(634636352258815115)
XLA Ops:
  0.0 0.0 copy-start
  0.0 14.1 %project.1 = (f32[4,5,64,128]{3,2,1,0:T(8,128)S(1)}, f32[4,5,64,128]{3,2,1,0:T(8,128)S(1)}, s32[8,640]{1,0:T(8,128)S(1)}, s32[8,640]{1,0:T(8,128)S(1)}, s32[8,128]{1,0:T(8,128)S(1)}) custom-call(s32[32]{0:T(128)} %slot_hbm.1, s32[32]{0:T(128)} %keep_hbm.1, s32[32]{0:T(128)} %rows_hbm.1, bf16[32,64,1024]{2,1,0:T(8,128)(2,1)} %panels.1, ...), custom_call_target="tpu_custom_call" | custom-call | flops 1073741824 | bytes 37748736 | tf_op jit(solution)/shard_map/project/pallas_call | solution.py:271
  14.1 0.5 %collective-permute-start = (f32[4,5,64,128]{3,2,1,0:T(8,128)S(1)}, f32[4,5,64,128]{3,2,1,0:T(8,128)S(1)}, u32[]{:S(2)}, u32[]{:S(2)}) collective-permute-start(f32[4,5,64,128]{3,2,1,0:T(8,128)S(1)} %get-tuple-element.14), channel_id=1, source_target_pairs={{0,1},{1,0},{2,3},{3,2},{4,5},{5,4},{6,7},{7,6},{8,9},{9,8},{10,11... | collective-permute-start | bytes 1966088 | tf_op jit(solution)/shard_map/ppermute | solution.py:344
  14.6 1.7 %collective-permute-done = f32[4,5,64,128]{3,2,1,0:T(8,128)S(1)} collective-permute-done((f32[4,5,64,128]{3,2,1,0:T(8,128)S(1)}, f32[4,5,64,128]{3,2,1,0:T(8,128)S(1)}, u32[]{:S(2)}, u32[]{:S(2)}) %collective-permute-start) | collective-permute-done | bytes 655392 | tf_op jit(solution)/shard_map/ppermute | solution.py:344
  16.3 0.1 fusion.7
  16.4 5.0 %collective-permute-start.3 = (bf16[5,64,128]{2,1,0:T(8,128)(2,1)S(1)}, bf16[5,64,128]{2,1,0:T(8,128)(2,1)S(1)}, u32[]{:S(2)}, u32[]{:S(2)}) collective-permute-start(bf16[5,64,128]{2,1,0:T(8,128)(2,1)S(1)} %get-tuple-element.15), channel_id=1, source_target_pairs={{0,12},{4,8},{8,4},{12,0},{1,13},{5,9},{9,5},{13,1},{2,14},{6,10},... | collective-permute-start | bytes 245768 | tf_op jit(solution)/shard_map/ppermute | solution.py:347
  21.4 0.0 collective-permute-start.2
  21.4 0.6 %collective-permute-start.1 = (bf16[5,64,128]{2,1,0:T(8,128)(2,1)S(1)}, bf16[5,64,128]{2,1,0:T(8,128)(2,1)S(1)}, u32[]{:S(2)}, u32[]{:S(2)}) collective-permute-start(bf16[5,64,128]{2,1,0:T(8,128)(2,1)S(1)} %get-tuple-element.17), channel_id=1, source_target_pairs={{0,4},{4,0},{8,12},{12,8},{1,5},{5,1},{9,13},{13,9},{2,6},{6,2},{1... | collective-permute-start | bytes 245768 | tf_op jit(solution)/shard_map/ppermute | solution.py:347
  22.1 2.7 %collective-permute-done.3.refs_3_ = bf16[5,64,128]{2,1,0:T(8,128)(2,1)S(1)} collective-permute-done((bf16[5,64,128]{2,1,0:T(8,128)(2,1)S(1)}, bf16[5,64,128]{2,1,0:T(8,128)(2,1)S(1)}, u32[]{:S(2)}, u32[]{:S(2)}) %collective-permute-start.3) | collective-permute-done | bytes 81952 | tf_op jit(solution)/shard_map/ppermute | solution.py:347
  24.8 3.8 %collective-permute-done.2.refs_2_ = bf16[5,64,128]{2,1,0:T(8,128)(2,1)S(1)} collective-permute-done((bf16[5,64,128]{2,1,0:T(8,128)(2,1)S(1)}, bf16[5,64,128]{2,1,0:T(8,128)(2,1)S(1)}, u32[]{:S(2)}, u32[]{:S(2)}) %collective-permute-start.2) | collective-permute-done | bytes 81952 | tf_op jit(solution)/shard_map/ppermute | solution.py:347
  28.6 0.0 collective-permute-done.1.refs_1_
  28.6 0.0 copy-done
  28.6 0.3 kl_project.3
  29.0 1.6 %collective-permute-start.4 = (bf16[64,640]{1,0:T(8,128)(2,1)S(1)}, bf16[64,640]{1,0:T(8,128)(2,1)S(1)}, u32[]{:S(2)}, u32[]{:S(2)}) collective-permute-start(bf16[64,640]{1,0:T(8,128)(2,1)S(1)} %kl_project.3), channel_id=1, source_target_pairs={{0,2},{2,0},{1,3},{3,1},{4,6},{6,4},{5,7},{7,5},{8,10},{10,8},{9,1... | collective-permute-start | bytes 245768 | tf_op jit(solution)/shard_map/ppermute | solution.py:351
  30.5 0.3 kl_project.2.mine
  30.9 2.6 %collective-permute-done.4.got = bf16[64,640]{1,0:T(8,128)(2,1)S(1)} collective-permute-done((bf16[64,640]{1,0:T(8,128)(2,1)S(1)}, bf16[64,640]{1,0:T(8,128)(2,1)S(1)}, u32[]{:S(2)}, u32[]{:S(2)}) %collective-permute-start.4) | collective-permute-done | bytes 81952 | tf_op jit(solution)/shard_map/ppermute | solution.py:351
  33.5 1.1 %unpack.1 = f32[4,64,256]{2,1,0:T(8,128)} custom-call(s32[8,128]{1,0:T(8,128)S(1)} %get-tuple-element.10.scalars, f32[64,640]{1,0:T(8,128)S(1)} %kl_project.2.mine, bf16[64,640]{1,0:T(8,128)(2,1)S(1)} %collective-permute-done.4.got), custom_call_target="tpu_custom_call" | custom-call | flops 40960 | bytes 409600 | tf_op jit(solution)/shard_map/unpack/pallas_call | solution.py:319
Async XLA Ops:
  0.0 28.6 %copy-start = (bf16[4,128,256]{2,1,0:T(8,128)(2,1)S(1)}, bf16[4,128,256]{2,1,0:T(8,128)(2,1)}, u32[]{:S(2)}) copy-start(bf16[4,128,256]{2,1,0:T(8,128)(2,1)} %kl.3) | copy-start | bytes 786436
  14.1 2.2 %collective-permute-start = (f32[4,5,64,128]{3,2,1,0:T(8,128)S(1)}, f32[4,5,64,128]{3,2,1,0:T(8,128)S(1)}, u32[]{:S(2)}, u32[]{:S(2)}) collective-permute-start(f32[4,5,64,128]{3,2,1,0:T(8,128)S(1)} %get-tuple-element.14), channel_id=1, source_target_pairs={{0,1},{1,0},{2,3},{3,2},{4,5},{5,4},{6,7},{7,6},{8,9},{9,8},{10,11... | collective-permute-start | bytes 1966088 | tf_op jit(solution)/shard_map/ppermute | solution.py:344
  16.4 8.4 %collective-permute-start.3 = (bf16[5,64,128]{2,1,0:T(8,128)(2,1)S(1)}, bf16[5,64,128]{2,1,0:T(8,128)(2,1)S(1)}, u32[]{:S(2)}, u32[]{:S(2)}) collective-permute-start(bf16[5,64,128]{2,1,0:T(8,128)(2,1)S(1)} %get-tuple-element.15), channel_id=1, source_target_pairs={{0,12},{4,8},{8,4},{12,0},{1,13},{5,9},{9,5},{13,1},{2,14},{6,10},... | collective-permute-start | bytes 245768 | tf_op jit(solution)/shard_map/ppermute | solution.py:347
  21.4 7.2 %collective-permute-start.2 = (bf16[5,64,128]{2,1,0:T(8,128)(2,1)S(1)}, bf16[5,64,128]{2,1,0:T(8,128)(2,1)S(1)}, u32[]{:S(2)}, u32[]{:S(2)}) collective-permute-start(bf16[5,64,128]{2,1,0:T(8,128)(2,1)S(1)} %get-tuple-element.16), channel_id=1, source_target_pairs={{0,8},{4,12},{8,0},{12,4},{1,9},{5,13},{9,1},{13,5},{2,10},{6,14},... | collective-permute-start | bytes 245768 | tf_op jit(solution)/shard_map/ppermute | solution.py:347
  21.4 7.2 %collective-permute-start.1 = (bf16[5,64,128]{2,1,0:T(8,128)(2,1)S(1)}, bf16[5,64,128]{2,1,0:T(8,128)(2,1)S(1)}, u32[]{:S(2)}, u32[]{:S(2)}) collective-permute-start(bf16[5,64,128]{2,1,0:T(8,128)(2,1)S(1)} %get-tuple-element.17), channel_id=1, source_target_pairs={{0,4},{4,0},{8,12},{12,8},{1,5},{5,1},{9,13},{13,9},{2,6},{6,2},{1... | collective-permute-start | bytes 245768 | tf_op jit(solution)/shard_map/ppermute | solution.py:347
  29.0 4.5 %collective-permute-start.4 = (bf16[64,640]{1,0:T(8,128)(2,1)S(1)}, bf16[64,640]{1,0:T(8,128)(2,1)S(1)}, u32[]{:S(2)}, u32[]{:S(2)}) collective-permute-start(bf16[64,640]{1,0:T(8,128)(2,1)S(1)} %kl_project.3), channel_id=1, source_target_pairs={{0,2},{2,0},{1,3},{3,1},{4,6},{6,4},{5,7},{7,5},{8,10},{10,8},{9,1... | collective-permute-start | bytes 245768 | tf_op jit(solution)/shard_map/ppermute | solution.py:351

commit v8 on v7

--- a/solution.py
+++ b/solution.py
@@ -48,10 +48,19 @@
     return lax.rem(value + count, count)
 
 
+def on_ring(z):
+    return z ^ (z // 2) if isinstance(z, int) else z ^ lax.shift_right_logical(z, 1)
+
+
+def far_step(owners):
+    return owners // 2
+
+
 def place_of(slot, owner_slots, half_slots):
     half = cyclic(lax.div(slot, half_slots) - lax.axis_index("pa"), lax.axis_size("pa"))
     within = lax.rem(slot, half_slots)
-    owner = lax.div(within, owner_slots) ^ lax.axis_index("ma")
+    owner = on_ring(lax.div(within, owner_slots)) - on_ring(lax.axis_index("ma"))
+    owner = cyclic(owner, lax.axis_size("ma"))
     return half * half_slots + owner * owner_slots + lax.rem(within, owner_slots)
 
 
@@ -67,7 +76,7 @@
             offset = offset + keep_place[place]
 
 
-def pack(out_v, mine, send, line, tables, owners_at):
+def pack(out_v, mine, far, near, line, tables, owners_at):
     tile_place, shift_place, owner_slots = tables
     owners, width_tiles = mine.shape[:2]
     slots = 2 * owners * owner_slots
@@ -81,7 +90,10 @@
         for place in range(owners_at[0] * owner_slots, (owners_at[-1] + 1) * owner_slots)
     }
     for at in owners_at:
-        to, owner = (mine, send)[at // owners], at % owners
+        to, owner = mine, at % owners
+        if at >= owners:
+            first = far_step(owners)
+            to, owner = (far, 0) if owner == first else (near, owner - (owner > first))
         values, tile_before = None, None
         for j in range(owner_slots):
             place = at * owner_slots + j
@@ -106,7 +118,7 @@
 
 def project_kernel(
     owner_slots, slot_hbm, keep_hbm, rows_hbm, panels, basis,
-    mine, send, slot_column, rows_column, scalars,
+    mine, far, near, slot_column, rows_column, scalars,
     slot_s, keep_s, rows_s, keep_place, rows_place, tile_place, shift_place,
     panels_v, basis_v, lhs_v, out_even, out_odd, small_sem, panel_sem, basis_sem,
 ):
@@ -193,7 +205,7 @@
                     at = (t * GROUP + f) * slots
                     out_v[at : at + slots, :] = product[:, t * LANES : (t + 1) * LANES]
             line = jnp.maximum(group - 1, 0) * GROUP
-            pack(out_before, mine, send, line, tables, all_owners[i * share : (i + 1) * share])
+            pack(out_before, mine, far, near, line, tables, all_owners[i * share : (i + 1) * share])
 
     @pl.loop(0, groups // 2)
     def _(pair):
@@ -202,7 +214,12 @@
 
     for i in range(per_group):
         part = all_owners[i * share : (i + 1) * share]
-        pack(out_odd, mine, send, (groups - 1) * GROUP, tables, part)
+        pack(out_odd, mine, far, near, (groups - 1) * GROUP, tables, part)
+
+
+def sum_kernel(steps, mine, got, *out):
+    for i, step in enumerate(steps):
+        out[i][...] = (mine[step] + got[i]).astype(out[i].dtype)
 
 
 def kl_kernel(part, owners, slot_column, rows_column, kl, *refs):
@@ -212,7 +229,7 @@
     per_source = freqs // owners
     me = lax.axis_index("ma")
     for step in range(owners):
-        source = me ^ step
+        source = on_ring(cyclic(on_ring(me) - step, owners))
         at = pl.multiple_of(source * per_source, GROUP)
         for t in range(blocks[step].shape[0]):
             packed_v[pl.ds(at, per_source), t * LANES : (t + 1) * LANES] = blocks[step][t]
@@ -264,15 +281,24 @@
 def project(panels, svd_basis, slot_of_m, svd_keep, kl_keep, owner_slots, width):
     slots, freqs, depth = panels.shape
     modes = svd_basis.shape[2]
-    packed = jax.ShapeDtypeStruct(
-        (lax.axis_size("ma"), width // LANES, freqs, LANES), jnp.float32
-    )
+    owners = lax.axis_size("ma")
+
+    def packed(count):
+        return jax.ShapeDtypeStruct((count, width // LANES, freqs, LANES), jnp.float32)
+
     column = jax.ShapeDtypeStruct((8, width), jnp.int32)
     return pl.pallas_call(
         functools.partial(project_kernel, owner_slots),
-        out_shape=(packed, packed, column, column, jax.ShapeDtypeStruct((8, LANES), jnp.int32)),
+        out_shape=(
+            packed(owners),
+            packed(1),
+            packed(owners - 1),
+            column,
+            column,
+            jax.ShapeDtypeStruct((8, LANES), jnp.int32),
+        ),
         in_specs=[HBM] * 5,
-        out_specs=(VMEM,) * 5,
+        out_specs=(VMEM,) * 6,
         scratch_shapes=[pltpu.SMEM((slots,), jnp.int32)] * 7
         + [
             pltpu.VMEM((slots, freqs, depth), jnp.bfloat16),
@@ -294,6 +320,21 @@
     )(*map(in_hbm, (slot_of_m, svd_keep, kl_keep, panels, svd_basis)))
 
 
+def sum_pair(steps, mine, got):
+    kind = jax.ShapeDtypeStruct(mine.shape[1:], jnp.bfloat16)
+    return pl.pallas_call(
+        functools.partial(sum_kernel, steps),
+        out_shape=(kind,) * len(steps),
+        in_specs=[VMEM] * 2,
+        out_specs=(VMEM,) * len(steps),
+        compiler_params=SMALL,
+        cost_estimate=pl.CostEstimate(
+            flops=got.size, bytes_accessed=10 * got.size, transcendentals=0
+        ),
+        name="sum_pair",
+    )(mine, got)
+
+
 def kl_project(part, kind, slot_column, rows_column, kl_basis, blocks):
     owners, shares = lax.axis_size("ma"), lax.axis_size("af")
     rows, freqs = kl_basis.shape[1:]
@@ -330,25 +371,36 @@
     )(scalars, mine, got)
 
 
-def pairs(axis, step):
-    return [(i, i ^ step) for i in range(lax.axis_size(axis))]
+def pairs(axis):
+    return [(i, i ^ 1) for i in range(lax.axis_size(axis))]
+
+
+def ring(step):
+    size = lax.axis_size("ma")
+    return [(i, on_ring((on_ring(i) + step) % size)) for i in range(size)]
 
 
 def shards(panels, svd_basis, kl_basis, slot_of_m, svd_keep, kl_keep):
     owner_slots, modes = kl_basis.shape[0], svd_basis.shape[2]
     owners = lax.axis_size("ma")
     width = -(-min(OWNER_BUDGET, owner_slots * modes) // LANES) * LANES
-    mine, send, slot_column, rows_column, scalars = project(
+    mine, far, near, slot_column, rows_column, scalars = project(
         panels, svd_basis, slot_of_m, svd_keep, kl_keep, owner_slots, width
     )
-    got = lax.ppermute(send, "pa", pairs("pa", 1))
-    summed = [(mine[step] + got[step]).astype(jnp.bfloat16) for step in range(owners)]
-    blocks = [summed[0]] + [
-        lax.ppermute(summed[step], "ma", pairs("ma", step)) for step in range(1, owners)
-    ]
-    tables = (slot_column, rows_column, kl_basis, blocks)
+    first = far_step(owners)
+    others = [step for step in range(owners) if step != first]
+    got_far = lax.ppermute(far, "pa", pairs("pa"))
+    near, got_far = lax.optimization_barrier((near, got_far))
+    got_near = lax.ppermute(near, "pa", pairs("pa"))
+    summed = dict(zip([first], sum_pair([first], mine, got_far)))
+    summed |= zip(others, sum_pair(others, mine, got_near))
+    blocks = {
+        step: lax.ppermute(summed[step], "ma", ring(step)) if step else summed[step]
+        for step in [first] + others
+    }
+    tables = (slot_column, rows_column, kl_basis, [blocks[step] for step in range(owners)])
     send = kl_project(1, jnp.bfloat16, *tables)
-    got = lax.ppermute(send, "af", pairs("af", 1))
+    got = lax.ppermute(send, "af", pairs("af"))
     mine = kl_project(0, jnp.float32, *tables)
     return unpack(scalars, mine, got, owner_slots, modes)
 
@@ -367,7 +419,7 @@
         and share_rows % GROUP == 0
         and mesh.shape["pa"] == 2
         and mesh.shape["af"] == 2
-        and mesh.shape["ma"] in (2, 4)
+        and mesh.shape["ma"] == 4
     )
 
 

time: 34.7 us -> 34.6 us (level)
  waiting for transfers between devices: 10.8 us -> 8.06 us
  starting transfers between devices: 7.75 us -> 10.2 us
  Pallas kernels: 15.8 us -> 16.2 us
    ppermute x5 -> x6, waiting for transfers between devices: 10.8 us -> 8.06 us  [the longest x3 4.41 us: shards(): lax.ppermute(summed[step], 'ma', ring(step))]
    ppermute x5 -> x6, starting transfers between devices: 7.75 us -> 10.2 us  [the longest x3 7.78 us: shards(): lax.ppermute(summed[step], 'ma', ring(step))]
  transfers between devices with their start and end apart: 5 -> 6, of which waited for: 4 -> 4; matrix products, arithmetic and copies ran while one was open for 0% -> 0% of each run, Pallas kernels for 1% -> 1%
where the time goes in v8:
time: 34.6 us; the launch traced here: 34.5 us
  Pallas kernels  16.2 us (47%)
  starting transfers between devices  10.2 us (29%)
  waiting for transfers between devices  8.06 us (23%)
    pallas_call x1, Pallas kernels, project(): pl.pallas_call(functools.partial(project_kernel, owner_slots), out_shape=...  14.4 us
    ppermute x3, starting transfers between devices, shards(): lax.ppermute(summed[step], 'ma', ring(step))  7.78 us
    ppermute x3, waiting for transfers between devices, shards(): lax.ppermute(summed[step], 'ma', ring(step))  4.41 us
    ppermute x1, waiting for transfers between devices, shards(): got = lax.ppermute(send, 'af', pairs('af'))  2.62 us
    ppermute x1, starting transfers between devices, shards(): got = lax.ppermute(send, 'af', pairs('af'))  1.55 us
    pallas_call x1, Pallas kernels, unpack(): pl.pallas_call(unpack_kernel, out_shape=jax.ShapeDtypeStruct((owner_slots...  1.09 us
    ppermute x1, waiting for transfers between devices, shards(): got_far = lax.ppermute(far, 'pa', pairs('pa'))  1.03 us
  transfers between devices with their start and end apart: 6, of which 4 were waited for; matrix products, arithmetic and copies ran while one was open for 0% of the time, Pallas kernels for 1%

profile of v8, /device:TPU:0, one launch (start us, length us, event | category | flops | bytes accessed | tf_op | source)
XLA Modules:
  0.0 34.5 jit_solution(1794465723905485060)
XLA Ops:
  0.0 0.0 copy-start
  0.0 14.4 %project.1 = (f32[4,5,64,128]{3,2,1,0:T(8,128)S(1)}, f32[1,5,64,128]{3,2,1,0:T(8,128)S(1)}, f32[3,5,64,128]{3,2,1,0:T(8,128)S(1)}, s32[8,640]{1,0:T(8,128)S(1)},...) custom-call(s32[32]{0:T(128)} %slot_hbm.1, s32[32]{0:T(128)} %keep_hbm.1, s32[32]{0:T(128)} %rows_hbm.1, ...), custom_call_target="tpu_custom_call" | custom-call | flops 1073741824 | bytes 37748736 | tf_op jit(solution)/shard_map/project/pallas_call | solution.py:290
  14.4 0.5 %collective-permute-start = (f32[1,5,64,128]{3,2,1,0:T(8,128)S(1)}, f32[1,5,64,128]{3,2,1,0:T(8,128)S(1)}, u32[]{:S(2)}, u32[]{:S(2)}) collective-permute-start(f32[1,5,64,128]{3,2,1,0:T(8,128)S(1)} %get-tuple-element.21), channel_id=1, source_target_pairs={{0,1},{1,0},{2,3},{3,2},{4,5},{5,4},{6,7},{7,6},{8,9},{9,8},{10,11... | collective-permute-start | bytes 491528 | tf_op jit(solution)/shard_map/ppermute | solution.py:392
  14.9 1.0 %collective-permute-done.got = f32[1,5,64,128]{3,2,1,0:T(8,128)S(1)} collective-permute-done((f32[1,5,64,128]{3,2,1,0:T(8,128)S(1)}, f32[1,5,64,128]{3,2,1,0:T(8,128)S(1)}, u32[]{:S(2)}, u32[]{:S(2)}) %collective-permute-start) | collective-permute-done | bytes 163872 | tf_op jit(solution)/shard_map/ppermute | solution.py:392
  15.9 0.4 %collective-permute-start.1 = (f32[3,5,64,128]{3,2,1,0:T(8,128)S(1)}, f32[3,5,64,128]{3,2,1,0:T(8,128)S(1)}, u32[]{:S(2)}, u32[]{:S(2)}) collective-permute-start(f32[3,5,64,128]{3,2,1,0:T(8,128)S(1)} %get-tuple-element.22), channel_id=1, source_target_pairs={{0,1},{1,0},{2,3},{3,2},{4,5},{5,4},{6,7},{7,6},{8,9},{9,8},{10,11... | collective-permute-start | bytes 1474568 | tf_op jit(solution)/shard_map/ppermute | solution.py:394
  16.3 4.8 %collective-permute-start.3 = (bf16[5,64,128]{2,1,0:T(8,128)(2,1)S(1)}, bf16[5,64,128]{2,1,0:T(8,128)(2,1)S(1)}, u32[]{:S(2)}, u32[]{:S(2)}) collective-permute-start(bf16[5,64,128]{2,1,0:T(8,128)(2,1)S(1)} %sum_pair.3), channel_id=1, source_target_pairs={{0,12},{4,8},{8,4},{12,0},{1,13},{5,9},{9,5},{13,1},{2,14},{6,10},... | collective-permute-start | bytes 245768 | tf_op jit(solution)/shard_map/ppermute | solution.py:398
  21.1 0.0 collective-permute-done.1.got
  21.2 0.1 collective-permute-start.2
  21.2 2.9 %collective-permute-start.4 = (bf16[5,64,128]{2,1,0:T(8,128)(2,1)S(1)}, bf16[5,64,128]{2,1,0:T(8,128)(2,1)S(1)}, u32[]{:S(2)}, u32[]{:S(2)}) collective-permute-start(bf16[5,64,128]{2,1,0:T(8,128)(2,1)S(1)} %get-tuple-element.26), channel_id=1, source_target_pairs={{0,8},{4,0},{8,12},{12,4},{1,9},{5,1},{9,13},{13,5},{2,10},{6,2},{... | collective-permute-start | bytes 245768 | tf_op jit(solution)/shard_map/ppermute | solution.py:398
  24.2 0.1 collective-permute-done.3.refs_2_
  24.2 4.3 %collective-permute-done.2.refs_1_ = bf16[5,64,128]{2,1,0:T(8,128)(2,1)S(1)} collective-permute-done((bf16[5,64,128]{2,1,0:T(8,128)(2,1)S(1)}, bf16[5,64,128]{2,1,0:T(8,128)(2,1)S(1)}, u32[]{:S(2)}, u32[]{:S(2)}) %collective-permute-start.2) | collective-permute-done | bytes 81952 | tf_op jit(solution)/shard_map/ppermute | solution.py:398
  28.6 0.0 collective-permute-done.4.refs_3_
  28.6 0.0 copy-done
  28.6 0.3 kl_project.3
  28.9 1.5 %collective-permute-start.5 = (bf16[64,640]{1,0:T(8,128)(2,1)S(1)}, bf16[64,640]{1,0:T(8,128)(2,1)S(1)}, u32[]{:S(2)}, u32[]{:S(2)}) collective-permute-start(bf16[64,640]{1,0:T(8,128)(2,1)S(1)} %kl_project.3), channel_id=1, source_target_pairs={{0,2},{2,0},{1,3},{3,1},{4,6},{6,4},{5,7},{7,5},{8,10},{10,8},{9,1... | collective-permute-start | bytes 245768 | tf_op jit(solution)/shard_map/ppermute | solution.py:403
  30.5 0.3 kl_project.2.mine
  30.8 2.6 %collective-permute-done.5.got = bf16[64,640]{1,0:T(8,128)(2,1)S(1)} collective-permute-done((bf16[64,640]{1,0:T(8,128)(2,1)S(1)}, bf16[64,640]{1,0:T(8,128)(2,1)S(1)}, u32[]{:S(2)}, u32[]{:S(2)}) %collective-permute-start.5) | collective-permute-done | bytes 81952 | tf_op jit(solution)/shard_map/ppermute | solution.py:403
  33.4 1.1 %unpack.1 = f32[4,64,256]{2,1,0:T(8,128)} custom-call(s32[8,128]{1,0:T(8,128)S(1)} %get-tuple-element.16.scalars, f32[64,640]{1,0:T(8,128)S(1)} %kl_project.2.mine, bf16[64,640]{1,0:T(8,128)(2,1)S(1)} %collective-permute-done.5.got), custom_call_target="tpu_custom_call" | custom-call | flops 40960 | bytes 409600 | tf_op jit(solution)/shard_map/unpack/pallas_call | solution.py:360
  (2 shorter events, 0.1 us)
Async XLA Ops:
  0.0 28.6 %copy-start = (bf16[4,128,256]{2,1,0:T(8,128)(2,1)S(1)}, bf16[4,128,256]{2,1,0:T(8,128)(2,1)}, u32[]{:S(2)}) copy-start(bf16[4,128,256]{2,1,0:T(8,128)(2,1)} %kl.3) | copy-start | bytes 786436
  14.4 1.6 %collective-permute-start = (f32[1,5,64,128]{3,2,1,0:T(8,128)S(1)}, f32[1,5,64,128]{3,2,1,0:T(8,128)S(1)}, u32[]{:S(2)}, u32[]{:S(2)}) collective-permute-start(f32[1,5,64,128]{3,2,1,0:T(8,128)S(1)} %get-tuple-element.21), channel_id=1, source_target_pairs={{0,1},{1,0},{2,3},{3,2},{4,5},{5,4},{6,7},{7,6},{8,9},{9,8},{10,11... | collective-permute-start | bytes 491528 | tf_op jit(solution)/shard_map/ppermute | solution.py:392
  15.9 5.2 %collective-permute-start.1 = (f32[3,5,64,128]{3,2,1,0:T(8,128)S(1)}, f32[3,5,64,128]{3,2,1,0:T(8,128)S(1)}, u32[]{:S(2)}, u32[]{:S(2)}) collective-permute-start(f32[3,5,64,128]{3,2,1,0:T(8,128)S(1)} %get-tuple-element.22), channel_id=1, source_target_pairs={{0,1},{1,0},{2,3},{3,2},{4,5},{5,4},{6,7},{7,6},{8,9},{9,8},{10,11... | collective-permute-start | bytes 1474568 | tf_op jit(solution)/shard_map/ppermute | solution.py:394
  16.3 7.9 %collective-permute-start.3 = (bf16[5,64,128]{2,1,0:T(8,128)(2,1)S(1)}, bf16[5,64,128]{2,1,0:T(8,128)(2,1)S(1)}, u32[]{:S(2)}, u32[]{:S(2)}) collective-permute-start(bf16[5,64,128]{2,1,0:T(8,128)(2,1)S(1)} %sum_pair.3), channel_id=1, source_target_pairs={{0,12},{4,8},{8,4},{12,0},{1,13},{5,9},{9,5},{13,1},{2,14},{6,10},... | collective-permute-start | bytes 245768 | tf_op jit(solution)/shard_map/ppermute | solution.py:398
  21.2 7.4 %collective-permute-start.2 = (bf16[5,64,128]{2,1,0:T(8,128)(2,1)S(1)}, bf16[5,64,128]{2,1,0:T(8,128)(2,1)S(1)}, u32[]{:S(2)}, u32[]{:S(2)}) collective-permute-start(bf16[5,64,128]{2,1,0:T(8,128)(2,1)S(1)} %get-tuple-element.24), channel_id=1, source_target_pairs={{0,4},{4,12},{8,0},{12,8},{1,5},{5,13},{9,1},{13,9},{2,6},{6,14},{... | collective-permute-start | bytes 245768 | tf_op jit(solution)/shard_map/ppermute | solution.py:398
  21.2 7.3 %collective-permute-start.4 = (bf16[5,64,128]{2,1,0:T(8,128)(2,1)S(1)}, bf16[5,64,128]{2,1,0:T(8,128)(2,1)S(1)}, u32[]{:S(2)}, u32[]{:S(2)}) collective-permute-start(bf16[5,64,128]{2,1,0:T(8,128)(2,1)S(1)} %get-tuple-element.26), channel_id=1, source_target_pairs={{0,8},{4,0},{8,12},{12,4},{1,9},{5,1},{9,13},{13,5},{2,10},{6,2},{... | collective-permute-start | bytes 245768 | tf_op jit(solution)/shard_map/ppermute | solution.py:398
  28.9 4.5 %collective-permute-start.5 = (bf16[64,640]{1,0:T(8,128)(2,1)S(1)}, bf16[64,640]{1,0:T(8,128)(2,1)S(1)}, u32[]{:S(2)}, u32[]{:S(2)}) collective-permute-start(bf16[64,640]{1,0:T(8,128)(2,1)S(1)} %kl_project.3), channel_id=1, source_target_pairs={{0,2},{2,0},{1,3},{3,1},{4,6},{6,4},{5,7},{7,5},{8,10},{10,8},{9,1... | collective-permute-start | bytes 245768 | tf_op jit(solution)/shard_map/ppermute | solution.py:403

commit v9 on v8

--- a/solution.py
+++ b/solution.py
@@ -9,7 +9,7 @@
 
 LANES = 128
 GROUP = 16
-PER_COPY = 4
+PER_COPY = 8
 OWNER_BUDGET = 576
 MIB = 2**20
 
@@ -138,7 +138,7 @@
         part = pl.ds(i * PER_COPY, PER_COPY)
         return pltpu.make_async_copy(basis.at[part], basis_v.at[part], basis_sem.at[i])
 
-    ahead = 2
+    ahead = 1
     for i in range(ahead):
         basis_copy(i).start()
     for copy in table_copies:

time: 34.6 us -> 33.8 us (0.977)
  Pallas kernels: 16.2 us -> 15.4 us
    pallas_call x1, Pallas kernels: 14.4 us -> 13.6 us  [project(): pl.pallas_call(functools.partial(project_kernel, owner_slots), out_shape=...]
where the time goes in v9:
time: 33.8 us; the launch traced here: 33.7 us
  Pallas kernels  15.4 us (46%)
  starting transfers between devices  10.2 us (30%)
  waiting for transfers between devices  8.03 us (24%)
    pallas_call x1, Pallas kernels, project(): pl.pallas_call(functools.partial(project_kernel, owner_slots), out_shape=...  13.6 us
    ppermute x3, starting transfers between devices, shards(): lax.ppermute(summed[step], 'ma', ring(step))  7.79 us
    ppermute x3, waiting for transfers between devices, shards(): lax.ppermute(summed[step], 'ma', ring(step))  4.39 us
    ppermute x1, waiting for transfers between devices, shards(): got = lax.ppermute(send, 'af', pairs('af'))  2.61 us
    ppermute x1, starting transfers between devices, shards(): got = lax.ppermute(send, 'af', pairs('af'))  1.56 us
    pallas_call x1, Pallas kernels, unpack(): pl.pallas_call(unpack_kernel, out_shape=jax.ShapeDtypeStruct((owner_slots...  1.09 us
    ppermute x1, waiting for transfers between devices, shards(): got_far = lax.ppermute(far, 'pa', pairs('pa'))  1.03 us
  transfers between devices with their start and end apart: 6, of which 4 were waited for; matrix products, arithmetic and copies ran while one was open for 0% of the time, Pallas kernels for 1%

profile of v9, /device:TPU:0, one launch (start us, length us, event | category | flops | bytes accessed | tf_op | source)
XLA Modules:
  0.0 33.7 jit_solution(12542533514198582616)
XLA Ops:
  0.0 0.0 copy-start
  0.0 13.6 %project.1 = (f32[4,5,64,128]{3,2,1,0:T(8,128)S(1)}, f32[1,5,64,128]{3,2,1,0:T(8,128)S(1)}, f32[3,5,64,128]{3,2,1,0:T(8,128)S(1)}, s32[8,640]{1,0:T(8,128)S(1)},...) custom-call(s32[32]{0:T(128)} %slot_hbm.1, s32[32]{0:T(128)} %keep_hbm.1, s32[32]{0:T(128)} %rows_hbm.1, ...), custom_call_target="tpu_custom_call" | custom-call | flops 1073741824 | bytes 37748736 | tf_op jit(solution)/shard_map/project/pallas_call | solution.py:290
  13.6 0.5 %collective-permute-start = (f32[1,5,64,128]{3,2,1,0:T(8,128)S(1)}, f32[1,5,64,128]{3,2,1,0:T(8,128)S(1)}, u32[]{:S(2)}, u32[]{:S(2)}) collective-permute-start(f32[1,5,64,128]{3,2,1,0:T(8,128)S(1)} %get-tuple-element.21), channel_id=1, source_target_pairs={{0,1},{1,0},{2,3},{3,2},{4,5},{5,4},{6,7},{7,6},{8,9},{9,8},{10,11... | collective-permute-start | bytes 491528 | tf_op jit(solution)/shard_map/ppermute | solution.py:392
  14.1 1.0 %collective-permute-done.got = f32[1,5,64,128]{3,2,1,0:T(8,128)S(1)} collective-permute-done((f32[1,5,64,128]{3,2,1,0:T(8,128)S(1)}, f32[1,5,64,128]{3,2,1,0:T(8,128)S(1)}, u32[]{:S(2)}, u32[]{:S(2)}) %collective-permute-start) | collective-permute-done | bytes 163872 | tf_op jit(solution)/shard_map/ppermute | solution.py:392
  15.1 0.4 %collective-permute-start.1 = (f32[3,5,64,128]{3,2,1,0:T(8,128)S(1)}, f32[3,5,64,128]{3,2,1,0:T(8,128)S(1)}, u32[]{:S(2)}, u32[]{:S(2)}) collective-permute-start(f32[3,5,64,128]{3,2,1,0:T(8,128)S(1)} %get-tuple-element.22), channel_id=1, source_target_pairs={{0,1},{1,0},{2,3},{3,2},{4,5},{5,4},{6,7},{7,6},{8,9},{9,8},{10,11... | collective-permute-start | bytes 1474568 | tf_op jit(solution)/shard_map/ppermute | solution.py:394
  15.5 4.8 %collective-permute-start.3 = (bf16[5,64,128]{2,1,0:T(8,128)(2,1)S(1)}, bf16[5,64,128]{2,1,0:T(8,128)(2,1)S(1)}, u32[]{:S(2)}, u32[]{:S(2)}) collective-permute-start(bf16[5,64,128]{2,1,0:T(8,128)(2,1)S(1)} %sum_pair.3), channel_id=1, source_target_pairs={{0,12},{4,8},{8,4},{12,0},{1,13},{5,9},{9,5},{13,1},{2,14},{6,10},... | collective-permute-start | bytes 245768 | tf_op jit(solution)/shard_map/ppermute | solution.py:398
  20.3 0.0 collective-permute-done.1.got
  20.4 0.1 collective-permute-start.2
  20.5 2.9 %collective-permute-start.4 = (bf16[5,64,128]{2,1,0:T(8,128)(2,1)S(1)}, bf16[5,64,128]{2,1,0:T(8,128)(2,1)S(1)}, u32[]{:S(2)}, u32[]{:S(2)}) collective-permute-start(bf16[5,64,128]{2,1,0:T(8,128)(2,1)S(1)} %get-tuple-element.26), channel_id=1, source_target_pairs={{0,8},{4,0},{8,12},{12,4},{1,9},{5,1},{9,13},{13,5},{2,10},{6,2},{... | collective-permute-start | bytes 245768 | tf_op jit(solution)/shard_map/ppermute | solution.py:398
  23.4 0.1 collective-permute-done.3.refs_2_
  23.4 4.3 %collective-permute-done.2.refs_1_ = bf16[5,64,128]{2,1,0:T(8,128)(2,1)S(1)} collective-permute-done((bf16[5,64,128]{2,1,0:T(8,128)(2,1)S(1)}, bf16[5,64,128]{2,1,0:T(8,128)(2,1)S(1)}, u32[]{:S(2)}, u32[]{:S(2)}) %collective-permute-start.2) | collective-permute-done | bytes 81952 | tf_op jit(solution)/shard_map/ppermute | solution.py:398
  27.8 0.0 collective-permute-done.4.refs_3_
  27.8 0.0 copy-done
  27.8 0.3 kl_project.3
  28.1 1.6 %collective-permute-start.5 = (bf16[64,640]{1,0:T(8,128)(2,1)S(1)}, bf16[64,640]{1,0:T(8,128)(2,1)S(1)}, u32[]{:S(2)}, u32[]{:S(2)}) collective-permute-start(bf16[64,640]{1,0:T(8,128)(2,1)S(1)} %kl_project.3), channel_id=1, source_target_pairs={{0,2},{2,0},{1,3},{3,1},{4,6},{6,4},{5,7},{7,5},{8,10},{10,8},{9,1... | collective-permute-start | bytes 245768 | tf_op jit(solution)/shard_map/ppermute | solution.py:403
  29.7 0.3 kl_project.2.mine
  30.0 2.6 %collective-permute-done.5.got = bf16[64,640]{1,0:T(8,128)(2,1)S(1)} collective-permute-done((bf16[64,640]{1,0:T(8,128)(2,1)S(1)}, bf16[64,640]{1,0:T(8,128)(2,1)S(1)}, u32[]{:S(2)}, u32[]{:S(2)}) %collective-permute-start.5) | collective-permute-done | bytes 81952 | tf_op jit(solution)/shard_map/ppermute | solution.py:403
  32.6 1.1 %unpack.1 = f32[4,64,256]{2,1,0:T(8,128)} custom-call(s32[8,128]{1,0:T(8,128)S(1)} %get-tuple-element.16.scalars, f32[64,640]{1,0:T(8,128)S(1)} %kl_project.2.mine, bf16[64,640]{1,0:T(8,128)(2,1)S(1)} %collective-permute-done.5.got), custom_call_target="tpu_custom_call" | custom-call | flops 40960 | bytes 409600 | tf_op jit(solution)/shard_map/unpack/pallas_call | solution.py:360
  (2 shorter events, 0.1 us)
Async XLA Ops:
  0.0 27.8 %copy-start = (bf16[4,128,256]{2,1,0:T(8,128)(2,1)S(1)}, bf16[4,128,256]{2,1,0:T(8,128)(2,1)}, u32[]{:S(2)}) copy-start(bf16[4,128,256]{2,1,0:T(8,128)(2,1)} %kl.3) | copy-start | bytes 786436
  13.6 1.5 %collective-permute-start = (f32[1,5,64,128]{3,2,1,0:T(8,128)S(1)}, f32[1,5,64,128]{3,2,1,0:T(8,128)S(1)}, u32[]{:S(2)}, u32[]{:S(2)}) collective-permute-start(f32[1,5,64,128]{3,2,1,0:T(8,128)S(1)} %get-tuple-element.21), channel_id=1, source_target_pairs={{0,1},{1,0},{2,3},{3,2},{4,5},{5,4},{6,7},{7,6},{8,9},{9,8},{10,11... | collective-permute-start | bytes 491528 | tf_op jit(solution)/shard_map/ppermute | solution.py:392
  15.1 5.2 %collective-permute-start.1 = (f32[3,5,64,128]{3,2,1,0:T(8,128)S(1)}, f32[3,5,64,128]{3,2,1,0:T(8,128)S(1)}, u32[]{:S(2)}, u32[]{:S(2)}) collective-permute-start(f32[3,5,64,128]{3,2,1,0:T(8,128)S(1)} %get-tuple-element.22), channel_id=1, source_target_pairs={{0,1},{1,0},{2,3},{3,2},{4,5},{5,4},{6,7},{7,6},{8,9},{9,8},{10,11... | collective-permute-start | bytes 1474568 | tf_op jit(solution)/shard_map/ppermute | solution.py:394
  15.5 7.9 %collective-permute-start.3 = (bf16[5,64,128]{2,1,0:T(8,128)(2,1)S(1)}, bf16[5,64,128]{2,1,0:T(8,128)(2,1)S(1)}, u32[]{:S(2)}, u32[]{:S(2)}) collective-permute-start(bf16[5,64,128]{2,1,0:T(8,128)(2,1)S(1)} %sum_pair.3), channel_id=1, source_target_pairs={{0,12},{4,8},{8,4},{12,0},{1,13},{5,9},{9,5},{13,1},{2,14},{6,10},... | collective-permute-start | bytes 245768 | tf_op jit(solution)/shard_map/ppermute | solution.py:398
  20.4 7.4 %collective-permute-start.2 = (bf16[5,64,128]{2,1,0:T(8,128)(2,1)S(1)}, bf16[5,64,128]{2,1,0:T(8,128)(2,1)S(1)}, u32[]{:S(2)}, u32[]{:S(2)}) collective-permute-start(bf16[5,64,128]{2,1,0:T(8,128)(2,1)S(1)} %get-tuple-element.24), channel_id=1, source_target_pairs={{0,4},{4,12},{8,0},{12,8},{1,5},{5,13},{9,1},{13,9},{2,6},{6,14},{... | collective-permute-start | bytes 245768 | tf_op jit(solution)/shard_map/ppermute | solution.py:398
  20.5 7.3 %collective-permute-start.4 = (bf16[5,64,128]{2,1,0:T(8,128)(2,1)S(1)}, bf16[5,64,128]{2,1,0:T(8,128)(2,1)S(1)}, u32[]{:S(2)}, u32[]{:S(2)}) collective-permute-start(bf16[5,64,128]{2,1,0:T(8,128)(2,1)S(1)} %get-tuple-element.26), channel_id=1, source_target_pairs={{0,8},{4,0},{8,12},{12,4},{1,9},{5,1},{9,13},{13,5},{2,10},{6,2},{... | collective-permute-start | bytes 245768 | tf_op jit(solution)/shard_map/ppermute | solution.py:398
  28.1 4.5 %collective-permute-start.5 = (bf16[64,640]{1,0:T(8,128)(2,1)S(1)}, bf16[64,640]{1,0:T(8,128)(2,1)S(1)}, u32[]{:S(2)}, u32[]{:S(2)}) collective-permute-start(bf16[64,640]{1,0:T(8,128)(2,1)S(1)} %kl_project.3), channel_id=1, source_target_pairs={{0,2},{2,0},{1,3},{3,1},{4,6},{6,4},{5,7},{7,5},{8,10},{10,8},{9,1... | collective-permute-start | bytes 245768 | tf_op jit(solution)/shard_map/ppermute | solution.py:403

commit v10 on v9

--- a/solution.py
+++ b/solution.py
@@ -217,12 +217,38 @@
         pack(out_odd, mine, far, near, (groups - 1) * GROUP, tables, part)
 
 
-def sum_kernel(steps, mine, got, *out):
+def folded_rows(rows, width):
+    whole, rest = divmod(width, LANES)
+    return rows * whole + (rows if rest > LANES // 2 else rows // 2 if rest else 0)
+
+
+def fold(tiles, out, width):
+    rows = tiles[0].shape[0]
+    lane = lax.broadcasted_iota(jnp.int32, (rows // 2, LANES), 1)
+    for t, tile in enumerate(tiles):
+        if t == len(tiles) - 1 and out.shape[0] < rows * len(tiles):
+            low, high = tile[: rows // 2], tile[rows // 2 :]
+            tile = jnp.where(lane < LANES // 2, low, pltpu.roll(high, LANES // 2, 1))
+        out[t * rows : t * rows + tile.shape[0], :] = tile.astype(out.dtype)
+
+
+def unfold(block, rows):
+    count = block.shape[0] // rows
+    tiles = [block[t * rows : (t + 1) * rows, :] for t in range(count)]
+    if count * rows < block.shape[0]:
+        low = block[count * rows :, :].astype(jnp.float32)
+        high = pltpu.roll(low, LANES // 2, 1)
+        tiles.append(jnp.concatenate([low, high], axis=0).astype(block.dtype))
+    return tiles
+
+
+def sum_kernel(steps, width, mine, got, *out):
     for i, step in enumerate(steps):
-        out[i][...] = (mine[step] + got[i]).astype(out[i].dtype)
-
-
-def kl_kernel(part, owners, slot_column, rows_column, kl, *refs):
+        tiles = [mine[step, t] + got[i, t] for t in range(mine.shape[1])]
+        fold(tiles, out[i], width)
+
+
+def kl_kernel(part, owners, width, slot_column, rows_column, kl, *refs):
     blocks, (out, packed_v) = refs[:owners], refs[owners:]
     owner_slots, rows, freqs = kl.shape
     shares = lax.axis_size("af")
@@ -231,42 +257,49 @@
     for step in range(owners):
         source = on_ring(cyclic(on_ring(me) - step, owners))
         at = pl.multiple_of(source * per_source, GROUP)
-        for t in range(blocks[step].shape[0]):
-            packed_v[pl.ds(at, per_source), t * LANES : (t + 1) * LANES] = blocks[step][t]
-    share_rows, width = out.shape
+        for t, tile in enumerate(unfold(blocks[step], per_source)):
+            packed_v[pl.ds(at, per_source), t * LANES : (t + 1) * LANES] = tile
+    share_rows = rows // shares
     at = pl.multiple_of(cyclic(lax.axis_index("af") + part, shares) * share_rows, GROUP)
     lhs = kl[:, pl.ds(at, share_rows), :].reshape(owner_slots * share_rows, freqs)
     product = jnp.dot(lhs, packed_v[...], preferred_element_type=jnp.float32)
-    line = lax.broadcasted_iota(jnp.int32, (share_rows, width), 0) + at
-    slot_at = slot_column[0:1, :]
-    total = jnp.zeros((share_rows, width), jnp.float32)
-    for j in range(owner_slots):
-        here = product[j * share_rows : (j + 1) * share_rows]
-        total = jnp.where(slot_at == j, here, total)
-    out[...] = jnp.where(line < rows_column[0:1, :], total, 0.0).astype(out.dtype)
-
-
-def unpack_kernel(scalars, mine, got, out, sum_v):
-    owner_slots, rows, modes = out.shape
-    width = mine.shape[1]
-    sum_v[:, :width] = mine[...] + got[...].astype(jnp.float32)
+    line = lax.broadcasted_iota(jnp.int32, (share_rows, LANES), 0) + at
+    tiles = []
+    for t in range(packed_v.shape[1] // LANES):
+        lanes = slice(t * LANES, (t + 1) * LANES)
+        slot_at = slot_column[0:1, lanes]
+        total = jnp.zeros((share_rows, LANES), jnp.float32)
+        for j in range(owner_slots):
+            here = product[j * share_rows : (j + 1) * share_rows, lanes]
+            total = jnp.where(slot_at == j, here, total)
+        tiles.append(jnp.where(line < rows_column[0:1, lanes], total, 0.0))
+    fold(tiles, out, width)
+
+
+def unpack_kernel(scalars, mine, got, out, sum_v, out_v, sems):
+    owner_slots, rows, modes = out_v.shape
+    places = [
+        [jnp.max(scalars[k * owner_slots + j : k * owner_slots + j + 1, :]) for k in range(2)]
+        for j in range(owner_slots)
+    ]
+    for t, (a, b) in enumerate(zip(unfold(mine, rows), unfold(got, rows))):
+        sum_v[t] = a + b.astype(jnp.float32)
     lane = lax.broadcasted_iota(jnp.int32, (rows, LANES), 1)
-    for j in range(owner_slots):
-        offset = jnp.max(scalars[j : j + 1, :])
-        keep = jnp.max(scalars[owner_slots + j : owner_slots + j + 1, :])
+    copies = []
+    for j, (offset, keep) in enumerate(places):
         tile = lax.div(offset, LANES)
         shift = offset - tile * LANES
         back = lax.rem(LANES - shift, LANES)
-        turned = [
-            pltpu.roll(
-                sum_v[:, pl.ds(pl.multiple_of((tile + t) * LANES, LANES), LANES)], back, 1
-            )
-            for t in range(modes // LANES + 1)
-        ]
+        turned = [pltpu.roll(sum_v[tile + t], back, 1) for t in range(modes // LANES + 1)]
         for t in range(modes // LANES):
             value = jnp.where(lane < LANES - shift, turned[t], turned[t + 1])
             value = jnp.where(lane < keep - t * LANES, value, 0.0)
-            out[j, :, t * LANES : (t + 1) * LANES] = value
+            out_v[j, :, t * LANES : (t + 1) * LANES] = value
+        copy = pltpu.make_async_copy(out_v.at[j], out.at[j], sems.at[j])
+        copy.start()
+        copies.append(copy)
+    for copy in copies:
+        copy.wait()
 
 
 HBM = pl.BlockSpec(memory_space=pltpu.HBM)
@@ -320,10 +353,10 @@
     )(*map(in_hbm, (slot_of_m, svd_keep, kl_keep, panels, svd_basis)))
 
 
-def sum_pair(steps, mine, got):
-    kind = jax.ShapeDtypeStruct(mine.shape[1:], jnp.bfloat16)
+def sum_pair(steps, width, mine, got):
+    kind = jax.ShapeDtypeStruct((folded_rows(mine.shape[2], width), LANES), jnp.bfloat16)
     return pl.pallas_call(
-        functools.partial(sum_kernel, steps),
+        functools.partial(sum_kernel, steps, width),
         out_shape=(kind,) * len(steps),
         in_specs=[VMEM] * 2,
         out_specs=(VMEM,) * len(steps),
@@ -335,19 +368,19 @@
     )(mine, got)
 
 
-def kl_project(part, kind, slot_column, rows_column, kl_basis, blocks):
+def kl_project(part, kind, width, slot_column, rows_column, kl_basis, blocks):
     owners, shares = lax.axis_size("ma"), lax.axis_size("af")
     rows, freqs = kl_basis.shape[1:]
-    width = slot_column.shape[1]
+    wide = slot_column.shape[1]
     return pl.pallas_call(
-        functools.partial(kl_kernel, part, owners),
-        out_shape=jax.ShapeDtypeStruct((rows // shares, width), kind),
+        functools.partial(kl_kernel, part, owners, width),
+        out_shape=jax.ShapeDtypeStruct((folded_rows(rows // shares, width), LANES), kind),
         in_specs=[VMEM] * (3 + owners),
         out_specs=VMEM,
-        scratch_shapes=[pltpu.VMEM((freqs, width), jnp.bfloat16)],
+        scratch_shapes=[pltpu.VMEM((freqs, wide), jnp.bfloat16)],
         compiler_params=SMALL,
         cost_estimate=pl.CostEstimate(
-            flops=2 * kl_basis.size * width // shares,
+            flops=2 * kl_basis.size * wide // shares,
             bytes_accessed=2 * kl_basis.size,
             transcendentals=0,
         ),
@@ -355,17 +388,21 @@
     )(slot_column, rows_column, kl_basis, *blocks)
 
 
-def unpack(scalars, mine, got, owner_slots, modes):
-    rows, width = mine.shape
+def unpack(scalars, mine, got, owner_slots, rows, modes, width):
+    tiles = -(-width // LANES) + modes // LANES + 1
     return pl.pallas_call(
         unpack_kernel,
         out_shape=jax.ShapeDtypeStruct((owner_slots, rows, modes), jnp.float32),
         in_specs=[VMEM] * 3,
-        out_specs=VMEM,
-        scratch_shapes=[pltpu.VMEM((rows, width + modes + LANES), jnp.float32)],
+        out_specs=HBM,
+        scratch_shapes=[
+            pltpu.VMEM((tiles, rows, LANES), jnp.float32),
+            pltpu.VMEM((owner_slots, rows, modes), jnp.float32),
+            pltpu.SemaphoreType.DMA((owner_slots,)),
+        ],
         compiler_params=SMALL,
         cost_estimate=pl.CostEstimate(
-            flops=rows * width, bytes_accessed=10 * rows * width, transcendentals=0
+            flops=mine.size, bytes_accessed=10 * mine.size, transcendentals=0
         ),
         name="unpack",
     )(scalars, mine, got)
@@ -383,26 +420,28 @@
 def shards(panels, svd_basis, kl_basis, slot_of_m, svd_keep, kl_keep):
     owner_slots, modes = kl_basis.shape[0], svd_basis.shape[2]
     owners = lax.axis_size("ma")
-    width = -(-min(OWNER_BUDGET, owner_slots * modes) // LANES) * LANES
+    width = min(OWNER_BUDGET, owner_slots * modes)
+    wide = -(-width // LANES) * LANES
     mine, far, near, slot_column, rows_column, scalars = project(
-        panels, svd_basis, slot_of_m, svd_keep, kl_keep, owner_slots, width
+        panels, svd_basis, slot_of_m, svd_keep, kl_keep, owner_slots, wide
     )
     first = far_step(owners)
     others = [step for step in range(owners) if step != first]
     got_far = lax.ppermute(far, "pa", pairs("pa"))
     near, got_far = lax.optimization_barrier((near, got_far))
     got_near = lax.ppermute(near, "pa", pairs("pa"))
-    summed = dict(zip([first], sum_pair([first], mine, got_far)))
-    summed |= zip(others, sum_pair(others, mine, got_near))
+    summed = dict(zip([first], sum_pair([first], width, mine, got_far)))
+    summed |= zip(others, sum_pair(others, width, mine, got_near))
     blocks = {
         step: lax.ppermute(summed[step], "ma", ring(step)) if step else summed[step]
         for step in [first] + others
     }
-    tables = (slot_column, rows_column, kl_basis, [blocks[step] for step in range(owners)])
+    tables = (width, slot_column, rows_column, kl_basis, [blocks[step] for step in range(owners)])
     send = kl_project(1, jnp.bfloat16, *tables)
     got = lax.ppermute(send, "af", pairs("af"))
     mine = kl_project(0, jnp.float32, *tables)
-    return unpack(scalars, mine, got, owner_slots, modes)
+    rows = kl_basis.shape[1] // lax.axis_size("af")
+    return unpack(scalars, mine, got, owner_slots, rows, modes, width)
 
 
 def kernels_fit(mesh, args):
@@ -416,7 +455,7 @@
         and slots % (GROUP * mesh.shape["pa"]) == 0
         and owner_slots == 4
         and svd_basis.shape[2] == 2 * LANES
-        and share_rows % GROUP == 0
+        and share_rows % (2 * GROUP) == 0
         and mesh.shape["pa"] == 2
         and mesh.shape["af"] == 2
         and mesh.shape["ma"] == 4

time: 33.8 us -> 32.5 us (0.962)
  waiting for transfers between devices: 8.03 us -> 6.58 us
    ppermute x3, waiting for transfers between devices: 4.39 us -> 3.13 us  [shards(): lax.ppermute(summed[step], 'ma', ring(step))]
  transfers between devices with their start and end apart: 6 -> 6, of which waited for: 4 -> 3; matrix products, arithmetic and copies ran while one was open for 0% -> 0% of each run, Pallas kernels for 1% -> 2%
where the time goes in v10:
time: 32.5 us; the launch traced here: 32.4 us
  Pallas kernels  15.7 us (48%)
  starting transfers between devices  10.1 us (31%)
  waiting for transfers between devices  6.58 us (20%)
    pallas_call x1, Pallas kernels, project(): pl.pallas_call(functools.partial(project_kernel, owner_slots), out_shape=...  13.6 us
    ppermute x3, starting transfers between devices, shards(): lax.ppermute(summed[step], 'ma', ring(step))  7.72 us
    ppermute x3, waiting for transfers between devices, shards(): lax.ppermute(summed[step], 'ma', ring(step))  3.13 us
    ppermute x1, waiting for transfers between devices, shards(): got = lax.ppermute(send, 'af', pairs('af'))  2.42 us
    ppermute x1, starting transfers between devices, shards(): got = lax.ppermute(send, 'af', pairs('af'))  1.5 us
    pallas_call x1, Pallas kernels, unpack(): pl.pallas_call(unpack_kernel, out_shape=jax.ShapeDtypeStruct((owner_slots...  1.04 us
    ppermute x1, waiting for transfers between devices, shards(): got_far = lax.ppermute(far, 'pa', pairs('pa'))  1.03 us
    pallas_call x2, Pallas kernels, kl_project(): pl.pallas_call(functools.partial(kl_kernel, part, owners, width), out_sha...  0.89 us
  transfers between devices with their start and end apart: 6, of which 3 were waited for; matrix products, arithmetic and copies ran while one was open for 0% of the time, Pallas kernels for 2%

profile of v10, /device:TPU:0, one launch (start us, length us, event | category | flops | bytes accessed | tf_op | source)
XLA Modules:
  0.0 32.4 jit_solution(10407031632342634263)
XLA Ops:
  0.0 0.0 copy-start
  0.0 13.6 %project.1 = (f32[4,5,64,128]{3,2,1,0:T(8,128)S(1)}, f32[1,5,64,128]{3,2,1,0:T(8,128)S(1)}, f32[3,5,64,128]{3,2,1,0:T(8,128)S(1)}, s32[8,640]{1,0:T(8,128)S(1)},...) custom-call(s32[32]{0:T(128)} %slot_hbm.1, s32[32]{0:T(128)} %keep_hbm.1, s32[32]{0:T(128)} %rows_hbm.1, ...), custom_call_target="tpu_custom_call" | custom-call | flops 1073741824 | bytes 37748736 | tf_op jit(solution)/shard_map/project/pallas_call | solution.py:323
  13.6 0.5 %collective-permute-start = (f32[1,5,64,128]{3,2,1,0:T(8,128)S(1)}, f32[1,5,64,128]{3,2,1,0:T(8,128)S(1)}, u32[]{:S(2)}, u32[]{:S(2)}) collective-permute-start(f32[1,5,64,128]{3,2,1,0:T(8,128)S(1)} %get-tuple-element.21), channel_id=1, source_target_pairs={{0,1},{1,0},{2,3},{3,2},{4,5},{5,4},{6,7},{7,6},{8,9},{9,8},{10,11... | collective-permute-start | bytes 491528 | tf_op jit(solution)/shard_map/ppermute | solution.py:430
  14.1 1.0 %collective-permute-done.got = f32[1,5,64,128]{3,2,1,0:T(8,128)S(1)} collective-permute-done((f32[1,5,64,128]{3,2,1,0:T(8,128)S(1)}, f32[1,5,64,128]{3,2,1,0:T(8,128)S(1)}, u32[]{:S(2)}, u32[]{:S(2)}) %collective-permute-start) | collective-permute-done | bytes 163872 | tf_op jit(solution)/shard_map/ppermute | solution.py:430
  15.1 0.4 %collective-permute-start.1 = (f32[3,5,64,128]{3,2,1,0:T(8,128)S(1)}, f32[3,5,64,128]{3,2,1,0:T(8,128)S(1)}, u32[]{:S(2)}, u32[]{:S(2)}) collective-permute-start(f32[3,5,64,128]{3,2,1,0:T(8,128)S(1)} %get-tuple-element.22), channel_id=1, source_target_pairs={{0,1},{1,0},{2,3},{3,2},{4,5},{5,4},{6,7},{7,6},{8,9},{9,8},{10,11... | collective-permute-start | bytes 1474568 | tf_op jit(solution)/shard_map/ppermute | solution.py:432
  15.5 0.1 sum_pair.3
  15.6 4.8 %collective-permute-start.3 = (bf16[288,128]{1,0:T(8,128)(2,1)S(1)}, bf16[288,128]{1,0:T(8,128)(2,1)S(1)}, u32[]{:S(2)}, u32[]{:S(2)}) collective-permute-start(bf16[288,128]{1,0:T(8,128)(2,1)S(1)} %sum_pair.3), channel_id=1, source_target_pairs={{0,12},{4,8},{8,4},{12,0},{1,13},{5,9},{9,5},{13,1},{2,14},{6,10},... | collective-permute-start | bytes 221192 | tf_op jit(solution)/shard_map/ppermute | solution.py:436
  20.3 0.0 collective-permute-done.1.got
  20.3 0.1 sum_pair.2
  20.4 0.0 collective-permute-start.2
  20.5 2.9 %collective-permute-start.4 = (bf16[288,128]{1,0:T(8,128)(2,1)S(1)}, bf16[288,128]{1,0:T(8,128)(2,1)S(1)}, u32[]{:S(2)}, u32[]{:S(2)}) collective-permute-start(bf16[288,128]{1,0:T(8,128)(2,1)S(1)} %get-tuple-element.26), channel_id=1, source_target_pairs={{0,8},{4,0},{8,12},{12,4},{1,9},{5,1},{9,13},{13,5},{2,10},{6,2},{... | collective-permute-start | bytes 221192 | tf_op jit(solution)/shard_map/ppermute | solution.py:436
  23.4 0.0 collective-permute-done.3.refs_2_
  23.4 3.1 %collective-permute-done.2.refs_1_ = bf16[288,128]{1,0:T(8,128)(2,1)S(1)} collective-permute-done((bf16[288,128]{1,0:T(8,128)(2,1)S(1)}, bf16[288,128]{1,0:T(8,128)(2,1)S(1)}, u32[]{:S(2)}, u32[]{:S(2)}) %collective-permute-start.2) | collective-permute-done | bytes 73760 | tf_op jit(solution)/shard_map/ppermute | solution.py:436
  26.5 0.0 collective-permute-done.4.refs_3_
  26.5 0.0 copy-done
  26.5 0.4 %kl_project.3 = bf16[288,128]{1,0:T(8,128)(2,1)S(1)} custom-call(s32[8,640]{1,0:T(8,128)S(1)} %get-tuple-element.17.slot_column, s32[8,640]{1,0:T(8,128)S(1)} %get-tuple-element.18.rows_column, bf16[4,128,256]{2,1,0:T(8,128)(2,1)S(1)} %copy-done, bf16[288,128]{1,0:T(8,128)(2,1)S(1)} %get-tuple-element.23.refs_0_, ...), custom_call_target="tpu_custom_call" | custom-call | flops 83886080 | bytes 262144 | tf_op jit(solution)/shard_map/kl_project/pallas_call | solution.py:375
  27.0 1.5 %collective-permute-start.5 = (bf16[288,128]{1,0:T(8,128)(2,1)S(1)}, bf16[288,128]{1,0:T(8,128)(2,1)S(1)}, u32[]{:S(2)}, u32[]{:S(2)}) collective-permute-start(bf16[288,128]{1,0:T(8,128)(2,1)S(1)} %kl_project.3), channel_id=1, source_target_pairs={{0,2},{2,0},{1,3},{3,1},{4,6},{6,4},{5,7},{7,5},{8,10},{10,8},{9,1... | collective-permute-start | bytes 221192 | tf_op jit(solution)/shard_map/ppermute | solution.py:441
  28.5 0.4 %kl_project.2.mine = f32[288,128]{1,0:T(8,128)S(1)} custom-call(s32[8,640]{1,0:T(8,128)S(1)} %get-tuple-element.17.slot_column, s32[8,640]{1,0:T(8,128)S(1)} %get-tuple-element.18.rows_column, bf16[4,128,256]{2,1,0:T(8,128)(2,1)S(1)} %copy-done, bf16[288,128]{1,0:T(8,128)(2,1)S(1)} %get-tuple-element.23.refs_0_, ...), custom_call_target="tpu_custom_call" | custom-call | flops 83886080 | bytes 262144 | tf_op jit(solution)/shard_map/kl_project/pallas_call | solution.py:375
  28.9 2.4 %collective-permute-done.5.got = bf16[288,128]{1,0:T(8,128)(2,1)S(1)} collective-permute-done((bf16[288,128]{1,0:T(8,128)(2,1)S(1)}, bf16[288,128]{1,0:T(8,128)(2,1)S(1)}, u32[]{:S(2)}, u32[]{:S(2)}) %collective-permute-start.5) | collective-permute-done | bytes 73760 | tf_op jit(solution)/shard_map/ppermute | solution.py:441
  31.3 1.0 %unpack.1 = f32[4,64,256]{2,1,0:T(8,128)} custom-call(s32[8,128]{1,0:T(8,128)S(1)} %get-tuple-element.16.scalars, f32[288,128]{1,0:T(8,128)S(1)} %kl_project.2.mine, bf16[288,128]{1,0:T(8,128)(2,1)S(1)} %collective-permute-done.5.got), custom_call_target="tpu_custom_call" | custom-call | flops 36864 | bytes 368640 | tf_op jit(solution)/shard_map/unpack/pallas_call | solution.py:393
Async XLA Ops:
  0.0 26.5 %copy-start = (bf16[4,128,256]{2,1,0:T(8,128)(2,1)S(1)}, bf16[4,128,256]{2,1,0:T(8,128)(2,1)}, u32[]{:S(2)}) copy-start(bf16[4,128,256]{2,1,0:T(8,128)(2,1)} %kl.3) | copy-start | bytes 786436
  13.6 1.5 %collective-permute-start = (f32[1,5,64,128]{3,2,1,0:T(8,128)S(1)}, f32[1,5,64,128]{3,2,1,0:T(8,128)S(1)}, u32[]{:S(2)}, u32[]{:S(2)}) collective-permute-start(f32[1,5,64,128]{3,2,1,0:T(8,128)S(1)} %get-tuple-element.21), channel_id=1, source_target_pairs={{0,1},{1,0},{2,3},{3,2},{4,5},{5,4},{6,7},{7,6},{8,9},{9,8},{10,11... | collective-permute-start | bytes 491528 | tf_op jit(solution)/shard_map/ppermute | solution.py:430
  15.1 5.2 %collective-permute-start.1 = (f32[3,5,64,128]{3,2,1,0:T(8,128)S(1)}, f32[3,5,64,128]{3,2,1,0:T(8,128)S(1)}, u32[]{:S(2)}, u32[]{:S(2)}) collective-permute-start(f32[3,5,64,128]{3,2,1,0:T(8,128)S(1)} %get-tuple-element.22), channel_id=1, source_target_pairs={{0,1},{1,0},{2,3},{3,2},{4,5},{5,4},{6,7},{7,6},{8,9},{9,8},{10,11... | collective-permute-start | bytes 1474568 | tf_op jit(solution)/shard_map/ppermute | solution.py:432
  15.6 7.8 %collective-permute-start.3 = (bf16[288,128]{1,0:T(8,128)(2,1)S(1)}, bf16[288,128]{1,0:T(8,128)(2,1)S(1)}, u32[]{:S(2)}, u32[]{:S(2)}) collective-permute-start(bf16[288,128]{1,0:T(8,128)(2,1)S(1)} %sum_pair.3), channel_id=1, source_target_pairs={{0,12},{4,8},{8,4},{12,0},{1,13},{5,9},{9,5},{13,1},{2,14},{6,10},... | collective-permute-start | bytes 221192 | tf_op jit(solution)/shard_map/ppermute | solution.py:436
  20.4 6.1 %collective-permute-start.2 = (bf16[288,128]{1,0:T(8,128)(2,1)S(1)}, bf16[288,128]{1,0:T(8,128)(2,1)S(1)}, u32[]{:S(2)}, u32[]{:S(2)}) collective-permute-start(bf16[288,128]{1,0:T(8,128)(2,1)S(1)} %get-tuple-element.24), channel_id=1, source_target_pairs={{0,4},{4,12},{8,0},{12,8},{1,5},{5,13},{9,1},{13,9},{2,6},{6,14},{... | collective-permute-start | bytes 221192 | tf_op jit(solution)/shard_map/ppermute | solution.py:436
  20.5 6.0 %collective-permute-start.4 = (bf16[288,128]{1,0:T(8,128)(2,1)S(1)}, bf16[288,128]{1,0:T(8,128)(2,1)S(1)}, u32[]{:S(2)}, u32[]{:S(2)}) collective-permute-start(bf16[288,128]{1,0:T(8,128)(2,1)S(1)} %get-tuple-element.26), channel_id=1, source_target_pairs={{0,8},{4,0},{8,12},{12,4},{1,9},{5,1},{9,13},{13,5},{2,10},{6,2},{... | collective-permute-start | bytes 221192 | tf_op jit(solution)/shard_map/ppermute | solution.py:436
  27.0 4.4 %collective-permute-start.5 = (bf16[288,128]{1,0:T(8,128)(2,1)S(1)}, bf16[288,128]{1,0:T(8,128)(2,1)S(1)}, u32[]{:S(2)}, u32[]{:S(2)}) collective-permute-start(bf16[288,128]{1,0:T(8,128)(2,1)S(1)} %kl_project.3), channel_id=1, source_target_pairs={{0,2},{2,0},{1,3},{3,1},{4,6},{6,4},{5,7},{7,5},{8,10},{10,8},{9,1... | collective-permute-start | bytes 221192 | tf_op jit(solution)/shard_map/ppermute | solution.py:441

commit v11 on v10

--- a/solution.py
+++ b/solution.py
@@ -48,19 +48,13 @@
     return lax.rem(value + count, count)
 
 
-def on_ring(z):
-    return z ^ (z // 2) if isinstance(z, int) else z ^ lax.shift_right_logical(z, 1)
-
-
-def far_step(owners):
-    return owners // 2
+FIRST = 1
 
 
 def place_of(slot, owner_slots, half_slots):
     half = cyclic(lax.div(slot, half_slots) - lax.axis_index("pa"), lax.axis_size("pa"))
     within = lax.rem(slot, half_slots)
-    owner = on_ring(lax.div(within, owner_slots)) - on_ring(lax.axis_index("ma"))
-    owner = cyclic(owner, lax.axis_size("ma"))
+    owner = cyclic(lax.div(within, owner_slots) - lax.axis_index("ma"), lax.axis_size("ma"))
     return half * half_slots + owner * owner_slots + lax.rem(within, owner_slots)
 
 
@@ -76,7 +70,7 @@
             offset = offset + keep_place[place]
 
 
-def pack(out_v, mine, far, near, line, tables, owners_at):
+def pack(out_v, mine, early, late, line, tables, owners_at):
     tile_place, shift_place, owner_slots = tables
     owners, width_tiles = mine.shape[:2]
     slots = 2 * owners * owner_slots
@@ -92,8 +86,7 @@
     for at in owners_at:
         to, owner = mine, at % owners
         if at >= owners:
-            first = far_step(owners)
-            to, owner = (far, 0) if owner == first else (near, owner - (owner > first))
+            to, owner = (early, 0) if owner == FIRST else (late, owner - (owner > FIRST))
         values, tile_before = None, None
         for j in range(owner_slots):
             place = at * owner_slots + j
@@ -118,7 +111,7 @@
 
 def project_kernel(
     owner_slots, slot_hbm, keep_hbm, rows_hbm, panels, basis,
-    mine, far, near, slot_column, rows_column, scalars,
+    mine, early, late, slot_column, rows_column, scalars,
     slot_s, keep_s, rows_s, keep_place, rows_place, tile_place, shift_place,
     panels_v, basis_v, lhs_v, out_even, out_odd, small_sem, panel_sem, basis_sem,
 ):
@@ -205,7 +198,7 @@
                     at = (t * GROUP + f) * slots
                     out_v[at : at + slots, :] = product[:, t * LANES : (t + 1) * LANES]
             line = jnp.maximum(group - 1, 0) * GROUP
-            pack(out_before, mine, far, near, line, tables, all_owners[i * share : (i + 1) * share])
+            pack(out_before, mine, early, late, line, tables, all_owners[i * share : (i + 1) * share])
 
     @pl.loop(0, groups // 2)
     def _(pair):
@@ -214,7 +207,7 @@
 
     for i in range(per_group):
         part = all_owners[i * share : (i + 1) * share]
-        pack(out_odd, mine, far, near, (groups - 1) * GROUP, tables, part)
+        pack(out_odd, mine, early, late, (groups - 1) * GROUP, tables, part)
 
 
 def folded_rows(rows, width):
@@ -255,7 +248,7 @@
     per_source = freqs // owners
     me = lax.axis_index("ma")
     for step in range(owners):
-        source = on_ring(cyclic(on_ring(me) - step, owners))
+        source = cyclic(me - step, owners)
         at = pl.multiple_of(source * per_source, GROUP)
         for t, tile in enumerate(unfold(blocks[step], per_source)):
             packed_v[pl.ds(at, per_source), t * LANES : (t + 1) * LANES] = tile
@@ -414,7 +407,7 @@
 
 def ring(step):
     size = lax.axis_size("ma")
-    return [(i, on_ring((on_ring(i) + step) % size)) for i in range(size)]
+    return [(i, (i + step) % size) for i in range(size)]
 
 
 def shards(panels, svd_basis, kl_basis, slot_of_m, svd_keep, kl_keep):
@@ -422,19 +415,18 @@
     owners = lax.axis_size("ma")
     width = min(OWNER_BUDGET, owner_slots * modes)
     wide = -(-width // LANES) * LANES
-    mine, far, near, slot_column, rows_column, scalars = project(
+    mine, early, late, slot_column, rows_column, scalars = project(
         panels, svd_basis, slot_of_m, svd_keep, kl_keep, owner_slots, wide
     )
-    first = far_step(owners)
-    others = [step for step in range(owners) if step != first]
-    got_far = lax.ppermute(far, "pa", pairs("pa"))
-    near, got_far = lax.optimization_barrier((near, got_far))
-    got_near = lax.ppermute(near, "pa", pairs("pa"))
-    summed = dict(zip([first], sum_pair([first], width, mine, got_far)))
-    summed |= zip(others, sum_pair(others, width, mine, got_near))
+    others = [step for step in range(owners) if step != FIRST]
+    got_early = lax.ppermute(early, "pa", pairs("pa"))
+    late, got_early = lax.optimization_barrier((late, got_early))
+    got_late = lax.ppermute(late, "pa", pairs("pa"))
+    summed = dict(zip([FIRST], sum_pair([FIRST], width, mine, got_early)))
+    summed |= zip(others, sum_pair(others, width, mine, got_late))
     blocks = {
         step: lax.ppermute(summed[step], "ma", ring(step)) if step else summed[step]
-        for step in [first] + others
+        for step in [FIRST] + others
     }
     tables = (width, slot_column, rows_column, kl_basis, [blocks[step] for step in range(owners)])
     send = kl_project(1, jnp.bfloat16, *tables)

time: 32.5 us -> 32.5 us (level)
  waiting for transfers between devices: 6.58 us -> 7.7 us
  starting transfers between devices: 10.1 us -> 9.15 us
    ppermute x3, waiting for transfers between devices: 3.13 us -> 4.2 us  [shards(): lax.ppermute(summed[step], 'ma', ring(step))]
    ppermute x3, starting transfers between devices: 7.72 us -> 6.77 us  [shards(): lax.ppermute(summed[step], 'ma', ring(step))]
  transfers between devices with their start and end apart: 6 -> 6, of which waited for: 3 -> 5; matrix products, arithmetic and copies ran while one was open for 0% -> 0% of each run, Pallas kernels for 2% -> 2%
where the time goes in v11:
time: 32.5 us; the launch traced here: 32.4 us
  Pallas kernels  15.5 us (48%)
  starting transfers between devices  9.15 us (28%)
  waiting for transfers between devices  7.7 us (24%)
    pallas_call x1, Pallas kernels, project(): pl.pallas_call(functools.partial(project_kernel, owner_slots), out_shape=...  13.5 us
    ppermute x3, starting transfers between devices, shards(): lax.ppermute(summed[step], 'ma', ring(step))  6.77 us
    ppermute x3, waiting for transfers between devices, shards(): lax.ppermute(summed[step], 'ma', ring(step))  4.2 us
    ppermute x1, waiting for transfers between devices, shards(): got = lax.ppermute(send, 'af', pairs('af'))  2.47 us
    ppermute x1, starting transfers between devices, shards(): got = lax.ppermute(send, 'af', pairs('af'))  1.5 us
    pallas_call x1, Pallas kernels, unpack(): pl.pallas_call(unpack_kernel, out_shape=jax.ShapeDtypeStruct((owner_slots...  1.04 us
    ppermute x1, waiting for transfers between devices, shards(): got_early = lax.ppermute(early, 'pa', pairs('pa'))  1.03 us
    pallas_call x2, Pallas kernels, kl_project(): pl.pallas_call(functools.partial(kl_kernel, part, owners, width), out_sha...  0.78 us
  transfers between devices with their start and end apart: 6, of which 5 were waited for; matrix products, arithmetic and copies ran while one was open for 0% of the time, Pallas kernels for 2%

profile of v11, /device:TPU:0, one launch (start us, length us, event | category | flops | bytes accessed | tf_op | source)
XLA Modules:
  0.0 32.4 jit_solution(10805256987152924734)
XLA Ops:
  0.0 0.0 copy-start
  0.0 13.5 %project.1 = (f32[4,5,64,128]{3,2,1,0:T(8,128)S(1)}, f32[1,5,64,128]{3,2,1,0:T(8,128)S(1)}, f32[3,5,64,128]{3,2,1,0:T(8,128)S(1)}, s32[8,640]{1,0:T(8,128)S(1)},...) custom-call(s32[32]{0:T(128)} %slot_hbm.1, s32[32]{0:T(128)} %keep_hbm.1, s32[32]{0:T(128)} %rows_hbm.1, ...), custom_call_target="tpu_custom_call" | custom-call | flops 1073741824 | bytes 37748736 | tf_op jit(solution)/shard_map/project/pallas_call | solution.py:316
  13.5 0.5 %collective-permute-start = (f32[1,5,64,128]{3,2,1,0:T(8,128)S(1)}, f32[1,5,64,128]{3,2,1,0:T(8,128)S(1)}, u32[]{:S(2)}, u32[]{:S(2)}) collective-permute-start(f32[1,5,64,128]{3,2,1,0:T(8,128)S(1)} %get-tuple-element.21), channel_id=1, source_target_pairs={{0,1},{1,0},{2,3},{3,2},{4,5},{5,4},{6,7},{7,6},{8,9},{9,8},{10,11... | collective-permute-start | bytes 491528 | tf_op jit(solution)/shard_map/ppermute | solution.py:422
  14.0 1.0 %collective-permute-done.got = f32[1,5,64,128]{3,2,1,0:T(8,128)S(1)} collective-permute-done((f32[1,5,64,128]{3,2,1,0:T(8,128)S(1)}, f32[1,5,64,128]{3,2,1,0:T(8,128)S(1)}, u32[]{:S(2)}, u32[]{:S(2)}) %collective-permute-start) | collective-permute-done | bytes 163872 | tf_op jit(solution)/shard_map/ppermute | solution.py:422
  15.1 0.4 %collective-permute-start.1 = (f32[3,5,64,128]{3,2,1,0:T(8,128)S(1)}, f32[3,5,64,128]{3,2,1,0:T(8,128)S(1)}, u32[]{:S(2)}, u32[]{:S(2)}) collective-permute-start(f32[3,5,64,128]{3,2,1,0:T(8,128)S(1)} %get-tuple-element.22), channel_id=1, source_target_pairs={{0,1},{1,0},{2,3},{3,2},{4,5},{5,4},{6,7},{7,6},{8,9},{9,8},{10,11... | collective-permute-start | bytes 1474568 | tf_op jit(solution)/shard_map/ppermute | solution.py:424
  15.4 0.1 sum_pair.3
  15.5 2.7 %collective-permute-start.2 = (bf16[288,128]{1,0:T(8,128)(2,1)S(1)}, bf16[288,128]{1,0:T(8,128)(2,1)S(1)}, u32[]{:S(2)}, u32[]{:S(2)}) collective-permute-start(bf16[288,128]{1,0:T(8,128)(2,1)S(1)} %sum_pair.3), channel_id=1, source_target_pairs={{0,4},{4,8},{8,12},{12,0},{1,5},{5,9},{9,13},{13,1},{2,6},{6,10},{... | collective-permute-start | bytes 221192 | tf_op jit(solution)/shard_map/ppermute | solution.py:428
  18.2 0.0 collective-permute-done.1.got
  18.3 0.1 sum_pair.2
  18.3 2.7 %collective-permute-start.3 = (bf16[288,128]{1,0:T(8,128)(2,1)S(1)}, bf16[288,128]{1,0:T(8,128)(2,1)S(1)}, u32[]{:S(2)}, u32[]{:S(2)}) collective-permute-start(bf16[288,128]{1,0:T(8,128)(2,1)S(1)} %get-tuple-element.25), channel_id=1, source_target_pairs={{0,8},{4,12},{8,0},{12,4},{1,9},{5,13},{9,1},{13,5},{2,10},{6,14},... | collective-permute-start | bytes 221192 | tf_op jit(solution)/shard_map/ppermute | solution.py:428
  21.0 1.3 %collective-permute-start.4 = (bf16[288,128]{1,0:T(8,128)(2,1)S(1)}, bf16[288,128]{1,0:T(8,128)(2,1)S(1)}, u32[]{:S(2)}, u32[]{:S(2)}) collective-permute-start(bf16[288,128]{1,0:T(8,128)(2,1)S(1)} %get-tuple-element.26), channel_id=1, source_target_pairs={{0,12},{4,0},{8,4},{12,8},{1,13},{5,1},{9,5},{13,9},{2,14},{6,2},{... | collective-permute-start | bytes 221192 | tf_op jit(solution)/shard_map/ppermute | solution.py:428
  22.4 0.8 %collective-permute-done.2.refs_1_ = bf16[288,128]{1,0:T(8,128)(2,1)S(1)} collective-permute-done((bf16[288,128]{1,0:T(8,128)(2,1)S(1)}, bf16[288,128]{1,0:T(8,128)(2,1)S(1)}, u32[]{:S(2)}, u32[]{:S(2)}) %collective-permute-start.2) | collective-permute-done | bytes 73760 | tf_op jit(solution)/shard_map/ppermute | solution.py:428
  23.2 3.2 %collective-permute-done.3.refs_2_ = bf16[288,128]{1,0:T(8,128)(2,1)S(1)} collective-permute-done((bf16[288,128]{1,0:T(8,128)(2,1)S(1)}, bf16[288,128]{1,0:T(8,128)(2,1)S(1)}, u32[]{:S(2)}, u32[]{:S(2)}) %collective-permute-start.3) | collective-permute-done | bytes 73760 | tf_op jit(solution)/shard_map/ppermute | solution.py:428
  26.3 0.2 collective-permute-done.4.refs_3_
  26.6 0.0 copy-done
  26.6 0.4 %kl_project.3 = bf16[288,128]{1,0:T(8,128)(2,1)S(1)} custom-call(s32[8,640]{1,0:T(8,128)S(1)} %get-tuple-element.17.slot_column, s32[8,640]{1,0:T(8,128)S(1)} %get-tuple-element.18.rows_column, bf16[4,128,256]{2,1,0:T(8,128)(2,1)S(1)} %copy-done, bf16[288,128]{1,0:T(8,128)(2,1)S(1)} %get-tuple-element.23.refs_0_, ...), custom_call_target="tpu_custom_call" | custom-call | flops 83886080 | bytes 262144 | tf_op jit(solution)/shard_map/kl_project/pallas_call | solution.py:368
  27.0 1.5 %collective-permute-start.5 = (bf16[288,128]{1,0:T(8,128)(2,1)S(1)}, bf16[288,128]{1,0:T(8,128)(2,1)S(1)}, u32[]{:S(2)}, u32[]{:S(2)}) collective-permute-start(bf16[288,128]{1,0:T(8,128)(2,1)S(1)} %kl_project.3), channel_id=1, source_target_pairs={{0,2},{2,0},{1,3},{3,1},{4,6},{6,4},{5,7},{7,5},{8,10},{10,8},{9,1... | collective-permute-start | bytes 221192 | tf_op jit(solution)/shard_map/ppermute | solution.py:433
  28.5 0.4 %kl_project.2.mine = f32[288,128]{1,0:T(8,128)S(1)} custom-call(s32[8,640]{1,0:T(8,128)S(1)} %get-tuple-element.17.slot_column, s32[8,640]{1,0:T(8,128)S(1)} %get-tuple-element.18.rows_column, bf16[4,128,256]{2,1,0:T(8,128)(2,1)S(1)} %copy-done, bf16[288,128]{1,0:T(8,128)(2,1)S(1)} %get-tuple-element.23.refs_0_, ...), custom_call_target="tpu_custom_call" | custom-call | flops 83886080 | bytes 262144 | tf_op jit(solution)/shard_map/kl_project/pallas_call | solution.py:368
  28.9 2.5 %collective-permute-done.5.got = bf16[288,128]{1,0:T(8,128)(2,1)S(1)} collective-permute-done((bf16[288,128]{1,0:T(8,128)(2,1)S(1)}, bf16[288,128]{1,0:T(8,128)(2,1)S(1)}, u32[]{:S(2)}, u32[]{:S(2)}) %collective-permute-start.5) | collective-permute-done | bytes 73760 | tf_op jit(solution)/shard_map/ppermute | solution.py:433
  31.3 1.0 %unpack.1 = f32[4,64,256]{2,1,0:T(8,128)} custom-call(s32[8,128]{1,0:T(8,128)S(1)} %get-tuple-element.16.scalars, f32[288,128]{1,0:T(8,128)S(1)} %kl_project.2.mine, bf16[288,128]{1,0:T(8,128)(2,1)S(1)} %collective-permute-done.5.got), custom_call_target="tpu_custom_call" | custom-call | flops 36864 | bytes 368640 | tf_op jit(solution)/shard_map/unpack/pallas_call | solution.py:386
Async XLA Ops:
  0.0 26.6 %copy-start = (bf16[4,128,256]{2,1,0:T(8,128)(2,1)S(1)}, bf16[4,128,256]{2,1,0:T(8,128)(2,1)}, u32[]{:S(2)}) copy-start(bf16[4,128,256]{2,1,0:T(8,128)(2,1)} %kl.3) | copy-start | bytes 786436
  13.5 1.5 %collective-permute-start = (f32[1,5,64,128]{3,2,1,0:T(8,128)S(1)}, f32[1,5,64,128]{3,2,1,0:T(8,128)S(1)}, u32[]{:S(2)}, u32[]{:S(2)}) collective-permute-start(f32[1,5,64,128]{3,2,1,0:T(8,128)S(1)} %get-tuple-element.21), channel_id=1, source_target_pairs={{0,1},{1,0},{2,3},{3,2},{4,5},{5,4},{6,7},{7,6},{8,9},{9,8},{10,11... | collective-permute-start | bytes 491528 | tf_op jit(solution)/shard_map/ppermute | solution.py:422
  15.1 3.2 %collective-permute-start.1 = (f32[3,5,64,128]{3,2,1,0:T(8,128)S(1)}, f32[3,5,64,128]{3,2,1,0:T(8,128)S(1)}, u32[]{:S(2)}, u32[]{:S(2)}) collective-permute-start(f32[3,5,64,128]{3,2,1,0:T(8,128)S(1)} %get-tuple-element.22), channel_id=1, source_target_pairs={{0,1},{1,0},{2,3},{3,2},{4,5},{5,4},{6,7},{7,6},{8,9},{9,8},{10,11... | collective-permute-start | bytes 1474568 | tf_op jit(solution)/shard_map/ppermute | solution.py:424
  15.5 7.6 %collective-permute-start.2 = (bf16[288,128]{1,0:T(8,128)(2,1)S(1)}, bf16[288,128]{1,0:T(8,128)(2,1)S(1)}, u32[]{:S(2)}, u32[]{:S(2)}) collective-permute-start(bf16[288,128]{1,0:T(8,128)(2,1)S(1)} %sum_pair.3), channel_id=1, source_target_pairs={{0,4},{4,8},{8,12},{12,0},{1,5},{5,9},{9,13},{13,1},{2,6},{6,10},{... | collective-permute-start | bytes 221192 | tf_op jit(solution)/shard_map/ppermute | solution.py:428
  18.3 8.0 %collective-permute-start.3 = (bf16[288,128]{1,0:T(8,128)(2,1)S(1)}, bf16[288,128]{1,0:T(8,128)(2,1)S(1)}, u32[]{:S(2)}, u32[]{:S(2)}) collective-permute-start(bf16[288,128]{1,0:T(8,128)(2,1)S(1)} %get-tuple-element.25), channel_id=1, source_target_pairs={{0,8},{4,12},{8,0},{12,4},{1,9},{5,13},{9,1},{13,5},{2,10},{6,14},... | collective-permute-start | bytes 221192 | tf_op jit(solution)/shard_map/ppermute | solution.py:428
  21.0 5.5 %collective-permute-start.4 = (bf16[288,128]{1,0:T(8,128)(2,1)S(1)}, bf16[288,128]{1,0:T(8,128)(2,1)S(1)}, u32[]{:S(2)}, u32[]{:S(2)}) collective-permute-start(bf16[288,128]{1,0:T(8,128)(2,1)S(1)} %get-tuple-element.26), channel_id=1, source_target_pairs={{0,12},{4,0},{8,4},{12,8},{1,13},{5,1},{9,5},{13,9},{2,14},{6,2},{... | collective-permute-start | bytes 221192 | tf_op jit(solution)/shard_map/ppermute | solution.py:428
  27.0 4.4 %collective-permute-start.5 = (bf16[288,128]{1,0:T(8,128)(2,1)S(1)}, bf16[288,128]{1,0:T(8,128)(2,1)S(1)}, u32[]{:S(2)}, u32[]{:S(2)}) collective-permute-start(bf16[288,128]{1,0:T(8,128)(2,1)S(1)} %kl_project.3), channel_id=1, source_target_pairs={{0,2},{2,0},{1,3},{3,1},{4,6},{6,4},{5,7},{7,5},{8,10},{10,8},{9,1... | collective-permute-start | bytes 221192 | tf_op jit(solution)/shard_map/ppermute | solution.py:433

commit v12 on v10

--- a/solution.py
+++ b/solution.py
@@ -9,7 +9,7 @@
 
 LANES = 128
 GROUP = 16
-PER_COPY = 8
+COPIES = ((8, 8), (8, 4, 2, 2))
 OWNER_BUDGET = 576
 MIB = 2**20
 
@@ -134,17 +134,20 @@
     for copy in table_copies:
         copy.start()
 
-    def basis_copy(i):
-        part = pl.ds(i * PER_COPY, PER_COPY)
-        return pltpu.make_async_copy(basis.at[part], basis_v.at[part], basis_sem.at[i])
-
-    ahead = 1
-    for i in range(ahead):
-        basis_copy(i).start()
+    def basis_copies(group, parity):
+        found, first = [], 0
+        for i, count in enumerate(COPIES[parity]):
+            part = pl.ds(group * GROUP + first, count)
+            sem = basis_sem.at[group * len(COPIES[1]) + i]
+            copy = pltpu.make_async_copy(basis.at[part], basis_v.at[part], sem)
+            found.append((copy, first, count))
+            first += count
+        return found
+
+    basis_copies(0, 0)[0][0].start()
     for copy in table_copies:
         copy.wait()
 
-    per_group = GROUP // PER_COPY
     for group in range(groups):
         part = pl.ds(group * GROUP, GROUP)
 
@@ -158,8 +161,8 @@
                 panels.at[m, part], panels_v.at[place, part], panel_sem.at[group]
             ).start()
 
-        for i in range(ahead + group * per_group, min(ahead + (group + 1) * per_group, groups * per_group)):
-            basis_copy(i).start()
+        for copy, _, _ in basis_copies(group, group % 2)[1 if group == 0 else 0 :]:
+            copy.start()
 
     offsets_of(keep_place, tile_place, shift_place, owner_slots)
     column = lax.broadcasted_iota(jnp.int32, slot_column.shape, 1)
@@ -183,9 +186,8 @@
 
     tables = (tile_place, shift_place, owner_slots)
     all_owners = range(mine.shape[0] * lax.axis_size("pa"))
-    share = len(all_owners) // per_group
-
-    def group_step(group, out_v, out_before):
+
+    def group_step(group, parity, out_v, out_before):
         here = pl.ds(pl.multiple_of(group * GROUP, GROUP), GROUP)
         pltpu.make_async_copy(
             panels_v.at[:, here], panels_v.at[:, here], panel_sem.at[group]
@@ -195,26 +197,27 @@
             tile = panels_v[blocks, here, :].reshape(side, depth)
             turned = jnp.dot(swap, tile, preferred_element_type=jnp.float32).astype(jnp.bfloat16)
             lhs_v[:, blocks, :] = turned.reshape(GROUP, GROUP, depth)
-        for i in range(per_group):
-            basis_copy(group * per_group + i).wait()
-            for f in range(i * PER_COPY, (i + 1) * PER_COPY):
+        for i, (copy, first, count) in enumerate(basis_copies(group, parity)):
+            copy.wait()
+            for f in range(first, first + count):
                 product = jnp.dot(
                     lhs_v[f], basis_v[group * GROUP + f], preferred_element_type=jnp.float32
                 )
                 for t in range(product.shape[1] // LANES):
                     at = (t * GROUP + f) * slots
                     out_v[at : at + slots, :] = product[:, t * LANES : (t + 1) * LANES]
-            line = jnp.maximum(group - 1, 0) * GROUP
-            pack(out_before, mine, far, near, line, tables, all_owners[i * share : (i + 1) * share])
+            if i < 2:
+                line = jnp.maximum(group - 1, 0) * GROUP
+                half = len(all_owners) // 2
+                part = all_owners[i * half : (i + 1) * half]
+                pack(out_before, mine, far, near, line, tables, part)
 
     @pl.loop(0, groups // 2)
     def _(pair):
-        group_step(2 * pair, out_even, out_odd)
-        group_step(2 * pair + 1, out_odd, out_even)
-
-    for i in range(per_group):
-        part = all_owners[i * share : (i + 1) * share]
-        pack(out_odd, mine, far, near, (groups - 1) * GROUP, tables, part)
+        group_step(2 * pair, 0, out_even, out_odd)
+        group_step(2 * pair + 1, 1, out_odd, out_even)
+
+    pack(out_odd, mine, far, near, (groups - 1) * GROUP, tables, all_owners)
 
 
 def folded_rows(rows, width):
@@ -341,7 +344,7 @@
             pltpu.VMEM((modes // LANES * GROUP * slots, LANES), jnp.float32),
             pltpu.SemaphoreType.DMA((3,)),
             pltpu.SemaphoreType.DMA((freqs // GROUP,)),
-            pltpu.SemaphoreType.DMA((freqs // PER_COPY,)),
+            pltpu.SemaphoreType.DMA((freqs // GROUP * len(COPIES[1]),)),
         ],
         compiler_params=pltpu.CompilerParams(vmem_limit_bytes=48 * MIB),
         cost_estimate=pl.CostEstimate(

time: 32.5 us -> 33 us (1.015)
  Pallas kernels: 15.7 us -> 16.1 us
    pallas_call x1, Pallas kernels: 13.6 us -> 14 us  [project(): pl.pallas_call(functools.partial(project_kernel, owner_slots), out_shape=...]
where the time goes in v12:
time: 33 us; the launch traced here: 32.8 us
  Pallas kernels  16.1 us (49%)
  starting transfers between devices  10.1 us (31%)
  waiting for transfers between devices  6.58 us (20%)
    pallas_call x1, Pallas kernels, project(): pl.pallas_call(functools.partial(project_kernel, owner_slots), out_shape=...  14 us
    ppermute x3, starting transfers between devices, shards(): lax.ppermute(summed[step], 'ma', ring(step))  7.72 us
    ppermute x3, waiting for transfers between devices, shards(): lax.ppermute(summed[step], 'ma', ring(step))  3.13 us
    ppermute x1, waiting for transfers between devices, shards(): got = lax.ppermute(send, 'af', pairs('af'))  2.42 us
    ppermute x1, starting transfers between devices, shards(): got = lax.ppermute(send, 'af', pairs('af'))  1.5 us
    pallas_call x1, Pallas kernels, unpack(): pl.pallas_call(unpack_kernel, out_shape=jax.ShapeDtypeStruct((owner_slots...  1.04 us
    ppermute x1, waiting for transfers between devices, shards(): got_far = lax.ppermute(far, 'pa', pairs('pa'))  1.03 us
    pallas_call x2, Pallas kernels, kl_project(): pl.pallas_call(functools.partial(kl_kernel, part, owners, width), out_sha...  0.89 us
  transfers between devices with their start and end apart: 6, of which 3 were waited for; matrix products, arithmetic and copies ran while one was open for 0% of the time, Pallas kernels for 2%

profile of v12, /device:TPU:0, one launch (start us, length us, event | category | flops | bytes accessed | tf_op | source)
XLA Modules:
  0.0 32.8 jit_solution(2761232672208681244)
XLA Ops:
  0.0 0.0 copy-start
  0.0 14.0 %project.1 = (f32[4,5,64,128]{3,2,1,0:T(8,128)S(1)}, f32[1,5,64,128]{3,2,1,0:T(8,128)S(1)}, f32[3,5,64,128]{3,2,1,0:T(8,128)S(1)}, s32[8,640]{1,0:T(8,128)S(1)},...) custom-call(s32[32]{0:T(128)} %slot_hbm.1, s32[32]{0:T(128)} %keep_hbm.1, s32[32]{0:T(128)} %rows_hbm.1, ...), custom_call_target="tpu_custom_call" | custom-call | flops 1073741824 | bytes 37748736 | tf_op jit(solution)/shard_map/project/pallas_call | solution.py:326
  14.1 0.5 %collective-permute-start = (f32[1,5,64,128]{3,2,1,0:T(8,128)S(1)}, f32[1,5,64,128]{3,2,1,0:T(8,128)S(1)}, u32[]{:S(2)}, u32[]{:S(2)}) collective-permute-start(f32[1,5,64,128]{3,2,1,0:T(8,128)S(1)} %get-tuple-element.21), channel_id=1, source_target_pairs={{0,1},{1,0},{2,3},{3,2},{4,5},{5,4},{6,7},{7,6},{8,9},{9,8},{10,11... | collective-permute-start | bytes 491528 | tf_op jit(solution)/shard_map/ppermute | solution.py:433
  14.6 1.0 %collective-permute-done.got = f32[1,5,64,128]{3,2,1,0:T(8,128)S(1)} collective-permute-done((f32[1,5,64,128]{3,2,1,0:T(8,128)S(1)}, f32[1,5,64,128]{3,2,1,0:T(8,128)S(1)}, u32[]{:S(2)}, u32[]{:S(2)}) %collective-permute-start) | collective-permute-done | bytes 163872 | tf_op jit(solution)/shard_map/ppermute | solution.py:433
  15.6 0.4 %collective-permute-start.1 = (f32[3,5,64,128]{3,2,1,0:T(8,128)S(1)}, f32[3,5,64,128]{3,2,1,0:T(8,128)S(1)}, u32[]{:S(2)}, u32[]{:S(2)}) collective-permute-start(f32[3,5,64,128]{3,2,1,0:T(8,128)S(1)} %get-tuple-element.22), channel_id=1, source_target_pairs={{0,1},{1,0},{2,3},{3,2},{4,5},{5,4},{6,7},{7,6},{8,9},{9,8},{10,11... | collective-permute-start | bytes 1474568 | tf_op jit(solution)/shard_map/ppermute | solution.py:435
  16.0 0.1 sum_pair.3
  16.0 4.8 %collective-permute-start.3 = (bf16[288,128]{1,0:T(8,128)(2,1)S(1)}, bf16[288,128]{1,0:T(8,128)(2,1)S(1)}, u32[]{:S(2)}, u32[]{:S(2)}) collective-permute-start(bf16[288,128]{1,0:T(8,128)(2,1)S(1)} %sum_pair.3), channel_id=1, source_target_pairs={{0,12},{4,8},{8,4},{12,0},{1,13},{5,9},{9,5},{13,1},{2,14},{6,10},... | collective-permute-start | bytes 221192 | tf_op jit(solution)/shard_map/ppermute | solution.py:439
  20.8 0.0 collective-permute-done.1.got
  20.8 0.1 sum_pair.2
  20.9 0.0 collective-permute-start.2
  20.9 2.9 %collective-permute-start.4 = (bf16[288,128]{1,0:T(8,128)(2,1)S(1)}, bf16[288,128]{1,0:T(8,128)(2,1)S(1)}, u32[]{:S(2)}, u32[]{:S(2)}) collective-permute-start(bf16[288,128]{1,0:T(8,128)(2,1)S(1)} %get-tuple-element.26), channel_id=1, source_target_pairs={{0,8},{4,0},{8,12},{12,4},{1,9},{5,1},{9,13},{13,5},{2,10},{6,2},{... | collective-permute-start | bytes 221192 | tf_op jit(solution)/shard_map/ppermute | solution.py:439
  23.9 0.0 collective-permute-done.3.refs_2_
  23.9 3.1 %collective-permute-done.2.refs_1_ = bf16[288,128]{1,0:T(8,128)(2,1)S(1)} collective-permute-done((bf16[288,128]{1,0:T(8,128)(2,1)S(1)}, bf16[288,128]{1,0:T(8,128)(2,1)S(1)}, u32[]{:S(2)}, u32[]{:S(2)}) %collective-permute-start.2) | collective-permute-done | bytes 73760 | tf_op jit(solution)/shard_map/ppermute | solution.py:439
  27.0 0.0 collective-permute-done.4.refs_3_
  27.0 0.0 copy-done
  27.0 0.4 %kl_project.3 = bf16[288,128]{1,0:T(8,128)(2,1)S(1)} custom-call(s32[8,640]{1,0:T(8,128)S(1)} %get-tuple-element.17.slot_column, s32[8,640]{1,0:T(8,128)S(1)} %get-tuple-element.18.rows_column, bf16[4,128,256]{2,1,0:T(8,128)(2,1)S(1)} %copy-done, bf16[288,128]{1,0:T(8,128)(2,1)S(1)} %get-tuple-element.23.refs_0_, ...), custom_call_target="tpu_custom_call" | custom-call | flops 83886080 | bytes 262144 | tf_op jit(solution)/shard_map/kl_project/pallas_call | solution.py:378
  27.4 1.5 %collective-permute-start.5 = (bf16[288,128]{1,0:T(8,128)(2,1)S(1)}, bf16[288,128]{1,0:T(8,128)(2,1)S(1)}, u32[]{:S(2)}, u32[]{:S(2)}) collective-permute-start(bf16[288,128]{1,0:T(8,128)(2,1)S(1)} %kl_project.3), channel_id=1, source_target_pairs={{0,2},{2,0},{1,3},{3,1},{4,6},{6,4},{5,7},{7,5},{8,10},{10,8},{9,1... | collective-permute-start | bytes 221192 | tf_op jit(solution)/shard_map/ppermute | solution.py:444
  28.9 0.4 %kl_project.2.mine = f32[288,128]{1,0:T(8,128)S(1)} custom-call(s32[8,640]{1,0:T(8,128)S(1)} %get-tuple-element.17.slot_column, s32[8,640]{1,0:T(8,128)S(1)} %get-tuple-element.18.rows_column, bf16[4,128,256]{2,1,0:T(8,128)(2,1)S(1)} %copy-done, bf16[288,128]{1,0:T(8,128)(2,1)S(1)} %get-tuple-element.23.refs_0_, ...), custom_call_target="tpu_custom_call" | custom-call | flops 83886080 | bytes 262144 | tf_op jit(solution)/shard_map/kl_project/pallas_call | solution.py:378
  29.4 2.4 %collective-permute-done.5.got = bf16[288,128]{1,0:T(8,128)(2,1)S(1)} collective-permute-done((bf16[288,128]{1,0:T(8,128)(2,1)S(1)}, bf16[288,128]{1,0:T(8,128)(2,1)S(1)}, u32[]{:S(2)}, u32[]{:S(2)}) %collective-permute-start.5) | collective-permute-done | bytes 73760 | tf_op jit(solution)/shard_map/ppermute | solution.py:444
  31.8 1.0 %unpack.1 = f32[4,64,256]{2,1,0:T(8,128)} custom-call(s32[8,128]{1,0:T(8,128)S(1)} %get-tuple-element.16.scalars, f32[288,128]{1,0:T(8,128)S(1)} %kl_project.2.mine, bf16[288,128]{1,0:T(8,128)(2,1)S(1)} %collective-permute-done.5.got), custom_call_target="tpu_custom_call" | custom-call | flops 36864 | bytes 368640 | tf_op jit(solution)/shard_map/unpack/pallas_call | solution.py:396
Async XLA Ops:
  0.0 27.0 %copy-start = (bf16[4,128,256]{2,1,0:T(8,128)(2,1)S(1)}, bf16[4,128,256]{2,1,0:T(8,128)(2,1)}, u32[]{:S(2)}) copy-start(bf16[4,128,256]{2,1,0:T(8,128)(2,1)} %kl.3) | copy-start | bytes 786436
  14.1 1.5 %collective-permute-start = (f32[1,5,64,128]{3,2,1,0:T(8,128)S(1)}, f32[1,5,64,128]{3,2,1,0:T(8,128)S(1)}, u32[]{:S(2)}, u32[]{:S(2)}) collective-permute-start(f32[1,5,64,128]{3,2,1,0:T(8,128)S(1)} %get-tuple-element.21), channel_id=1, source_target_pairs={{0,1},{1,0},{2,3},{3,2},{4,5},{5,4},{6,7},{7,6},{8,9},{9,8},{10,11... | collective-permute-start | bytes 491528 | tf_op jit(solution)/shard_map/ppermute | solution.py:433
  15.6 5.2 %collective-permute-start.1 = (f32[3,5,64,128]{3,2,1,0:T(8,128)S(1)}, f32[3,5,64,128]{3,2,1,0:T(8,128)S(1)}, u32[]{:S(2)}, u32[]{:S(2)}) collective-permute-start(f32[3,5,64,128]{3,2,1,0:T(8,128)S(1)} %get-tuple-element.22), channel_id=1, source_target_pairs={{0,1},{1,0},{2,3},{3,2},{4,5},{5,4},{6,7},{7,6},{8,9},{9,8},{10,11... | collective-permute-start | bytes 1474568 | tf_op jit(solution)/shard_map/ppermute | solution.py:435
  16.0 7.8 %collective-permute-start.3 = (bf16[288,128]{1,0:T(8,128)(2,1)S(1)}, bf16[288,128]{1,0:T(8,128)(2,1)S(1)}, u32[]{:S(2)}, u32[]{:S(2)}) collective-permute-start(bf16[288,128]{1,0:T(8,128)(2,1)S(1)} %sum_pair.3), channel_id=1, source_target_pairs={{0,12},{4,8},{8,4},{12,0},{1,13},{5,9},{9,5},{13,1},{2,14},{6,10},... | collective-permute-start | bytes 221192 | tf_op jit(solution)/shard_map/ppermute | solution.py:439
  20.9 6.1 %collective-permute-start.2 = (bf16[288,128]{1,0:T(8,128)(2,1)S(1)}, bf16[288,128]{1,0:T(8,128)(2,1)S(1)}, u32[]{:S(2)}, u32[]{:S(2)}) collective-permute-start(bf16[288,128]{1,0:T(8,128)(2,1)S(1)} %get-tuple-element.24), channel_id=1, source_target_pairs={{0,4},{4,12},{8,0},{12,8},{1,5},{5,13},{9,1},{13,9},{2,6},{6,14},{... | collective-permute-start | bytes 221192 | tf_op jit(solution)/shard_map/ppermute | solution.py:439
  20.9 6.0 %collective-permute-start.4 = (bf16[288,128]{1,0:T(8,128)(2,1)S(1)}, bf16[288,128]{1,0:T(8,128)(2,1)S(1)}, u32[]{:S(2)}, u32[]{:S(2)}) collective-permute-start(bf16[288,128]{1,0:T(8,128)(2,1)S(1)} %get-tuple-element.26), channel_id=1, source_target_pairs={{0,8},{4,0},{8,12},{12,4},{1,9},{5,1},{9,13},{13,5},{2,10},{6,2},{... | collective-permute-start | bytes 221192 | tf_op jit(solution)/shard_map/ppermute | solution.py:439
  27.4 4.4 %collective-permute-start.5 = (bf16[288,128]{1,0:T(8,128)(2,1)S(1)}, bf16[288,128]{1,0:T(8,128)(2,1)S(1)}, u32[]{:S(2)}, u32[]{:S(2)}) collective-permute-start(bf16[288,128]{1,0:T(8,128)(2,1)S(1)} %kl_project.3), channel_id=1, source_target_pairs={{0,2},{2,0},{1,3},{3,1},{4,6},{6,4},{5,7},{7,5},{8,10},{10,8},{9,1... | collective-permute-start | bytes 221192 | tf_op jit(solution)/shard_map/ppermute | solution.py:444

commit v13 on v12

--- a/solution.py
+++ b/solution.py
@@ -9,7 +9,9 @@
 
 LANES = 128
 GROUP = 16
-COPIES = ((8, 8), (8, 4, 2, 2))
+COPIES = ((8, 8), (8, 8))
+UNITS = 2
+SIDE = 256
 OWNER_BUDGET = 576
 MIB = 2**20
 
@@ -116,6 +118,59 @@
                 to[owner, jnp.minimum(tile + t, width_tiles - 1), rows, :] = values[t]
 
 
+def products(lhs, basis, out_v, start, first, count, *totals):
+    slots = lhs.shape[1]
+
+    def store(pair, here):
+        for unit, total in enumerate(here):
+            product = pltpu.matmul_pop(total)
+            for t in range(SIDE // LANES):
+                at = (t * GROUP + pair + unit) * slots
+                out_v[at : at + slots, :] = product[:, t * LANES : (t + 1) * LANES]
+
+    before = None
+    for pair in range(first, first + count, UNITS):
+        here = totals[UNITS * ((pair // UNITS) % 2) :][:UNITS]
+        for k in range(lhs.shape[2] // SIDE):
+            depth = slice(k * SIDE, (k + 1) * SIDE)
+            for unit, total in enumerate(here):
+                pltpu.matmul_push_rhs(basis[start + pair + unit, depth, :], k % 2, unit)
+                pltpu.matmul_acc_lhs(total, lhs[pair + unit, :, depth], load_staged_rhs=k % 2)
+        if before:
+            store(*before)
+        before = pair, here
+    store(*before)
+
+
+def turn(swap, panels, here, lhs, *totals):
+    def store(jobs, units):
+        for (blocks, columns), total in zip(jobs, units):
+            turned = pltpu.matmul_pop(total).astype(jnp.bfloat16)
+            lhs[:, blocks, columns] = turned.reshape(GROUP, GROUP, SIDE)
+
+    jobs = [
+        (slice(block, block + GROUP), slice(column, column + SIDE))
+        for block in range(0, panels.shape[0], GROUP)
+        for column in range(0, panels.shape[2], SIDE)
+    ]
+    before = None
+    for i in range(0, len(jobs), UNITS):
+        reg = (i // UNITS) % 2
+        now = jobs[i : i + UNITS], totals[UNITS * reg :][:UNITS]
+        for unit, ((blocks, columns), total) in enumerate(zip(*now)):
+            tile = panels[blocks, here, columns].reshape(SIDE, SIDE)
+            pltpu.matmul_push_rhs(tile, reg, unit)
+            pltpu.matmul_acc_lhs(total, swap, load_staged_rhs=reg)
+        if before:
+            store(*before)
+        before = now
+    store(*before)
+
+
+def on_units(step, rows):
+    pl.run_scoped(step, *[pltpu.ACC(i % UNITS)((rows, SIDE), jnp.float32) for i in range(2 * UNITS)])
+
+
 def project_kernel(
     owner_slots, slot_hbm, keep_hbm, rows_hbm, panels, basis,
     mine, far, near, slot_column, rows_column, scalars,
@@ -144,7 +199,8 @@
             first += count
         return found
 
-    basis_copies(0, 0)[0][0].start()
+    early_copies = basis_copies(0, 0)
+    early_copies[0][0].start()
     for copy in table_copies:
         copy.wait()
 
@@ -161,7 +217,7 @@
                 panels.at[m, part], panels_v.at[place, part], panel_sem.at[group]
             ).start()
 
-        for copy, _, _ in basis_copies(group, group % 2)[1 if group == 0 else 0 :]:
+        for copy, _, _ in early_copies[1:] if group == 0 else basis_copies(group, group % 2):
             copy.start()
 
     offsets_of(keep_place, tile_place, shift_place, owner_slots)
@@ -192,20 +248,11 @@
         pltpu.make_async_copy(
             panels_v.at[:, here], panels_v.at[:, here], panel_sem.at[group]
         ).wait()
-        for block in range(slots // GROUP):
-            blocks = slice(block * GROUP, (block + 1) * GROUP)
-            tile = panels_v[blocks, here, :].reshape(side, depth)
-            turned = jnp.dot(swap, tile, preferred_element_type=jnp.float32).astype(jnp.bfloat16)
-            lhs_v[:, blocks, :] = turned.reshape(GROUP, GROUP, depth)
+        on_units(functools.partial(turn, swap, panels_v, here, lhs_v), SIDE)
         for i, (copy, first, count) in enumerate(basis_copies(group, parity)):
             copy.wait()
-            for f in range(first, first + count):
-                product = jnp.dot(
-                    lhs_v[f], basis_v[group * GROUP + f], preferred_element_type=jnp.float32
-                )
-                for t in range(product.shape[1] // LANES):
-                    at = (t * GROUP + f) * slots
-                    out_v[at : at + slots, :] = product[:, t * LANES : (t + 1) * LANES]
+            step = functools.partial(products, lhs_v, basis_v, out_v, group * GROUP, first, count)
+            on_units(step, slots)
             if i < 2:
                 line = jnp.maximum(group - 1, 0) * GROUP
                 half = len(all_owners) // 2

time: 33 us -> 32.5 us (0.985)
  Pallas kernels: 16.1 us -> 15.7 us
    pallas_call x1, Pallas kernels: 14 us -> 13.6 us  [project(): pl.pallas_call(functools.partial(project_kernel, owner_slots), out_shape=...]
where the time goes in v13:
time: 32.5 us; the launch traced here: 32.4 us
  Pallas kernels  15.7 us (48%)
  starting transfers between devices  10.1 us (31%)
  waiting for transfers between devices  6.57 us (20%)
    pallas_call x1, Pallas kernels, project(): pl.pallas_call(functools.partial(project_kernel, owner_slots), out_shape=...  13.6 us
    ppermute x3, starting transfers between devices, shards(): lax.ppermute(summed[step], 'ma', ring(step))  7.73 us
    ppermute x3, waiting for transfers between devices, shards(): lax.ppermute(summed[step], 'ma', ring(step))  3.13 us
    ppermute x1, waiting for transfers between devices, shards(): got = lax.ppermute(send, 'af', pairs('af'))  2.41 us
    ppermute x1, starting transfers between devices, shards(): got = lax.ppermute(send, 'af', pairs('af'))  1.5 us
    pallas_call x1, Pallas kernels, unpack(): pl.pallas_call(unpack_kernel, out_shape=jax.ShapeDtypeStruct((owner_slots...  1.04 us
    ppermute x1, waiting for transfers between devices, shards(): got_far = lax.ppermute(far, 'pa', pairs('pa'))  1.03 us
    pallas_call x2, Pallas kernels, kl_project(): pl.pallas_call(functools.partial(kl_kernel, part, owners, width), out_sha...  0.89 us
  transfers between devices with their start and end apart: 6, of which 3 were waited for; matrix products, arithmetic and copies ran while one was open for 0% of the time, Pallas kernels for 2%

profile of v13, /device:TPU:0, one launch (start us, length us, event | category | flops | bytes accessed | tf_op | source)
XLA Modules:
  0.0 32.4 jit_solution(9222532294374781456)
XLA Ops:
  0.0 0.0 copy-start
  0.0 13.6 %project.1 = (f32[4,5,64,128]{3,2,1,0:T(8,128)S(1)}, f32[1,5,64,128]{3,2,1,0:T(8,128)S(1)}, f32[3,5,64,128]{3,2,1,0:T(8,128)S(1)}, s32[8,640]{1,0:T(8,128)S(1)},...) custom-call(s32[32]{0:T(128)} %slot_hbm.1, s32[32]{0:T(128)} %keep_hbm.1, s32[32]{0:T(128)} %rows_hbm.1, ...), custom_call_target="tpu_custom_call" | custom-call | flops 1073741824 | bytes 37748736 | tf_op jit(solution)/shard_map/project/pallas_call | solution.py:373
  13.6 0.5 %collective-permute-start = (f32[1,5,64,128]{3,2,1,0:T(8,128)S(1)}, f32[1,5,64,128]{3,2,1,0:T(8,128)S(1)}, u32[]{:S(2)}, u32[]{:S(2)}) collective-permute-start(f32[1,5,64,128]{3,2,1,0:T(8,128)S(1)} %get-tuple-element.21), channel_id=1, source_target_pairs={{0,1},{1,0},{2,3},{3,2},{4,5},{5,4},{6,7},{7,6},{8,9},{9,8},{10,11... | collective-permute-start | bytes 491528 | tf_op jit(solution)/shard_map/ppermute | solution.py:480
  14.1 1.0 %collective-permute-done.got = f32[1,5,64,128]{3,2,1,0:T(8,128)S(1)} collective-permute-done((f32[1,5,64,128]{3,2,1,0:T(8,128)S(1)}, f32[1,5,64,128]{3,2,1,0:T(8,128)S(1)}, u32[]{:S(2)}, u32[]{:S(2)}) %collective-permute-start) | collective-permute-done | bytes 163872 | tf_op jit(solution)/shard_map/ppermute | solution.py:480
  15.1 0.4 %collective-permute-start.1 = (f32[3,5,64,128]{3,2,1,0:T(8,128)S(1)}, f32[3,5,64,128]{3,2,1,0:T(8,128)S(1)}, u32[]{:S(2)}, u32[]{:S(2)}) collective-permute-start(f32[3,5,64,128]{3,2,1,0:T(8,128)S(1)} %get-tuple-element.22), channel_id=1, source_target_pairs={{0,1},{1,0},{2,3},{3,2},{4,5},{5,4},{6,7},{7,6},{8,9},{9,8},{10,11... | collective-permute-start | bytes 1474568 | tf_op jit(solution)/shard_map/ppermute | solution.py:482
  15.5 0.1 sum_pair.3
  15.6 4.8 %collective-permute-start.3 = (bf16[288,128]{1,0:T(8,128)(2,1)S(1)}, bf16[288,128]{1,0:T(8,128)(2,1)S(1)}, u32[]{:S(2)}, u32[]{:S(2)}) collective-permute-start(bf16[288,128]{1,0:T(8,128)(2,1)S(1)} %sum_pair.3), channel_id=1, source_target_pairs={{0,12},{4,8},{8,4},{12,0},{1,13},{5,9},{9,5},{13,1},{2,14},{6,10},... | collective-permute-start | bytes 221192 | tf_op jit(solution)/shard_map/ppermute | solution.py:486
  20.4 0.0 collective-permute-done.1.got
  20.4 0.1 sum_pair.2
  20.4 0.0 collective-permute-start.2
  20.5 2.9 %collective-permute-start.4 = (bf16[288,128]{1,0:T(8,128)(2,1)S(1)}, bf16[288,128]{1,0:T(8,128)(2,1)S(1)}, u32[]{:S(2)}, u32[]{:S(2)}) collective-permute-start(bf16[288,128]{1,0:T(8,128)(2,1)S(1)} %get-tuple-element.26), channel_id=1, source_target_pairs={{0,8},{4,0},{8,12},{12,4},{1,9},{5,1},{9,13},{13,5},{2,10},{6,2},{... | collective-permute-start | bytes 221192 | tf_op jit(solution)/shard_map/ppermute | solution.py:486
  23.4 0.0 collective-permute-done.3.refs_2_
  23.4 3.1 %collective-permute-done.2.refs_1_ = bf16[288,128]{1,0:T(8,128)(2,1)S(1)} collective-permute-done((bf16[288,128]{1,0:T(8,128)(2,1)S(1)}, bf16[288,128]{1,0:T(8,128)(2,1)S(1)}, u32[]{:S(2)}, u32[]{:S(2)}) %collective-permute-start.2) | collective-permute-done | bytes 73760 | tf_op jit(solution)/shard_map/ppermute | solution.py:486
  26.5 0.0 collective-permute-done.4.refs_3_
  26.5 0.0 copy-done
  26.5 0.4 %kl_project.3 = bf16[288,128]{1,0:T(8,128)(2,1)S(1)} custom-call(s32[8,640]{1,0:T(8,128)S(1)} %get-tuple-element.17.slot_column, s32[8,640]{1,0:T(8,128)S(1)} %get-tuple-element.18.rows_column, bf16[4,128,256]{2,1,0:T(8,128)(2,1)S(1)} %copy-done, bf16[288,128]{1,0:T(8,128)(2,1)S(1)} %get-tuple-element.23.refs_0_, ...), custom_call_target="tpu_custom_call" | custom-call | flops 83886080 | bytes 262144 | tf_op jit(solution)/shard_map/kl_project/pallas_call | solution.py:425
  27.0 1.5 %collective-permute-start.5 = (bf16[288,128]{1,0:T(8,128)(2,1)S(1)}, bf16[288,128]{1,0:T(8,128)(2,1)S(1)}, u32[]{:S(2)}, u32[]{:S(2)}) collective-permute-start(bf16[288,128]{1,0:T(8,128)(2,1)S(1)} %kl_project.3), channel_id=1, source_target_pairs={{0,2},{2,0},{1,3},{3,1},{4,6},{6,4},{5,7},{7,5},{8,10},{10,8},{9,1... | collective-permute-start | bytes 221192 | tf_op jit(solution)/shard_map/ppermute | solution.py:491
  28.5 0.4 %kl_project.2.mine = f32[288,128]{1,0:T(8,128)S(1)} custom-call(s32[8,640]{1,0:T(8,128)S(1)} %get-tuple-element.17.slot_column, s32[8,640]{1,0:T(8,128)S(1)} %get-tuple-element.18.rows_column, bf16[4,128,256]{2,1,0:T(8,128)(2,1)S(1)} %copy-done, bf16[288,128]{1,0:T(8,128)(2,1)S(1)} %get-tuple-element.23.refs_0_, ...), custom_call_target="tpu_custom_call" | custom-call | flops 83886080 | bytes 262144 | tf_op jit(solution)/shard_map/kl_project/pallas_call | solution.py:425
  28.9 2.4 %collective-permute-done.5.got = bf16[288,128]{1,0:T(8,128)(2,1)S(1)} collective-permute-done((bf16[288,128]{1,0:T(8,128)(2,1)S(1)}, bf16[288,128]{1,0:T(8,128)(2,1)S(1)}, u32[]{:S(2)}, u32[]{:S(2)}) %collective-permute-start.5) | collective-permute-done | bytes 73760 | tf_op jit(solution)/shard_map/ppermute | solution.py:491
  31.3 1.0 %unpack.1 = f32[4,64,256]{2,1,0:T(8,128)} custom-call(s32[8,128]{1,0:T(8,128)S(1)} %get-tuple-element.16.scalars, f32[288,128]{1,0:T(8,128)S(1)} %kl_project.2.mine, bf16[288,128]{1,0:T(8,128)(2,1)S(1)} %collective-permute-done.5.got), custom_call_target="tpu_custom_call" | custom-call | flops 36864 | bytes 368640 | tf_op jit(solution)/shard_map/unpack/pallas_call | solution.py:443
Async XLA Ops:
  0.0 26.5 %copy-start = (bf16[4,128,256]{2,1,0:T(8,128)(2,1)S(1)}, bf16[4,128,256]{2,1,0:T(8,128)(2,1)}, u32[]{:S(2)}) copy-start(bf16[4,128,256]{2,1,0:T(8,128)(2,1)} %kl.3) | copy-start | bytes 786436
  13.6 1.5 %collective-permute-start = (f32[1,5,64,128]{3,2,1,0:T(8,128)S(1)}, f32[1,5,64,128]{3,2,1,0:T(8,128)S(1)}, u32[]{:S(2)}, u32[]{:S(2)}) collective-permute-start(f32[1,5,64,128]{3,2,1,0:T(8,128)S(1)} %get-tuple-element.21), channel_id=1, source_target_pairs={{0,1},{1,0},{2,3},{3,2},{4,5},{5,4},{6,7},{7,6},{8,9},{9,8},{10,11... | collective-permute-start | bytes 491528 | tf_op jit(solution)/shard_map/ppermute | solution.py:480
  15.1 5.2 %collective-permute-start.1 = (f32[3,5,64,128]{3,2,1,0:T(8,128)S(1)}, f32[3,5,64,128]{3,2,1,0:T(8,128)S(1)}, u32[]{:S(2)}, u32[]{:S(2)}) collective-permute-start(f32[3,5,64,128]{3,2,1,0:T(8,128)S(1)} %get-tuple-element.22), channel_id=1, source_target_pairs={{0,1},{1,0},{2,3},{3,2},{4,5},{5,4},{6,7},{7,6},{8,9},{9,8},{10,11... | collective-permute-start | bytes 1474568 | tf_op jit(solution)/shard_map/ppermute | solution.py:482
  15.6 7.8 %collective-permute-start.3 = (bf16[288,128]{1,0:T(8,128)(2,1)S(1)}, bf16[288,128]{1,0:T(8,128)(2,1)S(1)}, u32[]{:S(2)}, u32[]{:S(2)}) collective-permute-start(bf16[288,128]{1,0:T(8,128)(2,1)S(1)} %sum_pair.3), channel_id=1, source_target_pairs={{0,12},{4,8},{8,4},{12,0},{1,13},{5,9},{9,5},{13,1},{2,14},{6,10},... | collective-permute-start | bytes 221192 | tf_op jit(solution)/shard_map/ppermute | solution.py:486
  20.4 6.1 %collective-permute-start.2 = (bf16[288,128]{1,0:T(8,128)(2,1)S(1)}, bf16[288,128]{1,0:T(8,128)(2,1)S(1)}, u32[]{:S(2)}, u32[]{:S(2)}) collective-permute-start(bf16[288,128]{1,0:T(8,128)(2,1)S(1)} %get-tuple-element.24), channel_id=1, source_target_pairs={{0,4},{4,12},{8,0},{12,8},{1,5},{5,13},{9,1},{13,9},{2,6},{6,14},{... | collective-permute-start | bytes 221192 | tf_op jit(solution)/shard_map/ppermute | solution.py:486
  20.5 6.0 %collective-permute-start.4 = (bf16[288,128]{1,0:T(8,128)(2,1)S(1)}, bf16[288,128]{1,0:T(8,128)(2,1)S(1)}, u32[]{:S(2)}, u32[]{:S(2)}) collective-permute-start(bf16[288,128]{1,0:T(8,128)(2,1)S(1)} %get-tuple-element.26), channel_id=1, source_target_pairs={{0,8},{4,0},{8,12},{12,4},{1,9},{5,1},{9,13},{13,5},{2,10},{6,2},{... | collective-permute-start | bytes 221192 | tf_op jit(solution)/shard_map/ppermute | solution.py:486
  27.0 4.4 %collective-permute-start.5 = (bf16[288,128]{1,0:T(8,128)(2,1)S(1)}, bf16[288,128]{1,0:T(8,128)(2,1)S(1)}, u32[]{:S(2)}, u32[]{:S(2)}) collective-permute-start(bf16[288,128]{1,0:T(8,128)(2,1)S(1)} %kl_project.3), channel_id=1, source_target_pairs={{0,2},{2,0},{1,3},{3,1},{4,6},{6,4},{5,7},{7,5},{8,10},{10,8},{9,1... | collective-permute-start | bytes 221192 | tf_op jit(solution)/shard_map/ppermute | solution.py:491

commit v14 on v10

--- a/solution.py
+++ b/solution.py
@@ -9,7 +9,7 @@
 
 LANES = 128
 GROUP = 16
-PER_COPY = 8
+COPIES = (8, 8)
 OWNER_BUDGET = 576
 MIB = 2**20
 
@@ -119,7 +119,7 @@
 def project_kernel(
     owner_slots, slot_hbm, keep_hbm, rows_hbm, panels, basis,
     mine, far, near, slot_column, rows_column, scalars,
-    slot_s, keep_s, rows_s, keep_place, rows_place, tile_place, shift_place,
+    slot_s, keep_s, rows_s, order_place, keep_place, rows_place, tile_place, shift_place,
     panels_v, basis_v, lhs_v, out_even, out_odd, small_sem, panel_sem, basis_sem,
 ):
     slots, freqs, depth = panels_v.shape
@@ -134,32 +134,28 @@
     for copy in table_copies:
         copy.start()
 
-    def basis_copy(i):
-        part = pl.ds(i * PER_COPY, PER_COPY)
-        return pltpu.make_async_copy(basis.at[part], basis_v.at[part], basis_sem.at[i])
-
-    ahead = 1
-    for i in range(ahead):
-        basis_copy(i).start()
+    def panels_copy(group):
+        part = pl.ds(group * GROUP, GROUP)
+        return pltpu.make_async_copy(panels.at[:, part], panels_v.at[:, part], panel_sem.at[group])
+
+    def basis_copy(group, i):
+        part = pl.ds(group * GROUP + sum(COPIES[:i]), COPIES[i])
+        sem = basis_sem.at[group * len(COPIES) + i]
+        return pltpu.make_async_copy(basis.at[part], basis_v.at[part], sem)
+
+    for group in range(groups):
+        panels_copy(group).start()
+        for i in range(len(COPIES)):
+            basis_copy(group, i).start()
     for copy in table_copies:
         copy.wait()
 
-    per_group = GROUP // PER_COPY
-    for group in range(groups):
-        part = pl.ds(group * GROUP, GROUP)
-
-        @pl.loop(0, slots)
-        def _(m):
-            place = place_of(slot_s[m], owner_slots, half_slots)
-            if group == 0:
-                keep_place[place] = keep_s[m]
-                rows_place[place] = rows_s[m]
-            pltpu.make_async_copy(
-                panels.at[m, part], panels_v.at[place, part], panel_sem.at[group]
-            ).start()
-
-        for i in range(ahead + group * per_group, min(ahead + (group + 1) * per_group, groups * per_group)):
-            basis_copy(i).start()
+    @pl.loop(0, slots)
+    def _(m):
+        place = place_of(slot_s[m], owner_slots, half_slots)
+        order_place[place] = m
+        keep_place[place] = keep_s[m]
+        rows_place[place] = rows_s[m]
 
     offsets_of(keep_place, tile_place, shift_place, owner_slots)
     column = lax.broadcasted_iota(jnp.int32, slot_column.shape, 1)
@@ -183,21 +179,19 @@
 
     tables = (tile_place, shift_place, owner_slots)
     all_owners = range(mine.shape[0] * lax.axis_size("pa"))
-    share = len(all_owners) // per_group
 
     def group_step(group, out_v, out_before):
         here = pl.ds(pl.multiple_of(group * GROUP, GROUP), GROUP)
-        pltpu.make_async_copy(
-            panels_v.at[:, here], panels_v.at[:, here], panel_sem.at[group]
-        ).wait()
-        for block in range(slots // GROUP):
-            blocks = slice(block * GROUP, (block + 1) * GROUP)
-            tile = panels_v[blocks, here, :].reshape(side, depth)
+        panels_copy(group).wait()
+        for block in range(0, slots, GROUP):
+            tile = jnp.concatenate(
+                [panels_v[order_place[place], here, :] for place in range(block, block + GROUP)]
+            )
             turned = jnp.dot(swap, tile, preferred_element_type=jnp.float32).astype(jnp.bfloat16)
-            lhs_v[:, blocks, :] = turned.reshape(GROUP, GROUP, depth)
-        for i in range(per_group):
-            basis_copy(group * per_group + i).wait()
-            for f in range(i * PER_COPY, (i + 1) * PER_COPY):
+            lhs_v[:, block : block + GROUP, :] = turned.reshape(GROUP, GROUP, depth)
+        for i in range(len(COPIES)):
+            basis_copy(group, i).wait()
+            for f in range(sum(COPIES[:i]), sum(COPIES[: i + 1])):
                 product = jnp.dot(
                     lhs_v[f], basis_v[group * GROUP + f], preferred_element_type=jnp.float32
                 )
@@ -205,16 +199,16 @@
                     at = (t * GROUP + f) * slots
                     out_v[at : at + slots, :] = product[:, t * LANES : (t + 1) * LANES]
             line = jnp.maximum(group - 1, 0) * GROUP
-            pack(out_before, mine, far, near, line, tables, all_owners[i * share : (i + 1) * share])
+            share = len(all_owners) // len(COPIES)
+            part = all_owners[i * share : (i + 1) * share]
+            pack(out_before, mine, far, near, line, tables, part)
 
     @pl.loop(0, groups // 2)
     def _(pair):
         group_step(2 * pair, out_even, out_odd)
         group_step(2 * pair + 1, out_odd, out_even)
 
-    for i in range(per_group):
-        part = all_owners[i * share : (i + 1) * share]
-        pack(out_odd, mine, far, near, (groups - 1) * GROUP, tables, part)
+    pack(out_odd, mine, far, near, (groups - 1) * GROUP, tables, all_owners)
 
 
 def folded_rows(rows, width):
@@ -332,7 +326,7 @@
         ),
         in_specs=[HBM] * 5,
         out_specs=(VMEM,) * 6,
-        scratch_shapes=[pltpu.SMEM((slots,), jnp.int32)] * 7
+        scratch_shapes=[pltpu.SMEM((slots,), jnp.int32)] * 8
         + [
             pltpu.VMEM((slots, freqs, depth), jnp.bfloat16),
             pltpu.VMEM((freqs, depth, modes), jnp.bfloat16),
@@ -341,7 +335,7 @@
             pltpu.VMEM((modes // LANES * GROUP * slots, LANES), jnp.float32),
             pltpu.SemaphoreType.DMA((3,)),
             pltpu.SemaphoreType.DMA((freqs // GROUP,)),
-            pltpu.SemaphoreType.DMA((freqs // PER_COPY,)),
+            pltpu.SemaphoreType.DMA((freqs // GROUP * len(COPIES),)),
         ],
         compiler_params=pltpu.CompilerParams(vmem_limit_bytes=48 * MIB),
         cost_estimate=pl.CostEstimate(

time: 32.5 us -> 34.4 us (1.058)
  Pallas kernels: 15.7 us -> 17.6 us
    pallas_call x1, Pallas kernels: 13.6 us -> 15.5 us  [project(): pl.pallas_call(functools.partial(project_kernel, owner_slots), out_shape=...]
where the time goes in v14:
time: 34.4 us; the launch traced here: 34.3 us
  Pallas kernels  17.6 us (51%)
  starting transfers between devices  10.1 us (29%)
  waiting for transfers between devices  6.57 us (19%)
    pallas_call x1, Pallas kernels, project(): pl.pallas_call(functools.partial(project_kernel, owner_slots), out_shape=...  15.5 us
    ppermute x3, starting transfers between devices, shards(): lax.ppermute(summed[step], 'ma', ring(step))  7.71 us
    ppermute x3, waiting for transfers between devices, shards(): lax.ppermute(summed[step], 'ma', ring(step))  3.13 us
    ppermute x1, waiting for transfers between devices, shards(): got = lax.ppermute(send, 'af', pairs('af'))  2.41 us
    ppermute x1, starting transfers between devices, shards(): got = lax.ppermute(send, 'af', pairs('af'))  1.51 us
    pallas_call x1, Pallas kernels, unpack(): pl.pallas_call(unpack_kernel, out_shape=jax.ShapeDtypeStruct((owner_slots...  1.04 us
    ppermute x1, waiting for transfers between devices, shards(): got_far = lax.ppermute(far, 'pa', pairs('pa'))  1.03 us
    pallas_call x2, Pallas kernels, kl_project(): pl.pallas_call(functools.partial(kl_kernel, part, owners, width), out_sha...  0.89 us
  transfers between devices with their start and end apart: 6, of which 3 were waited for; matrix products, arithmetic and copies ran while one was open for 0% of the time, Pallas kernels for 2%

profile of v14, /device:TPU:0, one launch (start us, length us, event | category | flops | bytes accessed | tf_op | source)
XLA Modules:
  0.0 34.3 jit_solution(17725348844659733855)
XLA Ops:
  0.0 0.0 copy-start
  0.0 15.5 %project.1 = (f32[4,5,64,128]{3,2,1,0:T(8,128)S(1)}, f32[1,5,64,128]{3,2,1,0:T(8,128)S(1)}, f32[3,5,64,128]{3,2,1,0:T(8,128)S(1)}, s32[8,640]{1,0:T(8,128)S(1)},...) custom-call(s32[32]{0:T(128)} %slot_hbm.1, s32[32]{0:T(128)} %keep_hbm.1, s32[32]{0:T(128)} %rows_hbm.1, ...), custom_call_target="tpu_custom_call" | custom-call | flops 1073741824 | bytes 37748736 | tf_op jit(solution)/shard_map/project/pallas_call | solution.py:317
  15.5 0.5 %collective-permute-start = (f32[1,5,64,128]{3,2,1,0:T(8,128)S(1)}, f32[1,5,64,128]{3,2,1,0:T(8,128)S(1)}, u32[]{:S(2)}, u32[]{:S(2)}) collective-permute-start(f32[1,5,64,128]{3,2,1,0:T(8,128)S(1)} %get-tuple-element.21), channel_id=1, source_target_pairs={{0,1},{1,0},{2,3},{3,2},{4,5},{5,4},{6,7},{7,6},{8,9},{9,8},{10,11... | collective-permute-start | bytes 491528 | tf_op jit(solution)/shard_map/ppermute | solution.py:424
  16.0 1.0 %collective-permute-done.got = f32[1,5,64,128]{3,2,1,0:T(8,128)S(1)} collective-permute-done((f32[1,5,64,128]{3,2,1,0:T(8,128)S(1)}, f32[1,5,64,128]{3,2,1,0:T(8,128)S(1)}, u32[]{:S(2)}, u32[]{:S(2)}) %collective-permute-start) | collective-permute-done | bytes 163872 | tf_op jit(solution)/shard_map/ppermute | solution.py:424
  17.0 0.4 %collective-permute-start.1 = (f32[3,5,64,128]{3,2,1,0:T(8,128)S(1)}, f32[3,5,64,128]{3,2,1,0:T(8,128)S(1)}, u32[]{:S(2)}, u32[]{:S(2)}) collective-permute-start(f32[3,5,64,128]{3,2,1,0:T(8,128)S(1)} %get-tuple-element.22), channel_id=1, source_target_pairs={{0,1},{1,0},{2,3},{3,2},{4,5},{5,4},{6,7},{7,6},{8,9},{9,8},{10,11... | collective-permute-start | bytes 1474568 | tf_op jit(solution)/shard_map/ppermute | solution.py:426
  17.4 0.1 sum_pair.3
  17.5 4.8 %collective-permute-start.3 = (bf16[288,128]{1,0:T(8,128)(2,1)S(1)}, bf16[288,128]{1,0:T(8,128)(2,1)S(1)}, u32[]{:S(2)}, u32[]{:S(2)}) collective-permute-start(bf16[288,128]{1,0:T(8,128)(2,1)S(1)} %sum_pair.3), channel_id=1, source_target_pairs={{0,12},{4,8},{8,4},{12,0},{1,13},{5,9},{9,5},{13,1},{2,14},{6,10},... | collective-permute-start | bytes 221192 | tf_op jit(solution)/shard_map/ppermute | solution.py:430
  22.2 0.0 collective-permute-done.1.got
  22.2 0.1 sum_pair.2
  22.3 0.0 collective-permute-start.2
  22.4 2.9 %collective-permute-start.4 = (bf16[288,128]{1,0:T(8,128)(2,1)S(1)}, bf16[288,128]{1,0:T(8,128)(2,1)S(1)}, u32[]{:S(2)}, u32[]{:S(2)}) collective-permute-start(bf16[288,128]{1,0:T(8,128)(2,1)S(1)} %get-tuple-element.26), channel_id=1, source_target_pairs={{0,8},{4,0},{8,12},{12,4},{1,9},{5,1},{9,13},{13,5},{2,10},{6,2},{... | collective-permute-start | bytes 221192 | tf_op jit(solution)/shard_map/ppermute | solution.py:430
  25.3 0.0 collective-permute-done.3.refs_2_
  25.3 3.1 %collective-permute-done.2.refs_1_ = bf16[288,128]{1,0:T(8,128)(2,1)S(1)} collective-permute-done((bf16[288,128]{1,0:T(8,128)(2,1)S(1)}, bf16[288,128]{1,0:T(8,128)(2,1)S(1)}, u32[]{:S(2)}, u32[]{:S(2)}) %collective-permute-start.2) | collective-permute-done | bytes 73760 | tf_op jit(solution)/shard_map/ppermute | solution.py:430
  28.4 0.0 collective-permute-done.4.refs_3_
  28.4 0.0 copy-done
  28.4 0.4 %kl_project.3 = bf16[288,128]{1,0:T(8,128)(2,1)S(1)} custom-call(s32[8,640]{1,0:T(8,128)S(1)} %get-tuple-element.17.slot_column, s32[8,640]{1,0:T(8,128)S(1)} %get-tuple-element.18.rows_column, bf16[4,128,256]{2,1,0:T(8,128)(2,1)S(1)} %copy-done, bf16[288,128]{1,0:T(8,128)(2,1)S(1)} %get-tuple-element.23.refs_0_, ...), custom_call_target="tpu_custom_call" | custom-call | flops 83886080 | bytes 262144 | tf_op jit(solution)/shard_map/kl_project/pallas_call | solution.py:369
  28.9 1.5 %collective-permute-start.5 = (bf16[288,128]{1,0:T(8,128)(2,1)S(1)}, bf16[288,128]{1,0:T(8,128)(2,1)S(1)}, u32[]{:S(2)}, u32[]{:S(2)}) collective-permute-start(bf16[288,128]{1,0:T(8,128)(2,1)S(1)} %kl_project.3), channel_id=1, source_target_pairs={{0,2},{2,0},{1,3},{3,1},{4,6},{6,4},{5,7},{7,5},{8,10},{10,8},{9,1... | collective-permute-start | bytes 221192 | tf_op jit(solution)/shard_map/ppermute | solution.py:435
  30.4 0.4 %kl_project.2.mine = f32[288,128]{1,0:T(8,128)S(1)} custom-call(s32[8,640]{1,0:T(8,128)S(1)} %get-tuple-element.17.slot_column, s32[8,640]{1,0:T(8,128)S(1)} %get-tuple-element.18.rows_column, bf16[4,128,256]{2,1,0:T(8,128)(2,1)S(1)} %copy-done, bf16[288,128]{1,0:T(8,128)(2,1)S(1)} %get-tuple-element.23.refs_0_, ...), custom_call_target="tpu_custom_call" | custom-call | flops 83886080 | bytes 262144 | tf_op jit(solution)/shard_map/kl_project/pallas_call | solution.py:369
  30.8 2.4 %collective-permute-done.5.got = bf16[288,128]{1,0:T(8,128)(2,1)S(1)} collective-permute-done((bf16[288,128]{1,0:T(8,128)(2,1)S(1)}, bf16[288,128]{1,0:T(8,128)(2,1)S(1)}, u32[]{:S(2)}, u32[]{:S(2)}) %collective-permute-start.5) | collective-permute-done | bytes 73760 | tf_op jit(solution)/shard_map/ppermute | solution.py:435
  33.2 1.0 %unpack.1 = f32[4,64,256]{2,1,0:T(8,128)} custom-call(s32[8,128]{1,0:T(8,128)S(1)} %get-tuple-element.16.scalars, f32[288,128]{1,0:T(8,128)S(1)} %kl_project.2.mine, bf16[288,128]{1,0:T(8,128)(2,1)S(1)} %collective-permute-done.5.got), custom_call_target="tpu_custom_call" | custom-call | flops 36864 | bytes 368640 | tf_op jit(solution)/shard_map/unpack/pallas_call | solution.py:387
Async XLA Ops:
  0.0 28.4 %copy-start = (bf16[4,128,256]{2,1,0:T(8,128)(2,1)S(1)}, bf16[4,128,256]{2,1,0:T(8,128)(2,1)}, u32[]{:S(2)}) copy-start(bf16[4,128,256]{2,1,0:T(8,128)(2,1)} %kl.3) | copy-start | bytes 786436
  15.5 1.5 %collective-permute-start = (f32[1,5,64,128]{3,2,1,0:T(8,128)S(1)}, f32[1,5,64,128]{3,2,1,0:T(8,128)S(1)}, u32[]{:S(2)}, u32[]{:S(2)}) collective-permute-start(f32[1,5,64,128]{3,2,1,0:T(8,128)S(1)} %get-tuple-element.21), channel_id=1, source_target_pairs={{0,1},{1,0},{2,3},{3,2},{4,5},{5,4},{6,7},{7,6},{8,9},{9,8},{10,11... | collective-permute-start | bytes 491528 | tf_op jit(solution)/shard_map/ppermute | solution.py:424
  17.0 5.2 %collective-permute-start.1 = (f32[3,5,64,128]{3,2,1,0:T(8,128)S(1)}, f32[3,5,64,128]{3,2,1,0:T(8,128)S(1)}, u32[]{:S(2)}, u32[]{:S(2)}) collective-permute-start(f32[3,5,64,128]{3,2,1,0:T(8,128)S(1)} %get-tuple-element.22), channel_id=1, source_target_pairs={{0,1},{1,0},{2,3},{3,2},{4,5},{5,4},{6,7},{7,6},{8,9},{9,8},{10,11... | collective-permute-start | bytes 1474568 | tf_op jit(solution)/shard_map/ppermute | solution.py:426
  17.5 7.8 %collective-permute-start.3 = (bf16[288,128]{1,0:T(8,128)(2,1)S(1)}, bf16[288,128]{1,0:T(8,128)(2,1)S(1)}, u32[]{:S(2)}, u32[]{:S(2)}) collective-permute-start(bf16[288,128]{1,0:T(8,128)(2,1)S(1)} %sum_pair.3), channel_id=1, source_target_pairs={{0,12},{4,8},{8,4},{12,0},{1,13},{5,9},{9,5},{13,1},{2,14},{6,10},... | collective-permute-start | bytes 221192 | tf_op jit(solution)/shard_map/ppermute | solution.py:430
  22.3 6.1 %collective-permute-start.2 = (bf16[288,128]{1,0:T(8,128)(2,1)S(1)}, bf16[288,128]{1,0:T(8,128)(2,1)S(1)}, u32[]{:S(2)}, u32[]{:S(2)}) collective-permute-start(bf16[288,128]{1,0:T(8,128)(2,1)S(1)} %get-tuple-element.24), channel_id=1, source_target_pairs={{0,4},{4,12},{8,0},{12,8},{1,5},{5,13},{9,1},{13,9},{2,6},{6,14},{... | collective-permute-start | bytes 221192 | tf_op jit(solution)/shard_map/ppermute | solution.py:430
  22.4 6.0 %collective-permute-start.4 = (bf16[288,128]{1,0:T(8,128)(2,1)S(1)}, bf16[288,128]{1,0:T(8,128)(2,1)S(1)}, u32[]{:S(2)}, u32[]{:S(2)}) collective-permute-start(bf16[288,128]{1,0:T(8,128)(2,1)S(1)} %get-tuple-element.26), channel_id=1, source_target_pairs={{0,8},{4,0},{8,12},{12,4},{1,9},{5,1},{9,13},{13,5},{2,10},{6,2},{... | collective-permute-start | bytes 221192 | tf_op jit(solution)/shard_map/ppermute | solution.py:430
  28.9 4.4 %collective-permute-start.5 = (bf16[288,128]{1,0:T(8,128)(2,1)S(1)}, bf16[288,128]{1,0:T(8,128)(2,1)S(1)}, u32[]{:S(2)}, u32[]{:S(2)}) collective-permute-start(bf16[288,128]{1,0:T(8,128)(2,1)S(1)} %kl_project.3), channel_id=1, source_target_pairs={{0,2},{2,0},{1,3},{3,1},{4,6},{6,4},{5,7},{7,5},{8,10},{10,8},{9,1... | collective-permute-start | bytes 221192 | tf_op jit(solution)/shard_map/ppermute | solution.py:435

commit v15 on v14

--- a/solution.py
+++ b/solution.py
@@ -9,7 +9,7 @@
 
 LANES = 128
 GROUP = 16
-COPIES = (8, 8)
+TOGETHER = 8
 OWNER_BUDGET = 576
 MIB = 2**20
 
@@ -119,11 +119,11 @@
 def project_kernel(
     owner_slots, slot_hbm, keep_hbm, rows_hbm, panels, basis,
     mine, far, near, slot_column, rows_column, scalars,
-    slot_s, keep_s, rows_s, order_place, keep_place, rows_place, tile_place, shift_place,
+    slot_s, keep_s, rows_s, place_m, keep_place, rows_place, tile_place, shift_place,
     panels_v, basis_v, lhs_v, out_even, out_odd, small_sem, panel_sem, basis_sem,
 ):
     slots, freqs, depth = panels_v.shape
-    groups = freqs // GROUP
+    groups, waits = freqs // GROUP, GROUP // TOGETHER
     half_slots = slots // lax.axis_size("pa")
 
     table_copies = [
@@ -134,28 +134,41 @@
     for copy in table_copies:
         copy.start()
 
-    def panels_copy(group):
-        part = pl.ds(group * GROUP, GROUP)
-        return pltpu.make_async_copy(panels.at[:, part], panels_v.at[:, part], panel_sem.at[group])
-
-    def basis_copy(group, i):
-        part = pl.ds(group * GROUP + sum(COPIES[:i]), COPIES[i])
-        sem = basis_sem.at[group * len(COPIES) + i]
-        return pltpu.make_async_copy(basis.at[part], basis_v.at[part], sem)
-
-    for group in range(groups):
-        panels_copy(group).start()
-        for i in range(len(COPIES)):
-            basis_copy(group, i).start()
+    def start_basis(group, i):
+        first = group * GROUP + i * TOGETHER
+
+        @pl.loop(first, first + TOGETHER)
+        def _(f):
+            sem = basis_sem.at[group * waits + i]
+            pltpu.make_async_copy(basis.at[f], basis_v.at[f], sem).start()
+
+    def wait_basis(group, i):
+        part = pl.ds(group * GROUP + i * TOGETHER, TOGETHER)
+        sem = basis_sem.at[group * waits + i]
+        pltpu.make_async_copy(basis_v.at[part], basis_v.at[part], sem).wait()
+
+    start_basis(0, 0)
     for copy in table_copies:
         copy.wait()
 
     @pl.loop(0, slots)
     def _(m):
         place = place_of(slot_s[m], owner_slots, half_slots)
-        order_place[place] = m
+        place_m[m] = place
         keep_place[place] = keep_s[m]
         rows_place[place] = rows_s[m]
+
+    for group in range(groups):
+        part = pl.ds(group * GROUP, GROUP)
+
+        @pl.loop(0, slots)
+        def _(m):
+            pltpu.make_async_copy(
+                panels.at[m, part], panels_v.at[place_m[m], part], panel_sem.at[group]
+            ).start()
+
+        for i in range(1 if group == 0 else 0, waits):
+            start_basis(group, i)
 
     offsets_of(keep_place, tile_place, shift_place, owner_slots)
     column = lax.broadcasted_iota(jnp.int32, slot_column.shape, 1)
@@ -182,16 +195,16 @@
 
     def group_step(group, out_v, out_before):
         here = pl.ds(pl.multiple_of(group * GROUP, GROUP), GROUP)
-        panels_copy(group).wait()
+        pltpu.make_async_copy(
+            panels_v.at[:, here], panels_v.at[:, here], panel_sem.at[group]
+        ).wait()
         for block in range(0, slots, GROUP):
-            tile = jnp.concatenate(
-                [panels_v[order_place[place], here, :] for place in range(block, block + GROUP)]
-            )
+            tile = panels_v[block : block + GROUP, here, :].reshape(side, depth)
             turned = jnp.dot(swap, tile, preferred_element_type=jnp.float32).astype(jnp.bfloat16)
             lhs_v[:, block : block + GROUP, :] = turned.reshape(GROUP, GROUP, depth)
-        for i in range(len(COPIES)):
-            basis_copy(group, i).wait()
-            for f in range(sum(COPIES[:i]), sum(COPIES[: i + 1])):
+        for i in range(waits):
+            wait_basis(group, i)
+            for f in range(i * TOGETHER, (i + 1) * TOGETHER):
                 product = jnp.dot(
                     lhs_v[f], basis_v[group * GROUP + f], preferred_element_type=jnp.float32
                 )
@@ -199,7 +212,7 @@
                     at = (t * GROUP + f) * slots
                     out_v[at : at + slots, :] = product[:, t * LANES : (t + 1) * LANES]
             line = jnp.maximum(group - 1, 0) * GROUP
-            share = len(all_owners) // len(COPIES)
+            share = len(all_owners) // waits
             part = all_owners[i * share : (i + 1) * share]
             pack(out_before, mine, far, near, line, tables, part)
 
@@ -335,7 +348,7 @@
             pltpu.VMEM((modes // LANES * GROUP * slots, LANES), jnp.float32),
             pltpu.SemaphoreType.DMA((3,)),
             pltpu.SemaphoreType.DMA((freqs // GROUP,)),
-            pltpu.SemaphoreType.DMA((freqs // GROUP * len(COPIES),)),
+            pltpu.SemaphoreType.DMA((freqs // TOGETHER,)),
         ],
         compiler_params=pltpu.CompilerParams(vmem_limit_bytes=48 * MIB),
         cost_estimate=pl.CostEstimate(

time: 34.4 us -> 32.6 us (0.948)
  Pallas kernels: 17.6 us -> 15.8 us
    pallas_call x1, Pallas kernels: 15.5 us -> 13.7 us  [project(): pl.pallas_call(functools.partial(project_kernel, owner_slots), out_shape=...]
where the time goes in v15:
time: 32.6 us; the launch traced here: 32.5 us
  Pallas kernels  15.8 us (48%)
  starting transfers between devices  10.1 us (31%)
  waiting for transfers between devices  6.57 us (20%)
    pallas_call x1, Pallas kernels, project(): pl.pallas_call(functools.partial(project_kernel, owner_slots), out_shape=...  13.7 us
    ppermute x3, starting transfers between devices, shards(): lax.ppermute(summed[step], 'ma', ring(step))  7.72 us
    ppermute x3, waiting for transfers between devices, shards(): lax.ppermute(summed[step], 'ma', ring(step))  3.13 us
    ppermute x1, waiting for transfers between devices, shards(): got = lax.ppermute(send, 'af', pairs('af'))  2.42 us
    ppermute x1, starting transfers between devices, shards(): got = lax.ppermute(send, 'af', pairs('af'))  1.5 us
    pallas_call x1, Pallas kernels, unpack(): pl.pallas_call(unpack_kernel, out_shape=jax.ShapeDtypeStruct((owner_slots...  1.04 us
    ppermute x1, waiting for transfers between devices, shards(): got_far = lax.ppermute(far, 'pa', pairs('pa'))  1.03 us
    pallas_call x2, Pallas kernels, kl_project(): pl.pallas_call(functools.partial(kl_kernel, part, owners, width), out_sha...  0.89 us
  transfers between devices with their start and end apart: 6, of which 3 were waited for; matrix products, arithmetic and copies ran while one was open for 0% of the time, Pallas kernels for 2%

profile of v15, /device:TPU:0, one launch (start us, length us, event | category | flops | bytes accessed | tf_op | source)
XLA Modules:
  0.0 32.5 jit_solution(9268698994216042774)
XLA Ops:
  0.0 0.0 copy-start
  0.0 13.7 %project.1 = (f32[4,5,64,128]{3,2,1,0:T(8,128)S(1)}, f32[1,5,64,128]{3,2,1,0:T(8,128)S(1)}, f32[3,5,64,128]{3,2,1,0:T(8,128)S(1)}, s32[8,640]{1,0:T(8,128)S(1)},...) custom-call(s32[32]{0:T(128)} %slot_hbm.1, s32[32]{0:T(128)} %keep_hbm.1, s32[32]{0:T(128)} %rows_hbm.1, ...), custom_call_target="tpu_custom_call" | custom-call | flops 1073741824 | bytes 37748736 | tf_op jit(solution)/shard_map/project/pallas_call | solution.py:330
  13.7 0.5 %collective-permute-start = (f32[1,5,64,128]{3,2,1,0:T(8,128)S(1)}, f32[1,5,64,128]{3,2,1,0:T(8,128)S(1)}, u32[]{:S(2)}, u32[]{:S(2)}) collective-permute-start(f32[1,5,64,128]{3,2,1,0:T(8,128)S(1)} %get-tuple-element.21), channel_id=1, source_target_pairs={{0,1},{1,0},{2,3},{3,2},{4,5},{5,4},{6,7},{7,6},{8,9},{9,8},{10,11... | collective-permute-start | bytes 491528 | tf_op jit(solution)/shard_map/ppermute | solution.py:437
  14.2 1.0 %collective-permute-done.got = f32[1,5,64,128]{3,2,1,0:T(8,128)S(1)} collective-permute-done((f32[1,5,64,128]{3,2,1,0:T(8,128)S(1)}, f32[1,5,64,128]{3,2,1,0:T(8,128)S(1)}, u32[]{:S(2)}, u32[]{:S(2)}) %collective-permute-start) | collective-permute-done | bytes 163872 | tf_op jit(solution)/shard_map/ppermute | solution.py:437
  15.2 0.4 %collective-permute-start.1 = (f32[3,5,64,128]{3,2,1,0:T(8,128)S(1)}, f32[3,5,64,128]{3,2,1,0:T(8,128)S(1)}, u32[]{:S(2)}, u32[]{:S(2)}) collective-permute-start(f32[3,5,64,128]{3,2,1,0:T(8,128)S(1)} %get-tuple-element.22), channel_id=1, source_target_pairs={{0,1},{1,0},{2,3},{3,2},{4,5},{5,4},{6,7},{7,6},{8,9},{9,8},{10,11... | collective-permute-start | bytes 1474568 | tf_op jit(solution)/shard_map/ppermute | solution.py:439
  15.6 0.1 sum_pair.3
  15.7 4.8 %collective-permute-start.3 = (bf16[288,128]{1,0:T(8,128)(2,1)S(1)}, bf16[288,128]{1,0:T(8,128)(2,1)S(1)}, u32[]{:S(2)}, u32[]{:S(2)}) collective-permute-start(bf16[288,128]{1,0:T(8,128)(2,1)S(1)} %sum_pair.3), channel_id=1, source_target_pairs={{0,12},{4,8},{8,4},{12,0},{1,13},{5,9},{9,5},{13,1},{2,14},{6,10},... | collective-permute-start | bytes 221192 | tf_op jit(solution)/shard_map/ppermute | solution.py:443
  20.5 0.0 collective-permute-done.1.got
  20.5 0.1 sum_pair.2
  20.5 0.0 collective-permute-start.2
  20.6 2.9 %collective-permute-start.4 = (bf16[288,128]{1,0:T(8,128)(2,1)S(1)}, bf16[288,128]{1,0:T(8,128)(2,1)S(1)}, u32[]{:S(2)}, u32[]{:S(2)}) collective-permute-start(bf16[288,128]{1,0:T(8,128)(2,1)S(1)} %get-tuple-element.26), channel_id=1, source_target_pairs={{0,8},{4,0},{8,12},{12,4},{1,9},{5,1},{9,13},{13,5},{2,10},{6,2},{... | collective-permute-start | bytes 221192 | tf_op jit(solution)/shard_map/ppermute | solution.py:443
  23.5 0.0 collective-permute-done.3.refs_2_
  23.5 3.1 %collective-permute-done.2.refs_1_ = bf16[288,128]{1,0:T(8,128)(2,1)S(1)} collective-permute-done((bf16[288,128]{1,0:T(8,128)(2,1)S(1)}, bf16[288,128]{1,0:T(8,128)(2,1)S(1)}, u32[]{:S(2)}, u32[]{:S(2)}) %collective-permute-start.2) | collective-permute-done | bytes 73760 | tf_op jit(solution)/shard_map/ppermute | solution.py:443
  26.6 0.0 collective-permute-done.4.refs_3_
  26.6 0.0 copy-done
  26.6 0.4 %kl_project.3 = bf16[288,128]{1,0:T(8,128)(2,1)S(1)} custom-call(s32[8,640]{1,0:T(8,128)S(1)} %get-tuple-element.17.slot_column, s32[8,640]{1,0:T(8,128)S(1)} %get-tuple-element.18.rows_column, bf16[4,128,256]{2,1,0:T(8,128)(2,1)S(1)} %copy-done, bf16[288,128]{1,0:T(8,128)(2,1)S(1)} %get-tuple-element.23.refs_0_, ...), custom_call_target="tpu_custom_call" | custom-call | flops 83886080 | bytes 262144 | tf_op jit(solution)/shard_map/kl_project/pallas_call | solution.py:382
  27.1 1.5 %collective-permute-start.5 = (bf16[288,128]{1,0:T(8,128)(2,1)S(1)}, bf16[288,128]{1,0:T(8,128)(2,1)S(1)}, u32[]{:S(2)}, u32[]{:S(2)}) collective-permute-start(bf16[288,128]{1,0:T(8,128)(2,1)S(1)} %kl_project.3), channel_id=1, source_target_pairs={{0,2},{2,0},{1,3},{3,1},{4,6},{6,4},{5,7},{7,5},{8,10},{10,8},{9,1... | collective-permute-start | bytes 221192 | tf_op jit(solution)/shard_map/ppermute | solution.py:448
  28.6 0.4 %kl_project.2.mine = f32[288,128]{1,0:T(8,128)S(1)} custom-call(s32[8,640]{1,0:T(8,128)S(1)} %get-tuple-element.17.slot_column, s32[8,640]{1,0:T(8,128)S(1)} %get-tuple-element.18.rows_column, bf16[4,128,256]{2,1,0:T(8,128)(2,1)S(1)} %copy-done, bf16[288,128]{1,0:T(8,128)(2,1)S(1)} %get-tuple-element.23.refs_0_, ...), custom_call_target="tpu_custom_call" | custom-call | flops 83886080 | bytes 262144 | tf_op jit(solution)/shard_map/kl_project/pallas_call | solution.py:382
  29.0 2.4 %collective-permute-done.5.got = bf16[288,128]{1,0:T(8,128)(2,1)S(1)} collective-permute-done((bf16[288,128]{1,0:T(8,128)(2,1)S(1)}, bf16[288,128]{1,0:T(8,128)(2,1)S(1)}, u32[]{:S(2)}, u32[]{:S(2)}) %collective-permute-start.5) | collective-permute-done | bytes 73760 | tf_op jit(solution)/shard_map/ppermute | solution.py:448
  31.4 1.0 %unpack.1 = f32[4,64,256]{2,1,0:T(8,128)} custom-call(s32[8,128]{1,0:T(8,128)S(1)} %get-tuple-element.16.scalars, f32[288,128]{1,0:T(8,128)S(1)} %kl_project.2.mine, bf16[288,128]{1,0:T(8,128)(2,1)S(1)} %collective-permute-done.5.got), custom_call_target="tpu_custom_call" | custom-call | flops 36864 | bytes 368640 | tf_op jit(solution)/shard_map/unpack/pallas_call | solution.py:400
Async XLA Ops:
  0.0 26.6 %copy-start = (bf16[4,128,256]{2,1,0:T(8,128)(2,1)S(1)}, bf16[4,128,256]{2,1,0:T(8,128)(2,1)}, u32[]{:S(2)}) copy-start(bf16[4,128,256]{2,1,0:T(8,128)(2,1)} %kl.3) | copy-start | bytes 786436
  13.7 1.5 %collective-permute-start = (f32[1,5,64,128]{3,2,1,0:T(8,128)S(1)}, f32[1,5,64,128]{3,2,1,0:T(8,128)S(1)}, u32[]{:S(2)}, u32[]{:S(2)}) collective-permute-start(f32[1,5,64,128]{3,2,1,0:T(8,128)S(1)} %get-tuple-element.21), channel_id=1, source_target_pairs={{0,1},{1,0},{2,3},{3,2},{4,5},{5,4},{6,7},{7,6},{8,9},{9,8},{10,11... | collective-permute-start | bytes 491528 | tf_op jit(solution)/shard_map/ppermute | solution.py:437
  15.2 5.2 %collective-permute-start.1 = (f32[3,5,64,128]{3,2,1,0:T(8,128)S(1)}, f32[3,5,64,128]{3,2,1,0:T(8,128)S(1)}, u32[]{:S(2)}, u32[]{:S(2)}) collective-permute-start(f32[3,5,64,128]{3,2,1,0:T(8,128)S(1)} %get-tuple-element.22), channel_id=1, source_target_pairs={{0,1},{1,0},{2,3},{3,2},{4,5},{5,4},{6,7},{7,6},{8,9},{9,8},{10,11... | collective-permute-start | bytes 1474568 | tf_op jit(solution)/shard_map/ppermute | solution.py:439
  15.7 7.8 %collective-permute-start.3 = (bf16[288,128]{1,0:T(8,128)(2,1)S(1)}, bf16[288,128]{1,0:T(8,128)(2,1)S(1)}, u32[]{:S(2)}, u32[]{:S(2)}) collective-permute-start(bf16[288,128]{1,0:T(8,128)(2,1)S(1)} %sum_pair.3), channel_id=1, source_target_pairs={{0,12},{4,8},{8,4},{12,0},{1,13},{5,9},{9,5},{13,1},{2,14},{6,10},... | collective-permute-start | bytes 221192 | tf_op jit(solution)/shard_map/ppermute | solution.py:443
  20.5 6.1 %collective-permute-start.2 = (bf16[288,128]{1,0:T(8,128)(2,1)S(1)}, bf16[288,128]{1,0:T(8,128)(2,1)S(1)}, u32[]{:S(2)}, u32[]{:S(2)}) collective-permute-start(bf16[288,128]{1,0:T(8,128)(2,1)S(1)} %get-tuple-element.24), channel_id=1, source_target_pairs={{0,4},{4,12},{8,0},{12,8},{1,5},{5,13},{9,1},{13,9},{2,6},{6,14},{... | collective-permute-start | bytes 221192 | tf_op jit(solution)/shard_map/ppermute | solution.py:443
  20.6 6.0 %collective-permute-start.4 = (bf16[288,128]{1,0:T(8,128)(2,1)S(1)}, bf16[288,128]{1,0:T(8,128)(2,1)S(1)}, u32[]{:S(2)}, u32[]{:S(2)}) collective-permute-start(bf16[288,128]{1,0:T(8,128)(2,1)S(1)} %get-tuple-element.26), channel_id=1, source_target_pairs={{0,8},{4,0},{8,12},{12,4},{1,9},{5,1},{9,13},{13,5},{2,10},{6,2},{... | collective-permute-start | bytes 221192 | tf_op jit(solution)/shard_map/ppermute | solution.py:443
  27.1 4.4 %collective-permute-start.5 = (bf16[288,128]{1,0:T(8,128)(2,1)S(1)}, bf16[288,128]{1,0:T(8,128)(2,1)S(1)}, u32[]{:S(2)}, u32[]{:S(2)}) collective-permute-start(bf16[288,128]{1,0:T(8,128)(2,1)S(1)} %kl_project.3), channel_id=1, source_target_pairs={{0,2},{2,0},{1,3},{3,1},{4,6},{6,4},{5,7},{7,5},{8,10},{10,8},{9,1... | collective-permute-start | bytes 221192 | tf_op jit(solution)/shard_map/ppermute | solution.py:448

commit v16 on v10

--- a/solution.py
+++ b/solution.py
@@ -82,7 +82,7 @@
     slots = 2 * owners * owner_slots
     tiles = out_v.shape[0] // (GROUP * slots)
     lane = lax.broadcasted_iota(jnp.int32, (GROUP, LANES), 1)
-    rows = pl.ds(pl.multiple_of(line, GROUP), GROUP)
+    rows = slice(line, line + GROUP)
     turned = {
         place: pltpu.roll(
             out_v[pl.ds(place, tiles * GROUP, stride=slots), :], shift_place[place], 1
@@ -186,7 +186,7 @@
     share = len(all_owners) // per_group
 
     def group_step(group, out_v, out_before):
-        here = pl.ds(pl.multiple_of(group * GROUP, GROUP), GROUP)
+        here = slice(group * GROUP, (group + 1) * GROUP)
         pltpu.make_async_copy(
             panels_v.at[:, here], panels_v.at[:, here], panel_sem.at[group]
         ).wait()
@@ -204,17 +204,17 @@
                 for t in range(product.shape[1] // LANES):
                     at = (t * GROUP + f) * slots
                     out_v[at : at + slots, :] = product[:, t * LANES : (t + 1) * LANES]
-            line = jnp.maximum(group - 1, 0) * GROUP
-            pack(out_before, mine, far, near, line, tables, all_owners[i * share : (i + 1) * share])
-
-    @pl.loop(0, groups // 2)
-    def _(pair):
-        group_step(2 * pair, out_even, out_odd)
-        group_step(2 * pair + 1, out_odd, out_even)
+            if group > 0:
+                line = (group - 1) * GROUP
+                pack(out_before, mine, far, near, line, tables, all_owners[i * share : (i + 1) * share])
+
+    outs = (out_even, out_odd)
+    for group in range(groups):
+        group_step(group, outs[group % 2], outs[(group + 1) % 2])
 
     for i in range(per_group):
         part = all_owners[i * share : (i + 1) * share]
-        pack(out_odd, mine, far, near, (groups - 1) * GROUP, tables, part)
+        pack(outs[(groups - 1) % 2], mine, far, near, (groups - 1) * GROUP, tables, part)
 
 
 def folded_rows(rows, width):
@@ -451,7 +451,8 @@
     owner_slots = kl_basis.shape[0] // (mesh.shape["pa"] * mesh.shape["ma"])
     share_rows = kl_basis.shape[1] // mesh.shape["af"]
     return (
-        freqs % (2 * GROUP) == 0
+        freqs % GROUP == 0
+        and freqs <= 8 * GROUP
         and slots % (GROUP * mesh.shape["pa"]) == 0
         and owner_slots == 4
         and svd_basis.shape[2] == 2 * LANES

time: 32.5 us -> 32.5 us (level)
  no operation moved by 1% of the time
where the time goes in v16:
time: 32.5 us; the launch traced here: 32.4 us
  Pallas kernels  15.7 us (48%)
  starting transfers between devices  10.1 us (31%)
  waiting for transfers between devices  6.57 us (20%)
    pallas_call x1, Pallas kernels, project(): pl.pallas_call(functools.partial(project_kernel, owner_slots), out_shape=...  13.6 us
    ppermute x3, starting transfers between devices, shards(): lax.ppermute(summed[step], 'ma', ring(step))  7.72 us
    ppermute x3, waiting for transfers between devices, shards(): lax.ppermute(summed[step], 'ma', ring(step))  3.13 us
    ppermute x1, waiting for transfers between devices, shards(): got = lax.ppermute(send, 'af', pairs('af'))  2.42 us
    ppermute x1, starting transfers between devices, shards(): got = lax.ppermute(send, 'af', pairs('af'))  1.5 us
    pallas_call x1, Pallas kernels, unpack(): pl.pallas_call(unpack_kernel, out_shape=jax.ShapeDtypeStruct((owner_slots...  1.04 us
    ppermute x1, waiting for transfers between devices, shards(): got_far = lax.ppermute(far, 'pa', pairs('pa'))  1.03 us
    pallas_call x2, Pallas kernels, kl_project(): pl.pallas_call(functools.partial(kl_kernel, part, owners, width), out_sha...  0.89 us
  transfers between devices with their start and end apart: 6, of which 3 were waited for; matrix products, arithmetic and copies ran while one was open for 0% of the time, Pallas kernels for 2%

profile of v16, /device:TPU:0, one launch (start us, length us, event | category | flops | bytes accessed | tf_op | source)
XLA Modules:
  0.0 32.4 jit_solution(9598572535777553958)
XLA Ops:
  0.0 0.0 copy-start
  0.0 13.6 %project.1 = (f32[4,5,64,128]{3,2,1,0:T(8,128)S(1)}, f32[1,5,64,128]{3,2,1,0:T(8,128)S(1)}, f32[3,5,64,128]{3,2,1,0:T(8,128)S(1)}, s32[8,640]{1,0:T(8,128)S(1)},...) custom-call(s32[32]{0:T(128)} %slot_hbm.1, s32[32]{0:T(128)} %keep_hbm.1, s32[32]{0:T(128)} %rows_hbm.1, ...), custom_call_target="tpu_custom_call" | custom-call | flops 1073741824 | bytes 37748736 | tf_op jit(solution)/shard_map/project/pallas_call | solution.py:323
  13.6 0.5 %collective-permute-start = (f32[1,5,64,128]{3,2,1,0:T(8,128)S(1)}, f32[1,5,64,128]{3,2,1,0:T(8,128)S(1)}, u32[]{:S(2)}, u32[]{:S(2)}) collective-permute-start(f32[1,5,64,128]{3,2,1,0:T(8,128)S(1)} %get-tuple-element.21), channel_id=1, source_target_pairs={{0,1},{1,0},{2,3},{3,2},{4,5},{5,4},{6,7},{7,6},{8,9},{9,8},{10,11... | collective-permute-start | bytes 491528 | tf_op jit(solution)/shard_map/ppermute | solution.py:430
  14.1 1.0 %collective-permute-done.got = f32[1,5,64,128]{3,2,1,0:T(8,128)S(1)} collective-permute-done((f32[1,5,64,128]{3,2,1,0:T(8,128)S(1)}, f32[1,5,64,128]{3,2,1,0:T(8,128)S(1)}, u32[]{:S(2)}, u32[]{:S(2)}) %collective-permute-start) | collective-permute-done | bytes 163872 | tf_op jit(solution)/shard_map/ppermute | solution.py:430
  15.1 0.4 %collective-permute-start.1 = (f32[3,5,64,128]{3,2,1,0:T(8,128)S(1)}, f32[3,5,64,128]{3,2,1,0:T(8,128)S(1)}, u32[]{:S(2)}, u32[]{:S(2)}) collective-permute-start(f32[3,5,64,128]{3,2,1,0:T(8,128)S(1)} %get-tuple-element.22), channel_id=1, source_target_pairs={{0,1},{1,0},{2,3},{3,2},{4,5},{5,4},{6,7},{7,6},{8,9},{9,8},{10,11... | collective-permute-start | bytes 1474568 | tf_op jit(solution)/shard_map/ppermute | solution.py:432
  15.5 0.1 sum_pair.3
  15.6 4.8 %collective-permute-start.3 = (bf16[288,128]{1,0:T(8,128)(2,1)S(1)}, bf16[288,128]{1,0:T(8,128)(2,1)S(1)}, u32[]{:S(2)}, u32[]{:S(2)}) collective-permute-start(bf16[288,128]{1,0:T(8,128)(2,1)S(1)} %sum_pair.3), channel_id=1, source_target_pairs={{0,12},{4,8},{8,4},{12,0},{1,13},{5,9},{9,5},{13,1},{2,14},{6,10},... | collective-permute-start | bytes 221192 | tf_op jit(solution)/shard_map/ppermute | solution.py:436
  20.3 0.0 collective-permute-done.1.got
  20.4 0.1 sum_pair.2
  20.4 0.0 collective-permute-start.2
  20.5 2.9 %collective-permute-start.4 = (bf16[288,128]{1,0:T(8,128)(2,1)S(1)}, bf16[288,128]{1,0:T(8,128)(2,1)S(1)}, u32[]{:S(2)}, u32[]{:S(2)}) collective-permute-start(bf16[288,128]{1,0:T(8,128)(2,1)S(1)} %get-tuple-element.26), channel_id=1, source_target_pairs={{0,8},{4,0},{8,12},{12,4},{1,9},{5,1},{9,13},{13,5},{2,10},{6,2},{... | collective-permute-start | bytes 221192 | tf_op jit(solution)/shard_map/ppermute | solution.py:436
  23.4 0.0 collective-permute-done.3.refs_2_
  23.4 3.1 %collective-permute-done.2.refs_1_ = bf16[288,128]{1,0:T(8,128)(2,1)S(1)} collective-permute-done((bf16[288,128]{1,0:T(8,128)(2,1)S(1)}, bf16[288,128]{1,0:T(8,128)(2,1)S(1)}, u32[]{:S(2)}, u32[]{:S(2)}) %collective-permute-start.2) | collective-permute-done | bytes 73760 | tf_op jit(solution)/shard_map/ppermute | solution.py:436
  26.5 0.0 collective-permute-done.4.refs_3_
  26.5 0.0 copy-done
  26.5 0.4 %kl_project.3 = bf16[288,128]{1,0:T(8,128)(2,1)S(1)} custom-call(s32[8,640]{1,0:T(8,128)S(1)} %get-tuple-element.17.slot_column, s32[8,640]{1,0:T(8,128)S(1)} %get-tuple-element.18.rows_column, bf16[4,128,256]{2,1,0:T(8,128)(2,1)S(1)} %copy-done, bf16[288,128]{1,0:T(8,128)(2,1)S(1)} %get-tuple-element.23.refs_0_, ...), custom_call_target="tpu_custom_call" | custom-call | flops 83886080 | bytes 262144 | tf_op jit(solution)/shard_map/kl_project/pallas_call | solution.py:375
  27.0 1.5 %collective-permute-start.5 = (bf16[288,128]{1,0:T(8,128)(2,1)S(1)}, bf16[288,128]{1,0:T(8,128)(2,1)S(1)}, u32[]{:S(2)}, u32[]{:S(2)}) collective-permute-start(bf16[288,128]{1,0:T(8,128)(2,1)S(1)} %kl_project.3), channel_id=1, source_target_pairs={{0,2},{2,0},{1,3},{3,1},{4,6},{6,4},{5,7},{7,5},{8,10},{10,8},{9,1... | collective-permute-start | bytes 221192 | tf_op jit(solution)/shard_map/ppermute | solution.py:441
  28.5 0.4 %kl_project.2.mine = f32[288,128]{1,0:T(8,128)S(1)} custom-call(s32[8,640]{1,0:T(8,128)S(1)} %get-tuple-element.17.slot_column, s32[8,640]{1,0:T(8,128)S(1)} %get-tuple-element.18.rows_column, bf16[4,128,256]{2,1,0:T(8,128)(2,1)S(1)} %copy-done, bf16[288,128]{1,0:T(8,128)(2,1)S(1)} %get-tuple-element.23.refs_0_, ...), custom_call_target="tpu_custom_call" | custom-call | flops 83886080 | bytes 262144 | tf_op jit(solution)/shard_map/kl_project/pallas_call | solution.py:375
  28.9 2.4 %collective-permute-done.5.got = bf16[288,128]{1,0:T(8,128)(2,1)S(1)} collective-permute-done((bf16[288,128]{1,0:T(8,128)(2,1)S(1)}, bf16[288,128]{1,0:T(8,128)(2,1)S(1)}, u32[]{:S(2)}, u32[]{:S(2)}) %collective-permute-start.5) | collective-permute-done | bytes 73760 | tf_op jit(solution)/shard_map/ppermute | solution.py:441
  31.3 1.0 %unpack.1 = f32[4,64,256]{2,1,0:T(8,128)} custom-call(s32[8,128]{1,0:T(8,128)S(1)} %get-tuple-element.16.scalars, f32[288,128]{1,0:T(8,128)S(1)} %kl_project.2.mine, bf16[288,128]{1,0:T(8,128)(2,1)S(1)} %collective-permute-done.5.got), custom_call_target="tpu_custom_call" | custom-call | flops 36864 | bytes 368640 | tf_op jit(solution)/shard_map/unpack/pallas_call | solution.py:393
Async XLA Ops:
  0.0 26.5 %copy-start = (bf16[4,128,256]{2,1,0:T(8,128)(2,1)S(1)}, bf16[4,128,256]{2,1,0:T(8,128)(2,1)}, u32[]{:S(2)}) copy-start(bf16[4,128,256]{2,1,0:T(8,128)(2,1)} %kl.3) | copy-start | bytes 786436
  13.6 1.5 %collective-permute-start = (f32[1,5,64,128]{3,2,1,0:T(8,128)S(1)}, f32[1,5,64,128]{3,2,1,0:T(8,128)S(1)}, u32[]{:S(2)}, u32[]{:S(2)}) collective-permute-start(f32[1,5,64,128]{3,2,1,0:T(8,128)S(1)} %get-tuple-element.21), channel_id=1, source_target_pairs={{0,1},{1,0},{2,3},{3,2},{4,5},{5,4},{6,7},{7,6},{8,9},{9,8},{10,11... | collective-permute-start | bytes 491528 | tf_op jit(solution)/shard_map/ppermute | solution.py:430
  15.1 5.2 %collective-permute-start.1 = (f32[3,5,64,128]{3,2,1,0:T(8,128)S(1)}, f32[3,5,64,128]{3,2,1,0:T(8,128)S(1)}, u32[]{:S(2)}, u32[]{:S(2)}) collective-permute-start(f32[3,5,64,128]{3,2,1,0:T(8,128)S(1)} %get-tuple-element.22), channel_id=1, source_target_pairs={{0,1},{1,0},{2,3},{3,2},{4,5},{5,4},{6,7},{7,6},{8,9},{9,8},{10,11... | collective-permute-start | bytes 1474568 | tf_op jit(solution)/shard_map/ppermute | solution.py:432
  15.6 7.8 %collective-permute-start.3 = (bf16[288,128]{1,0:T(8,128)(2,1)S(1)}, bf16[288,128]{1,0:T(8,128)(2,1)S(1)}, u32[]{:S(2)}, u32[]{:S(2)}) collective-permute-start(bf16[288,128]{1,0:T(8,128)(2,1)S(1)} %sum_pair.3), channel_id=1, source_target_pairs={{0,12},{4,8},{8,4},{12,0},{1,13},{5,9},{9,5},{13,1},{2,14},{6,10},... | collective-permute-start | bytes 221192 | tf_op jit(solution)/shard_map/ppermute | solution.py:436
  20.4 6.1 %collective-permute-start.2 = (bf16[288,128]{1,0:T(8,128)(2,1)S(1)}, bf16[288,128]{1,0:T(8,128)(2,1)S(1)}, u32[]{:S(2)}, u32[]{:S(2)}) collective-permute-start(bf16[288,128]{1,0:T(8,128)(2,1)S(1)} %get-tuple-element.24), channel_id=1, source_target_pairs={{0,4},{4,12},{8,0},{12,8},{1,5},{5,13},{9,1},{13,9},{2,6},{6,14},{... | collective-permute-start | bytes 221192 | tf_op jit(solution)/shard_map/ppermute | solution.py:436
  20.5 6.0 %collective-permute-start.4 = (bf16[288,128]{1,0:T(8,128)(2,1)S(1)}, bf16[288,128]{1,0:T(8,128)(2,1)S(1)}, u32[]{:S(2)}, u32[]{:S(2)}) collective-permute-start(bf16[288,128]{1,0:T(8,128)(2,1)S(1)} %get-tuple-element.26), channel_id=1, source_target_pairs={{0,8},{4,0},{8,12},{12,4},{1,9},{5,1},{9,13},{13,5},{2,10},{6,2},{... | collective-permute-start | bytes 221192 | tf_op jit(solution)/shard_map/ppermute | solution.py:436
  27.0 4.4 %collective-permute-start.5 = (bf16[288,128]{1,0:T(8,128)(2,1)S(1)}, bf16[288,128]{1,0:T(8,128)(2,1)S(1)}, u32[]{:S(2)}, u32[]{:S(2)}) collective-permute-start(bf16[288,128]{1,0:T(8,128)(2,1)S(1)} %kl_project.3), channel_id=1, source_target_pairs={{0,2},{2,0},{1,3},{3,1},{4,6},{6,4},{5,7},{7,5},{8,10},{10,8},{9,1... | collective-permute-start | bytes 221192 | tf_op jit(solution)/shard_map/ppermute | solution.py:441

commit v17 on v10

--- a/solution.py
+++ b/solution.py
@@ -9,6 +9,7 @@
 
 LANES = 128
 GROUP = 16
+BATCH = 2
 PER_COPY = 8
 OWNER_BUDGET = 576
 MIB = 2**20
@@ -77,6 +78,11 @@
 
 
 def pack(out_v, mine, far, near, line, tables, owners_at):
+    for i in range(0, len(owners_at), BATCH):
+        pack_batch(out_v, mine, far, near, line, tables, owners_at[i : i + BATCH])
+
+
+def pack_batch(out_v, mine, far, near, line, tables, owners_at):
     tile_place, shift_place, owner_slots = tables
     owners, width_tiles = mine.shape[:2]
     slots = 2 * owners * owner_slots
@@ -119,7 +125,7 @@
 def project_kernel(
     owner_slots, slot_hbm, keep_hbm, rows_hbm, panels, basis,
     mine, far, near, slot_column, rows_column, scalars,
-    slot_s, keep_s, rows_s, keep_place, rows_place, tile_place, shift_place,
+    slot_s, keep_s, rows_s, place_m, keep_place, rows_place, tile_place, shift_place,
     panels_v, basis_v, lhs_v, out_even, out_odd, small_sem, panel_sem, basis_sem,
 ):
     slots, freqs, depth = panels_v.shape
@@ -144,18 +150,21 @@
     for copy in table_copies:
         copy.wait()
 
+    @pl.loop(0, slots)
+    def _(m):
+        place = place_of(slot_s[m], owner_slots, half_slots)
+        place_m[m] = place
+        keep_place[place] = keep_s[m]
+        rows_place[place] = rows_s[m]
+
     per_group = GROUP // PER_COPY
     for group in range(groups):
         part = pl.ds(group * GROUP, GROUP)
 
         @pl.loop(0, slots)
         def _(m):
-            place = place_of(slot_s[m], owner_slots, half_slots)
-            if group == 0:
-                keep_place[place] = keep_s[m]
-                rows_place[place] = rows_s[m]
             pltpu.make_async_copy(
-                panels.at[m, part], panels_v.at[place, part], panel_sem.at[group]
+                panels.at[m, part], panels_v.at[place_m[m], part], panel_sem.at[group]
             ).start()
 
         for i in range(ahead + group * per_group, min(ahead + (group + 1) * per_group, groups * per_group)):
@@ -332,7 +341,7 @@
         ),
         in_specs=[HBM] * 5,
         out_specs=(VMEM,) * 6,
-        scratch_shapes=[pltpu.SMEM((slots,), jnp.int32)] * 7
+        scratch_shapes=[pltpu.SMEM((slots,), jnp.int32)] * 8
         + [
             pltpu.VMEM((slots, freqs, depth), jnp.bfloat16),
             pltpu.VMEM((freqs, depth, modes), jnp.bfloat16),

time: 32.5 us -> 33.7 us (1.037)
  Pallas kernels: 15.7 us -> 16.8 us
    pallas_call x1, Pallas kernels: 13.6 us -> 14.7 us  [project(): pl.pallas_call(functools.partial(project_kernel, owner_slots), out_shape=...]
where the time goes in v17:
time: 33.7 us; the launch traced here: 33.5 us
  Pallas kernels  16.8 us (50%)
  starting transfers between devices  10.1 us (30%)
  waiting for transfers between devices  6.58 us (20%)
    pallas_call x1, Pallas kernels, project(): pl.pallas_call(functools.partial(project_kernel, owner_slots), out_shape=...  14.7 us
    ppermute x3, starting transfers between devices, shards(): lax.ppermute(summed[step], 'ma', ring(step))  7.72 us
    ppermute x3, waiting for transfers between devices, shards(): lax.ppermute(summed[step], 'ma', ring(step))  3.13 us
    ppermute x1, waiting for transfers between devices, shards(): got = lax.ppermute(send, 'af', pairs('af'))  2.42 us
    ppermute x1, starting transfers between devices, shards(): got = lax.ppermute(send, 'af', pairs('af'))  1.5 us
    pallas_call x1, Pallas kernels, unpack(): pl.pallas_call(unpack_kernel, out_shape=jax.ShapeDtypeStruct((owner_slots...  1.04 us
    ppermute x1, waiting for transfers between devices, shards(): got_far = lax.ppermute(far, 'pa', pairs('pa'))  1.03 us
    pallas_call x2, Pallas kernels, kl_project(): pl.pallas_call(functools.partial(kl_kernel, part, owners, width), out_sha...  0.89 us
  transfers between devices with their start and end apart: 6, of which 3 were waited for; matrix products, arithmetic and copies ran while one was open for 0% of the time, Pallas kernels for 2%

profile of v17, /device:TPU:0, one launch (start us, length us, event | category | flops | bytes accessed | tf_op | source)
XLA Modules:
  0.0 33.5 jit_solution(1260400463345065482)
XLA Ops:
  0.0 0.0 copy-start
  0.0 14.7 %project.1 = (f32[4,5,64,128]{3,2,1,0:T(8,128)S(1)}, f32[1,5,64,128]{3,2,1,0:T(8,128)S(1)}, f32[3,5,64,128]{3,2,1,0:T(8,128)S(1)}, s32[8,640]{1,0:T(8,128)S(1)},...) custom-call(s32[32]{0:T(128)} %slot_hbm.1, s32[32]{0:T(128)} %keep_hbm.1, s32[32]{0:T(128)} %rows_hbm.1, ...), custom_call_target="tpu_custom_call" | custom-call | flops 1073741824 | bytes 37748736 | tf_op jit(solution)/shard_map/project/pallas_call | solution.py:332
  14.7 0.5 %collective-permute-start = (f32[1,5,64,128]{3,2,1,0:T(8,128)S(1)}, f32[1,5,64,128]{3,2,1,0:T(8,128)S(1)}, u32[]{:S(2)}, u32[]{:S(2)}) collective-permute-start(f32[1,5,64,128]{3,2,1,0:T(8,128)S(1)} %get-tuple-element.21), channel_id=1, source_target_pairs={{0,1},{1,0},{2,3},{3,2},{4,5},{5,4},{6,7},{7,6},{8,9},{9,8},{10,11... | collective-permute-start | bytes 491528 | tf_op jit(solution)/shard_map/ppermute | solution.py:439
  15.2 1.0 %collective-permute-done.got = f32[1,5,64,128]{3,2,1,0:T(8,128)S(1)} collective-permute-done((f32[1,5,64,128]{3,2,1,0:T(8,128)S(1)}, f32[1,5,64,128]{3,2,1,0:T(8,128)S(1)}, u32[]{:S(2)}, u32[]{:S(2)}) %collective-permute-start) | collective-permute-done | bytes 163872 | tf_op jit(solution)/shard_map/ppermute | solution.py:439
  16.3 0.4 %collective-permute-start.1 = (f32[3,5,64,128]{3,2,1,0:T(8,128)S(1)}, f32[3,5,64,128]{3,2,1,0:T(8,128)S(1)}, u32[]{:S(2)}, u32[]{:S(2)}) collective-permute-start(f32[3,5,64,128]{3,2,1,0:T(8,128)S(1)} %get-tuple-element.22), channel_id=1, source_target_pairs={{0,1},{1,0},{2,3},{3,2},{4,5},{5,4},{6,7},{7,6},{8,9},{9,8},{10,11... | collective-permute-start | bytes 1474568 | tf_op jit(solution)/shard_map/ppermute | solution.py:441
  16.6 0.1 sum_pair.3
  16.7 4.8 %collective-permute-start.3 = (bf16[288,128]{1,0:T(8,128)(2,1)S(1)}, bf16[288,128]{1,0:T(8,128)(2,1)S(1)}, u32[]{:S(2)}, u32[]{:S(2)}) collective-permute-start(bf16[288,128]{1,0:T(8,128)(2,1)S(1)} %sum_pair.3), channel_id=1, source_target_pairs={{0,12},{4,8},{8,4},{12,0},{1,13},{5,9},{9,5},{13,1},{2,14},{6,10},... | collective-permute-start | bytes 221192 | tf_op jit(solution)/shard_map/ppermute | solution.py:445
  21.5 0.0 collective-permute-done.1.got
  21.5 0.1 sum_pair.2
  21.6 0.0 collective-permute-start.2
  21.6 2.9 %collective-permute-start.4 = (bf16[288,128]{1,0:T(8,128)(2,1)S(1)}, bf16[288,128]{1,0:T(8,128)(2,1)S(1)}, u32[]{:S(2)}, u32[]{:S(2)}) collective-permute-start(bf16[288,128]{1,0:T(8,128)(2,1)S(1)} %get-tuple-element.26), channel_id=1, source_target_pairs={{0,8},{4,0},{8,12},{12,4},{1,9},{5,1},{9,13},{13,5},{2,10},{6,2},{... | collective-permute-start | bytes 221192 | tf_op jit(solution)/shard_map/ppermute | solution.py:445
  24.5 0.0 collective-permute-done.3.refs_2_
  24.5 3.1 %collective-permute-done.2.refs_1_ = bf16[288,128]{1,0:T(8,128)(2,1)S(1)} collective-permute-done((bf16[288,128]{1,0:T(8,128)(2,1)S(1)}, bf16[288,128]{1,0:T(8,128)(2,1)S(1)}, u32[]{:S(2)}, u32[]{:S(2)}) %collective-permute-start.2) | collective-permute-done | bytes 73760 | tf_op jit(solution)/shard_map/ppermute | solution.py:445
  27.7 0.0 collective-permute-done.4.refs_3_
  27.7 0.0 copy-done
  27.7 0.4 %kl_project.3 = bf16[288,128]{1,0:T(8,128)(2,1)S(1)} custom-call(s32[8,640]{1,0:T(8,128)S(1)} %get-tuple-element.17.slot_column, s32[8,640]{1,0:T(8,128)S(1)} %get-tuple-element.18.rows_column, bf16[4,128,256]{2,1,0:T(8,128)(2,1)S(1)} %copy-done, bf16[288,128]{1,0:T(8,128)(2,1)S(1)} %get-tuple-element.23.refs_0_, ...), custom_call_target="tpu_custom_call" | custom-call | flops 83886080 | bytes 262144 | tf_op jit(solution)/shard_map/kl_project/pallas_call | solution.py:384
  28.1 1.5 %collective-permute-start.5 = (bf16[288,128]{1,0:T(8,128)(2,1)S(1)}, bf16[288,128]{1,0:T(8,128)(2,1)S(1)}, u32[]{:S(2)}, u32[]{:S(2)}) collective-permute-start(bf16[288,128]{1,0:T(8,128)(2,1)S(1)} %kl_project.3), channel_id=1, source_target_pairs={{0,2},{2,0},{1,3},{3,1},{4,6},{6,4},{5,7},{7,5},{8,10},{10,8},{9,1... | collective-permute-start | bytes 221192 | tf_op jit(solution)/shard_map/ppermute | solution.py:450
  29.6 0.4 %kl_project.2.mine = f32[288,128]{1,0:T(8,128)S(1)} custom-call(s32[8,640]{1,0:T(8,128)S(1)} %get-tuple-element.17.slot_column, s32[8,640]{1,0:T(8,128)S(1)} %get-tuple-element.18.rows_column, bf16[4,128,256]{2,1,0:T(8,128)(2,1)S(1)} %copy-done, bf16[288,128]{1,0:T(8,128)(2,1)S(1)} %get-tuple-element.23.refs_0_, ...), custom_call_target="tpu_custom_call" | custom-call | flops 83886080 | bytes 262144 | tf_op jit(solution)/shard_map/kl_project/pallas_call | solution.py:384
  30.1 2.4 %collective-permute-done.5.got = bf16[288,128]{1,0:T(8,128)(2,1)S(1)} collective-permute-done((bf16[288,128]{1,0:T(8,128)(2,1)S(1)}, bf16[288,128]{1,0:T(8,128)(2,1)S(1)}, u32[]{:S(2)}, u32[]{:S(2)}) %collective-permute-start.5) | collective-permute-done | bytes 73760 | tf_op jit(solution)/shard_map/ppermute | solution.py:450
  32.5 1.0 %unpack.1 = f32[4,64,256]{2,1,0:T(8,128)} custom-call(s32[8,128]{1,0:T(8,128)S(1)} %get-tuple-element.16.scalars, f32[288,128]{1,0:T(8,128)S(1)} %kl_project.2.mine, bf16[288,128]{1,0:T(8,128)(2,1)S(1)} %collective-permute-done.5.got), custom_call_target="tpu_custom_call" | custom-call | flops 36864 | bytes 368640 | tf_op jit(solution)/shard_map/unpack/pallas_call | solution.py:402
Async XLA Ops:
  0.0 27.7 %copy-start = (bf16[4,128,256]{2,1,0:T(8,128)(2,1)S(1)}, bf16[4,128,256]{2,1,0:T(8,128)(2,1)}, u32[]{:S(2)}) copy-start(bf16[4,128,256]{2,1,0:T(8,128)(2,1)} %kl.3) | copy-start | bytes 786436
  14.7 1.5 %collective-permute-start = (f32[1,5,64,128]{3,2,1,0:T(8,128)S(1)}, f32[1,5,64,128]{3,2,1,0:T(8,128)S(1)}, u32[]{:S(2)}, u32[]{:S(2)}) collective-permute-start(f32[1,5,64,128]{3,2,1,0:T(8,128)S(1)} %get-tuple-element.21), channel_id=1, source_target_pairs={{0,1},{1,0},{2,3},{3,2},{4,5},{5,4},{6,7},{7,6},{8,9},{9,8},{10,11... | collective-permute-start | bytes 491528 | tf_op jit(solution)/shard_map/ppermute | solution.py:439
  16.3 5.2 %collective-permute-start.1 = (f32[3,5,64,128]{3,2,1,0:T(8,128)S(1)}, f32[3,5,64,128]{3,2,1,0:T(8,128)S(1)}, u32[]{:S(2)}, u32[]{:S(2)}) collective-permute-start(f32[3,5,64,128]{3,2,1,0:T(8,128)S(1)} %get-tuple-element.22), channel_id=1, source_target_pairs={{0,1},{1,0},{2,3},{3,2},{4,5},{5,4},{6,7},{7,6},{8,9},{9,8},{10,11... | collective-permute-start | bytes 1474568 | tf_op jit(solution)/shard_map/ppermute | solution.py:441
  16.7 7.8 %collective-permute-start.3 = (bf16[288,128]{1,0:T(8,128)(2,1)S(1)}, bf16[288,128]{1,0:T(8,128)(2,1)S(1)}, u32[]{:S(2)}, u32[]{:S(2)}) collective-permute-start(bf16[288,128]{1,0:T(8,128)(2,1)S(1)} %sum_pair.3), channel_id=1, source_target_pairs={{0,12},{4,8},{8,4},{12,0},{1,13},{5,9},{9,5},{13,1},{2,14},{6,10},... | collective-permute-start | bytes 221192 | tf_op jit(solution)/shard_map/ppermute | solution.py:445
  21.6 6.1 %collective-permute-start.2 = (bf16[288,128]{1,0:T(8,128)(2,1)S(1)}, bf16[288,128]{1,0:T(8,128)(2,1)S(1)}, u32[]{:S(2)}, u32[]{:S(2)}) collective-permute-start(bf16[288,128]{1,0:T(8,128)(2,1)S(1)} %get-tuple-element.24), channel_id=1, source_target_pairs={{0,4},{4,12},{8,0},{12,8},{1,5},{5,13},{9,1},{13,9},{2,6},{6,14},{... | collective-permute-start | bytes 221192 | tf_op jit(solution)/shard_map/ppermute | solution.py:445
  21.6 6.0 %collective-permute-start.4 = (bf16[288,128]{1,0:T(8,128)(2,1)S(1)}, bf16[288,128]{1,0:T(8,128)(2,1)S(1)}, u32[]{:S(2)}, u32[]{:S(2)}) collective-permute-start(bf16[288,128]{1,0:T(8,128)(2,1)S(1)} %get-tuple-element.26), channel_id=1, source_target_pairs={{0,8},{4,0},{8,12},{12,4},{1,9},{5,1},{9,13},{13,5},{2,10},{6,2},{... | collective-permute-start | bytes 221192 | tf_op jit(solution)/shard_map/ppermute | solution.py:445
  28.1 4.4 %collective-permute-start.5 = (bf16[288,128]{1,0:T(8,128)(2,1)S(1)}, bf16[288,128]{1,0:T(8,128)(2,1)S(1)}, u32[]{:S(2)}, u32[]{:S(2)}) collective-permute-start(bf16[288,128]{1,0:T(8,128)(2,1)S(1)} %kl_project.3), channel_id=1, source_target_pairs={{0,2},{2,0},{1,3},{3,1},{4,6},{6,4},{5,7},{7,5},{8,10},{10,8},{9,1... | collective-permute-start | bytes 221192 | tf_op jit(solution)/shard_map/ppermute | solution.py:450

commit v18 on v10

--- a/solution.py
+++ b/solution.py
@@ -183,7 +183,6 @@
 
     tables = (tile_place, shift_place, owner_slots)
     all_owners = range(mine.shape[0] * lax.axis_size("pa"))
-    share = len(all_owners) // per_group
 
     def group_step(group, out_v, out_before):
         here = pl.ds(pl.multiple_of(group * GROUP, GROUP), GROUP)
@@ -204,17 +203,16 @@
                 for t in range(product.shape[1] // LANES):
                     at = (t * GROUP + f) * slots
                     out_v[at : at + slots, :] = product[:, t * LANES : (t + 1) * LANES]
-            line = jnp.maximum(group - 1, 0) * GROUP
-            pack(out_before, mine, far, near, line, tables, all_owners[i * share : (i + 1) * share])
+            if i == 0:
+                line = jnp.maximum(group - 1, 0) * GROUP
+                pack(out_before, mine, far, near, line, tables, all_owners)
 
     @pl.loop(0, groups // 2)
     def _(pair):
         group_step(2 * pair, out_even, out_odd)
         group_step(2 * pair + 1, out_odd, out_even)
 
-    for i in range(per_group):
-        part = all_owners[i * share : (i + 1) * share]
-        pack(out_odd, mine, far, near, (groups - 1) * GROUP, tables, part)
+    pack(out_odd, mine, far, near, (groups - 1) * GROUP, tables, all_owners)
 
 
 def folded_rows(rows, width):

time: 32.5 us -> 32.8 us (level)
  no operation moved by 1% of the time
where the time goes in v18:
time: 32.8 us; the launch traced here: 32.6 us
  Pallas kernels  15.9 us (48%)
  starting transfers between devices  10.1 us (31%)
  waiting for transfers between devices  6.56 us (20%)
    pallas_call x1, Pallas kernels, project(): pl.pallas_call(functools.partial(project_kernel, owner_slots), out_shape=...  13.8 us
    ppermute x3, starting transfers between devices, shards(): lax.ppermute(summed[step], 'ma', ring(step))  7.72 us
    ppermute x3, waiting for transfers between devices, shards(): lax.ppermute(summed[step], 'ma', ring(step))  3.13 us
    ppermute x1, waiting for transfers between devices, shards(): got = lax.ppermute(send, 'af', pairs('af'))  2.4 us
    ppermute x1, starting transfers between devices, shards(): got = lax.ppermute(send, 'af', pairs('af'))  1.51 us
    pallas_call x1, Pallas kernels, unpack(): pl.pallas_call(unpack_kernel, out_shape=jax.ShapeDtypeStruct((owner_slots...  1.04 us
    ppermute x1, waiting for transfers between devices, shards(): got_far = lax.ppermute(far, 'pa', pairs('pa'))  1.03 us
    pallas_call x2, Pallas kernels, kl_project(): pl.pallas_call(functools.partial(kl_kernel, part, owners, width), out_sha...  0.89 us
  transfers between devices with their start and end apart: 6, of which 3 were waited for; matrix products, arithmetic and copies ran while one was open for 0% of the time, Pallas kernels for 2%

profile of v18, /device:TPU:0, one launch (start us, length us, event | category | flops | bytes accessed | tf_op | source)
XLA Modules:
  0.0 32.6 jit_solution(6047787934700126501)
XLA Ops:
  0.0 0.0 copy-start
  0.0 13.8 %project.1 = (f32[4,5,64,128]{3,2,1,0:T(8,128)S(1)}, f32[1,5,64,128]{3,2,1,0:T(8,128)S(1)}, f32[3,5,64,128]{3,2,1,0:T(8,128)S(1)}, s32[8,640]{1,0:T(8,128)S(1)},...) custom-call(s32[32]{0:T(128)} %slot_hbm.1, s32[32]{0:T(128)} %keep_hbm.1, s32[32]{0:T(128)} %rows_hbm.1, ...), custom_call_target="tpu_custom_call" | custom-call | flops 1073741824 | bytes 37748736 | tf_op jit(solution)/shard_map/project/pallas_call | solution.py:321
  13.8 0.5 %collective-permute-start = (f32[1,5,64,128]{3,2,1,0:T(8,128)S(1)}, f32[1,5,64,128]{3,2,1,0:T(8,128)S(1)}, u32[]{:S(2)}, u32[]{:S(2)}) collective-permute-start(f32[1,5,64,128]{3,2,1,0:T(8,128)S(1)} %get-tuple-element.21), channel_id=1, source_target_pairs={{0,1},{1,0},{2,3},{3,2},{4,5},{5,4},{6,7},{7,6},{8,9},{9,8},{10,11... | collective-permute-start | bytes 491528 | tf_op jit(solution)/shard_map/ppermute | solution.py:428
  14.4 1.0 %collective-permute-done.got = f32[1,5,64,128]{3,2,1,0:T(8,128)S(1)} collective-permute-done((f32[1,5,64,128]{3,2,1,0:T(8,128)S(1)}, f32[1,5,64,128]{3,2,1,0:T(8,128)S(1)}, u32[]{:S(2)}, u32[]{:S(2)}) %collective-permute-start) | collective-permute-done | bytes 163872 | tf_op jit(solution)/shard_map/ppermute | solution.py:428
  15.4 0.4 %collective-permute-start.1 = (f32[3,5,64,128]{3,2,1,0:T(8,128)S(1)}, f32[3,5,64,128]{3,2,1,0:T(8,128)S(1)}, u32[]{:S(2)}, u32[]{:S(2)}) collective-permute-start(f32[3,5,64,128]{3,2,1,0:T(8,128)S(1)} %get-tuple-element.22), channel_id=1, source_target_pairs={{0,1},{1,0},{2,3},{3,2},{4,5},{5,4},{6,7},{7,6},{8,9},{9,8},{10,11... | collective-permute-start | bytes 1474568 | tf_op jit(solution)/shard_map/ppermute | solution.py:430
  15.8 0.1 sum_pair.3
  15.8 4.8 %collective-permute-start.3 = (bf16[288,128]{1,0:T(8,128)(2,1)S(1)}, bf16[288,128]{1,0:T(8,128)(2,1)S(1)}, u32[]{:S(2)}, u32[]{:S(2)}) collective-permute-start(bf16[288,128]{1,0:T(8,128)(2,1)S(1)} %sum_pair.3), channel_id=1, source_target_pairs={{0,12},{4,8},{8,4},{12,0},{1,13},{5,9},{9,5},{13,1},{2,14},{6,10},... | collective-permute-start | bytes 221192 | tf_op jit(solution)/shard_map/ppermute | solution.py:434
  20.6 0.0 collective-permute-done.1.got
  20.6 0.1 sum_pair.2
  20.7 0.0 collective-permute-start.2
  20.7 2.9 %collective-permute-start.4 = (bf16[288,128]{1,0:T(8,128)(2,1)S(1)}, bf16[288,128]{1,0:T(8,128)(2,1)S(1)}, u32[]{:S(2)}, u32[]{:S(2)}) collective-permute-start(bf16[288,128]{1,0:T(8,128)(2,1)S(1)} %get-tuple-element.26), channel_id=1, source_target_pairs={{0,8},{4,0},{8,12},{12,4},{1,9},{5,1},{9,13},{13,5},{2,10},{6,2},{... | collective-permute-start | bytes 221192 | tf_op jit(solution)/shard_map/ppermute | solution.py:434
  23.7 0.0 collective-permute-done.3.refs_2_
  23.7 3.1 %collective-permute-done.2.refs_1_ = bf16[288,128]{1,0:T(8,128)(2,1)S(1)} collective-permute-done((bf16[288,128]{1,0:T(8,128)(2,1)S(1)}, bf16[288,128]{1,0:T(8,128)(2,1)S(1)}, u32[]{:S(2)}, u32[]{:S(2)}) %collective-permute-start.2) | collective-permute-done | bytes 73760 | tf_op jit(solution)/shard_map/ppermute | solution.py:434
  26.8 0.0 collective-permute-done.4.refs_3_
  26.8 0.0 copy-done
  26.8 0.4 %kl_project.3 = bf16[288,128]{1,0:T(8,128)(2,1)S(1)} custom-call(s32[8,640]{1,0:T(8,128)S(1)} %get-tuple-element.17.slot_column, s32[8,640]{1,0:T(8,128)S(1)} %get-tuple-element.18.rows_column, bf16[4,128,256]{2,1,0:T(8,128)(2,1)S(1)} %copy-done, bf16[288,128]{1,0:T(8,128)(2,1)S(1)} %get-tuple-element.23.refs_0_, ...), custom_call_target="tpu_custom_call" | custom-call | flops 83886080 | bytes 262144 | tf_op jit(solution)/shard_map/kl_project/pallas_call | solution.py:373
  27.2 1.5 %collective-permute-start.5 = (bf16[288,128]{1,0:T(8,128)(2,1)S(1)}, bf16[288,128]{1,0:T(8,128)(2,1)S(1)}, u32[]{:S(2)}, u32[]{:S(2)}) collective-permute-start(bf16[288,128]{1,0:T(8,128)(2,1)S(1)} %kl_project.3), channel_id=1, source_target_pairs={{0,2},{2,0},{1,3},{3,1},{4,6},{6,4},{5,7},{7,5},{8,10},{10,8},{9,1... | collective-permute-start | bytes 221192 | tf_op jit(solution)/shard_map/ppermute | solution.py:439
  28.7 0.4 %kl_project.2.mine = f32[288,128]{1,0:T(8,128)S(1)} custom-call(s32[8,640]{1,0:T(8,128)S(1)} %get-tuple-element.17.slot_column, s32[8,640]{1,0:T(8,128)S(1)} %get-tuple-element.18.rows_column, bf16[4,128,256]{2,1,0:T(8,128)(2,1)S(1)} %copy-done, bf16[288,128]{1,0:T(8,128)(2,1)S(1)} %get-tuple-element.23.refs_0_, ...), custom_call_target="tpu_custom_call" | custom-call | flops 83886080 | bytes 262144 | tf_op jit(solution)/shard_map/kl_project/pallas_call | solution.py:373
  29.2 2.4 %collective-permute-done.5.got = bf16[288,128]{1,0:T(8,128)(2,1)S(1)} collective-permute-done((bf16[288,128]{1,0:T(8,128)(2,1)S(1)}, bf16[288,128]{1,0:T(8,128)(2,1)S(1)}, u32[]{:S(2)}, u32[]{:S(2)}) %collective-permute-start.5) | collective-permute-done | bytes 73760 | tf_op jit(solution)/shard_map/ppermute | solution.py:439
  31.6 1.0 %unpack.1 = f32[4,64,256]{2,1,0:T(8,128)} custom-call(s32[8,128]{1,0:T(8,128)S(1)} %get-tuple-element.16.scalars, f32[288,128]{1,0:T(8,128)S(1)} %kl_project.2.mine, bf16[288,128]{1,0:T(8,128)(2,1)S(1)} %collective-permute-done.5.got), custom_call_target="tpu_custom_call" | custom-call | flops 36864 | bytes 368640 | tf_op jit(solution)/shard_map/unpack/pallas_call | solution.py:391
Async XLA Ops:
  0.0 26.8 %copy-start = (bf16[4,128,256]{2,1,0:T(8,128)(2,1)S(1)}, bf16[4,128,256]{2,1,0:T(8,128)(2,1)}, u32[]{:S(2)}) copy-start(bf16[4,128,256]{2,1,0:T(8,128)(2,1)} %kl.3) | copy-start | bytes 786436
  13.8 1.6 %collective-permute-start = (f32[1,5,64,128]{3,2,1,0:T(8,128)S(1)}, f32[1,5,64,128]{3,2,1,0:T(8,128)S(1)}, u32[]{:S(2)}, u32[]{:S(2)}) collective-permute-start(f32[1,5,64,128]{3,2,1,0:T(8,128)S(1)} %get-tuple-element.21), channel_id=1, source_target_pairs={{0,1},{1,0},{2,3},{3,2},{4,5},{5,4},{6,7},{7,6},{8,9},{9,8},{10,11... | collective-permute-start | bytes 491528 | tf_op jit(solution)/shard_map/ppermute | solution.py:428
  15.4 5.2 %collective-permute-start.1 = (f32[3,5,64,128]{3,2,1,0:T(8,128)S(1)}, f32[3,5,64,128]{3,2,1,0:T(8,128)S(1)}, u32[]{:S(2)}, u32[]{:S(2)}) collective-permute-start(f32[3,5,64,128]{3,2,1,0:T(8,128)S(1)} %get-tuple-element.22), channel_id=1, source_target_pairs={{0,1},{1,0},{2,3},{3,2},{4,5},{5,4},{6,7},{7,6},{8,9},{9,8},{10,11... | collective-permute-start | bytes 1474568 | tf_op jit(solution)/shard_map/ppermute | solution.py:430
  15.8 7.8 %collective-permute-start.3 = (bf16[288,128]{1,0:T(8,128)(2,1)S(1)}, bf16[288,128]{1,0:T(8,128)(2,1)S(1)}, u32[]{:S(2)}, u32[]{:S(2)}) collective-permute-start(bf16[288,128]{1,0:T(8,128)(2,1)S(1)} %sum_pair.3), channel_id=1, source_target_pairs={{0,12},{4,8},{8,4},{12,0},{1,13},{5,9},{9,5},{13,1},{2,14},{6,10},... | collective-permute-start | bytes 221192 | tf_op jit(solution)/shard_map/ppermute | solution.py:434
  20.7 6.1 %collective-permute-start.2 = (bf16[288,128]{1,0:T(8,128)(2,1)S(1)}, bf16[288,128]{1,0:T(8,128)(2,1)S(1)}, u32[]{:S(2)}, u32[]{:S(2)}) collective-permute-start(bf16[288,128]{1,0:T(8,128)(2,1)S(1)} %get-tuple-element.24), channel_id=1, source_target_pairs={{0,4},{4,12},{8,0},{12,8},{1,5},{5,13},{9,1},{13,9},{2,6},{6,14},{... | collective-permute-start | bytes 221192 | tf_op jit(solution)/shard_map/ppermute | solution.py:434
  20.7 6.0 %collective-permute-start.4 = (bf16[288,128]{1,0:T(8,128)(2,1)S(1)}, bf16[288,128]{1,0:T(8,128)(2,1)S(1)}, u32[]{:S(2)}, u32[]{:S(2)}) collective-permute-start(bf16[288,128]{1,0:T(8,128)(2,1)S(1)} %get-tuple-element.26), channel_id=1, source_target_pairs={{0,8},{4,0},{8,12},{12,4},{1,9},{5,1},{9,13},{13,5},{2,10},{6,2},{... | collective-permute-start | bytes 221192 | tf_op jit(solution)/shard_map/ppermute | solution.py:434
  27.2 4.4 %collective-permute-start.5 = (bf16[288,128]{1,0:T(8,128)(2,1)S(1)}, bf16[288,128]{1,0:T(8,128)(2,1)S(1)}, u32[]{:S(2)}, u32[]{:S(2)}) collective-permute-start(bf16[288,128]{1,0:T(8,128)(2,1)S(1)} %kl_project.3), channel_id=1, source_target_pairs={{0,2},{2,0},{1,3},{3,1},{4,6},{6,4},{5,7},{7,5},{8,10},{10,8},{9,1... | collective-permute-start | bytes 221192 | tf_op jit(solution)/shard_map/ppermute | solution.py:439

commit v19 on v10

--- a/solution.py
+++ b/solution.py
@@ -138,7 +138,7 @@
         part = pl.ds(i * PER_COPY, PER_COPY)
         return pltpu.make_async_copy(basis.at[part], basis_v.at[part], basis_sem.at[i])
 
-    ahead = 1
+    ahead = 0
     for i in range(ahead):
         basis_copy(i).start()
     for copy in table_copies:

time: 32.5 us -> 33.7 us (1.037)
  Pallas kernels: 15.7 us -> 16.9 us
    pallas_call x1, Pallas kernels: 13.6 us -> 14.8 us  [project(): pl.pallas_call(functools.partial(project_kernel, owner_slots), out_shape=...]
where the time goes in v19:
time: 33.7 us; the launch traced here: 33.6 us
  Pallas kernels  16.9 us (50%)
  starting transfers between devices  10.1 us (30%)
  waiting for transfers between devices  6.57 us (19%)
    pallas_call x1, Pallas kernels, project(): pl.pallas_call(functools.partial(project_kernel, owner_slots), out_shape=...  14.8 us
    ppermute x3, starting transfers between devices, shards(): lax.ppermute(summed[step], 'ma', ring(step))  7.72 us
    ppermute x3, waiting for transfers between devices, shards(): lax.ppermute(summed[step], 'ma', ring(step))  3.13 us
    ppermute x1, waiting for transfers between devices, shards(): got = lax.ppermute(send, 'af', pairs('af'))  2.42 us
    ppermute x1, starting transfers between devices, shards(): got = lax.ppermute(send, 'af', pairs('af'))  1.5 us
    pallas_call x1, Pallas kernels, unpack(): pl.pallas_call(unpack_kernel, out_shape=jax.ShapeDtypeStruct((owner_slots...  1.04 us
    ppermute x1, waiting for transfers between devices, shards(): got_far = lax.ppermute(far, 'pa', pairs('pa'))  1.03 us
    pallas_call x2, Pallas kernels, kl_project(): pl.pallas_call(functools.partial(kl_kernel, part, owners, width), out_sha...  0.89 us
  transfers between devices with their start and end apart: 6, of which 3 were waited for; matrix products, arithmetic and copies ran while one was open for 0% of the time, Pallas kernels for 2%

profile of v19, /device:TPU:0, one launch (start us, length us, event | category | flops | bytes accessed | tf_op | source)
XLA Modules:
  0.0 33.6 jit_solution(13286572241562800787)
XLA Ops:
  0.0 0.0 copy-start
  0.0 14.8 %project.1 = (f32[4,5,64,128]{3,2,1,0:T(8,128)S(1)}, f32[1,5,64,128]{3,2,1,0:T(8,128)S(1)}, f32[3,5,64,128]{3,2,1,0:T(8,128)S(1)}, s32[8,640]{1,0:T(8,128)S(1)},...) custom-call(s32[32]{0:T(128)} %slot_hbm.1, s32[32]{0:T(128)} %keep_hbm.1, s32[32]{0:T(128)} %rows_hbm.1, ...), custom_call_target="tpu_custom_call" | custom-call | flops 1073741824 | bytes 37748736 | tf_op jit(solution)/shard_map/project/pallas_call | solution.py:323
  14.8 0.5 %collective-permute-start = (f32[1,5,64,128]{3,2,1,0:T(8,128)S(1)}, f32[1,5,64,128]{3,2,1,0:T(8,128)S(1)}, u32[]{:S(2)}, u32[]{:S(2)}) collective-permute-start(f32[1,5,64,128]{3,2,1,0:T(8,128)S(1)} %get-tuple-element.21), channel_id=1, source_target_pairs={{0,1},{1,0},{2,3},{3,2},{4,5},{5,4},{6,7},{7,6},{8,9},{9,8},{10,11... | collective-permute-start | bytes 491528 | tf_op jit(solution)/shard_map/ppermute | solution.py:430
  15.3 1.0 %collective-permute-done.got = f32[1,5,64,128]{3,2,1,0:T(8,128)S(1)} collective-permute-done((f32[1,5,64,128]{3,2,1,0:T(8,128)S(1)}, f32[1,5,64,128]{3,2,1,0:T(8,128)S(1)}, u32[]{:S(2)}, u32[]{:S(2)}) %collective-permute-start) | collective-permute-done | bytes 163872 | tf_op jit(solution)/shard_map/ppermute | solution.py:430
  16.4 0.4 %collective-permute-start.1 = (f32[3,5,64,128]{3,2,1,0:T(8,128)S(1)}, f32[3,5,64,128]{3,2,1,0:T(8,128)S(1)}, u32[]{:S(2)}, u32[]{:S(2)}) collective-permute-start(f32[3,5,64,128]{3,2,1,0:T(8,128)S(1)} %get-tuple-element.22), channel_id=1, source_target_pairs={{0,1},{1,0},{2,3},{3,2},{4,5},{5,4},{6,7},{7,6},{8,9},{9,8},{10,11... | collective-permute-start | bytes 1474568 | tf_op jit(solution)/shard_map/ppermute | solution.py:432
  16.7 0.1 sum_pair.3
  16.8 4.8 %collective-permute-start.3 = (bf16[288,128]{1,0:T(8,128)(2,1)S(1)}, bf16[288,128]{1,0:T(8,128)(2,1)S(1)}, u32[]{:S(2)}, u32[]{:S(2)}) collective-permute-start(bf16[288,128]{1,0:T(8,128)(2,1)S(1)} %sum_pair.3), channel_id=1, source_target_pairs={{0,12},{4,8},{8,4},{12,0},{1,13},{5,9},{9,5},{13,1},{2,14},{6,10},... | collective-permute-start | bytes 221192 | tf_op jit(solution)/shard_map/ppermute | solution.py:436
  21.6 0.0 collective-permute-done.1.got
  21.6 0.1 sum_pair.2
  21.7 0.0 collective-permute-start.2
  21.7 2.9 %collective-permute-start.4 = (bf16[288,128]{1,0:T(8,128)(2,1)S(1)}, bf16[288,128]{1,0:T(8,128)(2,1)S(1)}, u32[]{:S(2)}, u32[]{:S(2)}) collective-permute-start(bf16[288,128]{1,0:T(8,128)(2,1)S(1)} %get-tuple-element.26), channel_id=1, source_target_pairs={{0,8},{4,0},{8,12},{12,4},{1,9},{5,1},{9,13},{13,5},{2,10},{6,2},{... | collective-permute-start | bytes 221192 | tf_op jit(solution)/shard_map/ppermute | solution.py:436
  24.6 0.0 collective-permute-done.3.refs_2_
  24.6 3.1 %collective-permute-done.2.refs_1_ = bf16[288,128]{1,0:T(8,128)(2,1)S(1)} collective-permute-done((bf16[288,128]{1,0:T(8,128)(2,1)S(1)}, bf16[288,128]{1,0:T(8,128)(2,1)S(1)}, u32[]{:S(2)}, u32[]{:S(2)}) %collective-permute-start.2) | collective-permute-done | bytes 73760 | tf_op jit(solution)/shard_map/ppermute | solution.py:436
  27.7 0.0 collective-permute-done.4.refs_3_
  27.7 0.0 copy-done
  27.7 0.4 %kl_project.3 = bf16[288,128]{1,0:T(8,128)(2,1)S(1)} custom-call(s32[8,640]{1,0:T(8,128)S(1)} %get-tuple-element.17.slot_column, s32[8,640]{1,0:T(8,128)S(1)} %get-tuple-element.18.rows_column, bf16[4,128,256]{2,1,0:T(8,128)(2,1)S(1)} %copy-done, bf16[288,128]{1,0:T(8,128)(2,1)S(1)} %get-tuple-element.23.refs_0_, ...), custom_call_target="tpu_custom_call" | custom-call | flops 83886080 | bytes 262144 | tf_op jit(solution)/shard_map/kl_project/pallas_call | solution.py:375
  28.2 1.5 %collective-permute-start.5 = (bf16[288,128]{1,0:T(8,128)(2,1)S(1)}, bf16[288,128]{1,0:T(8,128)(2,1)S(1)}, u32[]{:S(2)}, u32[]{:S(2)}) collective-permute-start(bf16[288,128]{1,0:T(8,128)(2,1)S(1)} %kl_project.3), channel_id=1, source_target_pairs={{0,2},{2,0},{1,3},{3,1},{4,6},{6,4},{5,7},{7,5},{8,10},{10,8},{9,1... | collective-permute-start | bytes 221192 | tf_op jit(solution)/shard_map/ppermute | solution.py:441
  29.7 0.4 %kl_project.2.mine = f32[288,128]{1,0:T(8,128)S(1)} custom-call(s32[8,640]{1,0:T(8,128)S(1)} %get-tuple-element.17.slot_column, s32[8,640]{1,0:T(8,128)S(1)} %get-tuple-element.18.rows_column, bf16[4,128,256]{2,1,0:T(8,128)(2,1)S(1)} %copy-done, bf16[288,128]{1,0:T(8,128)(2,1)S(1)} %get-tuple-element.23.refs_0_, ...), custom_call_target="tpu_custom_call" | custom-call | flops 83886080 | bytes 262144 | tf_op jit(solution)/shard_map/kl_project/pallas_call | solution.py:375
  30.1 2.4 %collective-permute-done.5.got = bf16[288,128]{1,0:T(8,128)(2,1)S(1)} collective-permute-done((bf16[288,128]{1,0:T(8,128)(2,1)S(1)}, bf16[288,128]{1,0:T(8,128)(2,1)S(1)}, u32[]{:S(2)}, u32[]{:S(2)}) %collective-permute-start.5) | collective-permute-done | bytes 73760 | tf_op jit(solution)/shard_map/ppermute | solution.py:441
  32.6 1.0 %unpack.1 = f32[4,64,256]{2,1,0:T(8,128)} custom-call(s32[8,128]{1,0:T(8,128)S(1)} %get-tuple-element.16.scalars, f32[288,128]{1,0:T(8,128)S(1)} %kl_project.2.mine, bf16[288,128]{1,0:T(8,128)(2,1)S(1)} %collective-permute-done.5.got), custom_call_target="tpu_custom_call" | custom-call | flops 36864 | bytes 368640 | tf_op jit(solution)/shard_map/unpack/pallas_call | solution.py:393
Async XLA Ops:
  0.0 27.7 %copy-start = (bf16[4,128,256]{2,1,0:T(8,128)(2,1)S(1)}, bf16[4,128,256]{2,1,0:T(8,128)(2,1)}, u32[]{:S(2)}) copy-start(bf16[4,128,256]{2,1,0:T(8,128)(2,1)} %kl.3) | copy-start | bytes 786436
  14.8 1.5 %collective-permute-start = (f32[1,5,64,128]{3,2,1,0:T(8,128)S(1)}, f32[1,5,64,128]{3,2,1,0:T(8,128)S(1)}, u32[]{:S(2)}, u32[]{:S(2)}) collective-permute-start(f32[1,5,64,128]{3,2,1,0:T(8,128)S(1)} %get-tuple-element.21), channel_id=1, source_target_pairs={{0,1},{1,0},{2,3},{3,2},{4,5},{5,4},{6,7},{7,6},{8,9},{9,8},{10,11... | collective-permute-start | bytes 491528 | tf_op jit(solution)/shard_map/ppermute | solution.py:430
  16.4 5.2 %collective-permute-start.1 = (f32[3,5,64,128]{3,2,1,0:T(8,128)S(1)}, f32[3,5,64,128]{3,2,1,0:T(8,128)S(1)}, u32[]{:S(2)}, u32[]{:S(2)}) collective-permute-start(f32[3,5,64,128]{3,2,1,0:T(8,128)S(1)} %get-tuple-element.22), channel_id=1, source_target_pairs={{0,1},{1,0},{2,3},{3,2},{4,5},{5,4},{6,7},{7,6},{8,9},{9,8},{10,11... | collective-permute-start | bytes 1474568 | tf_op jit(solution)/shard_map/ppermute | solution.py:432
  16.8 7.8 %collective-permute-start.3 = (bf16[288,128]{1,0:T(8,128)(2,1)S(1)}, bf16[288,128]{1,0:T(8,128)(2,1)S(1)}, u32[]{:S(2)}, u32[]{:S(2)}) collective-permute-start(bf16[288,128]{1,0:T(8,128)(2,1)S(1)} %sum_pair.3), channel_id=1, source_target_pairs={{0,12},{4,8},{8,4},{12,0},{1,13},{5,9},{9,5},{13,1},{2,14},{6,10},... | collective-permute-start | bytes 221192 | tf_op jit(solution)/shard_map/ppermute | solution.py:436
  21.7 6.1 %collective-permute-start.2 = (bf16[288,128]{1,0:T(8,128)(2,1)S(1)}, bf16[288,128]{1,0:T(8,128)(2,1)S(1)}, u32[]{:S(2)}, u32[]{:S(2)}) collective-permute-start(bf16[288,128]{1,0:T(8,128)(2,1)S(1)} %get-tuple-element.24), channel_id=1, source_target_pairs={{0,4},{4,12},{8,0},{12,8},{1,5},{5,13},{9,1},{13,9},{2,6},{6,14},{... | collective-permute-start | bytes 221192 | tf_op jit(solution)/shard_map/ppermute | solution.py:436
  21.7 6.0 %collective-permute-start.4 = (bf16[288,128]{1,0:T(8,128)(2,1)S(1)}, bf16[288,128]{1,0:T(8,128)(2,1)S(1)}, u32[]{:S(2)}, u32[]{:S(2)}) collective-permute-start(bf16[288,128]{1,0:T(8,128)(2,1)S(1)} %get-tuple-element.26), channel_id=1, source_target_pairs={{0,8},{4,0},{8,12},{12,4},{1,9},{5,1},{9,13},{13,5},{2,10},{6,2},{... | collective-permute-start | bytes 221192 | tf_op jit(solution)/shard_map/ppermute | solution.py:436
  28.2 4.4 %collective-permute-start.5 = (bf16[288,128]{1,0:T(8,128)(2,1)S(1)}, bf16[288,128]{1,0:T(8,128)(2,1)S(1)}, u32[]{:S(2)}, u32[]{:S(2)}) collective-permute-start(bf16[288,128]{1,0:T(8,128)(2,1)S(1)} %kl_project.3), channel_id=1, source_target_pairs={{0,2},{2,0},{1,3},{3,1},{4,6},{6,4},{5,7},{7,5},{8,10},{10,8},{9,1... | collective-permute-start | bytes 221192 | tf_op jit(solution)/shard_map/ppermute | solution.py:441

commit v20 on v19

--- a/solution.py
+++ b/solution.py
@@ -138,7 +138,7 @@
         part = pl.ds(i * PER_COPY, PER_COPY)
         return pltpu.make_async_copy(basis.at[part], basis_v.at[part], basis_sem.at[i])
 
-    ahead = 0
+    ahead = 2
     for i in range(ahead):
         basis_copy(i).start()
     for copy in table_copies:

time: 33.7 us -> 33.4 us (level)
  no operation moved by 1% of the time
where the time goes in v20:
time: 33.4 us; the launch traced here: 33.3 us
  Pallas kernels  16.6 us (50%)
  starting transfers between devices  10.1 us (30%)
  waiting for transfers between devices  6.57 us (20%)
    pallas_call x1, Pallas kernels, project(): pl.pallas_call(functools.partial(project_kernel, owner_slots), out_shape=...  14.5 us
    ppermute x3, starting transfers between devices, shards(): lax.ppermute(summed[step], 'ma', ring(step))  7.72 us
    ppermute x3, waiting for transfers between devices, shards(): lax.ppermute(summed[step], 'ma', ring(step))  3.13 us
    ppermute x1, waiting for transfers between devices, shards(): got = lax.ppermute(send, 'af', pairs('af'))  2.42 us
    ppermute x1, starting transfers between devices, shards(): got = lax.ppermute(send, 'af', pairs('af'))  1.5 us
    pallas_call x1, Pallas kernels, unpack(): pl.pallas_call(unpack_kernel, out_shape=jax.ShapeDtypeStruct((owner_slots...  1.04 us
    ppermute x1, waiting for transfers between devices, shards(): got_far = lax.ppermute(far, 'pa', pairs('pa'))  1.03 us
    pallas_call x2, Pallas kernels, kl_project(): pl.pallas_call(functools.partial(kl_kernel, part, owners, width), out_sha...  0.89 us
  transfers between devices with their start and end apart: 6, of which 3 were waited for; matrix products, arithmetic and copies ran while one was open for 0% of the time, Pallas kernels for 2%

profile of v20, /device:TPU:0, one launch (start us, length us, event | category | flops | bytes accessed | tf_op | source)
XLA Modules:
  0.0 33.3 jit_solution(16157626069095913045)
XLA Ops:
  0.0 0.0 copy-start
  0.0 14.5 %project.1 = (f32[4,5,64,128]{3,2,1,0:T(8,128)S(1)}, f32[1,5,64,128]{3,2,1,0:T(8,128)S(1)}, f32[3,5,64,128]{3,2,1,0:T(8,128)S(1)}, s32[8,640]{1,0:T(8,128)S(1)},...) custom-call(s32[32]{0:T(128)} %slot_hbm.1, s32[32]{0:T(128)} %keep_hbm.1, s32[32]{0:T(128)} %rows_hbm.1, ...), custom_call_target="tpu_custom_call" | custom-call | flops 1073741824 | bytes 37748736 | tf_op jit(solution)/shard_map/project/pallas_call | solution.py:323
  14.5 0.5 %collective-permute-start = (f32[1,5,64,128]{3,2,1,0:T(8,128)S(1)}, f32[1,5,64,128]{3,2,1,0:T(8,128)S(1)}, u32[]{:S(2)}, u32[]{:S(2)}) collective-permute-start(f32[1,5,64,128]{3,2,1,0:T(8,128)S(1)} %get-tuple-element.21), channel_id=1, source_target_pairs={{0,1},{1,0},{2,3},{3,2},{4,5},{5,4},{6,7},{7,6},{8,9},{9,8},{10,11... | collective-permute-start | bytes 491528 | tf_op jit(solution)/shard_map/ppermute | solution.py:430
  15.0 1.0 %collective-permute-done.got = f32[1,5,64,128]{3,2,1,0:T(8,128)S(1)} collective-permute-done((f32[1,5,64,128]{3,2,1,0:T(8,128)S(1)}, f32[1,5,64,128]{3,2,1,0:T(8,128)S(1)}, u32[]{:S(2)}, u32[]{:S(2)}) %collective-permute-start) | collective-permute-done | bytes 163872 | tf_op jit(solution)/shard_map/ppermute | solution.py:430
  16.0 0.4 %collective-permute-start.1 = (f32[3,5,64,128]{3,2,1,0:T(8,128)S(1)}, f32[3,5,64,128]{3,2,1,0:T(8,128)S(1)}, u32[]{:S(2)}, u32[]{:S(2)}) collective-permute-start(f32[3,5,64,128]{3,2,1,0:T(8,128)S(1)} %get-tuple-element.22), channel_id=1, source_target_pairs={{0,1},{1,0},{2,3},{3,2},{4,5},{5,4},{6,7},{7,6},{8,9},{9,8},{10,11... | collective-permute-start | bytes 1474568 | tf_op jit(solution)/shard_map/ppermute | solution.py:432
  16.4 0.1 sum_pair.3
  16.5 4.8 %collective-permute-start.3 = (bf16[288,128]{1,0:T(8,128)(2,1)S(1)}, bf16[288,128]{1,0:T(8,128)(2,1)S(1)}, u32[]{:S(2)}, u32[]{:S(2)}) collective-permute-start(bf16[288,128]{1,0:T(8,128)(2,1)S(1)} %sum_pair.3), channel_id=1, source_target_pairs={{0,12},{4,8},{8,4},{12,0},{1,13},{5,9},{9,5},{13,1},{2,14},{6,10},... | collective-permute-start | bytes 221192 | tf_op jit(solution)/shard_map/ppermute | solution.py:436
  21.3 0.0 collective-permute-done.1.got
  21.3 0.1 sum_pair.2
  21.3 0.0 collective-permute-start.2
  21.4 2.9 %collective-permute-start.4 = (bf16[288,128]{1,0:T(8,128)(2,1)S(1)}, bf16[288,128]{1,0:T(8,128)(2,1)S(1)}, u32[]{:S(2)}, u32[]{:S(2)}) collective-permute-start(bf16[288,128]{1,0:T(8,128)(2,1)S(1)} %get-tuple-element.26), channel_id=1, source_target_pairs={{0,8},{4,0},{8,12},{12,4},{1,9},{5,1},{9,13},{13,5},{2,10},{6,2},{... | collective-permute-start | bytes 221192 | tf_op jit(solution)/shard_map/ppermute | solution.py:436
  24.3 0.0 collective-permute-done.3.refs_2_
  24.3 3.1 %collective-permute-done.2.refs_1_ = bf16[288,128]{1,0:T(8,128)(2,1)S(1)} collective-permute-done((bf16[288,128]{1,0:T(8,128)(2,1)S(1)}, bf16[288,128]{1,0:T(8,128)(2,1)S(1)}, u32[]{:S(2)}, u32[]{:S(2)}) %collective-permute-start.2) | collective-permute-done | bytes 73760 | tf_op jit(solution)/shard_map/ppermute | solution.py:436
  27.4 0.0 collective-permute-done.4.refs_3_
  27.4 0.0 copy-done
  27.4 0.4 %kl_project.3 = bf16[288,128]{1,0:T(8,128)(2,1)S(1)} custom-call(s32[8,640]{1,0:T(8,128)S(1)} %get-tuple-element.17.slot_column, s32[8,640]{1,0:T(8,128)S(1)} %get-tuple-element.18.rows_column, bf16[4,128,256]{2,1,0:T(8,128)(2,1)S(1)} %copy-done, bf16[288,128]{1,0:T(8,128)(2,1)S(1)} %get-tuple-element.23.refs_0_, ...), custom_call_target="tpu_custom_call" | custom-call | flops 83886080 | bytes 262144 | tf_op jit(solution)/shard_map/kl_project/pallas_call | solution.py:375
  27.9 1.5 %collective-permute-start.5 = (bf16[288,128]{1,0:T(8,128)(2,1)S(1)}, bf16[288,128]{1,0:T(8,128)(2,1)S(1)}, u32[]{:S(2)}, u32[]{:S(2)}) collective-permute-start(bf16[288,128]{1,0:T(8,128)(2,1)S(1)} %kl_project.3), channel_id=1, source_target_pairs={{0,2},{2,0},{1,3},{3,1},{4,6},{6,4},{5,7},{7,5},{8,10},{10,8},{9,1... | collective-permute-start | bytes 221192 | tf_op jit(solution)/shard_map/ppermute | solution.py:441
  29.4 0.4 %kl_project.2.mine = f32[288,128]{1,0:T(8,128)S(1)} custom-call(s32[8,640]{1,0:T(8,128)S(1)} %get-tuple-element.17.slot_column, s32[8,640]{1,0:T(8,128)S(1)} %get-tuple-element.18.rows_column, bf16[4,128,256]{2,1,0:T(8,128)(2,1)S(1)} %copy-done, bf16[288,128]{1,0:T(8,128)(2,1)S(1)} %get-tuple-element.23.refs_0_, ...), custom_call_target="tpu_custom_call" | custom-call | flops 83886080 | bytes 262144 | tf_op jit(solution)/shard_map/kl_project/pallas_call | solution.py:375
  29.8 2.4 %collective-permute-done.5.got = bf16[288,128]{1,0:T(8,128)(2,1)S(1)} collective-permute-done((bf16[288,128]{1,0:T(8,128)(2,1)S(1)}, bf16[288,128]{1,0:T(8,128)(2,1)S(1)}, u32[]{:S(2)}, u32[]{:S(2)}) %collective-permute-start.5) | collective-permute-done | bytes 73760 | tf_op jit(solution)/shard_map/ppermute | solution.py:441
  32.2 1.0 %unpack.1 = f32[4,64,256]{2,1,0:T(8,128)} custom-call(s32[8,128]{1,0:T(8,128)S(1)} %get-tuple-element.16.scalars, f32[288,128]{1,0:T(8,128)S(1)} %kl_project.2.mine, bf16[288,128]{1,0:T(8,128)(2,1)S(1)} %collective-permute-done.5.got), custom_call_target="tpu_custom_call" | custom-call | flops 36864 | bytes 368640 | tf_op jit(solution)/shard_map/unpack/pallas_call | solution.py:393
Async XLA Ops:
  0.0 27.4 %copy-start = (bf16[4,128,256]{2,1,0:T(8,128)(2,1)S(1)}, bf16[4,128,256]{2,1,0:T(8,128)(2,1)}, u32[]{:S(2)}) copy-start(bf16[4,128,256]{2,1,0:T(8,128)(2,1)} %kl.3) | copy-start | bytes 786436
  14.5 1.5 %collective-permute-start = (f32[1,5,64,128]{3,2,1,0:T(8,128)S(1)}, f32[1,5,64,128]{3,2,1,0:T(8,128)S(1)}, u32[]{:S(2)}, u32[]{:S(2)}) collective-permute-start(f32[1,5,64,128]{3,2,1,0:T(8,128)S(1)} %get-tuple-element.21), channel_id=1, source_target_pairs={{0,1},{1,0},{2,3},{3,2},{4,5},{5,4},{6,7},{7,6},{8,9},{9,8},{10,11... | collective-permute-start | bytes 491528 | tf_op jit(solution)/shard_map/ppermute | solution.py:430
  16.0 5.2 %collective-permute-start.1 = (f32[3,5,64,128]{3,2,1,0:T(8,128)S(1)}, f32[3,5,64,128]{3,2,1,0:T(8,128)S(1)}, u32[]{:S(2)}, u32[]{:S(2)}) collective-permute-start(f32[3,5,64,128]{3,2,1,0:T(8,128)S(1)} %get-tuple-element.22), channel_id=1, source_target_pairs={{0,1},{1,0},{2,3},{3,2},{4,5},{5,4},{6,7},{7,6},{8,9},{9,8},{10,11... | collective-permute-start | bytes 1474568 | tf_op jit(solution)/shard_map/ppermute | solution.py:432
  16.5 7.8 %collective-permute-start.3 = (bf16[288,128]{1,0:T(8,128)(2,1)S(1)}, bf16[288,128]{1,0:T(8,128)(2,1)S(1)}, u32[]{:S(2)}, u32[]{:S(2)}) collective-permute-start(bf16[288,128]{1,0:T(8,128)(2,1)S(1)} %sum_pair.3), channel_id=1, source_target_pairs={{0,12},{4,8},{8,4},{12,0},{1,13},{5,9},{9,5},{13,1},{2,14},{6,10},... | collective-permute-start | bytes 221192 | tf_op jit(solution)/shard_map/ppermute | solution.py:436
  21.3 6.1 %collective-permute-start.2 = (bf16[288,128]{1,0:T(8,128)(2,1)S(1)}, bf16[288,128]{1,0:T(8,128)(2,1)S(1)}, u32[]{:S(2)}, u32[]{:S(2)}) collective-permute-start(bf16[288,128]{1,0:T(8,128)(2,1)S(1)} %get-tuple-element.24), channel_id=1, source_target_pairs={{0,4},{4,12},{8,0},{12,8},{1,5},{5,13},{9,1},{13,9},{2,6},{6,14},{... | collective-permute-start | bytes 221192 | tf_op jit(solution)/shard_map/ppermute | solution.py:436
  21.4 6.0 %collective-permute-start.4 = (bf16[288,128]{1,0:T(8,128)(2,1)S(1)}, bf16[288,128]{1,0:T(8,128)(2,1)S(1)}, u32[]{:S(2)}, u32[]{:S(2)}) collective-permute-start(bf16[288,128]{1,0:T(8,128)(2,1)S(1)} %get-tuple-element.26), channel_id=1, source_target_pairs={{0,8},{4,0},{8,12},{12,4},{1,9},{5,1},{9,13},{13,5},{2,10},{6,2},{... | collective-permute-start | bytes 221192 | tf_op jit(solution)/shard_map/ppermute | solution.py:436
  27.9 4.4 %collective-permute-start.5 = (bf16[288,128]{1,0:T(8,128)(2,1)S(1)}, bf16[288,128]{1,0:T(8,128)(2,1)S(1)}, u32[]{:S(2)}, u32[]{:S(2)}) collective-permute-start(bf16[288,128]{1,0:T(8,128)(2,1)S(1)} %kl_project.3), channel_id=1, source_target_pairs={{0,2},{2,0},{1,3},{3,1},{4,6},{6,4},{5,7},{7,5},{8,10},{10,8},{9,1... | collective-permute-start | bytes 221192 | tf_op jit(solution)/shard_map/ppermute | solution.py:441

commit v21 on v10

--- a/solution.py
+++ b/solution.py
@@ -434,7 +434,7 @@
     summed |= zip(others, sum_pair(others, width, mine, got_near))
     blocks = {
         step: lax.ppermute(summed[step], "ma", ring(step)) if step else summed[step]
-        for step in [first] + others
+        for step in [first] + others[::-1]
     }
     tables = (width, slot_column, rows_column, kl_basis, [blocks[step] for step in range(owners)])
     send = kl_project(1, jnp.bfloat16, *tables)

time: 32.5 us -> 32.5 us (level)
  no operation moved by 1% of the time
where the time goes in v21:
time: 32.5 us; the launch traced here: 32.4 us
  Pallas kernels  15.7 us (48%)
  starting transfers between devices  10.1 us (31%)
  waiting for transfers between devices  6.58 us (20%)
    pallas_call x1, Pallas kernels, project(): pl.pallas_call(functools.partial(project_kernel, owner_slots), out_shape=...  13.6 us
    ppermute x3, starting transfers between devices, shards(): lax.ppermute(summed[step], 'ma', ring(step))  7.72 us
    ppermute x3, waiting for transfers between devices, shards(): lax.ppermute(summed[step], 'ma', ring(step))  3.13 us
    ppermute x1, waiting for transfers between devices, shards(): got = lax.ppermute(send, 'af', pairs('af'))  2.42 us
    ppermute x1, starting transfers between devices, shards(): got = lax.ppermute(send, 'af', pairs('af'))  1.5 us
    pallas_call x1, Pallas kernels, unpack(): pl.pallas_call(unpack_kernel, out_shape=jax.ShapeDtypeStruct((owner_slots...  1.04 us
    ppermute x1, waiting for transfers between devices, shards(): got_far = lax.ppermute(far, 'pa', pairs('pa'))  1.03 us
    pallas_call x2, Pallas kernels, kl_project(): pl.pallas_call(functools.partial(kl_kernel, part, owners, width), out_sha...  0.89 us
  transfers between devices with their start and end apart: 6, of which 3 were waited for; matrix products, arithmetic and copies ran while one was open for 0% of the time, Pallas kernels for 2%

profile of v21, /device:TPU:0, one launch (start us, length us, event | category | flops | bytes accessed | tf_op | source)
XLA Modules:
  0.0 32.4 jit_solution(10407031632342634263)
XLA Ops:
  0.0 0.0 copy-start
  0.0 13.6 %project.1 = (f32[4,5,64,128]{3,2,1,0:T(8,128)S(1)}, f32[1,5,64,128]{3,2,1,0:T(8,128)S(1)}, f32[3,5,64,128]{3,2,1,0:T(8,128)S(1)}, s32[8,640]{1,0:T(8,128)S(1)},...) custom-call(s32[32]{0:T(128)} %slot_hbm.1, s32[32]{0:T(128)} %keep_hbm.1, s32[32]{0:T(128)} %rows_hbm.1, ...), custom_call_target="tpu_custom_call" | custom-call | flops 1073741824 | bytes 37748736 | tf_op jit(solution)/shard_map/project/pallas_call | solution.py:323
  13.6 0.5 %collective-permute-start = (f32[1,5,64,128]{3,2,1,0:T(8,128)S(1)}, f32[1,5,64,128]{3,2,1,0:T(8,128)S(1)}, u32[]{:S(2)}, u32[]{:S(2)}) collective-permute-start(f32[1,5,64,128]{3,2,1,0:T(8,128)S(1)} %get-tuple-element.21), channel_id=1, source_target_pairs={{0,1},{1,0},{2,3},{3,2},{4,5},{5,4},{6,7},{7,6},{8,9},{9,8},{10,11... | collective-permute-start | bytes 491528 | tf_op jit(solution)/shard_map/ppermute | solution.py:430
  14.1 1.0 %collective-permute-done.got = f32[1,5,64,128]{3,2,1,0:T(8,128)S(1)} collective-permute-done((f32[1,5,64,128]{3,2,1,0:T(8,128)S(1)}, f32[1,5,64,128]{3,2,1,0:T(8,128)S(1)}, u32[]{:S(2)}, u32[]{:S(2)}) %collective-permute-start) | collective-permute-done | bytes 163872 | tf_op jit(solution)/shard_map/ppermute | solution.py:430
  15.1 0.4 %collective-permute-start.1 = (f32[3,5,64,128]{3,2,1,0:T(8,128)S(1)}, f32[3,5,64,128]{3,2,1,0:T(8,128)S(1)}, u32[]{:S(2)}, u32[]{:S(2)}) collective-permute-start(f32[3,5,64,128]{3,2,1,0:T(8,128)S(1)} %get-tuple-element.22), channel_id=1, source_target_pairs={{0,1},{1,0},{2,3},{3,2},{4,5},{5,4},{6,7},{7,6},{8,9},{9,8},{10,11... | collective-permute-start | bytes 1474568 | tf_op jit(solution)/shard_map/ppermute | solution.py:432
  15.5 0.1 sum_pair.3
  15.6 4.8 %collective-permute-start.3 = (bf16[288,128]{1,0:T(8,128)(2,1)S(1)}, bf16[288,128]{1,0:T(8,128)(2,1)S(1)}, u32[]{:S(2)}, u32[]{:S(2)}) collective-permute-start(bf16[288,128]{1,0:T(8,128)(2,1)S(1)} %sum_pair.3), channel_id=1, source_target_pairs={{0,12},{4,8},{8,4},{12,0},{1,13},{5,9},{9,5},{13,1},{2,14},{6,10},... | collective-permute-start | bytes 221192 | tf_op jit(solution)/shard_map/ppermute | solution.py:436
  20.3 0.0 collective-permute-done.1.got
  20.3 0.1 sum_pair.2
  20.4 0.0 collective-permute-start.2
  20.5 2.9 %collective-permute-start.4 = (bf16[288,128]{1,0:T(8,128)(2,1)S(1)}, bf16[288,128]{1,0:T(8,128)(2,1)S(1)}, u32[]{:S(2)}, u32[]{:S(2)}) collective-permute-start(bf16[288,128]{1,0:T(8,128)(2,1)S(1)} %get-tuple-element.26), channel_id=1, source_target_pairs={{0,8},{4,0},{8,12},{12,4},{1,9},{5,1},{9,13},{13,5},{2,10},{6,2},{... | collective-permute-start | bytes 221192 | tf_op jit(solution)/shard_map/ppermute | solution.py:436
  23.4 0.0 collective-permute-done.3.refs_2_
  23.4 3.1 %collective-permute-done.2.refs_1_ = bf16[288,128]{1,0:T(8,128)(2,1)S(1)} collective-permute-done((bf16[288,128]{1,0:T(8,128)(2,1)S(1)}, bf16[288,128]{1,0:T(8,128)(2,1)S(1)}, u32[]{:S(2)}, u32[]{:S(2)}) %collective-permute-start.2) | collective-permute-done | bytes 73760 | tf_op jit(solution)/shard_map/ppermute | solution.py:436
  26.5 0.0 collective-permute-done.4.refs_3_
  26.5 0.0 copy-done
  26.5 0.4 %kl_project.3 = bf16[288,128]{1,0:T(8,128)(2,1)S(1)} custom-call(s32[8,640]{1,0:T(8,128)S(1)} %get-tuple-element.17.slot_column, s32[8,640]{1,0:T(8,128)S(1)} %get-tuple-element.18.rows_column, bf16[4,128,256]{2,1,0:T(8,128)(2,1)S(1)} %copy-done, bf16[288,128]{1,0:T(8,128)(2,1)S(1)} %get-tuple-element.23.refs_0_, ...), custom_call_target="tpu_custom_call" | custom-call | flops 83886080 | bytes 262144 | tf_op jit(solution)/shard_map/kl_project/pallas_call | solution.py:375
  27.0 1.5 %collective-permute-start.5 = (bf16[288,128]{1,0:T(8,128)(2,1)S(1)}, bf16[288,128]{1,0:T(8,128)(2,1)S(1)}, u32[]{:S(2)}, u32[]{:S(2)}) collective-permute-start(bf16[288,128]{1,0:T(8,128)(2,1)S(1)} %kl_project.3), channel_id=1, source_target_pairs={{0,2},{2,0},{1,3},{3,1},{4,6},{6,4},{5,7},{7,5},{8,10},{10,8},{9,1... | collective-permute-start | bytes 221192 | tf_op jit(solution)/shard_map/ppermute | solution.py:441
  28.5 0.4 %kl_project.2.mine = f32[288,128]{1,0:T(8,128)S(1)} custom-call(s32[8,640]{1,0:T(8,128)S(1)} %get-tuple-element.17.slot_column, s32[8,640]{1,0:T(8,128)S(1)} %get-tuple-element.18.rows_column, bf16[4,128,256]{2,1,0:T(8,128)(2,1)S(1)} %copy-done, bf16[288,128]{1,0:T(8,128)(2,1)S(1)} %get-tuple-element.23.refs_0_, ...), custom_call_target="tpu_custom_call" | custom-call | flops 83886080 | bytes 262144 | tf_op jit(solution)/shard_map/kl_project/pallas_call | solution.py:375
  28.9 2.4 %collective-permute-done.5.got = bf16[288,128]{1,0:T(8,128)(2,1)S(1)} collective-permute-done((bf16[288,128]{1,0:T(8,128)(2,1)S(1)}, bf16[288,128]{1,0:T(8,128)(2,1)S(1)}, u32[]{:S(2)}, u32[]{:S(2)}) %collective-permute-start.5) | collective-permute-done | bytes 73760 | tf_op jit(solution)/shard_map/ppermute | solution.py:441
  31.3 1.0 %unpack.1 = f32[4,64,256]{2,1,0:T(8,128)} custom-call(s32[8,128]{1,0:T(8,128)S(1)} %get-tuple-element.16.scalars, f32[288,128]{1,0:T(8,128)S(1)} %kl_project.2.mine, bf16[288,128]{1,0:T(8,128)(2,1)S(1)} %collective-permute-done.5.got), custom_call_target="tpu_custom_call" | custom-call | flops 36864 | bytes 368640 | tf_op jit(solution)/shard_map/unpack/pallas_call | solution.py:393
Async XLA Ops:
  0.0 26.5 %copy-start = (bf16[4,128,256]{2,1,0:T(8,128)(2,1)S(1)}, bf16[4,128,256]{2,1,0:T(8,128)(2,1)}, u32[]{:S(2)}) copy-start(bf16[4,128,256]{2,1,0:T(8,128)(2,1)} %kl.3) | copy-start | bytes 786436
  13.6 1.5 %collective-permute-start = (f32[1,5,64,128]{3,2,1,0:T(8,128)S(1)}, f32[1,5,64,128]{3,2,1,0:T(8,128)S(1)}, u32[]{:S(2)}, u32[]{:S(2)}) collective-permute-start(f32[1,5,64,128]{3,2,1,0:T(8,128)S(1)} %get-tuple-element.21), channel_id=1, source_target_pairs={{0,1},{1,0},{2,3},{3,2},{4,5},{5,4},{6,7},{7,6},{8,9},{9,8},{10,11... | collective-permute-start | bytes 491528 | tf_op jit(solution)/shard_map/ppermute | solution.py:430
  15.1 5.2 %collective-permute-start.1 = (f32[3,5,64,128]{3,2,1,0:T(8,128)S(1)}, f32[3,5,64,128]{3,2,1,0:T(8,128)S(1)}, u32[]{:S(2)}, u32[]{:S(2)}) collective-permute-start(f32[3,5,64,128]{3,2,1,0:T(8,128)S(1)} %get-tuple-element.22), channel_id=1, source_target_pairs={{0,1},{1,0},{2,3},{3,2},{4,5},{5,4},{6,7},{7,6},{8,9},{9,8},{10,11... | collective-permute-start | bytes 1474568 | tf_op jit(solution)/shard_map/ppermute | solution.py:432
  15.6 7.8 %collective-permute-start.3 = (bf16[288,128]{1,0:T(8,128)(2,1)S(1)}, bf16[288,128]{1,0:T(8,128)(2,1)S(1)}, u32[]{:S(2)}, u32[]{:S(2)}) collective-permute-start(bf16[288,128]{1,0:T(8,128)(2,1)S(1)} %sum_pair.3), channel_id=1, source_target_pairs={{0,12},{4,8},{8,4},{12,0},{1,13},{5,9},{9,5},{13,1},{2,14},{6,10},... | collective-permute-start | bytes 221192 | tf_op jit(solution)/shard_map/ppermute | solution.py:436
  20.4 6.1 %collective-permute-start.2 = (bf16[288,128]{1,0:T(8,128)(2,1)S(1)}, bf16[288,128]{1,0:T(8,128)(2,1)S(1)}, u32[]{:S(2)}, u32[]{:S(2)}) collective-permute-start(bf16[288,128]{1,0:T(8,128)(2,1)S(1)} %get-tuple-element.24), channel_id=1, source_target_pairs={{0,4},{4,12},{8,0},{12,8},{1,5},{5,13},{9,1},{13,9},{2,6},{6,14},{... | collective-permute-start | bytes 221192 | tf_op jit(solution)/shard_map/ppermute | solution.py:436
  20.5 6.0 %collective-permute-start.4 = (bf16[288,128]{1,0:T(8,128)(2,1)S(1)}, bf16[288,128]{1,0:T(8,128)(2,1)S(1)}, u32[]{:S(2)}, u32[]{:S(2)}) collective-permute-start(bf16[288,128]{1,0:T(8,128)(2,1)S(1)} %get-tuple-element.26), channel_id=1, source_target_pairs={{0,8},{4,0},{8,12},{12,4},{1,9},{5,1},{9,13},{13,5},{2,10},{6,2},{... | collective-permute-start | bytes 221192 | tf_op jit(solution)/shard_map/ppermute | solution.py:436
  27.0 4.4 %collective-permute-start.5 = (bf16[288,128]{1,0:T(8,128)(2,1)S(1)}, bf16[288,128]{1,0:T(8,128)(2,1)S(1)}, u32[]{:S(2)}, u32[]{:S(2)}) collective-permute-start(bf16[288,128]{1,0:T(8,128)(2,1)S(1)} %kl_project.3), channel_id=1, source_target_pairs={{0,2},{2,0},{1,3},{3,1},{4,6},{6,4},{5,7},{7,5},{8,10},{10,8},{9,1... | collective-permute-start | bytes 221192 | tf_op jit(solution)/shard_map/ppermute | solution.py:441
